TPU v7x, 256 devices: a whole 4x4x8 slice. The times are simulated.
256 devices in a mesh: grp: 8 (over z_hi, core), blk: 32 (over y, x, z_lo).
Axes of the slice: x: 4, y: 4, z: 8 (z_hi: 4, z_lo: 2; z = z_hi * 2 + z_lo), core: 2. Of those that a mesh axis runs over, the one named last changes fastest.
Arguments:
- integrals: bfloat16 [2, 5120, 20480], P(None, 'blk', 'grp'), may hold values from -0.59765625 to 0.59765625
- tiles: bfloat16 [1440, 128, 128], P('grp'), may hold values from -0.1875 to 0.1875
- tile_index: int32 [1440, 2], P('grp'), may hold values from 0 to 159, as said below
- vir_energy: float32 [5120], replicated, may hold values from 0.5 to 4
- occ_energy: float32 [1000], replicated, may hold values from -3 to -0.5
- pair_index: int32 [2], replicated, may hold values from 0 to 999
Outputs:
- density: bfloat16 [5120, 20480], P('blk', 'grp')
Inputs may be any that keep to these rules, and one draw needn't show every extreme that they name: tile_index[s, 1] is 0 or 1. Where it is 1, tile_index[s, 0] is c(s) + (s % 9) - 4; where it is 0, it is c(s). Every slot with (s % 9) == 4 is listed.
All inputs are finite; a program needn't handle non-finite values.
Results may differ from a plain program's by a relative error of at most 0.0057.
Values may be sent and summed in bfloat16 or wider, within the bound.
No kernel may reach another device: no remote copies, remote signals or barrier semaphores. Data moves between devices by JAX's collectives and lax.ppermute only.
A program may use at most 128 MiB of HBM per device.

v0:
```python
import functools

import jax
import jax.numpy as jnp
from jax import lax
from jax.experimental import pallas as pl
from jax.experimental.pallas import tpu as pltpu
from jax.sharding import PartitionSpec as P

TILE = 128
HB = 4
BAND = 2 * HB + 1
ROWS = 160
AUX = 2560
HALO = HB * TILE
bf16 = jnp.bfloat16
f32 = jnp.float32
MIB = 1 << 20


def blk_index(y, x, z):
    return ((y % 4) * 4 + x % 4) * 2 + z


PLACES = [(y, x, z) for y in range(4) for x in range(4) for z in range(2)]


def send_y(v, step):
    pairs = [(blk_index(y, x, z), blk_index(y + step, x, z)) for y, x, z in PLACES]
    return lax.ppermute(v, "blk", pairs)


def send_x(v, step):
    pairs = [(blk_index(y, x, z), blk_index(y, x + step, z)) for y, x, z in PLACES]
    return lax.ppermute(v, "blk", pairs)


def send_z(v):
    pairs = [(blk_index(y, x, z), blk_index(y, x, 1 - z)) for y, x, z in PLACES]
    return lax.ppermute(v, "blk", pairs)


def send_core(v):
    return lax.ppermute(v, "grp", [(g, g ^ 1) for g in range(8)])


def send_high(v, step):
    return lax.ppermute(v, "grp", [(g, (g + 2 * step) % 8) for g in range(8)])


def params(mib=28):
    return pltpu.CompilerParams(vmem_limit_bytes=mib * MIB)


def cost():
    return pl.CostEstimate(flops=1000, bytes_accessed=1000, transcendentals=0)


def position():
    group = lax.axis_index("grp").astype(jnp.int32)
    me = lax.axis_index("blk").astype(jnp.int32)
    return group // 2, group % 2, me // 8, (me // 2) % 4, me % 2


ANY = pl.BlockSpec(memory_space=pl.ANY)
VMEM = pl.BlockSpec(memory_space=pltpu.VMEM)
SMEM = pl.BlockSpec(memory_space=pltpu.SMEM)
DMA = pltpu.SemaphoreType.DMA
HALF = ROWS // 2
SHARE = ROWS // 2
WIDE = 4 * ROWS
K2 = AUX // 2
K4 = AUX // 4


def hbm(shape, dtype=bf16):
    return jax.ShapeDtypeStruct(shape, dtype)


def vmem(shape, dtype=bf16):
    return pltpu.VMEM(shape, dtype)


def call(kernel, args, outs, scratch=(), name=None, aliases=None, mib=28):
    return pl.pallas_call(
        kernel,
        in_specs=[spec for _, spec in args],
        out_specs=[VMEM] * len(outs),
        out_shape=list(outs),
        scratch_shapes=list(scratch),
        input_output_aliases=aliases or {},
        compiler_params=params(mib),
        cost_estimate=cost(),
        name=name,
    )(*[a for a, _ in args])


INNER = (2, 3, 4, 5, 6, 7)
EDGE = (0, 1, 8, 9)


def fit_inner_kernel(index, own_in, tiles_in, a, b, own, edge, tiles, weights, own_sem, sems):
    own_copies = [
        pltpu.make_async_copy(
            own_in.at[pl.ds(i * ROWS, ROWS)], own.at[pl.ds(i * ROWS, ROWS)], own_sem.at[i]
        )
        for i in range(2)
    ]
    copies = {}
    for p in INNER + EDGE:
        part = pl.ds(p * 2 * BAND, 2 * BAND)
        copies[p] = pltpu.make_async_copy(tiles_in.at[part], tiles.at[part], sems.at[p])
    copies[INNER[0]].start()
    for c in own_copies:
        c.start()
    for p in (INNER + EDGE)[1:]:
        copies[p].start()
    zero = jnp.zeros((TILE, TILE), bf16)

    def build(p, out):
        out[:TILE, TILE:] = zero
        out[BAND * TILE :, :TILE] = zero
        for q in range(2):
            for o in range(BAND):
                slot = p * 2 * BAND + q * BAND + o
                at = (q + o) * TILE
                out[at : at + TILE, q * TILE : (q + 1) * TILE] = jnp.where(
                    index[1, slot] == 1, tiles[slot], zero
                )

    for p in INNER:
        copies[p].wait()
        if p == INNER[0]:
            for c in own_copies:
                c.wait()
        build(p, weights)
        window = own[:, (2 * p - HB) * TILE : (2 * p + HB + 2) * TILE]
        fitted = jnp.dot(window, weights[...], preferred_element_type=f32).astype(bf16)
        columns = slice(p * 2 * TILE, (p + 1) * 2 * TILE)
        a[:, columns] = fitted[:ROWS]
        b[:, columns] = fitted[ROWS:]
    for n, p in enumerate(EDGE):
        copies[p].wait()
        build(p, edge.at[n])


def fit_edge_kernel(left, right, own, edge, _, __, a, b, ext):
    ext[:, :HALO] = left[...]
    ext[:, HALO : 3 * HALO] = own[:, : 2 * HALO]
    ext[:, 3 * HALO : 5 * HALO] = own[:, AUX - 2 * HALO :]
    ext[:, 5 * HALO :] = right[...]
    for n, p in enumerate(EDGE):
        at = (0, 2, 12, 14)[n] * TILE
        window = ext[:, at : at + (BAND + 1) * TILE]
        fitted = jnp.dot(window, edge[n], preferred_element_type=f32).astype(bf16)
        columns = slice(p * 2 * TILE, (p + 1) * 2 * TILE)
        a[:, columns] = fitted[:ROWS]
        b[:, columns] = fitted[ROWS:]


def fit(index, own, tiles, left, right):
    banded = ((BAND + 1) * TILE, 2 * TILE)
    a, b, own, edge = call(
        fit_inner_kernel,
        [(index, SMEM), (own, ANY), (tiles, ANY)],
        [vmem((ROWS, AUX)), vmem((ROWS, AUX)), vmem((2 * ROWS, AUX)), vmem((4, *banded))],
        [pltpu.VMEM(tiles.shape, bf16), pltpu.VMEM(banded, bf16), DMA((2,)), DMA((10,))],
        name="fit_inner",
        mib=56,
    )
    return call(
        fit_edge_kernel,
        [(v, VMEM) for v in (left, right, own, edge, a, b)],
        [vmem((ROWS, AUX))] * 2,
        [pltpu.VMEM((2 * ROWS, 6 * HALO), bf16)],
        name="fit_edge",
        aliases={4: 0, 5: 1},
    )


def ends_kernel(own, last, first, sems):
    copies = [
        pltpu.make_async_copy(own.at[:, pl.ds(AUX - HALO, HALO)], last, sems.at[0]),
        pltpu.make_async_copy(own.at[:, pl.ds(0, HALO)], first, sems.at[1]),
    ]
    for c in copies:
        c.start()
    for c in copies:
        c.wait()


def ends(own):
    outs = [vmem((2 * ROWS, HALO))] * 2
    return call(ends_kernel, [(own, ANY)], outs, [DMA((2,))], name="ends", mib=60)


def cut(parts, after=(), name=None):
    def kernel(*refs):
        ins, outs, sems = refs[: len(parts)], refs[-1 - len(parts) : -1], refs[-1]
        copies = [
            pltpu.make_async_copy(i.at[pl.ds(r, n)], o, sems.at[j])
            for j, (i, o, (_, r, n)) in enumerate(zip(ins, outs, parts))
        ]
        for c in copies:
            c.start()
        for c in copies:
            c.wait()

    return pl.pallas_call(
        kernel,
        in_specs=[ANY] * (len(parts) + len(after)),
        out_specs=[ANY] * len(parts),
        out_shape=[hbm((n, AUX)) for _, _, n in parts],
        scratch_shapes=[DMA((len(parts),))],
        compiler_params=params(),
        cost_estimate=cost(),
        name=name,
    )(*[p[0] for p in parts], *after)


def arrive(parts, after):
    n = len(parts)
    return pl.pallas_call(
        lambda *refs: None,
        in_specs=[ANY] * (n + len(after)),
        out_specs=[ANY] * n,
        out_shape=[hbm(v.shape, v.dtype) for v in parts],
        input_output_aliases={i: i for i in range(n)},
        compiler_params=params(),
        cost_estimate=cost(),
        name="arrive",
    )(*parts, *after)


def row_copies(moves, out, sems, part):
    columns = pl.ds(pl.multiple_of(part * K4, K4), K4)
    return [
        pltpu.make_async_copy(
            v.at[pl.ds(r, n), columns], out.at[pl.ds(at, n), columns], sems.at[i, part]
        )
        for i, (v, r, n, at) in enumerate(moves)
    ]


def b_moves(parts, at=0):
    moves = []
    for p in parts:
        moves.append((p, 0, p.shape[0], at))
        at += p.shape[0]
    return moves


def products(copies, acat, bcat, wanted):
    for part in range(4):
        for c in copies(part):
            c.start()

    @pl.loop(0, 4)
    def _(part):
        for c in copies(part):
            c.wait()
        columns = pl.ds(pl.multiple_of(part * K4, K4), K4)
        for a_rows, b_rows, total in wanted:
            value = lax.dot_general(
                acat[a_rows, columns], bcat[b_rows, columns], (((1,), (1,)), ((), ())),
                preferred_element_type=f32,
            )

            @pl.when(part == 0)
            def _():
                total[...] = value

            @pl.when(part > 0)
            def _():
                total[...] += value


def pair_first_kernel(own, ax, am, *refs):
    b_refs = refs[:4]
    total, bcat, acat, a_sems, b_sems = refs[4:]
    a_moves = [
        (own, 0, ROWS, 0),
        (ax, 0, HALF, ROWS),
        (ax, HALF, HALF, 2 * ROWS),
        (am, 0, HALF, 2 * ROWS + HALF),
        (am, HALF, HALF, ROWS + HALF),
    ]
    rows = slice(0, 3 * ROWS)
    products(
        lambda part: row_copies(a_moves, acat, a_sems, part)
        + row_copies(b_moves(b_refs), bcat, b_sems, part),
        acat, bcat, [(rows, slice(0, WIDE), total.at[rows])],
    )


def pair_first(a_parts, b_parts):
    return call(
        pair_first_kernel,
        [(v, ANY) for v in (*a_parts, *b_parts)],
        [vmem((WIDE, WIDE), f32), vmem((2 * WIDE, AUX)), vmem((WIDE, AUX))],
        [DMA((5, 4)), DMA((4, 4))],
        name="pair_first",
    )


def pair_early_kernel(first_in, bcat_in, acat_in, ad, *refs):
    b_refs = refs[:3]
    first, bcat, acat, early, a_sems, b_sems = refs[3:]
    rows = slice(3 * ROWS, WIDE)
    products(
        lambda part: row_copies([(ad, 0, ROWS, 3 * ROWS)], acat, a_sems, part)
        + row_copies(b_moves(b_refs, WIDE), bcat, b_sems, part),
        acat, bcat,
        [
            (rows, slice(0, WIDE), first.at[rows]),
            (slice(0, WIDE), slice(WIDE, 7 * ROWS), early),
        ],
    )


def pair_early(first, bcat, acat, ad, b_parts):
    return call(
        pair_early_kernel,
        [(v, VMEM) for v in (first, bcat, acat)] + [(v, ANY) for v in (ad, *b_parts)],
        [
            vmem((WIDE, WIDE), f32),
            vmem((2 * WIDE, AUX)),
            vmem((WIDE, AUX)),
            vmem((WIDE, 3 * ROWS), f32),
        ],
        [DMA((1, 4)), DMA((3, 4))],
        name="pair_early",
        aliases={0: 0, 1: 1, 2: 2},
    )


def pair_late_kernel(first, early, acat, bcat_in, *refs):
    b_refs = refs[:3]
    keep, send, bcat, late, sems = refs[3:]
    products(
        lambda part: row_copies(b_moves(b_refs, 7 * ROWS), bcat, sems, part),
        acat, bcat, [(slice(0, WIDE), slice(7 * ROWS, 8 * ROWS), late)],
    )
    core = position()[1]
    split = 3 * ROWS

    @pl.when(core == 0)
    def _():
        keep[...] = first[...]
        send[:, :split] = early[...].astype(bf16)
        send[:, split:] = late[...].astype(bf16)

    @pl.when(core == 1)
    def _():
        send[...] = first[...].astype(bf16)
        keep[:, :split] = early[...]
        keep[:, split:] = late[...]


def pair_late(first, early, acat, bcat, b_parts):
    return call(
        pair_late_kernel,
        [(v, VMEM) for v in (first, early, acat, bcat)] + [(v, ANY) for v in b_parts],
        [vmem((WIDE, WIDE), f32), hbm((WIDE, WIDE)), vmem((2 * WIDE, AUX))],
        [pltpu.VMEM((WIDE, ROWS), f32), DMA((3, 4))],
        name="pair_late",
        aliases={3: 2},
    )


def core_sum_kernel(keep, got_in, own, s1, s2, s3, got, sem):
    copy = pltpu.make_async_copy(got_in, got, sem)
    copy.start()
    copy.wait()
    high = position()[0]
    for step, out in enumerate((own, s1, s2, s3)):
        for wave in range(2):
            at = pl.multiple_of((1 - wave) * 2 * ROWS + ((high + step) % 4) * SHARE, SHARE)
            value = keep[pl.ds(at, SHARE)] + got[pl.ds(at, SHARE)].astype(f32)
            out[wave * SHARE : (wave + 1) * SHARE] = value.astype(out.dtype)


def core_sum(keep, got):
    share = (2 * SHARE, WIDE)
    return call(
        core_sum_kernel,
        [(keep, VMEM), (got, ANY)],
        [vmem(share, f32)] + [hbm(share)] * 3,
        [pltpu.VMEM(got.shape, bf16), DMA(())],
        name="core_sum",
    )


BLOCKS = (((0, 0), (3, 0), (1, 0), (0, 1)), ((3, 1), (2, 0), (1, 1), (2, 1)))


def amplitude_kernel(vir, occ, chosen, own, *refs):
    arrived, outs, got, sems = refs[:3], refs[3:5], refs[5], refs[6]
    copies = [
        pltpu.make_async_copy(r, got.at[i], sems.at[i]) for i, r in enumerate(arrived)
    ]
    for c in copies:
        c.start()
    high, core, y, x, z = position()
    occ_total = occ[chosen[0]] + occ[chosen[1]]
    lane = lax.broadcasted_iota(jnp.int32, (SHARE, ROWS), 1)
    row = lax.broadcasted_iota(jnp.int32, (SHARE, ROWS), 0)

    def row_energy(shift, second):
        block = vir[pl.ds((y * 4 + (x + shift) % 4) * 2 + z, 1), :]
        own_lane = lane == row + second * SHARE
        return jnp.sum(jnp.where(own_lane, block, 0.0), axis=1, keepdims=True)

    rows = (
        row_energy(
            jnp.where(high == 0, 1, jnp.where(high == 1, 3, 2)),
            jnp.where((high == 0) | (high == 3), 1, 0),
        ),
        row_energy(jnp.where(high < 2, 0, 2 * high - 3), high % 2),
    )
    places = []
    for first, last in zip(*BLOCKS):
        step = jnp.where(core == 0, first[0], last[0])
        away = jnp.where(core == 0, first[1], last[1])
        places.append((((y + step) % 4) * 4 + x) * 2 + jnp.where(away == 1, 1 - z, z))
    columns = jnp.concatenate([vir[pl.ds(at, 1), :] for at in places], axis=1)
    for c in copies:
        c.wait()
    for wave, out in enumerate(outs):
        part = slice(wave * SHARE, (wave + 1) * SHARE)
        total = own[part]
        for i in range(3):
            total = total + got[i, part].astype(f32)
        denominator = (rows[wave] + columns) - occ_total
        out[...] = (total / denominator).astype(bf16)


def amplitude(vir, occ, chosen, own, arrived):
    return call(
        amplitude_kernel,
        [(vir, VMEM), (occ, SMEM), (chosen, SMEM), (own, VMEM)]
        + [(v, ANY) for v in arrived],
        [hbm((SHARE, WIDE))] * 2,
        [pltpu.VMEM((3, *own.shape), bf16), DMA((3,))],
        name="amplitude",
    )


def gather_rows(mine, other, tcat, sems):
    high, core = position()[:2]
    copies = []
    for k in range(4):
        rows = pl.ds(pl.multiple_of(((high - k + 4) % 4) * SHARE, SHARE), SHARE)
        for i, (v, of) in enumerate(((mine[k], core), (other[k], 1 - core))):
            columns = pl.ds(pl.multiple_of(of * WIDE, WIDE), WIDE)
            copies.append(pltpu.make_async_copy(v, tcat.at[rows, columns], sems.at[k, i]))
    for c in copies:
        c.start()
    return copies


def product(tcat, bcat, half):
    columns = pl.ds(pl.multiple_of(half * K2, K2), K2)
    return columns, jnp.dot(tcat[...], bcat[:, columns], preferred_element_type=f32)


TCAT = (2 * ROWS, 2 * WIDE)


def density_first_kernel(*refs):
    mine, other, bcat = refs[:4], refs[4:8], refs[8]
    outs, tcat, sems = refs[-6:-2], refs[-2], refs[-1]
    for c in gather_rows(mine, other, tcat, sems):
        c.wait()

    @pl.loop(0, 2)
    def _(half):
        columns, value = product(tcat, bcat, half)
        for i, out in enumerate(outs):
            out[:, columns] = value[i * HALF : (i + 1) * HALF].astype(bf16)


def density_first(mine, other, bcat, after):
    return call(
        density_first_kernel,
        [(v, ANY) for v in (*mine, *other)] + [(bcat, VMEM)] + [(v, ANY) for v in after],
        [hbm((HALF, AUX))] * 4,
        [pltpu.VMEM(TCAT, bf16), DMA((4, 2))],
        name="density_first",
    )


def density_second_kernel(*refs):
    mine, other, (bcat, from_m, from_x) = refs[:4], refs[4:8], refs[8:11]
    x1, m2, own, tcat, got_m, got_x, row_sems, sems = refs[11:]
    rows_copies = gather_rows(mine, other, tcat, row_sems)
    copies = [
        pltpu.make_async_copy(from_m, got_m, sems.at[0]),
        pltpu.make_async_copy(from_x, got_x, sems.at[1]),
    ]
    for c in copies:
        c.start()
    for c in rows_copies + copies:
        c.wait()

    @pl.loop(0, 2)
    def _(half):
        columns, value = product(tcat, bcat, half)
        x = value[ROWS : ROWS + HALF] + got_m[:, columns].astype(f32)
        m = value[ROWS + HALF :] + got_x[:, columns].astype(f32)
        x1[:, columns] = x.astype(bf16)
        m2[:, columns] = m.astype(bf16)
        own[:, columns] = value[:ROWS]


def density_second(mine, other, bcat, from_m, from_x):
    return call(
        density_second_kernel,
        [(v, ANY) for v in (*mine, *other)]
        + [(bcat, VMEM), (from_m, ANY), (from_x, ANY)],
        [hbm((HALF, AUX))] * 2 + [vmem((ROWS, AUX), f32)],
        [pltpu.VMEM(TCAT, bf16)]
        + [pltpu.VMEM((HALF, AUX), bf16)] * 2
        + [DMA((4, 2)), DMA((2,))],
        name="density_second",
    )


def add_kernel(own, one, two, out, got, sems):
    copies = [
        pltpu.make_async_copy(v, got.at[pl.ds(i * HALF, HALF)], sems.at[i])
        for i, v in enumerate((one, two))
    ]
    for c in copies:
        c.start()
    for c in copies:
        c.wait()
    out[...] = (own[...] + got[...].astype(f32)).astype(out.dtype)


def add(own, one, two, out):
    return call(
        add_kernel,
        [(own, VMEM), (one, ANY), (two, ANY)],
        [out],
        [pltpu.VMEM((ROWS, AUX), bf16), DMA((2,))],
        name="add",
    )[0]


def local(integrals, tiles, tile_index, vir_energy, occ_energy, pair_index):
    window = integrals.reshape(2 * ROWS, AUX)
    vir = vir_energy.reshape(-1, ROWS)
    up = [(g, g + 1) for g in range(7)]
    down = [(g + 1, g) for g in range(7)]
    last, first = ends(window)
    left = lax.ppermute(last, "grp", up)
    right = lax.ppermute(first, "grp", down)
    a, b = fit(tile_index.T, window, tiles, left, right)

    with jax.named_scope("first"):
        bm = send_y(b, 1)
        bp = send_y(b, -1)
        bo = send_z(b)
        ax = send_x(a, -1)
        am = send_x(a, 1)
    bo, bp, ax = arrive((bo, bp, ax), (bm, am, vir))
    with jax.named_scope("second"):
        bom = send_y(bo, 1)
        b2 = send_y(bp, -1)
        bop = send_z(bp)
        ad = send_x(ax, -1)
    early_sums, bcat, acat = pair_first((a, ax, am), (b, bm, bp, bo))
    c1, c2, c3 = cut([(b2, 0, 64), (bom, 64, 48), (bop, 112, 48)], (early_sums,), name="cut_b")
    with jax.named_scope("third"):
        c1 = send_z(c1)
        c2 = send_y(c2, 1)
        c3 = send_y(c3, -1)
    early_sums, bcat, acat, early = pair_early(early_sums, bcat, acat, ad, (bom, b2, bop))
    keep, send, bcat = pair_late(early_sums, early, acat, bcat, (c1, c2, c3))
    with jax.named_scope("core"):
        own, *s = core_sum(keep, send_core(send))
    with jax.named_scope("shares"):
        arrived = [send_high(v, k + 1) for k, v in enumerate(s)]
    mine = amplitude(vir, occ_energy, pair_index, own, arrived)

    def spread(wave):
        with jax.named_scope(f"spread_{wave}"):
            return [mine[wave]] + [send_high(mine[wave], k) for k in (1, 2, 3)]

    def other_core(wave, mine):
        with jax.named_scope(f"other_{wave}"):
            return [send_core(v) for v in mine]

    mine0, mine1 = spread(0), spread(1)
    other0 = other_core(0, mine0)
    other1 = other_core(1, mine1)
    x2, m1, to_d1, to_d2 = density_first(mine0, other0, bcat, (mine1[2],))
    with jax.named_scope("out"):
        from_m = send_x(to_d1, 1)
        from_x = send_x(to_d2, -1)
        got_x2 = send_x(x2, 1)
        got_m1 = send_x(m1, -1)
    x1, m2, own = density_second(mine1, other1, bcat, from_m, from_x)
    with jax.named_scope("out"):
        got_x1 = send_x(x1, 1)
        got_m2 = send_x(m2, -1)
    own = add(own, got_m1, got_x2, vmem((ROWS, AUX), f32))
    return add(own, got_x1, got_m2, hbm((ROWS, AUX)))


def solution(mesh):
    in_specs = (P(None, "blk", "grp"), P("grp", None, None), P("grp", None), P(), P(), P())
    return jax.shard_map(
        local, mesh=mesh, in_specs=in_specs, out_specs=P("blk", "grp"), check_vma=False
    )
```

profile of v0, /device:TPU:1, one launch (start us, length us, event | category | flops | bytes accessed | tf_op | source)
XLA Modules:
  0.0 172.1 jit_solution(10465515482038711588)
XLA Ops:
  0.0 1.1 ends.1
  1.1 6.3 %collective-permute-start = (bf16[320,512]{1,0:T(8,128)(2,1)S(1)}, bf16[320,512]{1,0:T(8,128)(2,1)S(1)}, u32[]{:S(2)}, u32[]{:S(2)}) collective-permute-start(bf16[320,512]{1,0:T(8,128)(2,1)S(1)} %get-tuple-element.42), channel_id=1, source_target_pairs={{0,32},{32,64},{64,96},{96,128},{128,160},{160,192},{192,224},{1,3... | collective-permute-start | bytes 983048 | tf_op jit(solution)/shard_map/ppermute | solution.py:557
  7.4 1.9 %collective-permute-start.1 = (bf16[320,512]{1,0:T(8,128)(2,1)S(1)}, bf16[320,512]{1,0:T(8,128)(2,1)S(1)}, u32[]{:S(2)}, u32[]{:S(2)}) collective-permute-start(bf16[320,512]{1,0:T(8,128)(2,1)S(1)} %get-tuple-element.43), channel_id=1, source_target_pairs={{32,0},{64,32},{96,64},{128,96},{160,128},{192,160},{224,192},{33,... | collective-permute-start | bytes 983048 | tf_op jit(solution)/shard_map/ppermute | solution.py:558
  9.3 8.0 %fit_inner.1 = (bf16[160,2560]{1,0:T(8,128)(2,1)S(1)}, bf16[160,2560]{1,0:T(8,128)(2,1)S(1)}, bf16[320,2560]{1,0:T(8,128)(2,1)S(1)}, bf16[4,1280,256]{2,1,0:T(8,128)(2,1)S(1)}) custom-call(s32[2,180]{1,0:T(2,128)} %bitcast.4, bf16[320,2560]{1,0:T(8,128)(2,1)} %bitcast.3, bf16[180,128,128]{2,1,0:T(8,128)(2,1)} %tiles_in.1), custom_call_target="tpu_custom_call" | custom-call | flops 1000 | bytes 1000 | tf_op jit(solution)/shard_map/fit_inner/pallas_call | solution.py:85
  17.3 3.1 %collective-permute-done.1.right = bf16[320,512]{1,0:T(8,128)(2,1)S(1)} collective-permute-done((bf16[320,512]{1,0:T(8,128)(2,1)S(1)}, bf16[320,512]{1,0:T(8,128)(2,1)S(1)}, u32[]{:S(2)}, u32[]{:S(2)}) %collective-permute-start.1) | collective-permute-done | bytes 327712 | tf_op jit(solution)/shard_map/ppermute | solution.py:558
  20.5 1.0 fit_edge.1
  21.5 1.0 collective-permute-start.6
  22.5 1.8 %collective-permute-start.4 = (bf16[160,2560]{1,0:T(8,128)(2,1)S(1)}, bf16[160,2560]{1,0:T(8,128)(2,1)}, u32[]{:S(2)}, u32[]{:S(2)}) collective-permute-start(bf16[160,2560]{1,0:T(8,128)(2,1)S(1)} %get-tuple-element.48.own), channel_id=1, source_target_pairs={{0,6},{1,7},{2,0},{3,1},{4,2},{5,3},{6,4},{7,5},{8,14},{9,15},{10,... | collective-permute-start | bytes 2457608 | tf_op jit(solution)/shard_map/first/ppermute | solution.py:35
  24.3 1.3 collective-permute-start.5
  25.6 1.4 collective-permute-start.3
  27.1 10.7 %collective-permute-done.6.refs_4_.am = bf16[160,2560]{1,0:T(8,128)(2,1)S(1)} collective-permute-done((bf16[160,2560]{1,0:T(8,128)(2,1)S(1)}, bf16[160,2560]{1,0:T(8,128)(2,1)S(1)}, u32[]{:S(2)}, u32[]{:S(2)}) %collective-permute-start.6) | collective-permute-done | bytes 819232 | tf_op jit(solution)/shard_map/first/ppermute | solution.py:35
  37.7 3.3 %collective-permute-done.5.refs_3_.refs_1_ = bf16[160,2560]{1,0:T(8,128)(2,1)} collective-permute-done((bf16[160,2560]{1,0:T(8,128)(2,1)S(1)}, bf16[160,2560]{1,0:T(8,128)(2,1)}, u32[]{:S(2)}, u32[]{:S(2)}) %collective-permute-start.5) | collective-permute-done | bytes 819232 | tf_op jit(solution)/shard_map/first/ppermute | solution.py:30
  41.1 2.0 %collective-permute-done.2.refs_0_ = bf16[160,2560]{1,0:T(8,128)(2,1)} collective-permute-done((bf16[160,2560]{1,0:T(8,128)(2,1)S(1)}, bf16[160,2560]{1,0:T(8,128)(2,1)}, u32[]{:S(2)}, u32[]{:S(2)}) %collective-permute-start.2) | collective-permute-done | bytes 819232 | tf_op jit(solution)/shard_map/first/ppermute | solution.py:40
  43.5 2.6 %collective-permute-start.9 = (bf16[160,2560]{1,0:T(8,128)(2,1)}, bf16[160,2560]{1,0:T(8,128)(2,1)S(1)}, u32[]{:S(2)}, u32[]{:S(2)}) collective-permute-start(bf16[160,2560]{1,0:T(8,128)(2,1)} %get-tuple-element.51.refs_2_), channel_id=1, source_target_pairs={{0,24},{1,25},{2,26},{3,27},{4,28},{5,29},{6,30},{7,31},{8,0},{9,1... | collective-permute-start | bytes 2457608 | tf_op jit(solution)/shard_map/second/ppermute | solution.py:30
  46.1 1.3 collective-permute-start.7
  47.4 4.9 %pair_first.1 = (f32[640,640]{1,0:T(8,128)S(1)}, bf16[1280,2560]{1,0:T(8,128)(2,1)S(1)}, bf16[640,2560]{1,0:T(8,128)(2,1)S(1)}) custom-call(bf16[160,2560]{1,0:T(8,128)(2,1)S(1)} %get-tuple-element.48.own, bf16[160,2560]{1,0:T(8,128)(2,1)} %get-tuple-element.50.ax, bf16[160,2560]{1,0:T(8,128)(2,1)S(1)} %collective-permute-done.6.refs_4_.am, ...), custom_call_target="tpu_custom_call" | custom-call | flops 1000 | bytes 1000 | tf_op jit(solution)/shard_map/pair_first/pallas_call | solution.py:85
  52.3 9.3 %collective-permute-done.8.refs_0_.refs_1_ = bf16[160,2560]{1,0:T(8,128)(2,1)S(1)} collective-permute-done((bf16[160,2560]{1,0:T(8,128)(2,1)}, bf16[160,2560]{1,0:T(8,128)(2,1)S(1)}, u32[]{:S(2)}, u32[]{:S(2)}) %collective-permute-start.8) | collective-permute-done | bytes 819232 | tf_op jit(solution)/shard_map/second/ppermute | solution.py:30
  61.6 1.2 collective-permute-done.9.refs_1_.refs_0_
  64.9 2.3 %collective-permute-start.13 = (bf16[48,2560]{1,0:T(8,128)(2,1)S(1)}, bf16[48,2560]{1,0:T(8,128)(2,1)S(1)}, u32[]{:S(2)}, u32[]{:S(2)}) collective-permute-start(bf16[48,2560]{1,0:T(8,128)(2,1)S(1)} %get-tuple-element.62), channel_id=1, source_target_pairs={{0,24},{1,25},{2,26},{3,27},{4,28},{5,29},{6,30},{7,31},{8,0},{9,1... | collective-permute-start | bytes 737288 | tf_op jit(solution)/shard_map/third/ppermute | solution.py:30
  67.2 5.7 %pair_early.1 = (f32[640,640]{1,0:T(8,128)S(1)}, bf16[1280,2560]{1,0:T(8,128)(2,1)S(1)}, bf16[640,2560]{1,0:T(8,128)(2,1)S(1)}, f32[640,480]{1,0:T(8,128)S(1)}) custom-call(f32[640,640]{1,0:T(8,128)S(1)} %get-tuple-element.53.first_in.refs_3_, ...), custom_call_target="tpu_custom_call", output_to_operand_aliasing={{0}: (0, {}), {1}: (1, {}), {2}: (2, {})} | custom-call | flops 1000 | bytes 1000 | tf_op jit(solution)/shard_map/pair_early/pallas_call | solution.py:85
  73.0 2.5 %pair_late.1 = (f32[640,640]{1,0:T(8,128)S(1)}, bf16[640,640]{1,0:T(8,128)(2,1)S(1)}, bf16[1280,2560]{1,0:T(8,128)(2,1)S(1)}) custom-call(f32[640,640]{1,0:T(8,128)S(1)} %get-tuple-element.56.first, f32[640,480]{1,0:T(8,128)S(1)} %get-tuple-element.57.early, bf16[640,2560]{1,0:T(8,128)(2,1)S(1)} %get-tuple-element.58.acat, ...), custom_call_target="tpu_custom_call", output_to_operand_aliasing={{2}: (3, {})} | custom-call | flops 1000 | bytes 1000 | tf_op jit(solution)/shard_map/pair_late/pallas_call | solution.py:85
  75.7 2.2 %collective-permute-done.14.got_in = bf16[640,640]{1,0:T(8,128)(2,1)S(1)} collective-permute-done((bf16[640,640]{1,0:T(8,128)(2,1)S(1)}, bf16[640,640]{1,0:T(8,128)(2,1)S(1)}, u32[]{:S(2)}, u32[]{:S(2)}) %collective-permute-start.14) | collective-permute-done | bytes 819232 | tf_op jit(solution)/shard_map/core/ppermute | solution.py:44
  78.2 7.5 %collective-permute-start.15 = (bf16[160,640]{1,0:T(8,128)(2,1)S(1)}, bf16[160,640]{1,0:T(8,128)(2,1)S(1)}, u32[]{:S(2)}, u32[]{:S(2)}) collective-permute-start(bf16[160,640]{1,0:T(8,128)(2,1)S(1)} %get-tuple-element.66), channel_id=1, source_target_pairs={{0,64},{32,96},{64,128},{96,160},{128,192},{160,224},{192,0},{224,... | collective-permute-start | bytes 614408 | tf_op jit(solution)/shard_map/shares/ppermute | solution.py:48
  85.7 3.7 %collective-permute-start.16 = (bf16[160,640]{1,0:T(8,128)(2,1)S(1)}, bf16[160,640]{1,0:T(8,128)(2,1)S(1)}, u32[]{:S(2)}, u32[]{:S(2)}) collective-permute-start(bf16[160,640]{1,0:T(8,128)(2,1)S(1)} %get-tuple-element.67), channel_id=1, source_target_pairs={{0,128},{32,160},{64,192},{96,224},{128,0},{160,32},{192,64},{224,... | collective-permute-start | bytes 614408 | tf_op jit(solution)/shard_map/shares/ppermute | solution.py:48
  89.4 3.5 %collective-permute-start.17 = (bf16[160,640]{1,0:T(8,128)(2,1)S(1)}, bf16[160,640]{1,0:T(8,128)(2,1)S(1)}, u32[]{:S(2)}, u32[]{:S(2)}) collective-permute-start(bf16[160,640]{1,0:T(8,128)(2,1)S(1)} %get-tuple-element.68), channel_id=1, source_target_pairs={{0,192},{32,224},{64,0},{96,32},{128,64},{160,96},{192,128},{224,1... | collective-permute-start | bytes 614408 | tf_op jit(solution)/shard_map/shares/ppermute | solution.py:48
  93.8 11.1 %collective-permute-done.16.refs_1_ = bf16[160,640]{1,0:T(8,128)(2,1)S(1)} collective-permute-done((bf16[160,640]{1,0:T(8,128)(2,1)S(1)}, bf16[160,640]{1,0:T(8,128)(2,1)S(1)}, u32[]{:S(2)}, u32[]{:S(2)}) %collective-permute-start.16) | collective-permute-done | bytes 204832 | tf_op jit(solution)/shard_map/shares/ppermute | solution.py:48
  104.9 3.4 %collective-permute-done.17.refs_2_ = bf16[160,640]{1,0:T(8,128)(2,1)S(1)} collective-permute-done((bf16[160,640]{1,0:T(8,128)(2,1)S(1)}, bf16[160,640]{1,0:T(8,128)(2,1)S(1)}, u32[]{:S(2)}, u32[]{:S(2)}) %collective-permute-start.17) | collective-permute-done | bytes 204832 | tf_op jit(solution)/shard_map/shares/ppermute | solution.py:48
  108.3 1.8 %amplitude.1 = (bf16[80,640]{1,0:T(8,128)(2,1)S(1)}, bf16[80,640]{1,0:T(8,128)(2,1)S(1)}) custom-call(f32[32,160]{1,0:T(8,128)S(1)} %reshape.6.refs_5_.vir, f32[1000]{0:T(1024)S(1)} %copy-done, s32[2]{0:T(128)S(1)} %copy-done.1, f32[160,640]{1,0:T(8,128)S(1)} %get-tuple-element.65.own, bf16[160,640]{1,0:T(8,128)(2,1)S(1)} %collective-permute-done.15.refs_0_, ...), custom_call_target="tpu_custom_call" | custom-call | flops 1000 | bytes 1000 | tf_op jit(solution)/shard_map/amplitude/pallas_call | solution.py:85
  110.1 3.5 %collective-permute-start.27 = (bf16[80,640]{1,0:T(8,128)(2,1)S(1)}, bf16[80,640]{1,0:T(8,128)(2,1)S(1)}, u32[]{:S(2)}, u32[]{:S(2)}) collective-permute-start(bf16[80,640]{1,0:T(8,128)(2,1)S(1)} %get-tuple-element.71.refs_0_), channel_id=1, source_target_pairs={{0,192},{32,224},{64,0},{96,32},{128,64},{160,96},{192,128},{224,1... | collective-permute-start | bytes 307208 | tf_op jit(solution)/shard_map/spread_0/ppermute | solution.py:48
  113.6 2.7 %collective-permute-start.26 = (bf16[80,640]{1,0:T(8,128)(2,1)S(1)}, bf16[80,640]{1,0:T(8,128)(2,1)S(1)}, u32[]{:S(2)}, u32[]{:S(2)}) collective-permute-start(bf16[80,640]{1,0:T(8,128)(2,1)S(1)} %get-tuple-element.71.refs_0_), channel_id=1, source_target_pairs={{0,128},{32,160},{64,192},{96,224},{128,0},{160,32},{192,64},{224,... | collective-permute-start | bytes 307208 | tf_op jit(solution)/shard_map/spread_0/ppermute | solution.py:48
  116.3 1.5 collective-permute-start.25
  117.8 1.3 collective-permute-start.28
  119.1 1.0 collective-permute-start.19
  121.2 4.9 %collective-permute-start.30 = (bf16[80,640]{1,0:T(8,128)(2,1)S(1)}, bf16[80,640]{1,0:T(8,128)(2,1)S(1)}, u32[]{:S(2)}, u32[]{:S(2)}) collective-permute-start(bf16[80,640]{1,0:T(8,128)(2,1)S(1)} %collective-permute-done.26.refs_2_), channel_id=1, source_target_pairs={{0,32},{32,0},{64,96},{96,64},{128,160},{160,128},{192,224},{224,1... | collective-permute-start | bytes 307208 | tf_op jit(solution)/shard_map/other_0/ppermute | solution.py:44
  126.1 2.4 %collective-permute-done.19.refs_9_.refs_2_ = bf16[80,640]{1,0:T(8,128)(2,1)S(1)} collective-permute-done((bf16[80,640]{1,0:T(8,128)(2,1)S(1)}, bf16[80,640]{1,0:T(8,128)(2,1)S(1)}, u32[]{:S(2)}, u32[]{:S(2)}) %collective-permute-start.19) | collective-permute-done | bytes 102432 | tf_op jit(solution)/shard_map/spread_1/ppermute | solution.py:48
  128.5 2.7 %density_first.1 = (bf16[80,2560]{1,0:T(8,128)(2,1)S(1)}, bf16[80,2560]{1,0:T(8,128)(2,1)S(1)}, bf16[80,2560]{1,0:T(8,128)(2,1)S(1)}, bf16[80,2560]{1,0:T(8,128)(2,1)S(1)}) custom-call(bf16[80,640]{1,0:T(8,128)(2,1)S(1)} %get-tuple-element.71.refs_0_, bf16[80,640]{1,0:T(8,128)(2,1)S(1)} %collective-permute-done.25.refs_1_, ...), custom_call_target="tpu_custom_call" | custom-call | flops 1000 | bytes 1000 | tf_op jit(solution)/shard_map/density_first/pallas_call | solution.py:85
  131.3 2.7 %collective-permute-start.33 = (bf16[80,2560]{1,0:T(8,128)(2,1)S(1)}, bf16[80,2560]{1,0:T(8,128)(2,1)S(1)}, u32[]{:S(2)}, u32[]{:S(2)}) collective-permute-start(bf16[80,2560]{1,0:T(8,128)(2,1)S(1)} %get-tuple-element.73), channel_id=1, source_target_pairs={{0,6},{1,7},{2,0},{3,1},{4,2},{5,3},{6,4},{7,5},{8,14},{9,15},{10,... | collective-permute-start | bytes 1228808 | tf_op jit(solution)/shard_map/out/ppermute | solution.py:35
  134.0 3.1 %collective-permute-start.20 = (bf16[80,640]{1,0:T(8,128)(2,1)S(1)}, bf16[80,640]{1,0:T(8,128)(2,1)S(1)}, u32[]{:S(2)}, u32[]{:S(2)}) collective-permute-start(bf16[80,640]{1,0:T(8,128)(2,1)S(1)} %get-tuple-element.69.refs_0_), channel_id=1, source_target_pairs={{0,192},{32,224},{64,0},{96,32},{128,64},{160,96},{192,128},{224,1... | collective-permute-start | bytes 307208 | tf_op jit(solution)/shard_map/spread_1/ppermute | solution.py:48
  137.1 2.7 %collective-permute-start.21 = (bf16[80,640]{1,0:T(8,128)(2,1)S(1)}, bf16[80,640]{1,0:T(8,128)(2,1)S(1)}, u32[]{:S(2)}, u32[]{:S(2)}) collective-permute-start(bf16[80,640]{1,0:T(8,128)(2,1)S(1)} %get-tuple-element.69.refs_0_), channel_id=1, source_target_pairs={{0,32},{32,0},{64,96},{96,64},{128,160},{160,128},{192,224},{224,1... | collective-permute-start | bytes 307208 | tf_op jit(solution)/shard_map/other_1/ppermute | solution.py:44
  139.8 3.0 %collective-permute-start.24 = (bf16[80,640]{1,0:T(8,128)(2,1)S(1)}, bf16[80,640]{1,0:T(8,128)(2,1)S(1)}, u32[]{:S(2)}, u32[]{:S(2)}) collective-permute-start(bf16[80,640]{1,0:T(8,128)(2,1)S(1)} %collective-permute-done.20.refs_3_), channel_id=1, source_target_pairs={{0,32},{32,0},{64,96},{96,64},{128,160},{160,128},{192,224},{224,1... | collective-permute-start | bytes 307208 | tf_op jit(solution)/shard_map/other_1/ppermute | solution.py:44
  142.9 3.7 %collective-permute-done.18.refs_1_ = bf16[80,640]{1,0:T(8,128)(2,1)S(1)} collective-permute-done((bf16[80,640]{1,0:T(8,128)(2,1)S(1)}, bf16[80,640]{1,0:T(8,128)(2,1)S(1)}, u32[]{:S(2)}, u32[]{:S(2)}) %collective-permute-start.18) | collective-permute-done | bytes 102432 | tf_op jit(solution)/shard_map/spread_1/ppermute | solution.py:48
  147.4 2.3 %collective-permute-start.34 = (bf16[80,2560]{1,0:T(8,128)(2,1)S(1)}, bf16[80,2560]{1,0:T(8,128)(2,1)S(1)}, u32[]{:S(2)}, u32[]{:S(2)}) collective-permute-start(bf16[80,2560]{1,0:T(8,128)(2,1)S(1)} %get-tuple-element.75), channel_id=1, source_target_pairs={{0,6},{1,7},{2,0},{3,1},{4,2},{5,3},{6,4},{7,5},{8,14},{9,15},{10,... | collective-permute-start | bytes 1228808 | tf_op jit(solution)/shard_map/out/ppermute | solution.py:35
  149.8 3.1 %density_second.1 = (bf16[80,2560]{1,0:T(8,128)(2,1)S(1)}, bf16[80,2560]{1,0:T(8,128)(2,1)S(1)}, f32[160,2560]{1,0:T(8,128)S(1)}) custom-call(bf16[80,640]{1,0:T(8,128)(2,1)S(1)} %get-tuple-element.69.refs_0_, bf16[80,640]{1,0:T(8,128)(2,1)S(1)} %collective-permute-done.18.refs_1_, bf16[80,640]{1,0:T(8,128)(2,1)S(1)} %collective-permute-done.19.refs_9_.refs_2_, ...), custom_call_target="tpu_custom_call" | custom-call | flops 1000 | bytes 1000 | tf_op jit(solution)/shard_map/density_second/pallas_call | solution.py:85
  153.0 2.7 %collective-permute-start.37 = (bf16[80,2560]{1,0:T(8,128)(2,1)S(1)}, bf16[80,2560]{1,0:T(8,128)(2,1)S(1)}, u32[]{:S(2)}, u32[]{:S(2)}) collective-permute-start(bf16[80,2560]{1,0:T(8,128)(2,1)S(1)} %get-tuple-element.78), channel_id=1, source_target_pairs={{0,6},{1,7},{2,0},{3,1},{4,2},{5,3},{6,4},{7,5},{8,14},{9,15},{10,... | collective-permute-start | bytes 1228808 | tf_op jit(solution)/shard_map/out/ppermute | solution.py:35
  155.7 2.9 %collective-permute-done.34.one = bf16[80,2560]{1,0:T(8,128)(2,1)S(1)} collective-permute-done((bf16[80,2560]{1,0:T(8,128)(2,1)S(1)}, bf16[80,2560]{1,0:T(8,128)(2,1)S(1)}, u32[]{:S(2)}, u32[]{:S(2)}) %collective-permute-start.34) | collective-permute-done | bytes 409632 | tf_op jit(solution)/shard_map/out/ppermute | solution.py:35
  158.6 3.1 %collective-permute-done.35.two = bf16[80,2560]{1,0:T(8,128)(2,1)S(1)} collective-permute-done((bf16[80,2560]{1,0:T(8,128)(2,1)S(1)}, bf16[80,2560]{1,0:T(8,128)(2,1)S(1)}, u32[]{:S(2)}, u32[]{:S(2)}) %collective-permute-start.35) | collective-permute-done | bytes 409632 | tf_op jit(solution)/shard_map/out/ppermute | solution.py:35
  162.3 8.2 %collective-permute-done.36.one = bf16[80,2560]{1,0:T(8,128)(2,1)S(1)} collective-permute-done((bf16[80,2560]{1,0:T(8,128)(2,1)S(1)}, bf16[80,2560]{1,0:T(8,128)(2,1)S(1)}, u32[]{:S(2)}, u32[]{:S(2)}) %collective-permute-start.36) | collective-permute-done | bytes 409632 | tf_op jit(solution)/shard_map/out/ppermute | solution.py:35
  170.5 1.5 add.3
  (49 shorter events, 6.6 us)
Async XLA Ops:
  1.1 16.2 %collective-permute-start = (bf16[320,512]{1,0:T(8,128)(2,1)S(1)}, bf16[320,512]{1,0:T(8,128)(2,1)S(1)}, u32[]{:S(2)}, u32[]{:S(2)}) collective-permute-start(bf16[320,512]{1,0:T(8,128)(2,1)S(1)} %get-tuple-element.42), channel_id=1, source_target_pairs={{0,32},{32,64},{64,96},{96,128},{128,160},{160,192},{192,224},{1,3... | collective-permute-start | bytes 983048 | tf_op jit(solution)/shard_map/ppermute | solution.py:557
  7.4 13.1 %collective-permute-start.1 = (bf16[320,512]{1,0:T(8,128)(2,1)S(1)}, bf16[320,512]{1,0:T(8,128)(2,1)S(1)}, u32[]{:S(2)}, u32[]{:S(2)}) collective-permute-start(bf16[320,512]{1,0:T(8,128)(2,1)S(1)} %get-tuple-element.43), channel_id=1, source_target_pairs={{32,0},{64,32},{96,64},{128,96},{160,128},{192,160},{224,192},{33,... | collective-permute-start | bytes 983048 | tf_op jit(solution)/shard_map/ppermute | solution.py:558
  20.5 6.5 %copy-start.2 = (f32[5120]{0:T(1024)S(1)}, f32[5120]{0:T(1024)}, u32[]{:S(2)}) copy-start(f32[5120]{0:T(1024)} %param.9) | copy-start | bytes 61444
  21.5 16.2 %collective-permute-start.6 = (bf16[160,2560]{1,0:T(8,128)(2,1)S(1)}, bf16[160,2560]{1,0:T(8,128)(2,1)S(1)}, u32[]{:S(2)}, u32[]{:S(2)}) collective-permute-start(bf16[160,2560]{1,0:T(8,128)(2,1)S(1)} %get-tuple-element.48.own), channel_id=1, source_target_pairs={{0,2},{1,3},{2,4},{3,5},{4,6},{5,7},{6,0},{7,1},{8,10},{9,11},{10,... | collective-permute-start | bytes 2457608 | tf_op jit(solution)/shard_map/first/ppermute | solution.py:35
  22.5 15.2 %collective-permute-start.4 = (bf16[160,2560]{1,0:T(8,128)(2,1)S(1)}, bf16[160,2560]{1,0:T(8,128)(2,1)}, u32[]{:S(2)}, u32[]{:S(2)}) collective-permute-start(bf16[160,2560]{1,0:T(8,128)(2,1)S(1)} %get-tuple-element.48.own), channel_id=1, source_target_pairs={{0,6},{1,7},{2,0},{3,1},{4,2},{5,3},{6,4},{7,5},{8,14},{9,15},{10,... | collective-permute-start | bytes 2457608 | tf_op jit(solution)/shard_map/first/ppermute | solution.py:35
  24.3 16.8 %collective-permute-start.5 = (bf16[160,2560]{1,0:T(8,128)(2,1)S(1)}, bf16[160,2560]{1,0:T(8,128)(2,1)}, u32[]{:S(2)}, u32[]{:S(2)}) collective-permute-start(bf16[160,2560]{1,0:T(8,128)(2,1)S(1)} %get-tuple-element.49.refs_0_), channel_id=1, source_target_pairs={{0,8},{1,9},{2,10},{3,11},{4,12},{5,13},{6,14},{7,15},{8,16},{9,17... | collective-permute-start | bytes 2457608 | tf_op jit(solution)/shard_map/first/ppermute | solution.py:30
  25.6 15.5 %collective-permute-start.3 = (bf16[160,2560]{1,0:T(8,128)(2,1)S(1)}, bf16[160,2560]{1,0:T(8,128)(2,1)}, u32[]{:S(2)}, u32[]{:S(2)}) collective-permute-start(bf16[160,2560]{1,0:T(8,128)(2,1)S(1)} %get-tuple-element.49.refs_0_), channel_id=1, source_target_pairs={{0,24},{1,25},{2,26},{3,27},{4,28},{5,29},{6,30},{7,31},{8,0},{9,1... | collective-permute-start | bytes 2457608 | tf_op jit(solution)/shard_map/first/ppermute | solution.py:30
  27.0 16.1 %collective-permute-start.2 = (bf16[160,2560]{1,0:T(8,128)(2,1)S(1)}, bf16[160,2560]{1,0:T(8,128)(2,1)}, u32[]{:S(2)}, u32[]{:S(2)}) collective-permute-start(bf16[160,2560]{1,0:T(8,128)(2,1)S(1)} %get-tuple-element.49.refs_0_), channel_id=1, source_target_pairs={{0,1},{1,0},{2,3},{3,2},{4,5},{5,4},{6,7},{7,6},{8,9},{9,8},{10,11... | collective-permute-start | bytes 2457608 | tf_op jit(solution)/shard_map/first/ppermute | solution.py:40
  43.1 18.5 %collective-permute-start.8 = (bf16[160,2560]{1,0:T(8,128)(2,1)}, bf16[160,2560]{1,0:T(8,128)(2,1)S(1)}, u32[]{:S(2)}, u32[]{:S(2)}) collective-permute-start(bf16[160,2560]{1,0:T(8,128)(2,1)} %get-tuple-element.52.refs_3_), channel_id=1, source_target_pairs={{0,8},{1,9},{2,10},{3,11},{4,12},{5,13},{6,14},{7,15},{8,16},{9,17... | collective-permute-start | bytes 2457608 | tf_op jit(solution)/shard_map/second/ppermute | solution.py:30
  43.1 18.5 %collective-permute-start.10 = (bf16[160,2560]{1,0:T(8,128)(2,1)}, bf16[160,2560]{1,0:T(8,128)(2,1)S(1)}, u32[]{:S(2)}, u32[]{:S(2)}) collective-permute-start(bf16[160,2560]{1,0:T(8,128)(2,1)} %get-tuple-element.51.refs_2_), channel_id=1, source_target_pairs={{0,1},{1,0},{2,3},{3,2},{4,5},{5,4},{6,7},{7,6},{8,9},{9,8},{10,11... | collective-permute-start | bytes 2457608 | tf_op jit(solution)/shard_map/second/ppermute | solution.py:40
  43.5 19.3 %collective-permute-start.9 = (bf16[160,2560]{1,0:T(8,128)(2,1)}, bf16[160,2560]{1,0:T(8,128)(2,1)S(1)}, u32[]{:S(2)}, u32[]{:S(2)}) collective-permute-start(bf16[160,2560]{1,0:T(8,128)(2,1)} %get-tuple-element.51.refs_2_), channel_id=1, source_target_pairs={{0,24},{1,25},{2,26},{3,27},{4,28},{5,29},{6,30},{7,31},{8,0},{9,1... | collective-permute-start | bytes 2457608 | tf_op jit(solution)/shard_map/second/ppermute | solution.py:30
  46.1 21.0 %collective-permute-start.7 = (bf16[160,2560]{1,0:T(8,128)(2,1)}, bf16[160,2560]{1,0:T(8,128)(2,1)S(1)}, u32[]{:S(2)}, u32[]{:S(2)}) collective-permute-start(bf16[160,2560]{1,0:T(8,128)(2,1)} %get-tuple-element.50.ax), channel_id=1, source_target_pairs={{0,6},{1,7},{2,0},{3,1},{4,2},{5,3},{6,4},{7,5},{8,14},{9,15},{10,... | collective-permute-start | bytes 2457608 | tf_op jit(solution)/shard_map/second/ppermute | solution.py:35
  63.6 9.3 %collective-permute-start.11 = (bf16[64,2560]{1,0:T(8,128)(2,1)S(1)}, bf16[64,2560]{1,0:T(8,128)(2,1)S(1)}, u32[]{:S(2)}, u32[]{:S(2)}) collective-permute-start(bf16[64,2560]{1,0:T(8,128)(2,1)S(1)} %get-tuple-element.60), channel_id=1, source_target_pairs={{0,1},{1,0},{2,3},{3,2},{4,5},{5,4},{6,7},{7,6},{8,9},{9,8},{10,11... | collective-permute-start | bytes 983048 | tf_op jit(solution)/shard_map/third/ppermute | solution.py:40
  64.2 8.8 %collective-permute-start.12 = (bf16[48,2560]{1,0:T(8,128)(2,1)S(1)}, bf16[48,2560]{1,0:T(8,128)(2,1)S(1)}, u32[]{:S(2)}, u32[]{:S(2)}) collective-permute-start(bf16[48,2560]{1,0:T(8,128)(2,1)S(1)} %get-tuple-element.61), channel_id=1, source_target_pairs={{0,8},{1,9},{2,10},{3,11},{4,12},{5,13},{6,14},{7,15},{8,16},{9,17... | collective-permute-start | bytes 737288 | tf_op jit(solution)/shard_map/third/ppermute | solution.py:30
  64.9 8.1 %collective-permute-start.13 = (bf16[48,2560]{1,0:T(8,128)(2,1)S(1)}, bf16[48,2560]{1,0:T(8,128)(2,1)S(1)}, u32[]{:S(2)}, u32[]{:S(2)}) collective-permute-start(bf16[48,2560]{1,0:T(8,128)(2,1)S(1)} %get-tuple-element.62), channel_id=1, source_target_pairs={{0,24},{1,25},{2,26},{3,27},{4,28},{5,29},{6,30},{7,31},{8,0},{9,1... | collective-permute-start | bytes 737288 | tf_op jit(solution)/shard_map/third/ppermute | solution.py:30
  75.5 32.8 %copy-start = (f32[1000]{0:T(1024)S(1)}, f32[1000]{0:T(1024)}, u32[]{:S(2)}) copy-start(f32[1000]{0:T(1024)} %occ.1) | copy-start | bytes 12004
  75.5 32.8 %copy-start.1 = (s32[2]{0:T(128)S(1)}, s32[2]{0:T(128)}, u32[]{:S(2)}) copy-start(s32[2]{0:T(128)} %chosen.1) | copy-start | bytes 28
  75.5 2.4 %collective-permute-start.14 = (bf16[640,640]{1,0:T(8,128)(2,1)S(1)}, bf16[640,640]{1,0:T(8,128)(2,1)S(1)}, u32[]{:S(2)}, u32[]{:S(2)}) collective-permute-start(bf16[640,640]{1,0:T(8,128)(2,1)S(1)} %get-tuple-element.64), channel_id=1, source_target_pairs={{0,32},{32,0},{64,96},{96,64},{128,160},{160,128},{192,224},{224,1... | collective-permute-start | bytes 2457608 | tf_op jit(solution)/shard_map/core/ppermute | solution.py:44
  78.2 15.5 %collective-permute-start.15 = (bf16[160,640]{1,0:T(8,128)(2,1)S(1)}, bf16[160,640]{1,0:T(8,128)(2,1)S(1)}, u32[]{:S(2)}, u32[]{:S(2)}) collective-permute-start(bf16[160,640]{1,0:T(8,128)(2,1)S(1)} %get-tuple-element.66), channel_id=1, source_target_pairs={{0,64},{32,96},{64,128},{96,160},{128,192},{160,224},{192,0},{224,... | collective-permute-start | bytes 614408 | tf_op jit(solution)/shard_map/shares/ppermute | solution.py:48
  85.7 19.2 %collective-permute-start.16 = (bf16[160,640]{1,0:T(8,128)(2,1)S(1)}, bf16[160,640]{1,0:T(8,128)(2,1)S(1)}, u32[]{:S(2)}, u32[]{:S(2)}) collective-permute-start(bf16[160,640]{1,0:T(8,128)(2,1)S(1)} %get-tuple-element.67), channel_id=1, source_target_pairs={{0,128},{32,160},{64,192},{96,224},{128,0},{160,32},{192,64},{224,... | collective-permute-start | bytes 614408 | tf_op jit(solution)/shard_map/shares/ppermute | solution.py:48
  89.4 18.9 %collective-permute-start.17 = (bf16[160,640]{1,0:T(8,128)(2,1)S(1)}, bf16[160,640]{1,0:T(8,128)(2,1)S(1)}, u32[]{:S(2)}, u32[]{:S(2)}) collective-permute-start(bf16[160,640]{1,0:T(8,128)(2,1)S(1)} %get-tuple-element.68), channel_id=1, source_target_pairs={{0,192},{32,224},{64,0},{96,32},{128,64},{160,96},{192,128},{224,1... | collective-permute-start | bytes 614408 | tf_op jit(solution)/shard_map/shares/ppermute | solution.py:48
  110.1 10.0 %collective-permute-start.27 = (bf16[80,640]{1,0:T(8,128)(2,1)S(1)}, bf16[80,640]{1,0:T(8,128)(2,1)S(1)}, u32[]{:S(2)}, u32[]{:S(2)}) collective-permute-start(bf16[80,640]{1,0:T(8,128)(2,1)S(1)} %get-tuple-element.71.refs_0_), channel_id=1, source_target_pairs={{0,192},{32,224},{64,0},{96,32},{128,64},{160,96},{192,128},{224,1... | collective-permute-start | bytes 307208 | tf_op jit(solution)/shard_map/spread_0/ppermute | solution.py:48
  113.6 7.6 %collective-permute-start.26 = (bf16[80,640]{1,0:T(8,128)(2,1)S(1)}, bf16[80,640]{1,0:T(8,128)(2,1)S(1)}, u32[]{:S(2)}, u32[]{:S(2)}) collective-permute-start(bf16[80,640]{1,0:T(8,128)(2,1)S(1)} %get-tuple-element.71.refs_0_), channel_id=1, source_target_pairs={{0,128},{32,160},{64,192},{96,224},{128,0},{160,32},{192,64},{224,... | collective-permute-start | bytes 307208 | tf_op jit(solution)/shard_map/spread_0/ppermute | solution.py:48
  116.3 9.8 %collective-permute-start.25 = (bf16[80,640]{1,0:T(8,128)(2,1)S(1)}, bf16[80,640]{1,0:T(8,128)(2,1)S(1)}, u32[]{:S(2)}, u32[]{:S(2)}) collective-permute-start(bf16[80,640]{1,0:T(8,128)(2,1)S(1)} %get-tuple-element.71.refs_0_), channel_id=1, source_target_pairs={{0,64},{32,96},{64,128},{96,160},{128,192},{160,224},{192,0},{224,... | collective-permute-start | bytes 307208 | tf_op jit(solution)/shard_map/spread_0/ppermute | solution.py:48
  117.8 10.8 %collective-permute-start.28 = (bf16[80,640]{1,0:T(8,128)(2,1)S(1)}, bf16[80,640]{1,0:T(8,128)(2,1)S(1)}, u32[]{:S(2)}, u32[]{:S(2)}) collective-permute-start(bf16[80,640]{1,0:T(8,128)(2,1)S(1)} %get-tuple-element.71.refs_0_), channel_id=1, source_target_pairs={{0,32},{32,0},{64,96},{96,64},{128,160},{160,128},{192,224},{224,1... | collective-permute-start | bytes 307208 | tf_op jit(solution)/shard_map/other_0/ppermute | solution.py:44
  119.1 9.4 %collective-permute-start.19 = (bf16[80,640]{1,0:T(8,128)(2,1)S(1)}, bf16[80,640]{1,0:T(8,128)(2,1)S(1)}, u32[]{:S(2)}, u32[]{:S(2)}) collective-permute-start(bf16[80,640]{1,0:T(8,128)(2,1)S(1)} %get-tuple-element.69.refs_0_), channel_id=1, source_target_pairs={{0,128},{32,160},{64,192},{96,224},{128,0},{160,32},{192,64},{224,... | collective-permute-start | bytes 307208 | tf_op jit(solution)/shard_map/spread_1/ppermute | solution.py:48
  120.1 8.4 %collective-permute-start.31 = (bf16[80,640]{1,0:T(8,128)(2,1)S(1)}, bf16[80,640]{1,0:T(8,128)(2,1)S(1)}, u32[]{:S(2)}, u32[]{:S(2)}) collective-permute-start(bf16[80,640]{1,0:T(8,128)(2,1)S(1)} %collective-permute-done.27.refs_3_), channel_id=1, source_target_pairs={{0,32},{32,0},{64,96},{96,64},{128,160},{160,128},{192,224},{224,1... | collective-permute-start | bytes 307208 | tf_op jit(solution)/shard_map/other_0/ppermute | solution.py:44
  121.2 7.3 %collective-permute-start.30 = (bf16[80,640]{1,0:T(8,128)(2,1)S(1)}, bf16[80,640]{1,0:T(8,128)(2,1)S(1)}, u32[]{:S(2)}, u32[]{:S(2)}) collective-permute-start(bf16[80,640]{1,0:T(8,128)(2,1)S(1)} %collective-permute-done.26.refs_2_), channel_id=1, source_target_pairs={{0,32},{32,0},{64,96},{96,64},{128,160},{160,128},{192,224},{224,1... | collective-permute-start | bytes 307208 | tf_op jit(solution)/shard_map/other_0/ppermute | solution.py:44
  126.1 2.4 %collective-permute-start.29 = (bf16[80,640]{1,0:T(8,128)(2,1)S(1)}, bf16[80,640]{1,0:T(8,128)(2,1)S(1)}, u32[]{:S(2)}, u32[]{:S(2)}) collective-permute-start(bf16[80,640]{1,0:T(8,128)(2,1)S(1)} %collective-permute-done.25.refs_1_), channel_id=1, source_target_pairs={{0,32},{32,0},{64,96},{96,64},{128,160},{160,128},{192,224},{224,1... | collective-permute-start | bytes 307208 | tf_op jit(solution)/shard_map/other_0/ppermute | solution.py:44
  131.2 18.5 %collective-permute-start.32 = (bf16[80,2560]{1,0:T(8,128)(2,1)S(1)}, bf16[80,2560]{1,0:T(8,128)(2,1)S(1)}, u32[]{:S(2)}, u32[]{:S(2)}) collective-permute-start(bf16[80,2560]{1,0:T(8,128)(2,1)S(1)} %get-tuple-element.72), channel_id=1, source_target_pairs={{0,2},{1,3},{2,4},{3,5},{4,6},{5,7},{6,0},{7,1},{8,10},{9,11},{10,... | collective-permute-start | bytes 1228808 | tf_op jit(solution)/shard_map/out/ppermute | solution.py:35
  131.3 18.4 %collective-permute-start.33 = (bf16[80,2560]{1,0:T(8,128)(2,1)S(1)}, bf16[80,2560]{1,0:T(8,128)(2,1)S(1)}, u32[]{:S(2)}, u32[]{:S(2)}) collective-permute-start(bf16[80,2560]{1,0:T(8,128)(2,1)S(1)} %get-tuple-element.73), channel_id=1, source_target_pairs={{0,6},{1,7},{2,0},{3,1},{4,2},{5,3},{6,4},{7,5},{8,14},{9,15},{10,... | collective-permute-start | bytes 1228808 | tf_op jit(solution)/shard_map/out/ppermute | solution.py:35
  134.0 5.8 %collective-permute-start.20 = (bf16[80,640]{1,0:T(8,128)(2,1)S(1)}, bf16[80,640]{1,0:T(8,128)(2,1)S(1)}, u32[]{:S(2)}, u32[]{:S(2)}) collective-permute-start(bf16[80,640]{1,0:T(8,128)(2,1)S(1)} %get-tuple-element.69.refs_0_), channel_id=1, source_target_pairs={{0,192},{32,224},{64,0},{96,32},{128,64},{160,96},{192,128},{224,1... | collective-permute-start | bytes 307208 | tf_op jit(solution)/shard_map/spread_1/ppermute | solution.py:48
  137.1 5.8 %collective-permute-start.21 = (bf16[80,640]{1,0:T(8,128)(2,1)S(1)}, bf16[80,640]{1,0:T(8,128)(2,1)S(1)}, u32[]{:S(2)}, u32[]{:S(2)}) collective-permute-start(bf16[80,640]{1,0:T(8,128)(2,1)S(1)} %get-tuple-element.69.refs_0_), channel_id=1, source_target_pairs={{0,32},{32,0},{64,96},{96,64},{128,160},{160,128},{192,224},{224,1... | collective-permute-start | bytes 307208 | tf_op jit(solution)/shard_map/other_1/ppermute | solution.py:44
  139.8 6.8 %collective-permute-start.18 = (bf16[80,640]{1,0:T(8,128)(2,1)S(1)}, bf16[80,640]{1,0:T(8,128)(2,1)S(1)}, u32[]{:S(2)}, u32[]{:S(2)}) collective-permute-start(bf16[80,640]{1,0:T(8,128)(2,1)S(1)} %get-tuple-element.69.refs_0_), channel_id=1, source_target_pairs={{0,64},{32,96},{64,128},{96,160},{128,192},{160,224},{192,0},{224,... | collective-permute-start | bytes 307208 | tf_op jit(solution)/shard_map/spread_1/ppermute | solution.py:48
  139.8 7.5 %collective-permute-start.24 = (bf16[80,640]{1,0:T(8,128)(2,1)S(1)}, bf16[80,640]{1,0:T(8,128)(2,1)S(1)}, u32[]{:S(2)}, u32[]{:S(2)}) collective-permute-start(bf16[80,640]{1,0:T(8,128)(2,1)S(1)} %collective-permute-done.20.refs_3_), channel_id=1, source_target_pairs={{0,32},{32,0},{64,96},{96,64},{128,160},{160,128},{192,224},{224,1... | collective-permute-start | bytes 307208 | tf_op jit(solution)/shard_map/other_1/ppermute | solution.py:44
  142.9 6.9 %collective-permute-start.23 = (bf16[80,640]{1,0:T(8,128)(2,1)S(1)}, bf16[80,640]{1,0:T(8,128)(2,1)S(1)}, u32[]{:S(2)}, u32[]{:S(2)}) collective-permute-start(bf16[80,640]{1,0:T(8,128)(2,1)S(1)} %collective-permute-done.19.refs_9_.refs_2_), channel_id=1, source_target_pairs={{0,32},{32,0},{64,96},{96,64},{128,160},{160,128},{192,224},{224,1... | collective-permute-start | bytes 307208 | tf_op jit(solution)/shard_map/other_1/ppermute | solution.py:44
  146.6 3.1 %collective-permute-start.22 = (bf16[80,640]{1,0:T(8,128)(2,1)S(1)}, bf16[80,640]{1,0:T(8,128)(2,1)S(1)}, u32[]{:S(2)}, u32[]{:S(2)}) collective-permute-start(bf16[80,640]{1,0:T(8,128)(2,1)S(1)} %collective-permute-done.18.refs_1_), channel_id=1, source_target_pairs={{0,32},{32,0},{64,96},{96,64},{128,160},{160,128},{192,224},{224,1... | collective-permute-start | bytes 307208 | tf_op jit(solution)/shard_map/other_1/ppermute | solution.py:44
  147.4 11.2 %collective-permute-start.34 = (bf16[80,2560]{1,0:T(8,128)(2,1)S(1)}, bf16[80,2560]{1,0:T(8,128)(2,1)S(1)}, u32[]{:S(2)}, u32[]{:S(2)}) collective-permute-start(bf16[80,2560]{1,0:T(8,128)(2,1)S(1)} %get-tuple-element.75), channel_id=1, source_target_pairs={{0,6},{1,7},{2,0},{3,1},{4,2},{5,3},{6,4},{7,5},{8,14},{9,15},{10,... | collective-permute-start | bytes 1228808 | tf_op jit(solution)/shard_map/out/ppermute | solution.py:35
  149.7 12.0 %collective-permute-start.35 = (bf16[80,2560]{1,0:T(8,128)(2,1)S(1)}, bf16[80,2560]{1,0:T(8,128)(2,1)S(1)}, u32[]{:S(2)}, u32[]{:S(2)}) collective-permute-start(bf16[80,2560]{1,0:T(8,128)(2,1)S(1)} %get-tuple-element.76), channel_id=1, source_target_pairs={{0,2},{1,3},{2,4},{3,5},{4,6},{5,7},{6,0},{7,1},{8,10},{9,11},{10,... | collective-permute-start | bytes 1228808 | tf_op jit(solution)/shard_map/out/ppermute | solution.py:35
  152.9 17.6 %collective-permute-start.36 = (bf16[80,2560]{1,0:T(8,128)(2,1)S(1)}, bf16[80,2560]{1,0:T(8,128)(2,1)S(1)}, u32[]{:S(2)}, u32[]{:S(2)}) collective-permute-start(bf16[80,2560]{1,0:T(8,128)(2,1)S(1)} %get-tuple-element.77), channel_id=1, source_target_pairs={{0,2},{1,3},{2,4},{3,5},{4,6},{5,7},{6,0},{7,1},{8,10},{9,11},{10,... | collective-permute-start | bytes 1228808 | tf_op jit(solution)/shard_map/out/ppermute | solution.py:35
  153.0 17.5 %collective-permute-start.37 = (bf16[80,2560]{1,0:T(8,128)(2,1)S(1)}, bf16[80,2560]{1,0:T(8,128)(2,1)S(1)}, u32[]{:S(2)}, u32[]{:S(2)}) collective-permute-start(bf16[80,2560]{1,0:T(8,128)(2,1)S(1)} %get-tuple-element.78), channel_id=1, source_target_pairs={{0,6},{1,7},{2,0},{3,1},{4,2},{5,3},{6,4},{7,5},{8,14},{9,15},{10,... | collective-permute-start | bytes 1228808 | tf_op jit(solution)/shard_map/out/ppermute | solution.py:35
where the time goes:
time: 172 us
  starting transfers between devices  69.1 us (40%)
  waiting for transfers between devices  68.5 us (40%)
  Pallas kernels  34 us (20%)
    pallas_call x12, Pallas kernels, call(): pl.pallas_call(kernel, in_specs=[spec for _, spec in args], out_specs=[VM...  33.2 us
    ppermute x9, starting transfers between devices, send_high(): return lax.ppermute(v, 'grp', [(g, (g + 2 * step) % 8) for g in range(8)])  26.4 us
    ppermute x9, waiting for transfers between devices, send_x(): return lax.ppermute(v, 'blk', pairs)  24.9 us
    ppermute x9, waiting for transfers between devices, send_high(): return lax.ppermute(v, 'grp', [(g, (g + 2 * step) % 8) for g in range(8)])  22.4 us
    ppermute x6, waiting for transfers between devices, send_y(): return lax.ppermute(v, 'blk', pairs)  13.9 us
    ppermute x9, starting transfers between devices, send_core(): return lax.ppermute(v, 'grp', [(g, g ^ 1) for g in range(8)])  13.3 us
    ppermute x9, starting transfers between devices, send_x(): return lax.ppermute(v, 'blk', pairs)  11.9 us
    ppermute x6, starting transfers between devices, send_y(): return lax.ppermute(v, 'blk', pairs)  8.34 us
  transfers between devices with their start and end apart: 38, of which 16 were waited for; matrix products, arithmetic and copies ran while one was open for 0% of the time, Pallas kernels for 13%

commit v1 on v0

--- a/solution.py
+++ b/solution.py
@@ -469,22 +469,24 @@
 
 def density_first_kernel(*refs):
     mine, other, bcat = refs[:4], refs[4:8], refs[8]
-    outs, tcat, sems = refs[-6:-2], refs[-2], refs[-1]
+    outs, tcat, sems = refs[9:11], refs[11], refs[12]
     for c in gather_rows(mine, other, tcat, sems):
         c.wait()
 
     @pl.loop(0, 2)
     def _(half):
         columns, value = product(tcat, bcat, half)
+        value = value.astype(bf16)
         for i, out in enumerate(outs):
-            out[:, columns] = value[i * HALF : (i + 1) * HALF].astype(bf16)
-
-
-def density_first(mine, other, bcat, after):
+            out[:HALF, columns] = value[i * HALF : (i + 1) * HALF]
+            out[HALF:, columns] = value[(i + 2) * HALF : (i + 3) * HALF]
+
+
+def density_first(mine, other, bcat):
     return call(
         density_first_kernel,
-        [(v, ANY) for v in (*mine, *other)] + [(bcat, VMEM)] + [(v, ANY) for v in after],
-        [hbm((HALF, AUX))] * 4,
+        [(v, ANY) for v in (*mine, *other)] + [(bcat, VMEM)],
+        [hbm((ROWS, AUX))] * 2,
         [pltpu.VMEM(TCAT, bf16), DMA((4, 2))],
         name="density_first",
     )
@@ -506,11 +508,12 @@
     @pl.loop(0, 2)
     def _(half):
         columns, value = product(tcat, bcat, half)
-        x = value[ROWS : ROWS + HALF] + got_m[:, columns].astype(f32)
-        m = value[ROWS + HALF :] + got_x[:, columns].astype(f32)
+        x = value[ROWS : ROWS + HALF] + got_m[HALF:, columns].astype(f32)
+        m = value[ROWS + HALF :] + got_x[HALF:, columns].astype(f32)
         x1[:, columns] = x.astype(bf16)
         m2[:, columns] = m.astype(bf16)
-        own[:, columns] = value[:ROWS]
+        own[:HALF, columns] = value[:HALF] + got_x[:HALF, columns].astype(f32)
+        own[HALF:, columns] = value[HALF:ROWS] + got_m[:HALF, columns].astype(f32)
 
 
 def density_second(mine, other, bcat, from_m, from_x):
@@ -520,7 +523,7 @@
         + [(bcat, VMEM), (from_m, ANY), (from_x, ANY)],
         [hbm((HALF, AUX))] * 2 + [vmem((ROWS, AUX), f32)],
         [pltpu.VMEM(TCAT, bf16)]
-        + [pltpu.VMEM((HALF, AUX), bf16)] * 2
+        + [pltpu.VMEM((ROWS, AUX), bf16)] * 2
         + [DMA((4, 2)), DMA((2,))],
         name="density_second",
     )
@@ -538,11 +541,11 @@
     out[...] = (own[...] + got[...].astype(f32)).astype(out.dtype)
 
 
-def add(own, one, two, out):
+def add(own, one, two):
     return call(
         add_kernel,
         [(own, VMEM), (one, ANY), (two, ANY)],
-        [out],
+        [hbm((ROWS, AUX))],
         [pltpu.VMEM((ROWS, AUX), bf16), DMA((2,))],
         name="add",
     )[0]
@@ -595,18 +598,15 @@
     mine0, mine1 = spread(0), spread(1)
     other0 = other_core(0, mine0)
     other1 = other_core(1, mine1)
-    x2, m1, to_d1, to_d2 = density_first(mine0, other0, bcat, (mine1[2],))
+    x2_d1, m1_d2 = density_first(mine0, other0, bcat)
     with jax.named_scope("out"):
-        from_m = send_x(to_d1, 1)
-        from_x = send_x(to_d2, -1)
-        got_x2 = send_x(x2, 1)
-        got_m1 = send_x(m1, -1)
+        from_m = send_x(x2_d1, 1)
+        from_x = send_x(m1_d2, -1)
     x1, m2, own = density_second(mine1, other1, bcat, from_m, from_x)
     with jax.named_scope("out"):
         got_x1 = send_x(x1, 1)
         got_m2 = send_x(m2, -1)
-    own = add(own, got_m1, got_x2, vmem((ROWS, AUX), f32))
-    return add(own, got_x1, got_m2, hbm((ROWS, AUX)))
+    return add(own, got_x1, got_m2)
 
 
 def solution(mesh):

time: 172 us -> 168 us (0.977)
  starting transfers between devices: 69.1 us -> 66.3 us
    ppermute x9 -> x7, waiting for transfers between devices: 24.9 us -> 21.3 us  [send_x(): return lax.ppermute(v, 'blk', pairs)]
    ppermute x9, waiting for transfers between devices: 2.23 us -> 4.82 us  [send_core(): return lax.ppermute(v, 'grp', [(g, g ^ 1) for g in range(8)])]
    ppermute x9 -> x7, starting transfers between devices: 11.9 us -> 9.74 us  [send_x(): return lax.ppermute(v, 'blk', pairs)]
    ppermute x9, starting transfers between devices: 13.3 us -> 11.2 us  [send_core(): return lax.ppermute(v, 'grp', [(g, g ^ 1) for g in range(8)])]
    pallas_call x12 -> x11, Pallas kernels: 33.2 us -> 32.3 us  [call(): pl.pallas_call(kernel, in_specs=[spec for _, spec in args], out_specs=[VM...]
  transfers between devices with their start and end apart: 38 -> 36, of which waited for: 16 -> 19; matrix products, arithmetic and copies ran while one was open for 0% -> 0% of each run, Pallas kernels for 13% -> 12%
where the time goes in v1:
time: 168 us; the launch traced here: 167 us
  waiting for transfers between devices  67.3 us (40%)
  starting transfers between devices  66.3 us (39%)
  Pallas kernels  33.1 us (20%)
    pallas_call x11, Pallas kernels, call(): pl.pallas_call(kernel, in_specs=[spec for _, spec in args], out_specs=[VM...  32.3 us
    ppermute x9, starting transfers between devices, send_high(): return lax.ppermute(v, 'grp', [(g, (g + 2 * step) % 8) for g in range(8)])  27.8 us
    ppermute x9, waiting for transfers between devices, send_high(): return lax.ppermute(v, 'grp', [(g, (g + 2 * step) % 8) for g in range(8)])  22.1 us
    ppermute x7, waiting for transfers between devices, send_x(): return lax.ppermute(v, 'blk', pairs)  21.3 us
    ppermute x6, waiting for transfers between devices, send_y(): return lax.ppermute(v, 'blk', pairs)  13.9 us
    ppermute x9, starting transfers between devices, send_core(): return lax.ppermute(v, 'grp', [(g, g ^ 1) for g in range(8)])  11.2 us
    ppermute x7, starting transfers between devices, send_x(): return lax.ppermute(v, 'blk', pairs)  9.74 us
    ppermute x6, starting transfers between devices, send_y(): return lax.ppermute(v, 'blk', pairs)  8.34 us
  transfers between devices with their start and end apart: 36, of which 19 were waited for; matrix products, arithmetic and copies ran while one was open for 0% of the time, Pallas kernels for 12%

profile of v1, /device:TPU:1, one launch (start us, length us, event | category | flops | bytes accessed | tf_op | source)
XLA Modules:
  0.0 167.1 jit_solution(17437332719781991367)
XLA Ops:
  0.0 1.1 ends.1
  1.1 6.3 %collective-permute-start = (bf16[320,512]{1,0:T(8,128)(2,1)S(1)}, bf16[320,512]{1,0:T(8,128)(2,1)S(1)}, u32[]{:S(2)}, u32[]{:S(2)}) collective-permute-start(bf16[320,512]{1,0:T(8,128)(2,1)S(1)} %get-tuple-element.40), channel_id=1, source_target_pairs={{0,32},{32,64},{64,96},{96,128},{128,160},{160,192},{192,224},{1,3... | collective-permute-start | bytes 983048 | tf_op jit(solution)/shard_map/ppermute | solution.py:560
  7.4 1.9 %collective-permute-start.1 = (bf16[320,512]{1,0:T(8,128)(2,1)S(1)}, bf16[320,512]{1,0:T(8,128)(2,1)S(1)}, u32[]{:S(2)}, u32[]{:S(2)}) collective-permute-start(bf16[320,512]{1,0:T(8,128)(2,1)S(1)} %get-tuple-element.41), channel_id=1, source_target_pairs={{32,0},{64,32},{96,64},{128,96},{160,128},{192,160},{224,192},{33,... | collective-permute-start | bytes 983048 | tf_op jit(solution)/shard_map/ppermute | solution.py:561
  9.3 8.0 %fit_inner.1 = (bf16[160,2560]{1,0:T(8,128)(2,1)S(1)}, bf16[160,2560]{1,0:T(8,128)(2,1)S(1)}, bf16[320,2560]{1,0:T(8,128)(2,1)S(1)}, bf16[4,1280,256]{2,1,0:T(8,128)(2,1)S(1)}) custom-call(s32[2,180]{1,0:T(2,128)} %bitcast.4, bf16[320,2560]{1,0:T(8,128)(2,1)} %bitcast.3, bf16[180,128,128]{2,1,0:T(8,128)(2,1)} %tiles_in.1), custom_call_target="tpu_custom_call" | custom-call | flops 1000 | bytes 1000 | tf_op jit(solution)/shard_map/fit_inner/pallas_call | solution.py:85
  17.3 3.1 %collective-permute-done.1.right = bf16[320,512]{1,0:T(8,128)(2,1)S(1)} collective-permute-done((bf16[320,512]{1,0:T(8,128)(2,1)S(1)}, bf16[320,512]{1,0:T(8,128)(2,1)S(1)}, u32[]{:S(2)}, u32[]{:S(2)}) %collective-permute-start.1) | collective-permute-done | bytes 327712 | tf_op jit(solution)/shard_map/ppermute | solution.py:561
  20.5 1.0 fit_edge.1
  21.5 1.0 collective-permute-start.6
  22.5 1.8 %collective-permute-start.4 = (bf16[160,2560]{1,0:T(8,128)(2,1)S(1)}, bf16[160,2560]{1,0:T(8,128)(2,1)}, u32[]{:S(2)}, u32[]{:S(2)}) collective-permute-start(bf16[160,2560]{1,0:T(8,128)(2,1)S(1)} %get-tuple-element.46.own), channel_id=1, source_target_pairs={{0,6},{1,7},{2,0},{3,1},{4,2},{5,3},{6,4},{7,5},{8,14},{9,15},{10,... | collective-permute-start | bytes 2457608 | tf_op jit(solution)/shard_map/first/ppermute | solution.py:35
  24.3 1.3 collective-permute-start.5
  25.6 1.4 collective-permute-start.3
  27.1 10.7 %collective-permute-done.6.refs_4_.am = bf16[160,2560]{1,0:T(8,128)(2,1)S(1)} collective-permute-done((bf16[160,2560]{1,0:T(8,128)(2,1)S(1)}, bf16[160,2560]{1,0:T(8,128)(2,1)S(1)}, u32[]{:S(2)}, u32[]{:S(2)}) %collective-permute-start.6) | collective-permute-done | bytes 819232 | tf_op jit(solution)/shard_map/first/ppermute | solution.py:35
  37.7 3.3 %collective-permute-done.5.refs_3_.refs_1_ = bf16[160,2560]{1,0:T(8,128)(2,1)} collective-permute-done((bf16[160,2560]{1,0:T(8,128)(2,1)S(1)}, bf16[160,2560]{1,0:T(8,128)(2,1)}, u32[]{:S(2)}, u32[]{:S(2)}) %collective-permute-start.5) | collective-permute-done | bytes 819232 | tf_op jit(solution)/shard_map/first/ppermute | solution.py:30
  41.1 2.0 %collective-permute-done.2.refs_0_ = bf16[160,2560]{1,0:T(8,128)(2,1)} collective-permute-done((bf16[160,2560]{1,0:T(8,128)(2,1)S(1)}, bf16[160,2560]{1,0:T(8,128)(2,1)}, u32[]{:S(2)}, u32[]{:S(2)}) %collective-permute-start.2) | collective-permute-done | bytes 819232 | tf_op jit(solution)/shard_map/first/ppermute | solution.py:40
  43.5 2.6 %collective-permute-start.9 = (bf16[160,2560]{1,0:T(8,128)(2,1)}, bf16[160,2560]{1,0:T(8,128)(2,1)S(1)}, u32[]{:S(2)}, u32[]{:S(2)}) collective-permute-start(bf16[160,2560]{1,0:T(8,128)(2,1)} %get-tuple-element.49.refs_2_), channel_id=1, source_target_pairs={{0,24},{1,25},{2,26},{3,27},{4,28},{5,29},{6,30},{7,31},{8,0},{9,1... | collective-permute-start | bytes 2457608 | tf_op jit(solution)/shard_map/second/ppermute | solution.py:30
  46.1 1.3 collective-permute-start.7
  47.4 4.9 %pair_first.1 = (f32[640,640]{1,0:T(8,128)S(1)}, bf16[1280,2560]{1,0:T(8,128)(2,1)S(1)}, bf16[640,2560]{1,0:T(8,128)(2,1)S(1)}) custom-call(bf16[160,2560]{1,0:T(8,128)(2,1)S(1)} %get-tuple-element.46.own, bf16[160,2560]{1,0:T(8,128)(2,1)} %get-tuple-element.48.ax, bf16[160,2560]{1,0:T(8,128)(2,1)S(1)} %collective-permute-done.6.refs_4_.am, ...), custom_call_target="tpu_custom_call" | custom-call | flops 1000 | bytes 1000 | tf_op jit(solution)/shard_map/pair_first/pallas_call | solution.py:85
  52.3 9.3 %collective-permute-done.8.refs_0_.refs_1_ = bf16[160,2560]{1,0:T(8,128)(2,1)S(1)} collective-permute-done((bf16[160,2560]{1,0:T(8,128)(2,1)}, bf16[160,2560]{1,0:T(8,128)(2,1)S(1)}, u32[]{:S(2)}, u32[]{:S(2)}) %collective-permute-start.8) | collective-permute-done | bytes 819232 | tf_op jit(solution)/shard_map/second/ppermute | solution.py:30
  61.6 1.2 collective-permute-done.9.refs_1_.refs_0_
  64.9 2.3 %collective-permute-start.13 = (bf16[48,2560]{1,0:T(8,128)(2,1)S(1)}, bf16[48,2560]{1,0:T(8,128)(2,1)S(1)}, u32[]{:S(2)}, u32[]{:S(2)}) collective-permute-start(bf16[48,2560]{1,0:T(8,128)(2,1)S(1)} %get-tuple-element.60), channel_id=1, source_target_pairs={{0,24},{1,25},{2,26},{3,27},{4,28},{5,29},{6,30},{7,31},{8,0},{9,1... | collective-permute-start | bytes 737288 | tf_op jit(solution)/shard_map/third/ppermute | solution.py:30
  67.2 5.7 %pair_early.1 = (f32[640,640]{1,0:T(8,128)S(1)}, bf16[1280,2560]{1,0:T(8,128)(2,1)S(1)}, bf16[640,2560]{1,0:T(8,128)(2,1)S(1)}, f32[640,480]{1,0:T(8,128)S(1)}) custom-call(f32[640,640]{1,0:T(8,128)S(1)} %get-tuple-element.51.first_in.refs_3_, ...), custom_call_target="tpu_custom_call", output_to_operand_aliasing={{0}: (0, {}), {1}: (1, {}), {2}: (2, {})} | custom-call | flops 1000 | bytes 1000 | tf_op jit(solution)/shard_map/pair_early/pallas_call | solution.py:85
  73.0 2.5 %pair_late.1 = (f32[640,640]{1,0:T(8,128)S(1)}, bf16[640,640]{1,0:T(8,128)(2,1)S(1)}, bf16[1280,2560]{1,0:T(8,128)(2,1)S(1)}) custom-call(f32[640,640]{1,0:T(8,128)S(1)} %get-tuple-element.54.first, f32[640,480]{1,0:T(8,128)S(1)} %get-tuple-element.55.early, bf16[640,2560]{1,0:T(8,128)(2,1)S(1)} %get-tuple-element.56.acat, ...), custom_call_target="tpu_custom_call", output_to_operand_aliasing={{2}: (3, {})} | custom-call | flops 1000 | bytes 1000 | tf_op jit(solution)/shard_map/pair_late/pallas_call | solution.py:85
  75.7 2.2 %collective-permute-done.14.got_in = bf16[640,640]{1,0:T(8,128)(2,1)S(1)} collective-permute-done((bf16[640,640]{1,0:T(8,128)(2,1)S(1)}, bf16[640,640]{1,0:T(8,128)(2,1)S(1)}, u32[]{:S(2)}, u32[]{:S(2)}) %collective-permute-start.14) | collective-permute-done | bytes 819232 | tf_op jit(solution)/shard_map/core/ppermute | solution.py:44
  78.2 7.5 %collective-permute-start.15 = (bf16[160,640]{1,0:T(8,128)(2,1)S(1)}, bf16[160,640]{1,0:T(8,128)(2,1)S(1)}, u32[]{:S(2)}, u32[]{:S(2)}) collective-permute-start(bf16[160,640]{1,0:T(8,128)(2,1)S(1)} %get-tuple-element.64), channel_id=1, source_target_pairs={{0,64},{32,96},{64,128},{96,160},{128,192},{160,224},{192,0},{224,... | collective-permute-start | bytes 614408 | tf_op jit(solution)/shard_map/shares/ppermute | solution.py:48
  85.8 3.6 %collective-permute-start.16 = (bf16[160,640]{1,0:T(8,128)(2,1)S(1)}, bf16[160,640]{1,0:T(8,128)(2,1)S(1)}, u32[]{:S(2)}, u32[]{:S(2)}) collective-permute-start(bf16[160,640]{1,0:T(8,128)(2,1)S(1)} %get-tuple-element.65), channel_id=1, source_target_pairs={{0,128},{32,160},{64,192},{96,224},{128,0},{160,32},{192,64},{224,... | collective-permute-start | bytes 614408 | tf_op jit(solution)/shard_map/shares/ppermute | solution.py:48
  89.4 3.5 %collective-permute-start.17 = (bf16[160,640]{1,0:T(8,128)(2,1)S(1)}, bf16[160,640]{1,0:T(8,128)(2,1)S(1)}, u32[]{:S(2)}, u32[]{:S(2)}) collective-permute-start(bf16[160,640]{1,0:T(8,128)(2,1)S(1)} %get-tuple-element.66), channel_id=1, source_target_pairs={{0,192},{32,224},{64,0},{96,32},{128,64},{160,96},{192,128},{224,1... | collective-permute-start | bytes 614408 | tf_op jit(solution)/shard_map/shares/ppermute | solution.py:48
  93.8 11.1 %collective-permute-done.16.refs_1_ = bf16[160,640]{1,0:T(8,128)(2,1)S(1)} collective-permute-done((bf16[160,640]{1,0:T(8,128)(2,1)S(1)}, bf16[160,640]{1,0:T(8,128)(2,1)S(1)}, u32[]{:S(2)}, u32[]{:S(2)}) %collective-permute-start.16) | collective-permute-done | bytes 204832 | tf_op jit(solution)/shard_map/shares/ppermute | solution.py:48
  104.9 3.4 %collective-permute-done.17.refs_2_ = bf16[160,640]{1,0:T(8,128)(2,1)S(1)} collective-permute-done((bf16[160,640]{1,0:T(8,128)(2,1)S(1)}, bf16[160,640]{1,0:T(8,128)(2,1)S(1)}, u32[]{:S(2)}, u32[]{:S(2)}) %collective-permute-start.17) | collective-permute-done | bytes 204832 | tf_op jit(solution)/shard_map/shares/ppermute | solution.py:48
  108.3 1.8 %amplitude.1 = (bf16[80,640]{1,0:T(8,128)(2,1)S(1)}, bf16[80,640]{1,0:T(8,128)(2,1)S(1)}) custom-call(f32[32,160]{1,0:T(8,128)S(1)} %reshape.6.refs_5_.vir, f32[1000]{0:T(1024)S(1)} %copy-done, s32[2]{0:T(128)S(1)} %copy-done.1, f32[160,640]{1,0:T(8,128)S(1)} %get-tuple-element.63.own, bf16[160,640]{1,0:T(8,128)(2,1)S(1)} %collective-permute-done.15.refs_0_, ...), custom_call_target="tpu_custom_call" | custom-call | flops 1000 | bytes 1000 | tf_op jit(solution)/shard_map/amplitude/pallas_call | solution.py:85
  110.1 3.5 %collective-permute-start.27 = (bf16[80,640]{1,0:T(8,128)(2,1)S(1)}, bf16[80,640]{1,0:T(8,128)(2,1)S(1)}, u32[]{:S(2)}, u32[]{:S(2)}) collective-permute-start(bf16[80,640]{1,0:T(8,128)(2,1)S(1)} %get-tuple-element.69.refs_0_), channel_id=1, source_target_pairs={{0,192},{32,224},{64,0},{96,32},{128,64},{160,96},{192,128},{224,1... | collective-permute-start | bytes 307208 | tf_op jit(solution)/shard_map/spread_0/ppermute | solution.py:48
  113.6 2.7 %collective-permute-start.26 = (bf16[80,640]{1,0:T(8,128)(2,1)S(1)}, bf16[80,640]{1,0:T(8,128)(2,1)S(1)}, u32[]{:S(2)}, u32[]{:S(2)}) collective-permute-start(bf16[80,640]{1,0:T(8,128)(2,1)S(1)} %get-tuple-element.69.refs_0_), channel_id=1, source_target_pairs={{0,128},{32,160},{64,192},{96,224},{128,0},{160,32},{192,64},{224,... | collective-permute-start | bytes 307208 | tf_op jit(solution)/shard_map/spread_0/ppermute | solution.py:48
  116.3 1.4 collective-permute-start.25
  117.8 1.3 collective-permute-start.28
  119.1 2.1 %collective-permute-done.26.refs_2_ = bf16[80,640]{1,0:T(8,128)(2,1)S(1)} collective-permute-done((bf16[80,640]{1,0:T(8,128)(2,1)S(1)}, bf16[80,640]{1,0:T(8,128)(2,1)S(1)}, u32[]{:S(2)}, u32[]{:S(2)}) %collective-permute-start.26) | collective-permute-done | bytes 102432 | tf_op jit(solution)/shard_map/spread_0/ppermute | solution.py:48
  121.2 4.9 %collective-permute-start.30 = (bf16[80,640]{1,0:T(8,128)(2,1)S(1)}, bf16[80,640]{1,0:T(8,128)(2,1)S(1)}, u32[]{:S(2)}, u32[]{:S(2)}) collective-permute-start(bf16[80,640]{1,0:T(8,128)(2,1)S(1)} %collective-permute-done.26.refs_2_), channel_id=1, source_target_pairs={{0,32},{32,0},{64,96},{96,64},{128,160},{160,128},{192,224},{224,1... | collective-permute-start | bytes 307208 | tf_op jit(solution)/shard_map/other_0/ppermute | solution.py:44
  126.1 0.9 collective-permute-done.30.refs_6_
  127.4 2.7 %density_first.1 = (bf16[160,2560]{1,0:T(8,128)(2,1)S(1)}, bf16[160,2560]{1,0:T(8,128)(2,1)S(1)}) custom-call(bf16[80,640]{1,0:T(8,128)(2,1)S(1)} %get-tuple-element.69.refs_0_, bf16[80,640]{1,0:T(8,128)(2,1)S(1)} %collective-permute-done.25.refs_1_, bf16[80,640]{1,0:T(8,128)(2,1)S(1)} %collective-permute-done.26.refs_2_, ...), custom_call_target="tpu_custom_call" | custom-call | flops 1000 | bytes 1000 | tf_op jit(solution)/shard_map/density_first/pallas_call | solution.py:85
  130.4 2.6 %collective-permute-start.33 = (bf16[160,2560]{1,0:T(8,128)(2,1)S(1)}, bf16[160,2560]{1,0:T(8,128)(2,1)S(1)}, u32[]{:S(2)}, u32[]{:S(2)}) collective-permute-start(bf16[160,2560]{1,0:T(8,128)(2,1)S(1)} %get-tuple-element.71), channel_id=1, source_target_pairs={{0,6},{1,7},{2,0},{3,1},{4,2},{5,3},{6,4},{7,5},{8,14},{9,15},{10,... | collective-permute-start | bytes 2457608 | tf_op jit(solution)/shard_map/out/ppermute | solution.py:35
  133.8 2.0 %collective-permute-start.20 = (bf16[80,640]{1,0:T(8,128)(2,1)S(1)}, bf16[80,640]{1,0:T(8,128)(2,1)S(1)}, u32[]{:S(2)}, u32[]{:S(2)}) collective-permute-start(bf16[80,640]{1,0:T(8,128)(2,1)S(1)} %get-tuple-element.67.refs_0_), channel_id=1, source_target_pairs={{0,192},{32,224},{64,0},{96,32},{128,64},{160,96},{192,128},{224,1... | collective-permute-start | bytes 307208 | tf_op jit(solution)/shard_map/spread_1/ppermute | solution.py:48
  135.8 2.2 %collective-permute-start.19 = (bf16[80,640]{1,0:T(8,128)(2,1)S(1)}, bf16[80,640]{1,0:T(8,128)(2,1)S(1)}, u32[]{:S(2)}, u32[]{:S(2)}) collective-permute-start(bf16[80,640]{1,0:T(8,128)(2,1)S(1)} %get-tuple-element.67.refs_0_), channel_id=1, source_target_pairs={{0,128},{32,160},{64,192},{96,224},{128,0},{160,32},{192,64},{224,... | collective-permute-start | bytes 307208 | tf_op jit(solution)/shard_map/spread_1/ppermute | solution.py:48
  138.0 1.4 collective-permute-start.18
  140.8 4.0 %collective-permute-done.19.refs_2_ = bf16[80,640]{1,0:T(8,128)(2,1)S(1)} collective-permute-done((bf16[80,640]{1,0:T(8,128)(2,1)S(1)}, bf16[80,640]{1,0:T(8,128)(2,1)S(1)}, u32[]{:S(2)}, u32[]{:S(2)}) %collective-permute-start.19) | collective-permute-done | bytes 102432 | tf_op jit(solution)/shard_map/spread_1/ppermute | solution.py:48
  144.8 3.1 %collective-permute-start.23 = (bf16[80,640]{1,0:T(8,128)(2,1)S(1)}, bf16[80,640]{1,0:T(8,128)(2,1)S(1)}, u32[]{:S(2)}, u32[]{:S(2)}) collective-permute-start(bf16[80,640]{1,0:T(8,128)(2,1)S(1)} %collective-permute-done.19.refs_2_), channel_id=1, source_target_pairs={{0,32},{32,0},{64,96},{96,64},{128,160},{160,128},{192,224},{224,1... | collective-permute-start | bytes 307208 | tf_op jit(solution)/shard_map/other_1/ppermute | solution.py:44
  147.9 0.9 collective-permute-done.23.refs_6_
  149.2 2.1 %collective-permute-done.32.refs_9_ = bf16[160,2560]{1,0:T(8,128)(2,1)S(1)} collective-permute-done((bf16[160,2560]{1,0:T(8,128)(2,1)S(1)}, bf16[160,2560]{1,0:T(8,128)(2,1)S(1)}, u32[]{:S(2)}, u32[]{:S(2)}) %collective-permute-start.32) | collective-permute-done | bytes 819232 | tf_op jit(solution)/shard_map/out/ppermute | solution.py:35
  151.3 2.9 %density_second.1 = (bf16[80,2560]{1,0:T(8,128)(2,1)S(1)}, bf16[80,2560]{1,0:T(8,128)(2,1)S(1)}, f32[160,2560]{1,0:T(8,128)S(1)}) custom-call(bf16[80,640]{1,0:T(8,128)(2,1)S(1)} %get-tuple-element.67.refs_0_, bf16[80,640]{1,0:T(8,128)(2,1)S(1)} %collective-permute-done.18.refs_1_, bf16[80,640]{1,0:T(8,128)(2,1)S(1)} %collective-permute-done.19.refs_2_, ...), custom_call_target="tpu_custom_call" | custom-call | flops 1000 | bytes 1000 | tf_op jit(solution)/shard_map/density_second/pallas_call | solution.py:85
  154.3 2.7 %collective-permute-start.35 = (bf16[80,2560]{1,0:T(8,128)(2,1)S(1)}, bf16[80,2560]{1,0:T(8,128)(2,1)S(1)}, u32[]{:S(2)}, u32[]{:S(2)}) collective-permute-start(bf16[80,2560]{1,0:T(8,128)(2,1)S(1)} %get-tuple-element.74), channel_id=1, source_target_pairs={{0,6},{1,7},{2,0},{3,1},{4,2},{5,3},{6,4},{7,5},{8,14},{9,15},{10,... | collective-permute-start | bytes 1228808 | tf_op jit(solution)/shard_map/out/ppermute | solution.py:35
  156.9 8.5 %collective-permute-done.34.one = bf16[80,2560]{1,0:T(8,128)(2,1)S(1)} collective-permute-done((bf16[80,2560]{1,0:T(8,128)(2,1)S(1)}, bf16[80,2560]{1,0:T(8,128)(2,1)S(1)}, u32[]{:S(2)}, u32[]{:S(2)}) %collective-permute-start.34) | collective-permute-done | bytes 409632 | tf_op jit(solution)/shard_map/out/ppermute | solution.py:35
  165.4 1.5 add.1
  (44 shorter events, 7.3 us)
Async XLA Ops:
  1.1 16.2 %collective-permute-start = (bf16[320,512]{1,0:T(8,128)(2,1)S(1)}, bf16[320,512]{1,0:T(8,128)(2,1)S(1)}, u32[]{:S(2)}, u32[]{:S(2)}) collective-permute-start(bf16[320,512]{1,0:T(8,128)(2,1)S(1)} %get-tuple-element.40), channel_id=1, source_target_pairs={{0,32},{32,64},{64,96},{96,128},{128,160},{160,192},{192,224},{1,3... | collective-permute-start | bytes 983048 | tf_op jit(solution)/shard_map/ppermute | solution.py:560
  7.4 13.1 %collective-permute-start.1 = (bf16[320,512]{1,0:T(8,128)(2,1)S(1)}, bf16[320,512]{1,0:T(8,128)(2,1)S(1)}, u32[]{:S(2)}, u32[]{:S(2)}) collective-permute-start(bf16[320,512]{1,0:T(8,128)(2,1)S(1)} %get-tuple-element.41), channel_id=1, source_target_pairs={{32,0},{64,32},{96,64},{128,96},{160,128},{192,160},{224,192},{33,... | collective-permute-start | bytes 983048 | tf_op jit(solution)/shard_map/ppermute | solution.py:561
  20.5 6.5 %copy-start.2 = (f32[5120]{0:T(1024)S(1)}, f32[5120]{0:T(1024)}, u32[]{:S(2)}) copy-start(f32[5120]{0:T(1024)} %param.9) | copy-start | bytes 61444
  21.5 16.2 %collective-permute-start.6 = (bf16[160,2560]{1,0:T(8,128)(2,1)S(1)}, bf16[160,2560]{1,0:T(8,128)(2,1)S(1)}, u32[]{:S(2)}, u32[]{:S(2)}) collective-permute-start(bf16[160,2560]{1,0:T(8,128)(2,1)S(1)} %get-tuple-element.46.own), channel_id=1, source_target_pairs={{0,2},{1,3},{2,4},{3,5},{4,6},{5,7},{6,0},{7,1},{8,10},{9,11},{10,... | collective-permute-start | bytes 2457608 | tf_op jit(solution)/shard_map/first/ppermute | solution.py:35
  22.5 15.2 %collective-permute-start.4 = (bf16[160,2560]{1,0:T(8,128)(2,1)S(1)}, bf16[160,2560]{1,0:T(8,128)(2,1)}, u32[]{:S(2)}, u32[]{:S(2)}) collective-permute-start(bf16[160,2560]{1,0:T(8,128)(2,1)S(1)} %get-tuple-element.46.own), channel_id=1, source_target_pairs={{0,6},{1,7},{2,0},{3,1},{4,2},{5,3},{6,4},{7,5},{8,14},{9,15},{10,... | collective-permute-start | bytes 2457608 | tf_op jit(solution)/shard_map/first/ppermute | solution.py:35
  24.3 16.8 %collective-permute-start.5 = (bf16[160,2560]{1,0:T(8,128)(2,1)S(1)}, bf16[160,2560]{1,0:T(8,128)(2,1)}, u32[]{:S(2)}, u32[]{:S(2)}) collective-permute-start(bf16[160,2560]{1,0:T(8,128)(2,1)S(1)} %get-tuple-element.47.refs_0_), channel_id=1, source_target_pairs={{0,8},{1,9},{2,10},{3,11},{4,12},{5,13},{6,14},{7,15},{8,16},{9,17... | collective-permute-start | bytes 2457608 | tf_op jit(solution)/shard_map/first/ppermute | solution.py:30
  25.6 15.5 %collective-permute-start.3 = (bf16[160,2560]{1,0:T(8,128)(2,1)S(1)}, bf16[160,2560]{1,0:T(8,128)(2,1)}, u32[]{:S(2)}, u32[]{:S(2)}) collective-permute-start(bf16[160,2560]{1,0:T(8,128)(2,1)S(1)} %get-tuple-element.47.refs_0_), channel_id=1, source_target_pairs={{0,24},{1,25},{2,26},{3,27},{4,28},{5,29},{6,30},{7,31},{8,0},{9,1... | collective-permute-start | bytes 2457608 | tf_op jit(solution)/shard_map/first/ppermute | solution.py:30
  27.0 16.1 %collective-permute-start.2 = (bf16[160,2560]{1,0:T(8,128)(2,1)S(1)}, bf16[160,2560]{1,0:T(8,128)(2,1)}, u32[]{:S(2)}, u32[]{:S(2)}) collective-permute-start(bf16[160,2560]{1,0:T(8,128)(2,1)S(1)} %get-tuple-element.47.refs_0_), channel_id=1, source_target_pairs={{0,1},{1,0},{2,3},{3,2},{4,5},{5,4},{6,7},{7,6},{8,9},{9,8},{10,11... | collective-permute-start | bytes 2457608 | tf_op jit(solution)/shard_map/first/ppermute | solution.py:40
  43.1 18.5 %collective-permute-start.8 = (bf16[160,2560]{1,0:T(8,128)(2,1)}, bf16[160,2560]{1,0:T(8,128)(2,1)S(1)}, u32[]{:S(2)}, u32[]{:S(2)}) collective-permute-start(bf16[160,2560]{1,0:T(8,128)(2,1)} %get-tuple-element.50.refs_3_), channel_id=1, source_target_pairs={{0,8},{1,9},{2,10},{3,11},{4,12},{5,13},{6,14},{7,15},{8,16},{9,17... | collective-permute-start | bytes 2457608 | tf_op jit(solution)/shard_map/second/ppermute | solution.py:30
  43.1 18.5 %collective-permute-start.10 = (bf16[160,2560]{1,0:T(8,128)(2,1)}, bf16[160,2560]{1,0:T(8,128)(2,1)S(1)}, u32[]{:S(2)}, u32[]{:S(2)}) collective-permute-start(bf16[160,2560]{1,0:T(8,128)(2,1)} %get-tuple-element.49.refs_2_), channel_id=1, source_target_pairs={{0,1},{1,0},{2,3},{3,2},{4,5},{5,4},{6,7},{7,6},{8,9},{9,8},{10,11... | collective-permute-start | bytes 2457608 | tf_op jit(solution)/shard_map/second/ppermute | solution.py:40
  43.5 19.3 %collective-permute-start.9 = (bf16[160,2560]{1,0:T(8,128)(2,1)}, bf16[160,2560]{1,0:T(8,128)(2,1)S(1)}, u32[]{:S(2)}, u32[]{:S(2)}) collective-permute-start(bf16[160,2560]{1,0:T(8,128)(2,1)} %get-tuple-element.49.refs_2_), channel_id=1, source_target_pairs={{0,24},{1,25},{2,26},{3,27},{4,28},{5,29},{6,30},{7,31},{8,0},{9,1... | collective-permute-start | bytes 2457608 | tf_op jit(solution)/shard_map/second/ppermute | solution.py:30
  46.1 21.0 %collective-permute-start.7 = (bf16[160,2560]{1,0:T(8,128)(2,1)}, bf16[160,2560]{1,0:T(8,128)(2,1)S(1)}, u32[]{:S(2)}, u32[]{:S(2)}) collective-permute-start(bf16[160,2560]{1,0:T(8,128)(2,1)} %get-tuple-element.48.ax), channel_id=1, source_target_pairs={{0,6},{1,7},{2,0},{3,1},{4,2},{5,3},{6,4},{7,5},{8,14},{9,15},{10,... | collective-permute-start | bytes 2457608 | tf_op jit(solution)/shard_map/second/ppermute | solution.py:35
  63.6 9.3 %collective-permute-start.11 = (bf16[64,2560]{1,0:T(8,128)(2,1)S(1)}, bf16[64,2560]{1,0:T(8,128)(2,1)S(1)}, u32[]{:S(2)}, u32[]{:S(2)}) collective-permute-start(bf16[64,2560]{1,0:T(8,128)(2,1)S(1)} %get-tuple-element.58), channel_id=1, source_target_pairs={{0,1},{1,0},{2,3},{3,2},{4,5},{5,4},{6,7},{7,6},{8,9},{9,8},{10,11... | collective-permute-start | bytes 983048 | tf_op jit(solution)/shard_map/third/ppermute | solution.py:40
  64.2 8.8 %collective-permute-start.12 = (bf16[48,2560]{1,0:T(8,128)(2,1)S(1)}, bf16[48,2560]{1,0:T(8,128)(2,1)S(1)}, u32[]{:S(2)}, u32[]{:S(2)}) collective-permute-start(bf16[48,2560]{1,0:T(8,128)(2,1)S(1)} %get-tuple-element.59), channel_id=1, source_target_pairs={{0,8},{1,9},{2,10},{3,11},{4,12},{5,13},{6,14},{7,15},{8,16},{9,17... | collective-permute-start | bytes 737288 | tf_op jit(solution)/shard_map/third/ppermute | solution.py:30
  64.9 8.1 %collective-permute-start.13 = (bf16[48,2560]{1,0:T(8,128)(2,1)S(1)}, bf16[48,2560]{1,0:T(8,128)(2,1)S(1)}, u32[]{:S(2)}, u32[]{:S(2)}) collective-permute-start(bf16[48,2560]{1,0:T(8,128)(2,1)S(1)} %get-tuple-element.60), channel_id=1, source_target_pairs={{0,24},{1,25},{2,26},{3,27},{4,28},{5,29},{6,30},{7,31},{8,0},{9,1... | collective-permute-start | bytes 737288 | tf_op jit(solution)/shard_map/third/ppermute | solution.py:30
  73.0 35.4 %copy-start = (f32[1000]{0:T(1024)S(1)}, f32[1000]{0:T(1024)}, u32[]{:S(2)}) copy-start(f32[1000]{0:T(1024)} %occ.1) | copy-start | bytes 12004
  73.0 35.4 %copy-start.1 = (s32[2]{0:T(128)S(1)}, s32[2]{0:T(128)}, u32[]{:S(2)}) copy-start(s32[2]{0:T(128)} %chosen.1) | copy-start | bytes 28
  75.5 2.4 %collective-permute-start.14 = (bf16[640,640]{1,0:T(8,128)(2,1)S(1)}, bf16[640,640]{1,0:T(8,128)(2,1)S(1)}, u32[]{:S(2)}, u32[]{:S(2)}) collective-permute-start(bf16[640,640]{1,0:T(8,128)(2,1)S(1)} %get-tuple-element.62), channel_id=1, source_target_pairs={{0,32},{32,0},{64,96},{96,64},{128,160},{160,128},{192,224},{224,1... | collective-permute-start | bytes 2457608 | tf_op jit(solution)/shard_map/core/ppermute | solution.py:44
  78.2 15.6 %collective-permute-start.15 = (bf16[160,640]{1,0:T(8,128)(2,1)S(1)}, bf16[160,640]{1,0:T(8,128)(2,1)S(1)}, u32[]{:S(2)}, u32[]{:S(2)}) collective-permute-start(bf16[160,640]{1,0:T(8,128)(2,1)S(1)} %get-tuple-element.64), channel_id=1, source_target_pairs={{0,64},{32,96},{64,128},{96,160},{128,192},{160,224},{192,0},{224,... | collective-permute-start | bytes 614408 | tf_op jit(solution)/shard_map/shares/ppermute | solution.py:48
  85.8 19.1 %collective-permute-start.16 = (bf16[160,640]{1,0:T(8,128)(2,1)S(1)}, bf16[160,640]{1,0:T(8,128)(2,1)S(1)}, u32[]{:S(2)}, u32[]{:S(2)}) collective-permute-start(bf16[160,640]{1,0:T(8,128)(2,1)S(1)} %get-tuple-element.65), channel_id=1, source_target_pairs={{0,128},{32,160},{64,192},{96,224},{128,0},{160,32},{192,64},{224,... | collective-permute-start | bytes 614408 | tf_op jit(solution)/shard_map/shares/ppermute | solution.py:48
  89.4 18.9 %collective-permute-start.17 = (bf16[160,640]{1,0:T(8,128)(2,1)S(1)}, bf16[160,640]{1,0:T(8,128)(2,1)S(1)}, u32[]{:S(2)}, u32[]{:S(2)}) collective-permute-start(bf16[160,640]{1,0:T(8,128)(2,1)S(1)} %get-tuple-element.66), channel_id=1, source_target_pairs={{0,192},{32,224},{64,0},{96,32},{128,64},{160,96},{192,128},{224,1... | collective-permute-start | bytes 614408 | tf_op jit(solution)/shard_map/shares/ppermute | solution.py:48
  110.1 9.0 %collective-permute-start.27 = (bf16[80,640]{1,0:T(8,128)(2,1)S(1)}, bf16[80,640]{1,0:T(8,128)(2,1)S(1)}, u32[]{:S(2)}, u32[]{:S(2)}) collective-permute-start(bf16[80,640]{1,0:T(8,128)(2,1)S(1)} %get-tuple-element.69.refs_0_), channel_id=1, source_target_pairs={{0,192},{32,224},{64,0},{96,32},{128,64},{160,96},{192,128},{224,1... | collective-permute-start | bytes 307208 | tf_op jit(solution)/shard_map/spread_0/ppermute | solution.py:48
  113.6 7.6 %collective-permute-start.26 = (bf16[80,640]{1,0:T(8,128)(2,1)S(1)}, bf16[80,640]{1,0:T(8,128)(2,1)S(1)}, u32[]{:S(2)}, u32[]{:S(2)}) collective-permute-start(bf16[80,640]{1,0:T(8,128)(2,1)S(1)} %get-tuple-element.69.refs_0_), channel_id=1, source_target_pairs={{0,128},{32,160},{64,192},{96,224},{128,0},{160,32},{192,64},{224,... | collective-permute-start | bytes 307208 | tf_op jit(solution)/shard_map/spread_0/ppermute | solution.py:48
  116.3 9.8 %collective-permute-start.25 = (bf16[80,640]{1,0:T(8,128)(2,1)S(1)}, bf16[80,640]{1,0:T(8,128)(2,1)S(1)}, u32[]{:S(2)}, u32[]{:S(2)}) collective-permute-start(bf16[80,640]{1,0:T(8,128)(2,1)S(1)} %get-tuple-element.69.refs_0_), channel_id=1, source_target_pairs={{0,64},{32,96},{64,128},{96,160},{128,192},{160,224},{192,0},{224,... | collective-permute-start | bytes 307208 | tf_op jit(solution)/shard_map/spread_0/ppermute | solution.py:48
  117.8 8.4 %collective-permute-start.28 = (bf16[80,640]{1,0:T(8,128)(2,1)S(1)}, bf16[80,640]{1,0:T(8,128)(2,1)S(1)}, u32[]{:S(2)}, u32[]{:S(2)}) collective-permute-start(bf16[80,640]{1,0:T(8,128)(2,1)S(1)} %get-tuple-element.69.refs_0_), channel_id=1, source_target_pairs={{0,32},{32,0},{64,96},{96,64},{128,160},{160,128},{192,224},{224,1... | collective-permute-start | bytes 307208 | tf_op jit(solution)/shard_map/other_0/ppermute | solution.py:44
  119.1 7.0 %collective-permute-start.31 = (bf16[80,640]{1,0:T(8,128)(2,1)S(1)}, bf16[80,640]{1,0:T(8,128)(2,1)S(1)}, u32[]{:S(2)}, u32[]{:S(2)}) collective-permute-start(bf16[80,640]{1,0:T(8,128)(2,1)S(1)} %collective-permute-done.27.refs_3_), channel_id=1, source_target_pairs={{0,32},{32,0},{64,96},{96,64},{128,160},{160,128},{192,224},{224,1... | collective-permute-start | bytes 307208 | tf_op jit(solution)/shard_map/other_0/ppermute | solution.py:44
  121.2 5.9 %collective-permute-start.30 = (bf16[80,640]{1,0:T(8,128)(2,1)S(1)}, bf16[80,640]{1,0:T(8,128)(2,1)S(1)}, u32[]{:S(2)}, u32[]{:S(2)}) collective-permute-start(bf16[80,640]{1,0:T(8,128)(2,1)S(1)} %collective-permute-done.26.refs_2_), channel_id=1, source_target_pairs={{0,32},{32,0},{64,96},{96,64},{128,160},{160,128},{192,224},{224,1... | collective-permute-start | bytes 307208 | tf_op jit(solution)/shard_map/other_0/ppermute | solution.py:44
  126.1 1.3 collective-permute-start.29
  130.1 21.2 %collective-permute-start.32 = (bf16[160,2560]{1,0:T(8,128)(2,1)S(1)}, bf16[160,2560]{1,0:T(8,128)(2,1)S(1)}, u32[]{:S(2)}, u32[]{:S(2)}) collective-permute-start(bf16[160,2560]{1,0:T(8,128)(2,1)S(1)} %get-tuple-element.70), channel_id=1, source_target_pairs={{0,2},{1,3},{2,4},{3,5},{4,6},{5,7},{6,0},{7,1},{8,10},{9,11},{10,... | collective-permute-start | bytes 2457608 | tf_op jit(solution)/shard_map/out/ppermute | solution.py:35
  130.4 20.9 %collective-permute-start.33 = (bf16[160,2560]{1,0:T(8,128)(2,1)S(1)}, bf16[160,2560]{1,0:T(8,128)(2,1)S(1)}, u32[]{:S(2)}, u32[]{:S(2)}) collective-permute-start(bf16[160,2560]{1,0:T(8,128)(2,1)S(1)} %get-tuple-element.71), channel_id=1, source_target_pairs={{0,6},{1,7},{2,0},{3,1},{4,2},{5,3},{6,4},{7,5},{8,14},{9,15},{10,... | collective-permute-start | bytes 2457608 | tf_op jit(solution)/shard_map/out/ppermute | solution.py:35
  133.1 4.9 %collective-permute-start.21 = (bf16[80,640]{1,0:T(8,128)(2,1)S(1)}, bf16[80,640]{1,0:T(8,128)(2,1)S(1)}, u32[]{:S(2)}, u32[]{:S(2)}) collective-permute-start(bf16[80,640]{1,0:T(8,128)(2,1)S(1)} %get-tuple-element.67.refs_0_), channel_id=1, source_target_pairs={{0,32},{32,0},{64,96},{96,64},{128,160},{160,128},{192,224},{224,1... | collective-permute-start | bytes 307208 | tf_op jit(solution)/shard_map/other_1/ppermute | solution.py:44
  133.8 6.1 %collective-permute-start.20 = (bf16[80,640]{1,0:T(8,128)(2,1)S(1)}, bf16[80,640]{1,0:T(8,128)(2,1)S(1)}, u32[]{:S(2)}, u32[]{:S(2)}) collective-permute-start(bf16[80,640]{1,0:T(8,128)(2,1)S(1)} %get-tuple-element.67.refs_0_), channel_id=1, source_target_pairs={{0,192},{32,224},{64,0},{96,32},{128,64},{160,96},{192,128},{224,1... | collective-permute-start | bytes 307208 | tf_op jit(solution)/shard_map/spread_1/ppermute | solution.py:48
  135.8 8.9 %collective-permute-start.19 = (bf16[80,640]{1,0:T(8,128)(2,1)S(1)}, bf16[80,640]{1,0:T(8,128)(2,1)S(1)}, u32[]{:S(2)}, u32[]{:S(2)}) collective-permute-start(bf16[80,640]{1,0:T(8,128)(2,1)S(1)} %get-tuple-element.67.refs_0_), channel_id=1, source_target_pairs={{0,128},{32,160},{64,192},{96,224},{128,0},{160,32},{192,64},{224,... | collective-permute-start | bytes 307208 | tf_op jit(solution)/shard_map/spread_1/ppermute | solution.py:48
  138.0 9.9 %collective-permute-start.18 = (bf16[80,640]{1,0:T(8,128)(2,1)S(1)}, bf16[80,640]{1,0:T(8,128)(2,1)S(1)}, u32[]{:S(2)}, u32[]{:S(2)}) collective-permute-start(bf16[80,640]{1,0:T(8,128)(2,1)S(1)} %get-tuple-element.67.refs_0_), channel_id=1, source_target_pairs={{0,64},{32,96},{64,128},{96,160},{128,192},{160,224},{192,0},{224,... | collective-permute-start | bytes 307208 | tf_op jit(solution)/shard_map/spread_1/ppermute | solution.py:48
  139.9 8.0 %collective-permute-start.24 = (bf16[80,640]{1,0:T(8,128)(2,1)S(1)}, bf16[80,640]{1,0:T(8,128)(2,1)S(1)}, u32[]{:S(2)}, u32[]{:S(2)}) collective-permute-start(bf16[80,640]{1,0:T(8,128)(2,1)S(1)} %collective-permute-done.20.refs_3_), channel_id=1, source_target_pairs={{0,32},{32,0},{64,96},{96,64},{128,160},{160,128},{192,224},{224,1... | collective-permute-start | bytes 307208 | tf_op jit(solution)/shard_map/other_1/ppermute | solution.py:44
  144.8 4.1 %collective-permute-start.23 = (bf16[80,640]{1,0:T(8,128)(2,1)S(1)}, bf16[80,640]{1,0:T(8,128)(2,1)S(1)}, u32[]{:S(2)}, u32[]{:S(2)}) collective-permute-start(bf16[80,640]{1,0:T(8,128)(2,1)S(1)} %collective-permute-done.19.refs_2_), channel_id=1, source_target_pairs={{0,32},{32,0},{64,96},{96,64},{128,160},{160,128},{192,224},{224,1... | collective-permute-start | bytes 307208 | tf_op jit(solution)/shard_map/other_1/ppermute | solution.py:44
  147.9 1.3 collective-permute-start.22
  154.2 11.3 %collective-permute-start.34 = (bf16[80,2560]{1,0:T(8,128)(2,1)S(1)}, bf16[80,2560]{1,0:T(8,128)(2,1)S(1)}, u32[]{:S(2)}, u32[]{:S(2)}) collective-permute-start(bf16[80,2560]{1,0:T(8,128)(2,1)S(1)} %get-tuple-element.73), channel_id=1, source_target_pairs={{0,2},{1,3},{2,4},{3,5},{4,6},{5,7},{6,0},{7,1},{8,10},{9,11},{10,... | collective-permute-start | bytes 1228808 | tf_op jit(solution)/shard_map/out/ppermute | solution.py:35
  154.3 11.2 %collective-permute-start.35 = (bf16[80,2560]{1,0:T(8,128)(2,1)S(1)}, bf16[80,2560]{1,0:T(8,128)(2,1)S(1)}, u32[]{:S(2)}, u32[]{:S(2)}) collective-permute-start(bf16[80,2560]{1,0:T(8,128)(2,1)S(1)} %get-tuple-element.74), channel_id=1, source_target_pairs={{0,6},{1,7},{2,0},{3,1},{4,2},{5,3},{6,4},{7,5},{8,14},{9,15},{10,... | collective-permute-start | bytes 1228808 | tf_op jit(solution)/shard_map/out/ppermute | solution.py:35

commit v2 on v1

--- a/solution.py
+++ b/solution.py
@@ -250,10 +250,20 @@
     return moves
 
 
-def products(copies, acat, bcat, wanted):
+def products(copies, acat, bcat, wanted, unroll=False):
     for part in range(4):
         for c in copies(part):
             c.start()
+
+    if unroll:
+        for c in (c for part in range(4) for c in copies(part)):
+            c.wait()
+        for a_rows, b_rows, total in wanted:
+            total[...] = lax.dot_general(
+                acat[a_rows], bcat[b_rows], (((1,), (1,)), ((), ())),
+                preferred_element_type=f32,
+            )
+        return
 
     @pl.loop(0, 4)
     def _(part):
@@ -339,7 +349,7 @@
     keep, send, bcat, late, sems = refs[3:]
     products(
         lambda part: row_copies(b_moves(b_refs, 7 * ROWS), bcat, sems, part),
-        acat, bcat, [(slice(0, WIDE), slice(7 * ROWS, 8 * ROWS), late)],
+        acat, bcat, [(slice(0, WIDE), slice(7 * ROWS, 8 * ROWS), late)], unroll=True,
     )
     core = position()[1]
     split = 3 * ROWS
@@ -562,12 +572,12 @@
     a, b = fit(tile_index.T, window, tiles, left, right)
 
     with jax.named_scope("first"):
-        bm = send_y(b, 1)
-        bp = send_y(b, -1)
-        bo = send_z(b)
         ax = send_x(a, -1)
         am = send_x(a, 1)
-    bo, bp, ax = arrive((bo, bp, ax), (bm, am, vir))
+        bo = send_z(b)
+        bp = send_y(b, -1)
+        bm = send_y(b, 1)
+    bo, bp = arrive((bo, bp), (bm, vir))
     with jax.named_scope("second"):
         bom = send_y(bo, 1)
         b2 = send_y(bp, -1)
@@ -584,12 +594,13 @@
     with jax.named_scope("core"):
         own, *s = core_sum(keep, send_core(send))
     with jax.named_scope("shares"):
-        arrived = [send_high(v, k + 1) for k, v in enumerate(s)]
+        arrived = [send_high(s[k - 1], k) for k in (2, 1, 3)]
     mine = amplitude(vir, occ_energy, pair_index, own, arrived)
 
     def spread(wave):
         with jax.named_scope(f"spread_{wave}"):
-            return [mine[wave]] + [send_high(mine[wave], k) for k in (1, 2, 3)]
+            sent = {k: send_high(mine[wave], k) for k in (1, 3, 2)}
+            return [mine[wave]] + [sent[k] for k in (1, 2, 3)]
 
     def other_core(wave, mine):
         with jax.named_scope(f"other_{wave}"):

time: 168 us -> 165 us (0.982)
  starting transfers between devices: 66.3 us -> 64.6 us
    ppermute x7, waiting for transfers between devices: 21.3 us -> 10.3 us  [send_x(): return lax.ppermute(v, 'blk', pairs)]
    ppermute x6, waiting for transfers between devices: 13.9 us -> 19.9 us  [send_y(): return lax.ppermute(v, 'blk', pairs)]
    ppermute x9, waiting for transfers between devices: 22.1 us -> 27.3 us  [send_high(): return lax.ppermute(v, 'grp', [(g, (g + 2 * step) % 8) for g in range(8)])]
    ppermute x9, starting transfers between devices: 11.2 us -> 8.09 us  [send_core(): return lax.ppermute(v, 'grp', [(g, g ^ 1) for g in range(8)])]
    ppermute x9, starting transfers between devices: 27.8 us -> 25.9 us  [send_high(): return lax.ppermute(v, 'grp', [(g, (g + 2 * step) % 8) for g in range(8)])]
    ppermute x3, starting transfers between devices: 0.96 us -> 2.67 us  [send_z(): return lax.ppermute(v, 'blk', pairs)]
  transfers between devices with their start and end apart: 36 -> 36, of which waited for: 19 -> 17; matrix products, arithmetic and copies ran while one was open for 0% -> 0% of each run, Pallas kernels for 12% -> 12%
where the time goes in v2:
time: 165 us; the launch traced here: 164 us
  waiting for transfers between devices  66.5 us (40%)
  starting transfers between devices  64.6 us (39%)
  Pallas kernels  32.1 us (19%)
    pallas_call x11, Pallas kernels, call(): pl.pallas_call(kernel, in_specs=[spec for _, spec in args], out_specs=[VM...  31.3 us
    ppermute x9, waiting for transfers between devices, send_high(): return lax.ppermute(v, 'grp', [(g, (g + 2 * step) % 8) for g in range(8)])  27.3 us
    ppermute x9, starting transfers between devices, send_high(): return lax.ppermute(v, 'grp', [(g, (g + 2 * step) % 8) for g in range(8)])  25.9 us
    ppermute x6, waiting for transfers between devices, send_y(): return lax.ppermute(v, 'blk', pairs)  19.9 us
    ppermute x7, starting transfers between devices, send_x(): return lax.ppermute(v, 'blk', pairs)  10.8 us
    ppermute x7, waiting for transfers between devices, send_x(): return lax.ppermute(v, 'blk', pairs)  10.3 us
    ppermute x6, starting transfers between devices, send_y(): return lax.ppermute(v, 'blk', pairs)  8.94 us
    ppermute x9, starting transfers between devices, send_core(): return lax.ppermute(v, 'grp', [(g, g ^ 1) for g in range(8)])  8.09 us
  transfers between devices with their start and end apart: 36, of which 17 were waited for; matrix products, arithmetic and copies ran while one was open for 0% of the time, Pallas kernels for 12%

profile of v2, /device:TPU:1, one launch (start us, length us, event | category | flops | bytes accessed | tf_op | source)
XLA Modules:
  0.0 163.6 jit_solution(14515998837591408408)
XLA Ops:
  0.0 1.1 ends.1
  1.1 6.3 %collective-permute-start = (bf16[320,512]{1,0:T(8,128)(2,1)S(1)}, bf16[320,512]{1,0:T(8,128)(2,1)S(1)}, u32[]{:S(2)}, u32[]{:S(2)}) collective-permute-start(bf16[320,512]{1,0:T(8,128)(2,1)S(1)} %get-tuple-element.39), channel_id=1, source_target_pairs={{0,32},{32,64},{64,96},{96,128},{128,160},{160,192},{192,224},{1,3... | collective-permute-start | bytes 983048 | tf_op jit(solution)/shard_map/ppermute | solution.py:570
  7.4 1.9 %collective-permute-start.1 = (bf16[320,512]{1,0:T(8,128)(2,1)S(1)}, bf16[320,512]{1,0:T(8,128)(2,1)S(1)}, u32[]{:S(2)}, u32[]{:S(2)}) collective-permute-start(bf16[320,512]{1,0:T(8,128)(2,1)S(1)} %get-tuple-element.40), channel_id=1, source_target_pairs={{32,0},{64,32},{96,64},{128,96},{160,128},{192,160},{224,192},{33,... | collective-permute-start | bytes 983048 | tf_op jit(solution)/shard_map/ppermute | solution.py:571
  9.3 8.0 %fit_inner.1 = (bf16[160,2560]{1,0:T(8,128)(2,1)S(1)}, bf16[160,2560]{1,0:T(8,128)(2,1)S(1)}, bf16[320,2560]{1,0:T(8,128)(2,1)S(1)}, bf16[4,1280,256]{2,1,0:T(8,128)(2,1)S(1)}) custom-call(s32[2,180]{1,0:T(2,128)} %bitcast.4, bf16[320,2560]{1,0:T(8,128)(2,1)} %bitcast.3, bf16[180,128,128]{2,1,0:T(8,128)(2,1)} %tiles_in.1), custom_call_target="tpu_custom_call" | custom-call | flops 1000 | bytes 1000 | tf_op jit(solution)/shard_map/fit_inner/pallas_call | solution.py:85
  17.3 2.9 %collective-permute-done.1.right = bf16[320,512]{1,0:T(8,128)(2,1)S(1)} collective-permute-done((bf16[320,512]{1,0:T(8,128)(2,1)S(1)}, bf16[320,512]{1,0:T(8,128)(2,1)S(1)}, u32[]{:S(2)}, u32[]{:S(2)}) %collective-permute-start.1) | collective-permute-done | bytes 327712 | tf_op jit(solution)/shard_map/ppermute | solution.py:571
  20.2 1.0 fit_edge.1
  21.2 3.2 %collective-permute-start.6 = (bf16[160,2560]{1,0:T(8,128)(2,1)S(1)}, bf16[160,2560]{1,0:T(8,128)(2,1)}, u32[]{:S(2)}, u32[]{:S(2)}) collective-permute-start(bf16[160,2560]{1,0:T(8,128)(2,1)S(1)} %get-tuple-element.46.refs_0_), channel_id=1, source_target_pairs={{0,24},{1,25},{2,26},{3,27},{4,28},{5,29},{6,30},{7,31},{8,0},{9,1... | collective-permute-start | bytes 2457608 | tf_op jit(solution)/shard_map/first/ppermute | solution.py:30
  24.5 2.5 %collective-permute-start.2 = (bf16[160,2560]{1,0:T(8,128)(2,1)S(1)}, bf16[160,2560]{1,0:T(8,128)(2,1)}, u32[]{:S(2)}, u32[]{:S(2)}) collective-permute-start(bf16[160,2560]{1,0:T(8,128)(2,1)S(1)} %get-tuple-element.45.own), channel_id=1, source_target_pairs={{0,6},{1,7},{2,0},{3,1},{4,2},{5,3},{6,4},{7,5},{8,14},{9,15},{10,... | collective-permute-start | bytes 2457608 | tf_op jit(solution)/shard_map/first/ppermute | solution.py:35
  27.1 9.7 %collective-permute-done.6.refs_1_ = bf16[160,2560]{1,0:T(8,128)(2,1)} collective-permute-done((bf16[160,2560]{1,0:T(8,128)(2,1)S(1)}, bf16[160,2560]{1,0:T(8,128)(2,1)}, u32[]{:S(2)}, u32[]{:S(2)}) %collective-permute-start.6) | collective-permute-done | bytes 819232 | tf_op jit(solution)/shard_map/first/ppermute | solution.py:30
  36.8 1.7 %collective-permute-done.5.refs_0_ = bf16[160,2560]{1,0:T(8,128)(2,1)} collective-permute-done((bf16[160,2560]{1,0:T(8,128)(2,1)S(1)}, bf16[160,2560]{1,0:T(8,128)(2,1)}, u32[]{:S(2)}, u32[]{:S(2)}) %collective-permute-start.5) | collective-permute-done | bytes 819232 | tf_op jit(solution)/shard_map/first/ppermute | solution.py:40
  38.6 2.8 %collective-permute-done.4.refs_2_.refs_1_ = bf16[160,2560]{1,0:T(8,128)(2,1)S(1)} collective-permute-done((bf16[160,2560]{1,0:T(8,128)(2,1)S(1)}, bf16[160,2560]{1,0:T(8,128)(2,1)S(1)}, u32[]{:S(2)}, u32[]{:S(2)}) %collective-permute-start.4) | collective-permute-done | bytes 819232 | tf_op jit(solution)/shard_map/first/ppermute | solution.py:30
  41.4 0.9 collective-permute-start.10
  42.3 2.7 %collective-permute-start.9 = (bf16[160,2560]{1,0:T(8,128)(2,1)}, bf16[160,2560]{1,0:T(8,128)(2,1)S(1)}, u32[]{:S(2)}, u32[]{:S(2)}) collective-permute-start(bf16[160,2560]{1,0:T(8,128)(2,1)} %get-tuple-element.47.refs_2_), channel_id=1, source_target_pairs={{0,24},{1,25},{2,26},{3,27},{4,28},{5,29},{6,30},{7,31},{8,0},{9,1... | collective-permute-start | bytes 2457608 | tf_op jit(solution)/shard_map/second/ppermute | solution.py:30
  45.0 2.5 %collective-permute-start.7 = (bf16[160,2560]{1,0:T(8,128)(2,1)}, bf16[160,2560]{1,0:T(8,128)(2,1)S(1)}, u32[]{:S(2)}, u32[]{:S(2)}) collective-permute-start(bf16[160,2560]{1,0:T(8,128)(2,1)} %collective-permute-done.2.ax), channel_id=1, source_target_pairs={{0,6},{1,7},{2,0},{3,1},{4,2},{5,3},{6,4},{7,5},{8,14},{9,15},{10,... | collective-permute-start | bytes 2457608 | tf_op jit(solution)/shard_map/second/ppermute | solution.py:35
  47.4 4.8 %pair_first.1 = (f32[640,640]{1,0:T(8,128)S(1)}, bf16[1280,2560]{1,0:T(8,128)(2,1)S(1)}, bf16[640,2560]{1,0:T(8,128)(2,1)S(1)}) custom-call(bf16[160,2560]{1,0:T(8,128)(2,1)S(1)} %get-tuple-element.45.own, bf16[160,2560]{1,0:T(8,128)(2,1)} %collective-permute-done.2.ax, bf16[160,2560]{1,0:T(8,128)(2,1)S(1)} %collective-permute-done.3.am, ...), custom_call_target="tpu_custom_call" | custom-call | flops 1000 | bytes 1000 | tf_op jit(solution)/shard_map/pair_first/pallas_call | solution.py:85
  52.3 7.3 %collective-permute-done.8.refs_0_.refs_1_ = bf16[160,2560]{1,0:T(8,128)(2,1)S(1)} collective-permute-done((bf16[160,2560]{1,0:T(8,128)(2,1)}, bf16[160,2560]{1,0:T(8,128)(2,1)S(1)}, u32[]{:S(2)}, u32[]{:S(2)}) %collective-permute-start.8) | collective-permute-done | bytes 819232 | tf_op jit(solution)/shard_map/second/ppermute | solution.py:30
  60.4 1.8 %collective-permute-start.11 = (bf16[64,2560]{1,0:T(8,128)(2,1)S(1)}, bf16[64,2560]{1,0:T(8,128)(2,1)S(1)}, u32[]{:S(2)}, u32[]{:S(2)}) collective-permute-start(bf16[64,2560]{1,0:T(8,128)(2,1)S(1)} %get-tuple-element.56), channel_id=1, source_target_pairs={{0,1},{1,0},{2,3},{3,2},{4,5},{5,4},{6,7},{7,6},{8,9},{9,8},{10,11... | collective-permute-start | bytes 983048 | tf_op jit(solution)/shard_map/third/ppermute | solution.py:40
  62.1 3.0 %collective-permute-start.13 = (bf16[48,2560]{1,0:T(8,128)(2,1)S(1)}, bf16[48,2560]{1,0:T(8,128)(2,1)S(1)}, u32[]{:S(2)}, u32[]{:S(2)}) collective-permute-start(bf16[48,2560]{1,0:T(8,128)(2,1)S(1)} %get-tuple-element.58), channel_id=1, source_target_pairs={{0,24},{1,25},{2,26},{3,27},{4,28},{5,29},{6,30},{7,31},{8,0},{9,1... | collective-permute-start | bytes 737288 | tf_op jit(solution)/shard_map/third/ppermute | solution.py:30
  65.2 5.7 %pair_early.1 = (f32[640,640]{1,0:T(8,128)S(1)}, bf16[1280,2560]{1,0:T(8,128)(2,1)S(1)}, bf16[640,2560]{1,0:T(8,128)(2,1)S(1)}, f32[640,480]{1,0:T(8,128)S(1)}) custom-call(f32[640,640]{1,0:T(8,128)S(1)} %get-tuple-element.49.first_in.refs_3_, ...), custom_call_target="tpu_custom_call", output_to_operand_aliasing={{0}: (0, {}), {1}: (1, {}), {2}: (2, {})} | custom-call | flops 1000 | bytes 1000 | tf_op jit(solution)/shard_map/pair_early/pallas_call | solution.py:85
  71.0 1.6 pair_late.1
  72.7 2.3 %collective-permute-done.14.got_in = bf16[640,640]{1,0:T(8,128)(2,1)S(1)} collective-permute-done((bf16[640,640]{1,0:T(8,128)(2,1)S(1)}, bf16[640,640]{1,0:T(8,128)(2,1)S(1)}, u32[]{:S(2)}, u32[]{:S(2)}) %collective-permute-start.14) | collective-permute-done | bytes 819232 | tf_op jit(solution)/shard_map/core/ppermute | solution.py:44
  75.3 12.3 %collective-permute-start.15 = (bf16[160,640]{1,0:T(8,128)(2,1)S(1)}, bf16[160,640]{1,0:T(8,128)(2,1)S(1)}, u32[]{:S(2)}, u32[]{:S(2)}) collective-permute-start(bf16[160,640]{1,0:T(8,128)(2,1)S(1)} %get-tuple-element.62), channel_id=1, source_target_pairs={{0,128},{32,160},{64,192},{96,224},{128,0},{160,32},{192,64},{224,... | collective-permute-start | bytes 614408 | tf_op jit(solution)/shard_map/shares/ppermute | solution.py:48
  87.6 3.6 %collective-permute-start.17 = (bf16[160,640]{1,0:T(8,128)(2,1)S(1)}, bf16[160,640]{1,0:T(8,128)(2,1)S(1)}, u32[]{:S(2)}, u32[]{:S(2)}) collective-permute-start(bf16[160,640]{1,0:T(8,128)(2,1)S(1)} %get-tuple-element.64), channel_id=1, source_target_pairs={{0,192},{32,224},{64,0},{96,32},{128,64},{160,96},{192,128},{224,1... | collective-permute-start | bytes 614408 | tf_op jit(solution)/shard_map/shares/ppermute | solution.py:48
  91.2 4.8 %collective-permute-done.15.refs_0_ = bf16[160,640]{1,0:T(8,128)(2,1)S(1)} collective-permute-done((bf16[160,640]{1,0:T(8,128)(2,1)S(1)}, bf16[160,640]{1,0:T(8,128)(2,1)S(1)}, u32[]{:S(2)}, u32[]{:S(2)}) %collective-permute-start.15) | collective-permute-done | bytes 204832 | tf_op jit(solution)/shard_map/shares/ppermute | solution.py:48
  96.0 8.9 %collective-permute-done.16.refs_1_ = bf16[160,640]{1,0:T(8,128)(2,1)S(1)} collective-permute-done((bf16[160,640]{1,0:T(8,128)(2,1)S(1)}, bf16[160,640]{1,0:T(8,128)(2,1)S(1)}, u32[]{:S(2)}, u32[]{:S(2)}) %collective-permute-start.16) | collective-permute-done | bytes 204832 | tf_op jit(solution)/shard_map/shares/ppermute | solution.py:48
  105.0 1.8 %amplitude.1 = (bf16[80,640]{1,0:T(8,128)(2,1)S(1)}, bf16[80,640]{1,0:T(8,128)(2,1)S(1)}) custom-call(f32[32,160]{1,0:T(8,128)S(1)} %reshape.6.refs_3_.vir, f32[1000]{0:T(1024)S(1)} %copy-done, s32[2]{0:T(128)S(1)} %copy-done.1, f32[160,640]{1,0:T(8,128)S(1)} %get-tuple-element.61.own, bf16[160,640]{1,0:T(8,128)(2,1)S(1)} %collective-permute-done.15.refs_0_, ...), custom_call_target="tpu_custom_call" | custom-call | flops 1000 | bytes 1000 | tf_op jit(solution)/shard_map/amplitude/pallas_call | solution.py:85
  106.7 2.6 %collective-permute-start.27 = (bf16[80,640]{1,0:T(8,128)(2,1)S(1)}, bf16[80,640]{1,0:T(8,128)(2,1)S(1)}, u32[]{:S(2)}, u32[]{:S(2)}) collective-permute-start(bf16[80,640]{1,0:T(8,128)(2,1)S(1)} %get-tuple-element.67.refs_0_), channel_id=1, source_target_pairs={{0,192},{32,224},{64,0},{96,32},{128,64},{160,96},{192,128},{224,1... | collective-permute-start | bytes 307208 | tf_op jit(solution)/shard_map/spread_0/ppermute | solution.py:48
  109.3 2.9 %collective-permute-start.26 = (bf16[80,640]{1,0:T(8,128)(2,1)S(1)}, bf16[80,640]{1,0:T(8,128)(2,1)S(1)}, u32[]{:S(2)}, u32[]{:S(2)}) collective-permute-start(bf16[80,640]{1,0:T(8,128)(2,1)S(1)} %get-tuple-element.67.refs_0_), channel_id=1, source_target_pairs={{0,128},{32,160},{64,192},{96,224},{128,0},{160,32},{192,64},{224,... | collective-permute-start | bytes 307208 | tf_op jit(solution)/shard_map/spread_0/ppermute | solution.py:48
  112.2 1.1 collective-permute-start.28
  113.8 1.4 collective-permute-start.31
  115.2 6.3 %collective-permute-done.26.refs_2_ = bf16[80,640]{1,0:T(8,128)(2,1)S(1)} collective-permute-done((bf16[80,640]{1,0:T(8,128)(2,1)S(1)}, bf16[80,640]{1,0:T(8,128)(2,1)S(1)}, u32[]{:S(2)}, u32[]{:S(2)}) %collective-permute-start.26) | collective-permute-done | bytes 102432 | tf_op jit(solution)/shard_map/spread_0/ppermute | solution.py:48
  122.1 1.3 collective-permute-start.29
  123.5 0.9 collective-permute-done.29.refs_5_
  124.4 2.7 %density_first.1 = (bf16[160,2560]{1,0:T(8,128)(2,1)S(1)}, bf16[160,2560]{1,0:T(8,128)(2,1)S(1)}) custom-call(bf16[80,640]{1,0:T(8,128)(2,1)S(1)} %get-tuple-element.67.refs_0_, bf16[80,640]{1,0:T(8,128)(2,1)S(1)} %collective-permute-done.25.refs_1_, bf16[80,640]{1,0:T(8,128)(2,1)S(1)} %collective-permute-done.26.refs_2_, ...), custom_call_target="tpu_custom_call" | custom-call | flops 1000 | bytes 1000 | tf_op jit(solution)/shard_map/density_first/pallas_call | solution.py:85
  127.1 1.5 collective-permute-start.32
  128.5 1.5 collective-permute-start.33
  130.0 0.9 collective-permute-start.21
  131.0 1.8 %collective-permute-start.20 = (bf16[80,640]{1,0:T(8,128)(2,1)S(1)}, bf16[80,640]{1,0:T(8,128)(2,1)S(1)}, u32[]{:S(2)}, u32[]{:S(2)}) collective-permute-start(bf16[80,640]{1,0:T(8,128)(2,1)S(1)} %get-tuple-element.65.refs_0_), channel_id=1, source_target_pairs={{0,192},{32,224},{64,0},{96,32},{128,64},{160,96},{192,128},{224,1... | collective-permute-start | bytes 307208 | tf_op jit(solution)/shard_map/spread_1/ppermute | solution.py:48
  132.8 2.2 %collective-permute-start.19 = (bf16[80,640]{1,0:T(8,128)(2,1)S(1)}, bf16[80,640]{1,0:T(8,128)(2,1)S(1)}, u32[]{:S(2)}, u32[]{:S(2)}) collective-permute-start(bf16[80,640]{1,0:T(8,128)(2,1)S(1)} %get-tuple-element.65.refs_0_), channel_id=1, source_target_pairs={{0,128},{32,160},{64,192},{96,224},{128,0},{160,32},{192,64},{224,... | collective-permute-start | bytes 307208 | tf_op jit(solution)/shard_map/spread_1/ppermute | solution.py:48
  135.5 1.3 collective-permute-done.20.refs_3_
  137.6 5.4 %collective-permute-done.19.refs_2_ = bf16[80,640]{1,0:T(8,128)(2,1)S(1)} collective-permute-done((bf16[80,640]{1,0:T(8,128)(2,1)S(1)}, bf16[80,640]{1,0:T(8,128)(2,1)S(1)}, u32[]{:S(2)}, u32[]{:S(2)}) %collective-permute-start.19) | collective-permute-done | bytes 102432 | tf_op jit(solution)/shard_map/spread_1/ppermute | solution.py:48
  143.0 1.7 %collective-permute-start.23 = (bf16[80,640]{1,0:T(8,128)(2,1)S(1)}, bf16[80,640]{1,0:T(8,128)(2,1)S(1)}, u32[]{:S(2)}, u32[]{:S(2)}) collective-permute-start(bf16[80,640]{1,0:T(8,128)(2,1)S(1)} %collective-permute-done.19.refs_2_), channel_id=1, source_target_pairs={{0,32},{32,0},{64,96},{96,64},{128,160},{160,128},{192,224},{224,1... | collective-permute-start | bytes 307208 | tf_op jit(solution)/shard_map/other_1/ppermute | solution.py:44
  146.0 2.0 %collective-permute-done.32.refs_9_ = bf16[160,2560]{1,0:T(8,128)(2,1)S(1)} collective-permute-done((bf16[160,2560]{1,0:T(8,128)(2,1)S(1)}, bf16[160,2560]{1,0:T(8,128)(2,1)S(1)}, u32[]{:S(2)}, u32[]{:S(2)}) %collective-permute-start.32) | collective-permute-done | bytes 819232 | tf_op jit(solution)/shard_map/out/ppermute | solution.py:35
  148.0 2.9 %density_second.1 = (bf16[80,2560]{1,0:T(8,128)(2,1)S(1)}, bf16[80,2560]{1,0:T(8,128)(2,1)S(1)}, f32[160,2560]{1,0:T(8,128)S(1)}) custom-call(bf16[80,640]{1,0:T(8,128)(2,1)S(1)} %get-tuple-element.65.refs_0_, bf16[80,640]{1,0:T(8,128)(2,1)S(1)} %collective-permute-done.18.refs_1_, bf16[80,640]{1,0:T(8,128)(2,1)S(1)} %collective-permute-done.19.refs_2_, ...), custom_call_target="tpu_custom_call" | custom-call | flops 1000 | bytes 1000 | tf_op jit(solution)/shard_map/density_second/pallas_call | solution.py:85
  150.9 0.9 collective-permute-start.34
  151.9 1.8 %collective-permute-start.35 = (bf16[80,2560]{1,0:T(8,128)(2,1)S(1)}, bf16[80,2560]{1,0:T(8,128)(2,1)S(1)}, u32[]{:S(2)}, u32[]{:S(2)}) collective-permute-start(bf16[80,2560]{1,0:T(8,128)(2,1)S(1)} %get-tuple-element.72), channel_id=1, source_target_pairs={{0,6},{1,7},{2,0},{3,1},{4,2},{5,3},{6,4},{7,5},{8,14},{9,15},{10,... | collective-permute-start | bytes 1228808 | tf_op jit(solution)/shard_map/out/ppermute | solution.py:35
  153.7 8.3 %collective-permute-done.34.one = bf16[80,2560]{1,0:T(8,128)(2,1)S(1)} collective-permute-done((bf16[80,2560]{1,0:T(8,128)(2,1)S(1)}, bf16[80,2560]{1,0:T(8,128)(2,1)S(1)}, u32[]{:S(2)}, u32[]{:S(2)}) %collective-permute-start.34) | collective-permute-done | bytes 409632 | tf_op jit(solution)/shard_map/out/ppermute | solution.py:35
  162.0 1.5 add.1
  (44 shorter events, 5.1 us)
Async XLA Ops:
  1.1 16.2 %collective-permute-start = (bf16[320,512]{1,0:T(8,128)(2,1)S(1)}, bf16[320,512]{1,0:T(8,128)(2,1)S(1)}, u32[]{:S(2)}, u32[]{:S(2)}) collective-permute-start(bf16[320,512]{1,0:T(8,128)(2,1)S(1)} %get-tuple-element.39), channel_id=1, source_target_pairs={{0,32},{32,64},{64,96},{96,128},{128,160},{160,192},{192,224},{1,3... | collective-permute-start | bytes 983048 | tf_op jit(solution)/shard_map/ppermute | solution.py:570
  7.4 12.8 %collective-permute-start.1 = (bf16[320,512]{1,0:T(8,128)(2,1)S(1)}, bf16[320,512]{1,0:T(8,128)(2,1)S(1)}, u32[]{:S(2)}, u32[]{:S(2)}) collective-permute-start(bf16[320,512]{1,0:T(8,128)(2,1)S(1)} %get-tuple-element.40), channel_id=1, source_target_pairs={{32,0},{64,32},{96,64},{128,96},{160,128},{192,160},{224,192},{33,... | collective-permute-start | bytes 983048 | tf_op jit(solution)/shard_map/ppermute | solution.py:571
  20.2 6.8 %copy-start.2 = (f32[5120]{0:T(1024)S(1)}, f32[5120]{0:T(1024)}, u32[]{:S(2)}) copy-start(f32[5120]{0:T(1024)} %param.9) | copy-start | bytes 61444
  21.2 15.6 %collective-permute-start.6 = (bf16[160,2560]{1,0:T(8,128)(2,1)S(1)}, bf16[160,2560]{1,0:T(8,128)(2,1)}, u32[]{:S(2)}, u32[]{:S(2)}) collective-permute-start(bf16[160,2560]{1,0:T(8,128)(2,1)S(1)} %get-tuple-element.46.refs_0_), channel_id=1, source_target_pairs={{0,24},{1,25},{2,26},{3,27},{4,28},{5,29},{6,30},{7,31},{8,0},{9,1... | collective-permute-start | bytes 2457608 | tf_op jit(solution)/shard_map/first/ppermute | solution.py:30
  24.5 14.1 %collective-permute-start.5 = (bf16[160,2560]{1,0:T(8,128)(2,1)S(1)}, bf16[160,2560]{1,0:T(8,128)(2,1)}, u32[]{:S(2)}, u32[]{:S(2)}) collective-permute-start(bf16[160,2560]{1,0:T(8,128)(2,1)S(1)} %get-tuple-element.46.refs_0_), channel_id=1, source_target_pairs={{0,1},{1,0},{2,3},{3,2},{4,5},{5,4},{6,7},{7,6},{8,9},{9,8},{10,11... | collective-permute-start | bytes 2457608 | tf_op jit(solution)/shard_map/first/ppermute | solution.py:40
  24.5 16.9 %collective-permute-start.4 = (bf16[160,2560]{1,0:T(8,128)(2,1)S(1)}, bf16[160,2560]{1,0:T(8,128)(2,1)S(1)}, u32[]{:S(2)}, u32[]{:S(2)}) collective-permute-start(bf16[160,2560]{1,0:T(8,128)(2,1)S(1)} %get-tuple-element.46.refs_0_), channel_id=1, source_target_pairs={{0,8},{1,9},{2,10},{3,11},{4,12},{5,13},{6,14},{7,15},{8,16},{9,17... | collective-permute-start | bytes 2457608 | tf_op jit(solution)/shard_map/first/ppermute | solution.py:30
  24.5 20.5 %collective-permute-start.2 = (bf16[160,2560]{1,0:T(8,128)(2,1)S(1)}, bf16[160,2560]{1,0:T(8,128)(2,1)}, u32[]{:S(2)}, u32[]{:S(2)}) collective-permute-start(bf16[160,2560]{1,0:T(8,128)(2,1)S(1)} %get-tuple-element.45.own), channel_id=1, source_target_pairs={{0,6},{1,7},{2,0},{3,1},{4,2},{5,3},{6,4},{7,5},{8,14},{9,15},{10,... | collective-permute-start | bytes 2457608 | tf_op jit(solution)/shard_map/first/ppermute | solution.py:35
  27.0 20.4 %collective-permute-start.3 = (bf16[160,2560]{1,0:T(8,128)(2,1)S(1)}, bf16[160,2560]{1,0:T(8,128)(2,1)S(1)}, u32[]{:S(2)}, u32[]{:S(2)}) collective-permute-start(bf16[160,2560]{1,0:T(8,128)(2,1)S(1)} %get-tuple-element.45.own), channel_id=1, source_target_pairs={{0,2},{1,3},{2,4},{3,5},{4,6},{5,7},{6,0},{7,1},{8,10},{9,11},{10,... | collective-permute-start | bytes 2457608 | tf_op jit(solution)/shard_map/first/ppermute | solution.py:35
  41.4 18.2 %collective-permute-start.8 = (bf16[160,2560]{1,0:T(8,128)(2,1)}, bf16[160,2560]{1,0:T(8,128)(2,1)S(1)}, u32[]{:S(2)}, u32[]{:S(2)}) collective-permute-start(bf16[160,2560]{1,0:T(8,128)(2,1)} %get-tuple-element.48.refs_3_), channel_id=1, source_target_pairs={{0,8},{1,9},{2,10},{3,11},{4,12},{5,13},{6,14},{7,15},{8,16},{9,17... | collective-permute-start | bytes 2457608 | tf_op jit(solution)/shard_map/second/ppermute | solution.py:30
  41.4 18.2 %collective-permute-start.10 = (bf16[160,2560]{1,0:T(8,128)(2,1)}, bf16[160,2560]{1,0:T(8,128)(2,1)S(1)}, u32[]{:S(2)}, u32[]{:S(2)}) collective-permute-start(bf16[160,2560]{1,0:T(8,128)(2,1)} %get-tuple-element.47.refs_2_), channel_id=1, source_target_pairs={{0,1},{1,0},{2,3},{3,2},{4,5},{5,4},{6,7},{7,6},{8,9},{9,8},{10,11... | collective-permute-start | bytes 2457608 | tf_op jit(solution)/shard_map/second/ppermute | solution.py:40
  42.3 17.3 %collective-permute-start.9 = (bf16[160,2560]{1,0:T(8,128)(2,1)}, bf16[160,2560]{1,0:T(8,128)(2,1)S(1)}, u32[]{:S(2)}, u32[]{:S(2)}) collective-permute-start(bf16[160,2560]{1,0:T(8,128)(2,1)} %get-tuple-element.47.refs_2_), channel_id=1, source_target_pairs={{0,24},{1,25},{2,26},{3,27},{4,28},{5,29},{6,30},{7,31},{8,0},{9,1... | collective-permute-start | bytes 2457608 | tf_op jit(solution)/shard_map/second/ppermute | solution.py:30
  45.0 20.2 %collective-permute-start.7 = (bf16[160,2560]{1,0:T(8,128)(2,1)}, bf16[160,2560]{1,0:T(8,128)(2,1)S(1)}, u32[]{:S(2)}, u32[]{:S(2)}) collective-permute-start(bf16[160,2560]{1,0:T(8,128)(2,1)} %collective-permute-done.2.ax), channel_id=1, source_target_pairs={{0,6},{1,7},{2,0},{3,1},{4,2},{5,3},{6,4},{7,5},{8,14},{9,15},{10,... | collective-permute-start | bytes 2457608 | tf_op jit(solution)/shard_map/second/ppermute | solution.py:35
  60.4 10.6 %collective-permute-start.11 = (bf16[64,2560]{1,0:T(8,128)(2,1)S(1)}, bf16[64,2560]{1,0:T(8,128)(2,1)S(1)}, u32[]{:S(2)}, u32[]{:S(2)}) collective-permute-start(bf16[64,2560]{1,0:T(8,128)(2,1)S(1)} %get-tuple-element.56), channel_id=1, source_target_pairs={{0,1},{1,0},{2,3},{3,2},{4,5},{5,4},{6,7},{7,6},{8,9},{9,8},{10,11... | collective-permute-start | bytes 983048 | tf_op jit(solution)/shard_map/third/ppermute | solution.py:40
  62.1 8.8 %collective-permute-start.12 = (bf16[48,2560]{1,0:T(8,128)(2,1)S(1)}, bf16[48,2560]{1,0:T(8,128)(2,1)S(1)}, u32[]{:S(2)}, u32[]{:S(2)}) collective-permute-start(bf16[48,2560]{1,0:T(8,128)(2,1)S(1)} %get-tuple-element.57), channel_id=1, source_target_pairs={{0,8},{1,9},{2,10},{3,11},{4,12},{5,13},{6,14},{7,15},{8,16},{9,17... | collective-permute-start | bytes 737288 | tf_op jit(solution)/shard_map/third/ppermute | solution.py:30
  62.1 8.8 %collective-permute-start.13 = (bf16[48,2560]{1,0:T(8,128)(2,1)S(1)}, bf16[48,2560]{1,0:T(8,128)(2,1)S(1)}, u32[]{:S(2)}, u32[]{:S(2)}) collective-permute-start(bf16[48,2560]{1,0:T(8,128)(2,1)S(1)} %get-tuple-element.58), channel_id=1, source_target_pairs={{0,24},{1,25},{2,26},{3,27},{4,28},{5,29},{6,30},{7,31},{8,0},{9,1... | collective-permute-start | bytes 737288 | tf_op jit(solution)/shard_map/third/ppermute | solution.py:30
  70.9 34.0 %copy-start = (f32[1000]{0:T(1024)S(1)}, f32[1000]{0:T(1024)}, u32[]{:S(2)}) copy-start(f32[1000]{0:T(1024)} %occ.1) | copy-start | bytes 12004
  71.0 34.0 %copy-start.1 = (s32[2]{0:T(128)S(1)}, s32[2]{0:T(128)}, u32[]{:S(2)}) copy-start(s32[2]{0:T(128)} %chosen.1) | copy-start | bytes 28
  72.6 2.4 %collective-permute-start.14 = (bf16[640,640]{1,0:T(8,128)(2,1)S(1)}, bf16[640,640]{1,0:T(8,128)(2,1)S(1)}, u32[]{:S(2)}, u32[]{:S(2)}) collective-permute-start(bf16[640,640]{1,0:T(8,128)(2,1)S(1)} %get-tuple-element.60), channel_id=1, source_target_pairs={{0,32},{32,0},{64,96},{96,64},{128,160},{160,128},{192,224},{224,1... | collective-permute-start | bytes 2457608 | tf_op jit(solution)/shard_map/core/ppermute | solution.py:44
  75.3 20.7 %collective-permute-start.15 = (bf16[160,640]{1,0:T(8,128)(2,1)S(1)}, bf16[160,640]{1,0:T(8,128)(2,1)S(1)}, u32[]{:S(2)}, u32[]{:S(2)}) collective-permute-start(bf16[160,640]{1,0:T(8,128)(2,1)S(1)} %get-tuple-element.62), channel_id=1, source_target_pairs={{0,128},{32,160},{64,192},{96,224},{128,0},{160,32},{192,64},{224,... | collective-permute-start | bytes 614408 | tf_op jit(solution)/shard_map/shares/ppermute | solution.py:48
  87.6 17.3 %collective-permute-start.16 = (bf16[160,640]{1,0:T(8,128)(2,1)S(1)}, bf16[160,640]{1,0:T(8,128)(2,1)S(1)}, u32[]{:S(2)}, u32[]{:S(2)}) collective-permute-start(bf16[160,640]{1,0:T(8,128)(2,1)S(1)} %get-tuple-element.63), channel_id=1, source_target_pairs={{0,64},{32,96},{64,128},{96,160},{128,192},{160,224},{192,0},{224,... | collective-permute-start | bytes 614408 | tf_op jit(solution)/shard_map/shares/ppermute | solution.py:48
  87.6 17.3 %collective-permute-start.17 = (bf16[160,640]{1,0:T(8,128)(2,1)S(1)}, bf16[160,640]{1,0:T(8,128)(2,1)S(1)}, u32[]{:S(2)}, u32[]{:S(2)}) collective-permute-start(bf16[160,640]{1,0:T(8,128)(2,1)S(1)} %get-tuple-element.64), channel_id=1, source_target_pairs={{0,192},{32,224},{64,0},{96,32},{128,64},{160,96},{192,128},{224,1... | collective-permute-start | bytes 614408 | tf_op jit(solution)/shard_map/shares/ppermute | solution.py:48
  106.7 7.1 %collective-permute-start.27 = (bf16[80,640]{1,0:T(8,128)(2,1)S(1)}, bf16[80,640]{1,0:T(8,128)(2,1)S(1)}, u32[]{:S(2)}, u32[]{:S(2)}) collective-permute-start(bf16[80,640]{1,0:T(8,128)(2,1)S(1)} %get-tuple-element.67.refs_0_), channel_id=1, source_target_pairs={{0,192},{32,224},{64,0},{96,32},{128,64},{160,96},{192,128},{224,1... | collective-permute-start | bytes 307208 | tf_op jit(solution)/shard_map/spread_0/ppermute | solution.py:48
  109.3 12.2 %collective-permute-start.26 = (bf16[80,640]{1,0:T(8,128)(2,1)S(1)}, bf16[80,640]{1,0:T(8,128)(2,1)S(1)}, u32[]{:S(2)}, u32[]{:S(2)}) collective-permute-start(bf16[80,640]{1,0:T(8,128)(2,1)S(1)} %get-tuple-element.67.refs_0_), channel_id=1, source_target_pairs={{0,128},{32,160},{64,192},{96,224},{128,0},{160,32},{192,64},{224,... | collective-permute-start | bytes 307208 | tf_op jit(solution)/shard_map/spread_0/ppermute | solution.py:48
  112.2 9.9 %collective-permute-start.25 = (bf16[80,640]{1,0:T(8,128)(2,1)S(1)}, bf16[80,640]{1,0:T(8,128)(2,1)S(1)}, u32[]{:S(2)}, u32[]{:S(2)}) collective-permute-start(bf16[80,640]{1,0:T(8,128)(2,1)S(1)} %get-tuple-element.67.refs_0_), channel_id=1, source_target_pairs={{0,64},{32,96},{64,128},{96,160},{128,192},{160,224},{192,0},{224,... | collective-permute-start | bytes 307208 | tf_op jit(solution)/shard_map/spread_0/ppermute | solution.py:48
  112.2 11.2 %collective-permute-start.28 = (bf16[80,640]{1,0:T(8,128)(2,1)S(1)}, bf16[80,640]{1,0:T(8,128)(2,1)S(1)}, u32[]{:S(2)}, u32[]{:S(2)}) collective-permute-start(bf16[80,640]{1,0:T(8,128)(2,1)S(1)} %get-tuple-element.67.refs_0_), channel_id=1, source_target_pairs={{0,32},{32,0},{64,96},{96,64},{128,160},{160,128},{192,224},{224,1... | collective-permute-start | bytes 307208 | tf_op jit(solution)/shard_map/other_0/ppermute | solution.py:44
  113.8 9.6 %collective-permute-start.31 = (bf16[80,640]{1,0:T(8,128)(2,1)S(1)}, bf16[80,640]{1,0:T(8,128)(2,1)S(1)}, u32[]{:S(2)}, u32[]{:S(2)}) collective-permute-start(bf16[80,640]{1,0:T(8,128)(2,1)S(1)} %collective-permute-done.27.refs_3_), channel_id=1, source_target_pairs={{0,32},{32,0},{64,96},{96,64},{128,160},{160,128},{192,224},{224,1... | collective-permute-start | bytes 307208 | tf_op jit(solution)/shard_map/other_0/ppermute | solution.py:44
  121.5 1.9 %collective-permute-start.30 = (bf16[80,640]{1,0:T(8,128)(2,1)S(1)}, bf16[80,640]{1,0:T(8,128)(2,1)S(1)}, u32[]{:S(2)}, u32[]{:S(2)}) collective-permute-start(bf16[80,640]{1,0:T(8,128)(2,1)S(1)} %collective-permute-done.26.refs_2_), channel_id=1, source_target_pairs={{0,32},{32,0},{64,96},{96,64},{128,160},{160,128},{192,224},{224,1... | collective-permute-start | bytes 307208 | tf_op jit(solution)/shard_map/other_0/ppermute | solution.py:44
  122.1 2.3 %collective-permute-start.29 = (bf16[80,640]{1,0:T(8,128)(2,1)S(1)}, bf16[80,640]{1,0:T(8,128)(2,1)S(1)}, u32[]{:S(2)}, u32[]{:S(2)}) collective-permute-start(bf16[80,640]{1,0:T(8,128)(2,1)S(1)} %collective-permute-done.25.refs_1_), channel_id=1, source_target_pairs={{0,32},{32,0},{64,96},{96,64},{128,160},{160,128},{192,224},{224,1... | collective-permute-start | bytes 307208 | tf_op jit(solution)/shard_map/other_0/ppermute | solution.py:44
  127.1 21.0 %collective-permute-start.32 = (bf16[160,2560]{1,0:T(8,128)(2,1)S(1)}, bf16[160,2560]{1,0:T(8,128)(2,1)S(1)}, u32[]{:S(2)}, u32[]{:S(2)}) collective-permute-start(bf16[160,2560]{1,0:T(8,128)(2,1)S(1)} %get-tuple-element.68), channel_id=1, source_target_pairs={{0,2},{1,3},{2,4},{3,5},{4,6},{5,7},{6,0},{7,1},{8,10},{9,11},{10,... | collective-permute-start | bytes 2457608 | tf_op jit(solution)/shard_map/out/ppermute | solution.py:35
  128.5 19.5 %collective-permute-start.33 = (bf16[160,2560]{1,0:T(8,128)(2,1)S(1)}, bf16[160,2560]{1,0:T(8,128)(2,1)S(1)}, u32[]{:S(2)}, u32[]{:S(2)}) collective-permute-start(bf16[160,2560]{1,0:T(8,128)(2,1)S(1)} %get-tuple-element.69), channel_id=1, source_target_pairs={{0,6},{1,7},{2,0},{3,1},{4,2},{5,3},{6,4},{7,5},{8,14},{9,15},{10,... | collective-permute-start | bytes 2457608 | tf_op jit(solution)/shard_map/out/ppermute | solution.py:35
  130.0 5.0 %collective-permute-start.21 = (bf16[80,640]{1,0:T(8,128)(2,1)S(1)}, bf16[80,640]{1,0:T(8,128)(2,1)S(1)}, u32[]{:S(2)}, u32[]{:S(2)}) collective-permute-start(bf16[80,640]{1,0:T(8,128)(2,1)S(1)} %get-tuple-element.65.refs_0_), channel_id=1, source_target_pairs={{0,32},{32,0},{64,96},{96,64},{128,160},{160,128},{192,224},{224,1... | collective-permute-start | bytes 307208 | tf_op jit(solution)/shard_map/other_1/ppermute | solution.py:44
  131.0 5.9 %collective-permute-start.20 = (bf16[80,640]{1,0:T(8,128)(2,1)S(1)}, bf16[80,640]{1,0:T(8,128)(2,1)S(1)}, u32[]{:S(2)}, u32[]{:S(2)}) collective-permute-start(bf16[80,640]{1,0:T(8,128)(2,1)S(1)} %get-tuple-element.65.refs_0_), channel_id=1, source_target_pairs={{0,192},{32,224},{64,0},{96,32},{128,64},{160,96},{192,128},{224,1... | collective-permute-start | bytes 307208 | tf_op jit(solution)/shard_map/spread_1/ppermute | solution.py:48
  132.8 10.2 %collective-permute-start.19 = (bf16[80,640]{1,0:T(8,128)(2,1)S(1)}, bf16[80,640]{1,0:T(8,128)(2,1)S(1)}, u32[]{:S(2)}, u32[]{:S(2)}) collective-permute-start(bf16[80,640]{1,0:T(8,128)(2,1)S(1)} %get-tuple-element.65.refs_0_), channel_id=1, source_target_pairs={{0,128},{32,160},{64,192},{96,224},{128,0},{160,32},{192,64},{224,... | collective-permute-start | bytes 307208 | tf_op jit(solution)/shard_map/spread_1/ppermute | solution.py:48
  135.0 9.7 %collective-permute-start.18 = (bf16[80,640]{1,0:T(8,128)(2,1)S(1)}, bf16[80,640]{1,0:T(8,128)(2,1)S(1)}, u32[]{:S(2)}, u32[]{:S(2)}) collective-permute-start(bf16[80,640]{1,0:T(8,128)(2,1)S(1)} %get-tuple-element.65.refs_0_), channel_id=1, source_target_pairs={{0,64},{32,96},{64,128},{96,160},{128,192},{160,224},{192,0},{224,... | collective-permute-start | bytes 307208 | tf_op jit(solution)/shard_map/spread_1/ppermute | solution.py:48
  136.8 8.2 %collective-permute-start.24 = (bf16[80,640]{1,0:T(8,128)(2,1)S(1)}, bf16[80,640]{1,0:T(8,128)(2,1)S(1)}, u32[]{:S(2)}, u32[]{:S(2)}) collective-permute-start(bf16[80,640]{1,0:T(8,128)(2,1)S(1)} %collective-permute-done.20.refs_3_), channel_id=1, source_target_pairs={{0,32},{32,0},{64,96},{96,64},{128,160},{160,128},{192,224},{224,1... | collective-permute-start | bytes 307208 | tf_op jit(solution)/shard_map/other_1/ppermute | solution.py:44
  143.0 2.6 %collective-permute-start.23 = (bf16[80,640]{1,0:T(8,128)(2,1)S(1)}, bf16[80,640]{1,0:T(8,128)(2,1)S(1)}, u32[]{:S(2)}, u32[]{:S(2)}) collective-permute-start(bf16[80,640]{1,0:T(8,128)(2,1)S(1)} %collective-permute-done.19.refs_2_), channel_id=1, source_target_pairs={{0,32},{32,0},{64,96},{96,64},{128,160},{160,128},{192,224},{224,1... | collective-permute-start | bytes 307208 | tf_op jit(solution)/shard_map/other_1/ppermute | solution.py:44
  144.7 1.3 collective-permute-start.22
  150.9 11.1 %collective-permute-start.34 = (bf16[80,2560]{1,0:T(8,128)(2,1)S(1)}, bf16[80,2560]{1,0:T(8,128)(2,1)S(1)}, u32[]{:S(2)}, u32[]{:S(2)}) collective-permute-start(bf16[80,2560]{1,0:T(8,128)(2,1)S(1)} %get-tuple-element.71), channel_id=1, source_target_pairs={{0,2},{1,3},{2,4},{3,5},{4,6},{5,7},{6,0},{7,1},{8,10},{9,11},{10,... | collective-permute-start | bytes 1228808 | tf_op jit(solution)/shard_map/out/ppermute | solution.py:35
  151.9 10.1 %collective-permute-start.35 = (bf16[80,2560]{1,0:T(8,128)(2,1)S(1)}, bf16[80,2560]{1,0:T(8,128)(2,1)S(1)}, u32[]{:S(2)}, u32[]{:S(2)}) collective-permute-start(bf16[80,2560]{1,0:T(8,128)(2,1)S(1)} %get-tuple-element.72), channel_id=1, source_target_pairs={{0,6},{1,7},{2,0},{3,1},{4,2},{5,3},{6,4},{7,5},{8,14},{9,15},{10,... | collective-permute-start | bytes 1228808 | tf_op jit(solution)/shard_map/out/ppermute | solution.py:35

commit v3 on v2

--- a/solution.py
+++ b/solution.py
@@ -325,6 +325,7 @@
             (rows, slice(0, WIDE), first.at[rows]),
             (slice(0, WIDE), slice(WIDE, 7 * ROWS), early),
         ],
+        unroll=True,
     )
 
 
@@ -378,10 +379,7 @@
     )
 
 
-def core_sum_kernel(keep, got_in, own, s1, s2, s3, got, sem):
-    copy = pltpu.make_async_copy(got_in, got, sem)
-    copy.start()
-    copy.wait()
+def core_sum_kernel(keep, got, own, s1, s2, s3):
     high = position()[0]
     for step, out in enumerate((own, s1, s2, s3)):
         for wave in range(2):
@@ -394,9 +392,8 @@
     share = (2 * SHARE, WIDE)
     return call(
         core_sum_kernel,
-        [(keep, VMEM), (got, ANY)],
+        [(keep, VMEM), (got, VMEM)],
         [vmem(share, f32)] + [hbm(share)] * 3,
-        [pltpu.VMEM(got.shape, bf16), DMA(())],
         name="core_sum",
     )
 
@@ -405,12 +402,7 @@
 
 
 def amplitude_kernel(vir, occ, chosen, own, *refs):
-    arrived, outs, got, sems = refs[:3], refs[3:5], refs[5], refs[6]
-    copies = [
-        pltpu.make_async_copy(r, got.at[i], sems.at[i]) for i, r in enumerate(arrived)
-    ]
-    for c in copies:
-        c.start()
+    arrived, outs = refs[:3], refs[3:5]
     high, core, y, x, z = position()
     occ_total = occ[chosen[0]] + occ[chosen[1]]
     lane = lax.broadcasted_iota(jnp.int32, (SHARE, ROWS), 1)
@@ -434,13 +426,11 @@
         away = jnp.where(core == 0, first[1], last[1])
         places.append((((y + step) % 4) * 4 + x) * 2 + jnp.where(away == 1, 1 - z, z))
     columns = jnp.concatenate([vir[pl.ds(at, 1), :] for at in places], axis=1)
-    for c in copies:
-        c.wait()
     for wave, out in enumerate(outs):
         part = slice(wave * SHARE, (wave + 1) * SHARE)
         total = own[part]
-        for i in range(3):
-            total = total + got[i, part].astype(f32)
+        for r in arrived:
+            total = total + r[part].astype(f32)
         denominator = (rows[wave] + columns) - occ_total
         out[...] = (total / denominator).astype(bf16)
 
@@ -449,24 +439,18 @@
     return call(
         amplitude_kernel,
         [(vir, VMEM), (occ, SMEM), (chosen, SMEM), (own, VMEM)]
-        + [(v, ANY) for v in arrived],
+        + [(v, VMEM) for v in arrived],
         [hbm((SHARE, WIDE))] * 2,
-        [pltpu.VMEM((3, *own.shape), bf16), DMA((3,))],
         name="amplitude",
     )
 
 
-def gather_rows(mine, other, tcat, sems):
+def gather_rows(mine, other, tcat):
     high, core = position()[:2]
-    copies = []
     for k in range(4):
         rows = pl.ds(pl.multiple_of(((high - k + 4) % 4) * SHARE, SHARE), SHARE)
-        for i, (v, of) in enumerate(((mine[k], core), (other[k], 1 - core))):
-            columns = pl.ds(pl.multiple_of(of * WIDE, WIDE), WIDE)
-            copies.append(pltpu.make_async_copy(v, tcat.at[rows, columns], sems.at[k, i]))
-    for c in copies:
-        c.start()
-    return copies
+        for v, of in ((mine[k], core), (other[k], 1 - core)):
+            tcat[rows, pl.ds(pl.multiple_of(of * WIDE, WIDE), WIDE)] = v[...]
 
 
 def product(tcat, bcat, half):
@@ -479,9 +463,8 @@
 
 def density_first_kernel(*refs):
     mine, other, bcat = refs[:4], refs[4:8], refs[8]
-    outs, tcat, sems = refs[9:11], refs[11], refs[12]
-    for c in gather_rows(mine, other, tcat, sems):
-        c.wait()
+    outs, tcat = refs[9:11], refs[11]
+    gather_rows(mine, other, tcat)
 
     @pl.loop(0, 2)
     def _(half):
@@ -495,25 +478,17 @@
 def density_first(mine, other, bcat):
     return call(
         density_first_kernel,
-        [(v, ANY) for v in (*mine, *other)] + [(bcat, VMEM)],
+        [(v, VMEM) for v in (*mine, *other, bcat)],
         [hbm((ROWS, AUX))] * 2,
-        [pltpu.VMEM(TCAT, bf16), DMA((4, 2))],
+        [pltpu.VMEM(TCAT, bf16)],
         name="density_first",
     )
 
 
 def density_second_kernel(*refs):
-    mine, other, (bcat, from_m, from_x) = refs[:4], refs[4:8], refs[8:11]
-    x1, m2, own, tcat, got_m, got_x, row_sems, sems = refs[11:]
-    rows_copies = gather_rows(mine, other, tcat, row_sems)
-    copies = [
-        pltpu.make_async_copy(from_m, got_m, sems.at[0]),
-        pltpu.make_async_copy(from_x, got_x, sems.at[1]),
-    ]
-    for c in copies:
-        c.start()
-    for c in rows_copies + copies:
-        c.wait()
+    mine, other, (bcat, got_m, got_x) = refs[:4], refs[4:8], refs[8:11]
+    x1, m2, own, tcat = refs[11:]
+    gather_rows(mine, other, tcat)
 
     @pl.loop(0, 2)
     def _(half):
@@ -529,34 +504,23 @@
 def density_second(mine, other, bcat, from_m, from_x):
     return call(
         density_second_kernel,
-        [(v, ANY) for v in (*mine, *other)]
-        + [(bcat, VMEM), (from_m, ANY), (from_x, ANY)],
+        [(v, VMEM) for v in (*mine, *other, bcat, from_m, from_x)],
         [hbm((HALF, AUX))] * 2 + [vmem((ROWS, AUX), f32)],
-        [pltpu.VMEM(TCAT, bf16)]
-        + [pltpu.VMEM((ROWS, AUX), bf16)] * 2
-        + [DMA((4, 2)), DMA((2,))],
+        [pltpu.VMEM(TCAT, bf16)],
         name="density_second",
     )
 
 
-def add_kernel(own, one, two, out, got, sems):
-    copies = [
-        pltpu.make_async_copy(v, got.at[pl.ds(i * HALF, HALF)], sems.at[i])
-        for i, v in enumerate((one, two))
-    ]
-    for c in copies:
-        c.start()
-    for c in copies:
-        c.wait()
-    out[...] = (own[...] + got[...].astype(f32)).astype(out.dtype)
+def add_kernel(own, one, two, out):
+    out[:HALF] = (own[:HALF] + one[...].astype(f32)).astype(bf16)
+    out[HALF:] = (own[HALF:] + two[...].astype(f32)).astype(bf16)
 
 
 def add(own, one, two):
     return call(
         add_kernel,
-        [(own, VMEM), (one, ANY), (two, ANY)],
+        [(own, VMEM), (one, VMEM), (two, VMEM)],
         [hbm((ROWS, AUX))],
-        [pltpu.VMEM((ROWS, AUX), bf16), DMA((2,))],
         name="add",
     )[0]
 

time: 165 us -> 162 us (0.982)
  waiting for transfers between devices: 66.5 us -> 59.1 us
  starting transfers between devices: 64.6 us -> 71.9 us
  Pallas kernels: 32.1 us -> 27.9 us
    ppermute x9, waiting for transfers between devices: 27.3 us -> 18.8 us  [send_high(): return lax.ppermute(v, 'grp', [(g, (g + 2 * step) % 8) for g in range(8)])]
    pallas_call x11, Pallas kernels: 31.3 us -> 27.1 us  [call(): pl.pallas_call(kernel, in_specs=[spec for _, spec in args], out_specs=[VM...]
    ppermute x9, starting transfers between devices: 8.09 us -> 12.3 us  [send_core(): return lax.ppermute(v, 'grp', [(g, g ^ 1) for g in range(8)])]
    ppermute x9, starting transfers between devices: 25.9 us -> 29.3 us  [send_high(): return lax.ppermute(v, 'grp', [(g, (g + 2 * step) % 8) for g in range(8)])]
  transfers between devices with their start and end apart: 36 -> 36, of which waited for: 17 -> 20; matrix products, arithmetic and copies ran while one was open for 0% -> 0% of each run, Pallas kernels for 12% -> 11%
where the time goes in v3:
time: 162 us; the launch traced here: 159 us
  starting transfers between devices  71.9 us (44%)
  waiting for transfers between devices  59.1 us (36%)
  Pallas kernels  27.9 us (17%)
    ppermute x9, starting transfers between devices, send_high(): return lax.ppermute(v, 'grp', [(g, (g + 2 * step) % 8) for g in range(8)])  29.3 us
    pallas_call x11, Pallas kernels, call(): pl.pallas_call(kernel, in_specs=[spec for _, spec in args], out_specs=[VM...  27.1 us
    ppermute x6, waiting for transfers between devices, send_y(): return lax.ppermute(v, 'blk', pairs)  21.1 us
    ppermute x9, waiting for transfers between devices, send_high(): return lax.ppermute(v, 'grp', [(g, (g + 2 * step) % 8) for g in range(8)])  18.8 us
    ppermute x9, starting transfers between devices, send_core(): return lax.ppermute(v, 'grp', [(g, g ^ 1) for g in range(8)])  12.3 us
    ppermute x7, starting transfers between devices, send_x(): return lax.ppermute(v, 'blk', pairs)  10.5 us
    ppermute x7, waiting for transfers between devices, send_x(): return lax.ppermute(v, 'blk', pairs)  10.4 us
    ppermute x6, starting transfers between devices, send_y(): return lax.ppermute(v, 'blk', pairs)  8.94 us
  transfers between devices with their start and end apart: 36, of which 20 were waited for; matrix products, arithmetic and copies ran while one was open for 0% of the time, Pallas kernels for 11%

profile of v3, /device:TPU:1, one launch (start us, length us, event | category | flops | bytes accessed | tf_op | source)
XLA Modules:
  0.0 159.2 jit_solution(16253427240991402188)
XLA Ops:
  0.0 1.1 ends.1
  1.1 6.3 %collective-permute-start = (bf16[320,512]{1,0:T(8,128)(2,1)S(1)}, bf16[320,512]{1,0:T(8,128)(2,1)S(1)}, u32[]{:S(2)}, u32[]{:S(2)}) collective-permute-start(bf16[320,512]{1,0:T(8,128)(2,1)S(1)} %get-tuple-element.39), channel_id=1, source_target_pairs={{0,32},{32,64},{64,96},{96,128},{128,160},{160,192},{192,224},{1,3... | collective-permute-start | bytes 983048 | tf_op jit(solution)/shard_map/ppermute | solution.py:534
  7.4 1.9 %collective-permute-start.1 = (bf16[320,512]{1,0:T(8,128)(2,1)S(1)}, bf16[320,512]{1,0:T(8,128)(2,1)S(1)}, u32[]{:S(2)}, u32[]{:S(2)}) collective-permute-start(bf16[320,512]{1,0:T(8,128)(2,1)S(1)} %get-tuple-element.40), channel_id=1, source_target_pairs={{32,0},{64,32},{96,64},{128,96},{160,128},{192,160},{224,192},{33,... | collective-permute-start | bytes 983048 | tf_op jit(solution)/shard_map/ppermute | solution.py:535
  9.3 8.0 %fit_inner.1 = (bf16[160,2560]{1,0:T(8,128)(2,1)S(1)}, bf16[160,2560]{1,0:T(8,128)(2,1)S(1)}, bf16[320,2560]{1,0:T(8,128)(2,1)S(1)}, bf16[4,1280,256]{2,1,0:T(8,128)(2,1)S(1)}) custom-call(s32[2,180]{1,0:T(2,128)} %bitcast.4, bf16[320,2560]{1,0:T(8,128)(2,1)} %bitcast.3, bf16[180,128,128]{2,1,0:T(8,128)(2,1)} %tiles_in.1), custom_call_target="tpu_custom_call" | custom-call | flops 1000 | bytes 1000 | tf_op jit(solution)/shard_map/fit_inner/pallas_call | solution.py:85
  17.3 2.9 %collective-permute-done.1.right = bf16[320,512]{1,0:T(8,128)(2,1)S(1)} collective-permute-done((bf16[320,512]{1,0:T(8,128)(2,1)S(1)}, bf16[320,512]{1,0:T(8,128)(2,1)S(1)}, u32[]{:S(2)}, u32[]{:S(2)}) %collective-permute-start.1) | collective-permute-done | bytes 327712 | tf_op jit(solution)/shard_map/ppermute | solution.py:535
  20.2 1.0 fit_edge.1
  21.2 3.2 %collective-permute-start.6 = (bf16[160,2560]{1,0:T(8,128)(2,1)S(1)}, bf16[160,2560]{1,0:T(8,128)(2,1)}, u32[]{:S(2)}, u32[]{:S(2)}) collective-permute-start(bf16[160,2560]{1,0:T(8,128)(2,1)S(1)} %get-tuple-element.46.refs_0_), channel_id=1, source_target_pairs={{0,24},{1,25},{2,26},{3,27},{4,28},{5,29},{6,30},{7,31},{8,0},{9,1... | collective-permute-start | bytes 2457608 | tf_op jit(solution)/shard_map/first/ppermute | solution.py:30
  24.5 2.5 %collective-permute-start.2 = (bf16[160,2560]{1,0:T(8,128)(2,1)S(1)}, bf16[160,2560]{1,0:T(8,128)(2,1)}, u32[]{:S(2)}, u32[]{:S(2)}) collective-permute-start(bf16[160,2560]{1,0:T(8,128)(2,1)S(1)} %get-tuple-element.45.own), channel_id=1, source_target_pairs={{0,6},{1,7},{2,0},{3,1},{4,2},{5,3},{6,4},{7,5},{8,14},{9,15},{10,... | collective-permute-start | bytes 2457608 | tf_op jit(solution)/shard_map/first/ppermute | solution.py:35
  27.1 9.7 %collective-permute-done.6.refs_1_ = bf16[160,2560]{1,0:T(8,128)(2,1)} collective-permute-done((bf16[160,2560]{1,0:T(8,128)(2,1)S(1)}, bf16[160,2560]{1,0:T(8,128)(2,1)}, u32[]{:S(2)}, u32[]{:S(2)}) %collective-permute-start.6) | collective-permute-done | bytes 819232 | tf_op jit(solution)/shard_map/first/ppermute | solution.py:30
  36.8 1.7 %collective-permute-done.5.refs_0_ = bf16[160,2560]{1,0:T(8,128)(2,1)} collective-permute-done((bf16[160,2560]{1,0:T(8,128)(2,1)S(1)}, bf16[160,2560]{1,0:T(8,128)(2,1)}, u32[]{:S(2)}, u32[]{:S(2)}) %collective-permute-start.5) | collective-permute-done | bytes 819232 | tf_op jit(solution)/shard_map/first/ppermute | solution.py:40
  38.6 2.8 %collective-permute-done.4.refs_2_.refs_1_ = bf16[160,2560]{1,0:T(8,128)(2,1)S(1)} collective-permute-done((bf16[160,2560]{1,0:T(8,128)(2,1)S(1)}, bf16[160,2560]{1,0:T(8,128)(2,1)S(1)}, u32[]{:S(2)}, u32[]{:S(2)}) %collective-permute-start.4) | collective-permute-done | bytes 819232 | tf_op jit(solution)/shard_map/first/ppermute | solution.py:30
  41.4 0.9 collective-permute-start.10
  42.3 2.7 %collective-permute-start.9 = (bf16[160,2560]{1,0:T(8,128)(2,1)}, bf16[160,2560]{1,0:T(8,128)(2,1)S(1)}, u32[]{:S(2)}, u32[]{:S(2)}) collective-permute-start(bf16[160,2560]{1,0:T(8,128)(2,1)} %get-tuple-element.47.refs_2_), channel_id=1, source_target_pairs={{0,24},{1,25},{2,26},{3,27},{4,28},{5,29},{6,30},{7,31},{8,0},{9,1... | collective-permute-start | bytes 2457608 | tf_op jit(solution)/shard_map/second/ppermute | solution.py:30
  45.0 2.5 %collective-permute-start.7 = (bf16[160,2560]{1,0:T(8,128)(2,1)}, bf16[160,2560]{1,0:T(8,128)(2,1)S(1)}, u32[]{:S(2)}, u32[]{:S(2)}) collective-permute-start(bf16[160,2560]{1,0:T(8,128)(2,1)} %collective-permute-done.2.ax), channel_id=1, source_target_pairs={{0,6},{1,7},{2,0},{3,1},{4,2},{5,3},{6,4},{7,5},{8,14},{9,15},{10,... | collective-permute-start | bytes 2457608 | tf_op jit(solution)/shard_map/second/ppermute | solution.py:35
  47.4 4.8 %pair_first.1 = (f32[640,640]{1,0:T(8,128)S(1)}, bf16[1280,2560]{1,0:T(8,128)(2,1)S(1)}, bf16[640,2560]{1,0:T(8,128)(2,1)S(1)}) custom-call(bf16[160,2560]{1,0:T(8,128)(2,1)S(1)} %get-tuple-element.45.own, bf16[160,2560]{1,0:T(8,128)(2,1)} %collective-permute-done.2.ax, bf16[160,2560]{1,0:T(8,128)(2,1)S(1)} %collective-permute-done.3.am, ...), custom_call_target="tpu_custom_call" | custom-call | flops 1000 | bytes 1000 | tf_op jit(solution)/shard_map/pair_first/pallas_call | solution.py:85
  52.3 7.3 %collective-permute-done.8.refs_0_.refs_1_ = bf16[160,2560]{1,0:T(8,128)(2,1)S(1)} collective-permute-done((bf16[160,2560]{1,0:T(8,128)(2,1)}, bf16[160,2560]{1,0:T(8,128)(2,1)S(1)}, u32[]{:S(2)}, u32[]{:S(2)}) %collective-permute-start.8) | collective-permute-done | bytes 819232 | tf_op jit(solution)/shard_map/second/ppermute | solution.py:30
  60.4 1.8 %collective-permute-start.11 = (bf16[64,2560]{1,0:T(8,128)(2,1)S(1)}, bf16[64,2560]{1,0:T(8,128)(2,1)S(1)}, u32[]{:S(2)}, u32[]{:S(2)}) collective-permute-start(bf16[64,2560]{1,0:T(8,128)(2,1)S(1)} %get-tuple-element.56), channel_id=1, source_target_pairs={{0,1},{1,0},{2,3},{3,2},{4,5},{5,4},{6,7},{7,6},{8,9},{9,8},{10,11... | collective-permute-start | bytes 983048 | tf_op jit(solution)/shard_map/third/ppermute | solution.py:40
  62.1 3.0 %collective-permute-start.13 = (bf16[48,2560]{1,0:T(8,128)(2,1)S(1)}, bf16[48,2560]{1,0:T(8,128)(2,1)S(1)}, u32[]{:S(2)}, u32[]{:S(2)}) collective-permute-start(bf16[48,2560]{1,0:T(8,128)(2,1)S(1)} %get-tuple-element.58), channel_id=1, source_target_pairs={{0,24},{1,25},{2,26},{3,27},{4,28},{5,29},{6,30},{7,31},{8,0},{9,1... | collective-permute-start | bytes 737288 | tf_op jit(solution)/shard_map/third/ppermute | solution.py:30
  65.2 3.4 %pair_early.1 = (f32[640,640]{1,0:T(8,128)S(1)}, bf16[1280,2560]{1,0:T(8,128)(2,1)S(1)}, bf16[640,2560]{1,0:T(8,128)(2,1)S(1)}, f32[640,480]{1,0:T(8,128)S(1)}) custom-call(f32[640,640]{1,0:T(8,128)S(1)} %get-tuple-element.49.first_in.refs_3_, ...), custom_call_target="tpu_custom_call", output_to_operand_aliasing={{0}: (0, {}), {1}: (1, {}), {2}: (2, {})} | custom-call | flops 1000 | bytes 1000 | tf_op jit(solution)/shard_map/pair_early/pallas_call | solution.py:85
  68.6 1.2 collective-permute-done.12.refs_1_
  69.9 1.6 %pair_late.1 = (f32[640,640]{1,0:T(8,128)S(1)}, bf16[640,640]{1,0:T(8,128)(2,1)S(1)}, bf16[1280,2560]{1,0:T(8,128)(2,1)S(1)}) custom-call(f32[640,640]{1,0:T(8,128)S(1)} %get-tuple-element.52.first, f32[640,480]{1,0:T(8,128)S(1)} %get-tuple-element.53.early, bf16[640,2560]{1,0:T(8,128)(2,1)S(1)} %get-tuple-element.54.acat, ...), custom_call_target="tpu_custom_call", output_to_operand_aliasing={{2}: (3, {})} | custom-call | flops 1000 | bytes 1000 | tf_op jit(solution)/shard_map/pair_late/pallas_call | solution.py:85
  71.6 2.3 %collective-permute-done.14.got = bf16[640,640]{1,0:T(8,128)(2,1)S(1)} collective-permute-done((bf16[640,640]{1,0:T(8,128)(2,1)S(1)}, bf16[640,640]{1,0:T(8,128)(2,1)S(1)}, u32[]{:S(2)}, u32[]{:S(2)}) %collective-permute-start.14) | collective-permute-done | bytes 819232 | tf_op jit(solution)/shard_map/core/ppermute | solution.py:44
  74.1 11.8 %collective-permute-start.15 = (bf16[160,640]{1,0:T(8,128)(2,1)S(1)}, bf16[160,640]{1,0:T(8,128)(2,1)S(1)}, u32[]{:S(2)}, u32[]{:S(2)}) collective-permute-start(bf16[160,640]{1,0:T(8,128)(2,1)S(1)} %get-tuple-element.62), channel_id=1, source_target_pairs={{0,128},{32,160},{64,192},{96,224},{128,0},{160,32},{192,64},{224,... | collective-permute-start | bytes 614408 | tf_op jit(solution)/shard_map/shares/ppermute | solution.py:48
  85.9 3.6 %collective-permute-start.17 = (bf16[160,640]{1,0:T(8,128)(2,1)S(1)}, bf16[160,640]{1,0:T(8,128)(2,1)S(1)}, u32[]{:S(2)}, u32[]{:S(2)}) collective-permute-start(bf16[160,640]{1,0:T(8,128)(2,1)S(1)} %get-tuple-element.64), channel_id=1, source_target_pairs={{0,192},{32,224},{64,0},{96,32},{128,64},{160,96},{192,128},{224,1... | collective-permute-start | bytes 614408 | tf_op jit(solution)/shard_map/shares/ppermute | solution.py:48
  89.5 6.2 %collective-permute-done.15.refs_0_ = bf16[160,640]{1,0:T(8,128)(2,1)S(1)} collective-permute-done((bf16[160,640]{1,0:T(8,128)(2,1)S(1)}, bf16[160,640]{1,0:T(8,128)(2,1)S(1)}, u32[]{:S(2)}, u32[]{:S(2)}) %collective-permute-start.15) | collective-permute-done | bytes 204832 | tf_op jit(solution)/shard_map/shares/ppermute | solution.py:48
  95.7 4.5 %collective-permute-done.16.refs_1_ = bf16[160,640]{1,0:T(8,128)(2,1)S(1)} collective-permute-done((bf16[160,640]{1,0:T(8,128)(2,1)S(1)}, bf16[160,640]{1,0:T(8,128)(2,1)S(1)}, u32[]{:S(2)}, u32[]{:S(2)}) %collective-permute-start.16) | collective-permute-done | bytes 204832 | tf_op jit(solution)/shard_map/shares/ppermute | solution.py:48
  100.2 1.2 collective-permute-done.17.refs_2_
  101.4 0.9 amplitude.1
  102.3 4.4 %collective-permute-start.27 = (bf16[80,640]{1,0:T(8,128)(2,1)S(1)}, bf16[80,640]{1,0:T(8,128)(2,1)S(1)}, u32[]{:S(2)}, u32[]{:S(2)}) collective-permute-start(bf16[80,640]{1,0:T(8,128)(2,1)S(1)} %get-tuple-element.67.refs_0_), channel_id=1, source_target_pairs={{0,192},{32,224},{64,0},{96,32},{128,64},{160,96},{192,128},{224,1... | collective-permute-start | bytes 307208 | tf_op jit(solution)/shard_map/spread_0/ppermute | solution.py:48
  106.7 4.3 %collective-permute-start.26 = (bf16[80,640]{1,0:T(8,128)(2,1)S(1)}, bf16[80,640]{1,0:T(8,128)(2,1)S(1)}, u32[]{:S(2)}, u32[]{:S(2)}) collective-permute-start(bf16[80,640]{1,0:T(8,128)(2,1)S(1)} %get-tuple-element.67.refs_0_), channel_id=1, source_target_pairs={{0,128},{32,160},{64,192},{96,224},{128,0},{160,32},{192,64},{224,... | collective-permute-start | bytes 307208 | tf_op jit(solution)/shard_map/spread_0/ppermute | solution.py:48
  110.9 1.1 collective-permute-start.28
  112.1 1.8 %collective-permute-start.31 = (bf16[80,640]{1,0:T(8,128)(2,1)S(1)}, bf16[80,640]{1,0:T(8,128)(2,1)S(1)}, u32[]{:S(2)}, u32[]{:S(2)}) collective-permute-start(bf16[80,640]{1,0:T(8,128)(2,1)S(1)} %collective-permute-done.27.refs_3_), channel_id=1, source_target_pairs={{0,32},{32,0},{64,96},{96,64},{128,160},{160,128},{192,224},{224,1... | collective-permute-start | bytes 307208 | tf_op jit(solution)/shard_map/other_0/ppermute | solution.py:44
  113.9 3.4 %collective-permute-done.26.refs_2_ = bf16[80,640]{1,0:T(8,128)(2,1)S(1)} collective-permute-done((bf16[80,640]{1,0:T(8,128)(2,1)S(1)}, bf16[80,640]{1,0:T(8,128)(2,1)S(1)}, u32[]{:S(2)}, u32[]{:S(2)}) %collective-permute-start.26) | collective-permute-done | bytes 102432 | tf_op jit(solution)/shard_map/spread_0/ppermute | solution.py:48
  117.3 2.2 %collective-permute-start.30 = (bf16[80,640]{1,0:T(8,128)(2,1)S(1)}, bf16[80,640]{1,0:T(8,128)(2,1)S(1)}, u32[]{:S(2)}, u32[]{:S(2)}) collective-permute-start(bf16[80,640]{1,0:T(8,128)(2,1)S(1)} %collective-permute-done.26.refs_2_), channel_id=1, source_target_pairs={{0,32},{32,0},{64,96},{96,64},{128,160},{160,128},{192,224},{224,1... | collective-permute-start | bytes 307208 | tf_op jit(solution)/shard_map/other_0/ppermute | solution.py:44
  121.2 2.5 %density_first.1 = (bf16[160,2560]{1,0:T(8,128)(2,1)S(1)}, bf16[160,2560]{1,0:T(8,128)(2,1)S(1)}) custom-call(bf16[80,640]{1,0:T(8,128)(2,1)S(1)} %get-tuple-element.67.refs_0_, bf16[80,640]{1,0:T(8,128)(2,1)S(1)} %collective-permute-done.25.refs_1_, bf16[80,640]{1,0:T(8,128)(2,1)S(1)} %collective-permute-done.26.refs_2_, ...), custom_call_target="tpu_custom_call" | custom-call | flops 1000 | bytes 1000 | tf_op jit(solution)/shard_map/density_first/pallas_call | solution.py:85
  123.8 1.0 collective-permute-start.32
  124.8 1.8 %collective-permute-start.33 = (bf16[160,2560]{1,0:T(8,128)(2,1)S(1)}, bf16[160,2560]{1,0:T(8,128)(2,1)S(1)}, u32[]{:S(2)}, u32[]{:S(2)}) collective-permute-start(bf16[160,2560]{1,0:T(8,128)(2,1)S(1)} %get-tuple-element.69), channel_id=1, source_target_pairs={{0,6},{1,7},{2,0},{3,1},{4,2},{5,3},{6,4},{7,5},{8,14},{9,15},{10,... | collective-permute-start | bytes 2457608 | tf_op jit(solution)/shard_map/out/ppermute | solution.py:35
  126.5 0.9 collective-permute-start.21
  127.5 1.4 collective-permute-start.20
  128.9 3.7 %collective-permute-start.19 = (bf16[80,640]{1,0:T(8,128)(2,1)S(1)}, bf16[80,640]{1,0:T(8,128)(2,1)S(1)}, u32[]{:S(2)}, u32[]{:S(2)}) collective-permute-start(bf16[80,640]{1,0:T(8,128)(2,1)S(1)} %get-tuple-element.65.refs_0_), channel_id=1, source_target_pairs={{0,128},{32,160},{64,192},{96,224},{128,0},{160,32},{192,64},{224,... | collective-permute-start | bytes 307208 | tf_op jit(solution)/shard_map/spread_1/ppermute | solution.py:48
  132.9 0.9 collective-permute-start.24
  133.8 3.2 %collective-permute-done.19.refs_2_ = bf16[80,640]{1,0:T(8,128)(2,1)S(1)} collective-permute-done((bf16[80,640]{1,0:T(8,128)(2,1)S(1)}, bf16[80,640]{1,0:T(8,128)(2,1)S(1)}, u32[]{:S(2)}, u32[]{:S(2)}) %collective-permute-start.19) | collective-permute-done | bytes 102432 | tf_op jit(solution)/shard_map/spread_1/ppermute | solution.py:48
  137.0 4.2 %collective-permute-start.23 = (bf16[80,640]{1,0:T(8,128)(2,1)S(1)}, bf16[80,640]{1,0:T(8,128)(2,1)S(1)}, u32[]{:S(2)}, u32[]{:S(2)}) collective-permute-start(bf16[80,640]{1,0:T(8,128)(2,1)S(1)} %collective-permute-done.19.refs_2_), channel_id=1, source_target_pairs={{0,32},{32,0},{64,96},{96,64},{128,160},{160,128},{192,224},{224,1... | collective-permute-start | bytes 307208 | tf_op jit(solution)/shard_map/other_1/ppermute | solution.py:44
  142.5 2.0 %collective-permute-done.32.refs_9_ = bf16[160,2560]{1,0:T(8,128)(2,1)S(1)} collective-permute-done((bf16[160,2560]{1,0:T(8,128)(2,1)S(1)}, bf16[160,2560]{1,0:T(8,128)(2,1)S(1)}, u32[]{:S(2)}, u32[]{:S(2)}) %collective-permute-start.32) | collective-permute-done | bytes 819232 | tf_op jit(solution)/shard_map/out/ppermute | solution.py:35
  144.5 2.6 %density_second.1 = (bf16[80,2560]{1,0:T(8,128)(2,1)S(1)}, bf16[80,2560]{1,0:T(8,128)(2,1)S(1)}, f32[160,2560]{1,0:T(8,128)S(1)}) custom-call(bf16[80,640]{1,0:T(8,128)(2,1)S(1)} %get-tuple-element.65.refs_0_, bf16[80,640]{1,0:T(8,128)(2,1)S(1)} %collective-permute-done.18.refs_1_, bf16[80,640]{1,0:T(8,128)(2,1)S(1)} %collective-permute-done.19.refs_2_, ...), custom_call_target="tpu_custom_call" | custom-call | flops 1000 | bytes 1000 | tf_op jit(solution)/shard_map/density_second/pallas_call | solution.py:85
  147.8 2.1 %collective-permute-start.35 = (bf16[80,2560]{1,0:T(8,128)(2,1)S(1)}, bf16[80,2560]{1,0:T(8,128)(2,1)S(1)}, u32[]{:S(2)}, u32[]{:S(2)}) collective-permute-start(bf16[80,2560]{1,0:T(8,128)(2,1)S(1)} %get-tuple-element.72), channel_id=1, source_target_pairs={{0,6},{1,7},{2,0},{3,1},{4,2},{5,3},{6,4},{7,5},{8,14},{9,15},{10,... | collective-permute-start | bytes 1228808 | tf_op jit(solution)/shard_map/out/ppermute | solution.py:35
  149.9 8.3 %collective-permute-done.34.one = bf16[80,2560]{1,0:T(8,128)(2,1)S(1)} collective-permute-done((bf16[80,2560]{1,0:T(8,128)(2,1)S(1)}, bf16[80,2560]{1,0:T(8,128)(2,1)S(1)}, u32[]{:S(2)}, u32[]{:S(2)}) %collective-permute-start.34) | collective-permute-done | bytes 409632 | tf_op jit(solution)/shard_map/out/ppermute | solution.py:35
  158.2 1.0 add.1
  (44 shorter events, 5.2 us)
Async XLA Ops:
  1.1 16.2 %collective-permute-start = (bf16[320,512]{1,0:T(8,128)(2,1)S(1)}, bf16[320,512]{1,0:T(8,128)(2,1)S(1)}, u32[]{:S(2)}, u32[]{:S(2)}) collective-permute-start(bf16[320,512]{1,0:T(8,128)(2,1)S(1)} %get-tuple-element.39), channel_id=1, source_target_pairs={{0,32},{32,64},{64,96},{96,128},{128,160},{160,192},{192,224},{1,3... | collective-permute-start | bytes 983048 | tf_op jit(solution)/shard_map/ppermute | solution.py:534
  7.4 12.8 %collective-permute-start.1 = (bf16[320,512]{1,0:T(8,128)(2,1)S(1)}, bf16[320,512]{1,0:T(8,128)(2,1)S(1)}, u32[]{:S(2)}, u32[]{:S(2)}) collective-permute-start(bf16[320,512]{1,0:T(8,128)(2,1)S(1)} %get-tuple-element.40), channel_id=1, source_target_pairs={{32,0},{64,32},{96,64},{128,96},{160,128},{192,160},{224,192},{33,... | collective-permute-start | bytes 983048 | tf_op jit(solution)/shard_map/ppermute | solution.py:535
  20.2 6.8 %copy-start.2 = (f32[5120]{0:T(1024)S(1)}, f32[5120]{0:T(1024)}, u32[]{:S(2)}) copy-start(f32[5120]{0:T(1024)} %param.9) | copy-start | bytes 61444
  21.2 15.6 %collective-permute-start.6 = (bf16[160,2560]{1,0:T(8,128)(2,1)S(1)}, bf16[160,2560]{1,0:T(8,128)(2,1)}, u32[]{:S(2)}, u32[]{:S(2)}) collective-permute-start(bf16[160,2560]{1,0:T(8,128)(2,1)S(1)} %get-tuple-element.46.refs_0_), channel_id=1, source_target_pairs={{0,24},{1,25},{2,26},{3,27},{4,28},{5,29},{6,30},{7,31},{8,0},{9,1... | collective-permute-start | bytes 2457608 | tf_op jit(solution)/shard_map/first/ppermute | solution.py:30
  24.5 14.1 %collective-permute-start.5 = (bf16[160,2560]{1,0:T(8,128)(2,1)S(1)}, bf16[160,2560]{1,0:T(8,128)(2,1)}, u32[]{:S(2)}, u32[]{:S(2)}) collective-permute-start(bf16[160,2560]{1,0:T(8,128)(2,1)S(1)} %get-tuple-element.46.refs_0_), channel_id=1, source_target_pairs={{0,1},{1,0},{2,3},{3,2},{4,5},{5,4},{6,7},{7,6},{8,9},{9,8},{10,11... | collective-permute-start | bytes 2457608 | tf_op jit(solution)/shard_map/first/ppermute | solution.py:40
  24.5 16.9 %collective-permute-start.4 = (bf16[160,2560]{1,0:T(8,128)(2,1)S(1)}, bf16[160,2560]{1,0:T(8,128)(2,1)S(1)}, u32[]{:S(2)}, u32[]{:S(2)}) collective-permute-start(bf16[160,2560]{1,0:T(8,128)(2,1)S(1)} %get-tuple-element.46.refs_0_), channel_id=1, source_target_pairs={{0,8},{1,9},{2,10},{3,11},{4,12},{5,13},{6,14},{7,15},{8,16},{9,17... | collective-permute-start | bytes 2457608 | tf_op jit(solution)/shard_map/first/ppermute | solution.py:30
  24.5 20.5 %collective-permute-start.2 = (bf16[160,2560]{1,0:T(8,128)(2,1)S(1)}, bf16[160,2560]{1,0:T(8,128)(2,1)}, u32[]{:S(2)}, u32[]{:S(2)}) collective-permute-start(bf16[160,2560]{1,0:T(8,128)(2,1)S(1)} %get-tuple-element.45.own), channel_id=1, source_target_pairs={{0,6},{1,7},{2,0},{3,1},{4,2},{5,3},{6,4},{7,5},{8,14},{9,15},{10,... | collective-permute-start | bytes 2457608 | tf_op jit(solution)/shard_map/first/ppermute | solution.py:35
  27.0 20.4 %collective-permute-start.3 = (bf16[160,2560]{1,0:T(8,128)(2,1)S(1)}, bf16[160,2560]{1,0:T(8,128)(2,1)S(1)}, u32[]{:S(2)}, u32[]{:S(2)}) collective-permute-start(bf16[160,2560]{1,0:T(8,128)(2,1)S(1)} %get-tuple-element.45.own), channel_id=1, source_target_pairs={{0,2},{1,3},{2,4},{3,5},{4,6},{5,7},{6,0},{7,1},{8,10},{9,11},{10,... | collective-permute-start | bytes 2457608 | tf_op jit(solution)/shard_map/first/ppermute | solution.py:35
  41.4 18.2 %collective-permute-start.8 = (bf16[160,2560]{1,0:T(8,128)(2,1)}, bf16[160,2560]{1,0:T(8,128)(2,1)S(1)}, u32[]{:S(2)}, u32[]{:S(2)}) collective-permute-start(bf16[160,2560]{1,0:T(8,128)(2,1)} %get-tuple-element.48.refs_3_), channel_id=1, source_target_pairs={{0,8},{1,9},{2,10},{3,11},{4,12},{5,13},{6,14},{7,15},{8,16},{9,17... | collective-permute-start | bytes 2457608 | tf_op jit(solution)/shard_map/second/ppermute | solution.py:30
  41.4 18.2 %collective-permute-start.10 = (bf16[160,2560]{1,0:T(8,128)(2,1)}, bf16[160,2560]{1,0:T(8,128)(2,1)S(1)}, u32[]{:S(2)}, u32[]{:S(2)}) collective-permute-start(bf16[160,2560]{1,0:T(8,128)(2,1)} %get-tuple-element.47.refs_2_), channel_id=1, source_target_pairs={{0,1},{1,0},{2,3},{3,2},{4,5},{5,4},{6,7},{7,6},{8,9},{9,8},{10,11... | collective-permute-start | bytes 2457608 | tf_op jit(solution)/shard_map/second/ppermute | solution.py:40
  42.3 17.3 %collective-permute-start.9 = (bf16[160,2560]{1,0:T(8,128)(2,1)}, bf16[160,2560]{1,0:T(8,128)(2,1)S(1)}, u32[]{:S(2)}, u32[]{:S(2)}) collective-permute-start(bf16[160,2560]{1,0:T(8,128)(2,1)} %get-tuple-element.47.refs_2_), channel_id=1, source_target_pairs={{0,24},{1,25},{2,26},{3,27},{4,28},{5,29},{6,30},{7,31},{8,0},{9,1... | collective-permute-start | bytes 2457608 | tf_op jit(solution)/shard_map/second/ppermute | solution.py:30
  45.0 20.2 %collective-permute-start.7 = (bf16[160,2560]{1,0:T(8,128)(2,1)}, bf16[160,2560]{1,0:T(8,128)(2,1)S(1)}, u32[]{:S(2)}, u32[]{:S(2)}) collective-permute-start(bf16[160,2560]{1,0:T(8,128)(2,1)} %collective-permute-done.2.ax), channel_id=1, source_target_pairs={{0,6},{1,7},{2,0},{3,1},{4,2},{5,3},{6,4},{7,5},{8,14},{9,15},{10,... | collective-permute-start | bytes 2457608 | tf_op jit(solution)/shard_map/second/ppermute | solution.py:35
  60.4 9.5 %collective-permute-start.11 = (bf16[64,2560]{1,0:T(8,128)(2,1)S(1)}, bf16[64,2560]{1,0:T(8,128)(2,1)S(1)}, u32[]{:S(2)}, u32[]{:S(2)}) collective-permute-start(bf16[64,2560]{1,0:T(8,128)(2,1)S(1)} %get-tuple-element.56), channel_id=1, source_target_pairs={{0,1},{1,0},{2,3},{3,2},{4,5},{5,4},{6,7},{7,6},{8,9},{9,8},{10,11... | collective-permute-start | bytes 983048 | tf_op jit(solution)/shard_map/third/ppermute | solution.py:40
  62.1 7.7 %collective-permute-start.12 = (bf16[48,2560]{1,0:T(8,128)(2,1)S(1)}, bf16[48,2560]{1,0:T(8,128)(2,1)S(1)}, u32[]{:S(2)}, u32[]{:S(2)}) collective-permute-start(bf16[48,2560]{1,0:T(8,128)(2,1)S(1)} %get-tuple-element.57), channel_id=1, source_target_pairs={{0,8},{1,9},{2,10},{3,11},{4,12},{5,13},{6,14},{7,15},{8,16},{9,17... | collective-permute-start | bytes 737288 | tf_op jit(solution)/shard_map/third/ppermute | solution.py:30
  62.1 7.7 %collective-permute-start.13 = (bf16[48,2560]{1,0:T(8,128)(2,1)S(1)}, bf16[48,2560]{1,0:T(8,128)(2,1)S(1)}, u32[]{:S(2)}, u32[]{:S(2)}) collective-permute-start(bf16[48,2560]{1,0:T(8,128)(2,1)S(1)} %get-tuple-element.58), channel_id=1, source_target_pairs={{0,24},{1,25},{2,26},{3,27},{4,28},{5,29},{6,30},{7,31},{8,0},{9,1... | collective-permute-start | bytes 737288 | tf_op jit(solution)/shard_map/third/ppermute | solution.py:30
  69.8 31.6 %copy-start = (f32[1000]{0:T(1024)S(1)}, f32[1000]{0:T(1024)}, u32[]{:S(2)}) copy-start(f32[1000]{0:T(1024)} %occ.1) | copy-start | bytes 12004
  69.8 31.6 %copy-start.1 = (s32[2]{0:T(128)S(1)}, s32[2]{0:T(128)}, u32[]{:S(2)}) copy-start(s32[2]{0:T(128)} %chosen.1) | copy-start | bytes 28
  71.5 2.4 %collective-permute-start.14 = (bf16[640,640]{1,0:T(8,128)(2,1)S(1)}, bf16[640,640]{1,0:T(8,128)(2,1)S(1)}, u32[]{:S(2)}, u32[]{:S(2)}) collective-permute-start(bf16[640,640]{1,0:T(8,128)(2,1)S(1)} %get-tuple-element.60), channel_id=1, source_target_pairs={{0,32},{32,0},{64,96},{96,64},{128,160},{160,128},{192,224},{224,1... | collective-permute-start | bytes 2457608 | tf_op jit(solution)/shard_map/core/ppermute | solution.py:44
  74.1 21.6 %collective-permute-start.15 = (bf16[160,640]{1,0:T(8,128)(2,1)S(1)}, bf16[160,640]{1,0:T(8,128)(2,1)S(1)}, u32[]{:S(2)}, u32[]{:S(2)}) collective-permute-start(bf16[160,640]{1,0:T(8,128)(2,1)S(1)} %get-tuple-element.62), channel_id=1, source_target_pairs={{0,128},{32,160},{64,192},{96,224},{128,0},{160,32},{192,64},{224,... | collective-permute-start | bytes 614408 | tf_op jit(solution)/shard_map/shares/ppermute | solution.py:48
  85.9 14.3 %collective-permute-start.16 = (bf16[160,640]{1,0:T(8,128)(2,1)S(1)}, bf16[160,640]{1,0:T(8,128)(2,1)S(1)}, u32[]{:S(2)}, u32[]{:S(2)}) collective-permute-start(bf16[160,640]{1,0:T(8,128)(2,1)S(1)} %get-tuple-element.63), channel_id=1, source_target_pairs={{0,64},{32,96},{64,128},{96,160},{128,192},{160,224},{192,0},{224,... | collective-permute-start | bytes 614408 | tf_op jit(solution)/shard_map/shares/ppermute | solution.py:48
  85.9 15.5 %collective-permute-start.17 = (bf16[160,640]{1,0:T(8,128)(2,1)S(1)}, bf16[160,640]{1,0:T(8,128)(2,1)S(1)}, u32[]{:S(2)}, u32[]{:S(2)}) collective-permute-start(bf16[160,640]{1,0:T(8,128)(2,1)S(1)} %get-tuple-element.64), channel_id=1, source_target_pairs={{0,192},{32,224},{64,0},{96,32},{128,64},{160,96},{192,128},{224,1... | collective-permute-start | bytes 614408 | tf_op jit(solution)/shard_map/shares/ppermute | solution.py:48
  102.3 9.8 %collective-permute-start.27 = (bf16[80,640]{1,0:T(8,128)(2,1)S(1)}, bf16[80,640]{1,0:T(8,128)(2,1)S(1)}, u32[]{:S(2)}, u32[]{:S(2)}) collective-permute-start(bf16[80,640]{1,0:T(8,128)(2,1)S(1)} %get-tuple-element.67.refs_0_), channel_id=1, source_target_pairs={{0,192},{32,224},{64,0},{96,32},{128,64},{160,96},{192,128},{224,1... | collective-permute-start | bytes 307208 | tf_op jit(solution)/shard_map/spread_0/ppermute | solution.py:48
  106.7 10.6 %collective-permute-start.26 = (bf16[80,640]{1,0:T(8,128)(2,1)S(1)}, bf16[80,640]{1,0:T(8,128)(2,1)S(1)}, u32[]{:S(2)}, u32[]{:S(2)}) collective-permute-start(bf16[80,640]{1,0:T(8,128)(2,1)S(1)} %get-tuple-element.67.refs_0_), channel_id=1, source_target_pairs={{0,128},{32,160},{64,192},{96,224},{128,0},{160,32},{192,64},{224,... | collective-permute-start | bytes 307208 | tf_op jit(solution)/shard_map/spread_0/ppermute | solution.py:48
  110.9 8.6 %collective-permute-start.25 = (bf16[80,640]{1,0:T(8,128)(2,1)S(1)}, bf16[80,640]{1,0:T(8,128)(2,1)S(1)}, u32[]{:S(2)}, u32[]{:S(2)}) collective-permute-start(bf16[80,640]{1,0:T(8,128)(2,1)S(1)} %get-tuple-element.67.refs_0_), channel_id=1, source_target_pairs={{0,64},{32,96},{64,128},{96,160},{128,192},{160,224},{192,0},{224,... | collective-permute-start | bytes 307208 | tf_op jit(solution)/shard_map/spread_0/ppermute | solution.py:48
  110.9 9.4 %collective-permute-start.28 = (bf16[80,640]{1,0:T(8,128)(2,1)S(1)}, bf16[80,640]{1,0:T(8,128)(2,1)S(1)}, u32[]{:S(2)}, u32[]{:S(2)}) collective-permute-start(bf16[80,640]{1,0:T(8,128)(2,1)S(1)} %get-tuple-element.67.refs_0_), channel_id=1, source_target_pairs={{0,32},{32,0},{64,96},{96,64},{128,160},{160,128},{192,224},{224,1... | collective-permute-start | bytes 307208 | tf_op jit(solution)/shard_map/other_0/ppermute | solution.py:44
  112.1 8.2 %collective-permute-start.31 = (bf16[80,640]{1,0:T(8,128)(2,1)S(1)}, bf16[80,640]{1,0:T(8,128)(2,1)S(1)}, u32[]{:S(2)}, u32[]{:S(2)}) collective-permute-start(bf16[80,640]{1,0:T(8,128)(2,1)S(1)} %collective-permute-done.27.refs_3_), channel_id=1, source_target_pairs={{0,32},{32,0},{64,96},{96,64},{128,160},{160,128},{192,224},{224,1... | collective-permute-start | bytes 307208 | tf_op jit(solution)/shard_map/other_0/ppermute | solution.py:44
  117.3 3.2 %collective-permute-start.30 = (bf16[80,640]{1,0:T(8,128)(2,1)S(1)}, bf16[80,640]{1,0:T(8,128)(2,1)S(1)}, u32[]{:S(2)}, u32[]{:S(2)}) collective-permute-start(bf16[80,640]{1,0:T(8,128)(2,1)S(1)} %collective-permute-done.26.refs_2_), channel_id=1, source_target_pairs={{0,32},{32,0},{64,96},{96,64},{128,160},{160,128},{192,224},{224,1... | collective-permute-start | bytes 307208 | tf_op jit(solution)/shard_map/other_0/ppermute | solution.py:44
  119.5 1.7 %collective-permute-start.29 = (bf16[80,640]{1,0:T(8,128)(2,1)S(1)}, bf16[80,640]{1,0:T(8,128)(2,1)S(1)}, u32[]{:S(2)}, u32[]{:S(2)}) collective-permute-start(bf16[80,640]{1,0:T(8,128)(2,1)S(1)} %collective-permute-done.25.refs_1_), channel_id=1, source_target_pairs={{0,32},{32,0},{64,96},{96,64},{128,160},{160,128},{192,224},{224,1... | collective-permute-start | bytes 307208 | tf_op jit(solution)/shard_map/other_0/ppermute | solution.py:44
  123.8 20.8 %collective-permute-start.32 = (bf16[160,2560]{1,0:T(8,128)(2,1)S(1)}, bf16[160,2560]{1,0:T(8,128)(2,1)S(1)}, u32[]{:S(2)}, u32[]{:S(2)}) collective-permute-start(bf16[160,2560]{1,0:T(8,128)(2,1)S(1)} %get-tuple-element.68), channel_id=1, source_target_pairs={{0,2},{1,3},{2,4},{3,5},{4,6},{5,7},{6,0},{7,1},{8,10},{9,11},{10,... | collective-permute-start | bytes 2457608 | tf_op jit(solution)/shard_map/out/ppermute | solution.py:35
  124.8 19.8 %collective-permute-start.33 = (bf16[160,2560]{1,0:T(8,128)(2,1)S(1)}, bf16[160,2560]{1,0:T(8,128)(2,1)S(1)}, u32[]{:S(2)}, u32[]{:S(2)}) collective-permute-start(bf16[160,2560]{1,0:T(8,128)(2,1)S(1)} %get-tuple-element.69), channel_id=1, source_target_pairs={{0,6},{1,7},{2,0},{3,1},{4,2},{5,3},{6,4},{7,5},{8,14},{9,15},{10,... | collective-permute-start | bytes 2457608 | tf_op jit(solution)/shard_map/out/ppermute | solution.py:35
  126.5 6.1 %collective-permute-start.21 = (bf16[80,640]{1,0:T(8,128)(2,1)S(1)}, bf16[80,640]{1,0:T(8,128)(2,1)S(1)}, u32[]{:S(2)}, u32[]{:S(2)}) collective-permute-start(bf16[80,640]{1,0:T(8,128)(2,1)S(1)} %get-tuple-element.65.refs_0_), channel_id=1, source_target_pairs={{0,32},{32,0},{64,96},{96,64},{128,160},{160,128},{192,224},{224,1... | collective-permute-start | bytes 307208 | tf_op jit(solution)/shard_map/other_1/ppermute | solution.py:44
  127.5 5.4 %collective-permute-start.20 = (bf16[80,640]{1,0:T(8,128)(2,1)S(1)}, bf16[80,640]{1,0:T(8,128)(2,1)S(1)}, u32[]{:S(2)}, u32[]{:S(2)}) collective-permute-start(bf16[80,640]{1,0:T(8,128)(2,1)S(1)} %get-tuple-element.65.refs_0_), channel_id=1, source_target_pairs={{0,192},{32,224},{64,0},{96,32},{128,64},{160,96},{192,128},{224,1... | collective-permute-start | bytes 307208 | tf_op jit(solution)/shard_map/spread_1/ppermute | solution.py:48
  128.9 8.1 %collective-permute-start.19 = (bf16[80,640]{1,0:T(8,128)(2,1)S(1)}, bf16[80,640]{1,0:T(8,128)(2,1)S(1)}, u32[]{:S(2)}, u32[]{:S(2)}) collective-permute-start(bf16[80,640]{1,0:T(8,128)(2,1)S(1)} %get-tuple-element.65.refs_0_), channel_id=1, source_target_pairs={{0,128},{32,160},{64,192},{96,224},{128,0},{160,32},{192,64},{224,... | collective-permute-start | bytes 307208 | tf_op jit(solution)/shard_map/spread_1/ppermute | solution.py:48
  132.6 8.6 %collective-permute-start.18 = (bf16[80,640]{1,0:T(8,128)(2,1)S(1)}, bf16[80,640]{1,0:T(8,128)(2,1)S(1)}, u32[]{:S(2)}, u32[]{:S(2)}) collective-permute-start(bf16[80,640]{1,0:T(8,128)(2,1)S(1)} %get-tuple-element.65.refs_0_), channel_id=1, source_target_pairs={{0,64},{32,96},{64,128},{96,160},{128,192},{160,224},{192,0},{224,... | collective-permute-start | bytes 307208 | tf_op jit(solution)/shard_map/spread_1/ppermute | solution.py:48
  132.9 8.7 %collective-permute-start.24 = (bf16[80,640]{1,0:T(8,128)(2,1)S(1)}, bf16[80,640]{1,0:T(8,128)(2,1)S(1)}, u32[]{:S(2)}, u32[]{:S(2)}) collective-permute-start(bf16[80,640]{1,0:T(8,128)(2,1)S(1)} %collective-permute-done.20.refs_3_), channel_id=1, source_target_pairs={{0,32},{32,0},{64,96},{96,64},{128,160},{160,128},{192,224},{224,1... | collective-permute-start | bytes 307208 | tf_op jit(solution)/shard_map/other_1/ppermute | solution.py:44
  137.0 5.1 %collective-permute-start.23 = (bf16[80,640]{1,0:T(8,128)(2,1)S(1)}, bf16[80,640]{1,0:T(8,128)(2,1)S(1)}, u32[]{:S(2)}, u32[]{:S(2)}) collective-permute-start(bf16[80,640]{1,0:T(8,128)(2,1)S(1)} %collective-permute-done.19.refs_2_), channel_id=1, source_target_pairs={{0,32},{32,0},{64,96},{96,64},{128,160},{160,128},{192,224},{224,1... | collective-permute-start | bytes 307208 | tf_op jit(solution)/shard_map/other_1/ppermute | solution.py:44
  141.2 1.3 collective-permute-start.22
  147.1 11.1 %collective-permute-start.34 = (bf16[80,2560]{1,0:T(8,128)(2,1)S(1)}, bf16[80,2560]{1,0:T(8,128)(2,1)S(1)}, u32[]{:S(2)}, u32[]{:S(2)}) collective-permute-start(bf16[80,2560]{1,0:T(8,128)(2,1)S(1)} %get-tuple-element.71), channel_id=1, source_target_pairs={{0,2},{1,3},{2,4},{3,5},{4,6},{5,7},{6,0},{7,1},{8,10},{9,11},{10,... | collective-permute-start | bytes 1228808 | tf_op jit(solution)/shard_map/out/ppermute | solution.py:35
  147.8 10.4 %collective-permute-start.35 = (bf16[80,2560]{1,0:T(8,128)(2,1)S(1)}, bf16[80,2560]{1,0:T(8,128)(2,1)S(1)}, u32[]{:S(2)}, u32[]{:S(2)}) collective-permute-start(bf16[80,2560]{1,0:T(8,128)(2,1)S(1)} %get-tuple-element.72), channel_id=1, source_target_pairs={{0,6},{1,7},{2,0},{3,1},{4,2},{5,3},{6,4},{7,5},{8,14},{9,15},{10,... | collective-permute-start | bytes 1228808 | tf_op jit(solution)/shard_map/out/ppermute | solution.py:35

commit v4 on v3

--- a/solution.py
+++ b/solution.py
@@ -315,7 +315,7 @@
 
 def pair_early_kernel(first_in, bcat_in, acat_in, ad, *refs):
     b_refs = refs[:3]
-    first, bcat, acat, early, a_sems, b_sems = refs[3:]
+    first, bcat, acat, keep, send, early, a_sems, b_sems = refs[3:]
     rows = slice(3 * ROWS, WIDE)
     products(
         lambda part: row_copies([(ad, 0, ROWS, 3 * ROWS)], acat, a_sems, part)
@@ -327,6 +327,18 @@
         ],
         unroll=True,
     )
+    core = position()[1]
+    split = 3 * ROWS
+
+    @pl.when(core == 0)
+    def _():
+        keep[...] = first[...]
+        send[:, :split] = early[...].astype(bf16)
+
+    @pl.when(core == 1)
+    def _():
+        send[...] = first[...].astype(bf16)
+        keep[:, :split] = early[...]
 
 
 def pair_early(first, bcat, acat, ad, b_parts):
@@ -337,15 +349,16 @@
             vmem((WIDE, WIDE), f32),
             vmem((2 * WIDE, AUX)),
             vmem((WIDE, AUX)),
-            vmem((WIDE, 3 * ROWS), f32),
+            vmem((WIDE, WIDE), f32),
+            vmem((WIDE, WIDE)),
         ],
-        [DMA((1, 4)), DMA((3, 4))],
+        [pltpu.VMEM((WIDE, 3 * ROWS), f32), DMA((1, 4)), DMA((3, 4))],
         name="pair_early",
         aliases={0: 0, 1: 1, 2: 2},
     )
 
 
-def pair_late_kernel(first, early, acat, bcat_in, *refs):
+def pair_late_kernel(keep_in, send_in, acat, bcat_in, *refs):
     b_refs = refs[:3]
     keep, send, bcat, late, sems = refs[3:]
     products(
@@ -353,29 +366,25 @@
         acat, bcat, [(slice(0, WIDE), slice(7 * ROWS, 8 * ROWS), late)], unroll=True,
     )
     core = position()[1]
-    split = 3 * ROWS
+    columns = slice(3 * ROWS, WIDE)
 
     @pl.when(core == 0)
     def _():
-        keep[...] = first[...]
-        send[:, :split] = early[...].astype(bf16)
-        send[:, split:] = late[...].astype(bf16)
+        send[:, columns] = late[...].astype(bf16)
 
     @pl.when(core == 1)
     def _():
-        send[...] = first[...].astype(bf16)
-        keep[:, :split] = early[...]
-        keep[:, split:] = late[...]
-
-
-def pair_late(first, early, acat, bcat, b_parts):
+        keep[:, columns] = late[...]
+
+
+def pair_late(keep, send, acat, bcat, b_parts):
     return call(
         pair_late_kernel,
-        [(v, VMEM) for v in (first, early, acat, bcat)] + [(v, ANY) for v in b_parts],
-        [vmem((WIDE, WIDE), f32), hbm((WIDE, WIDE)), vmem((2 * WIDE, AUX))],
+        [(v, VMEM) for v in (keep, send, acat, bcat)] + [(v, ANY) for v in b_parts],
+        [vmem((WIDE, WIDE), f32), vmem((WIDE, WIDE)), vmem((2 * WIDE, AUX))],
         [pltpu.VMEM((WIDE, ROWS), f32), DMA((3, 4))],
         name="pair_late",
-        aliases={3: 2},
+        aliases={0: 0, 1: 1, 3: 2},
     )
 
 
@@ -487,28 +496,44 @@
 
 def density_second_kernel(*refs):
     mine, other, (bcat, got_m, got_x) = refs[:4], refs[4:8], refs[8:11]
-    x1, m2, own, tcat = refs[11:]
+    x1, m2, own_rows, tcat = refs[11:]
     gather_rows(mine, other, tcat)
+    own_rows[...] = tcat[:ROWS]
 
     @pl.loop(0, 2)
     def _(half):
-        columns, value = product(tcat, bcat, half)
-        x = value[ROWS : ROWS + HALF] + got_m[HALF:, columns].astype(f32)
-        m = value[ROWS + HALF :] + got_x[HALF:, columns].astype(f32)
+        columns, value = product(tcat.at[ROWS:], bcat, half)
+        x = value[:HALF] + got_m[HALF:, columns].astype(f32)
+        m = value[HALF:] + got_x[HALF:, columns].astype(f32)
         x1[:, columns] = x.astype(bf16)
         m2[:, columns] = m.astype(bf16)
-        own[:HALF, columns] = value[:HALF] + got_x[:HALF, columns].astype(f32)
-        own[HALF:, columns] = value[HALF:ROWS] + got_m[:HALF, columns].astype(f32)
 
 
 def density_second(mine, other, bcat, from_m, from_x):
     return call(
         density_second_kernel,
         [(v, VMEM) for v in (*mine, *other, bcat, from_m, from_x)],
-        [hbm((HALF, AUX))] * 2 + [vmem((ROWS, AUX), f32)],
+        [hbm((HALF, AUX))] * 2 + [vmem((ROWS, 2 * WIDE))],
         [pltpu.VMEM(TCAT, bf16)],
         name="density_second",
     )
+
+
+def density_own_kernel(rows, bcat, got_m, got_x, own):
+    @pl.loop(0, 2)
+    def _(half):
+        columns, value = product(rows, bcat, half)
+        own[:HALF, columns] = value[:HALF] + got_x[:HALF, columns].astype(f32)
+        own[HALF:, columns] = value[HALF:] + got_m[:HALF, columns].astype(f32)
+
+
+def density_own(rows, bcat, from_m, from_x):
+    return call(
+        density_own_kernel,
+        [(v, VMEM) for v in (rows, bcat, from_m, from_x)],
+        [vmem((ROWS, AUX), f32)],
+        name="density_own",
+    )[0]
 
 
 def add_kernel(own, one, two, out):
@@ -553,8 +578,8 @@
         c1 = send_z(c1)
         c2 = send_y(c2, 1)
         c3 = send_y(c3, -1)
-    early_sums, bcat, acat, early = pair_early(early_sums, bcat, acat, ad, (bom, b2, bop))
-    keep, send, bcat = pair_late(early_sums, early, acat, bcat, (c1, c2, c3))
+    _, bcat, acat, keep, send = pair_early(early_sums, bcat, acat, ad, (bom, b2, bop))
+    keep, send, bcat = pair_late(keep, send, acat, bcat, (c1, c2, c3))
     with jax.named_scope("core"):
         own, *s = core_sum(keep, send_core(send))
     with jax.named_scope("shares"):
@@ -577,10 +602,11 @@
     with jax.named_scope("out"):
         from_m = send_x(x2_d1, 1)
         from_x = send_x(m1_d2, -1)
-    x1, m2, own = density_second(mine1, other1, bcat, from_m, from_x)
+    x1, m2, own_rows = density_second(mine1, other1, bcat, from_m, from_x)
     with jax.named_scope("out"):
         got_x1 = send_x(x1, 1)
         got_m2 = send_x(m2, -1)
+    own = density_own(own_rows, bcat, from_m, from_x)
     return add(own, got_x1, got_m2)
 
 

time: 162 us -> 161 us (level)
    pallas_call x11 -> x12, Pallas kernels: 27.1 us -> 27.6 us  [call(): pl.pallas_call(kernel, in_specs=[spec for _, spec in args], out_specs=[VM...]
  transfers between devices with their start and end apart: 36 -> 36, of which waited for: 20 -> 20; matrix products, arithmetic and copies ran while one was open for 0% -> 0% of each run, Pallas kernels for 11% -> 12%
where the time goes in v4:
time: 161 us; the launch traced here: 158 us
  starting transfers between devices  71.9 us (45%)
  waiting for transfers between devices  57.6 us (36%)
  Pallas kernels  28.3 us (18%)
    ppermute x9, starting transfers between devices, send_high(): return lax.ppermute(v, 'grp', [(g, (g + 2 * step) % 8) for g in range(8)])  29.3 us
    pallas_call x12, Pallas kernels, call(): pl.pallas_call(kernel, in_specs=[spec for _, spec in args], out_specs=[VM...  27.6 us
    ppermute x6, waiting for transfers between devices, send_y(): return lax.ppermute(v, 'blk', pairs)  21 us
    ppermute x9, waiting for transfers between devices, send_high(): return lax.ppermute(v, 'grp', [(g, (g + 2 * step) % 8) for g in range(8)])  18.8 us
    ppermute x9, starting transfers between devices, send_core(): return lax.ppermute(v, 'grp', [(g, g ^ 1) for g in range(8)])  12.2 us
    ppermute x7, starting transfers between devices, send_x(): return lax.ppermute(v, 'blk', pairs)  10.5 us
    ppermute x7, waiting for transfers between devices, send_x(): return lax.ppermute(v, 'blk', pairs)  8.94 us
    ppermute x6, starting transfers between devices, send_y(): return lax.ppermute(v, 'blk', pairs)  8.94 us
  transfers between devices with their start and end apart: 36, of which 20 were waited for; matrix products, arithmetic and copies ran while one was open for 0% of the time, Pallas kernels for 12%

profile of v4, /device:TPU:1, one launch (start us, length us, event | category | flops | bytes accessed | tf_op | source)
XLA Modules:
  0.0 158.1 jit_solution(3464176704076559158)
XLA Ops:
  0.0 1.1 ends.1
  1.1 6.3 %collective-permute-start = (bf16[320,512]{1,0:T(8,128)(2,1)S(1)}, bf16[320,512]{1,0:T(8,128)(2,1)S(1)}, u32[]{:S(2)}, u32[]{:S(2)}) collective-permute-start(bf16[320,512]{1,0:T(8,128)(2,1)S(1)} %get-tuple-element.39), channel_id=1, source_target_pairs={{0,32},{32,64},{64,96},{96,128},{128,160},{160,192},{192,224},{1,3... | collective-permute-start | bytes 983048 | tf_op jit(solution)/shard_map/ppermute | solution.py:559
  7.4 1.9 %collective-permute-start.1 = (bf16[320,512]{1,0:T(8,128)(2,1)S(1)}, bf16[320,512]{1,0:T(8,128)(2,1)S(1)}, u32[]{:S(2)}, u32[]{:S(2)}) collective-permute-start(bf16[320,512]{1,0:T(8,128)(2,1)S(1)} %get-tuple-element.40), channel_id=1, source_target_pairs={{32,0},{64,32},{96,64},{128,96},{160,128},{192,160},{224,192},{33,... | collective-permute-start | bytes 983048 | tf_op jit(solution)/shard_map/ppermute | solution.py:560
  9.3 8.0 %fit_inner.1 = (bf16[160,2560]{1,0:T(8,128)(2,1)S(1)}, bf16[160,2560]{1,0:T(8,128)(2,1)S(1)}, bf16[320,2560]{1,0:T(8,128)(2,1)S(1)}, bf16[4,1280,256]{2,1,0:T(8,128)(2,1)S(1)}) custom-call(s32[2,180]{1,0:T(2,128)} %bitcast.4, bf16[320,2560]{1,0:T(8,128)(2,1)} %bitcast.3, bf16[180,128,128]{2,1,0:T(8,128)(2,1)} %tiles_in.1), custom_call_target="tpu_custom_call" | custom-call | flops 1000 | bytes 1000 | tf_op jit(solution)/shard_map/fit_inner/pallas_call | solution.py:85
  17.3 2.9 %collective-permute-done.1.right = bf16[320,512]{1,0:T(8,128)(2,1)S(1)} collective-permute-done((bf16[320,512]{1,0:T(8,128)(2,1)S(1)}, bf16[320,512]{1,0:T(8,128)(2,1)S(1)}, u32[]{:S(2)}, u32[]{:S(2)}) %collective-permute-start.1) | collective-permute-done | bytes 327712 | tf_op jit(solution)/shard_map/ppermute | solution.py:560
  20.2 1.0 fit_edge.1
  21.2 3.2 %collective-permute-start.6 = (bf16[160,2560]{1,0:T(8,128)(2,1)S(1)}, bf16[160,2560]{1,0:T(8,128)(2,1)}, u32[]{:S(2)}, u32[]{:S(2)}) collective-permute-start(bf16[160,2560]{1,0:T(8,128)(2,1)S(1)} %get-tuple-element.46.refs_0_), channel_id=1, source_target_pairs={{0,24},{1,25},{2,26},{3,27},{4,28},{5,29},{6,30},{7,31},{8,0},{9,1... | collective-permute-start | bytes 2457608 | tf_op jit(solution)/shard_map/first/ppermute | solution.py:30
  24.5 2.5 %collective-permute-start.2 = (bf16[160,2560]{1,0:T(8,128)(2,1)S(1)}, bf16[160,2560]{1,0:T(8,128)(2,1)}, u32[]{:S(2)}, u32[]{:S(2)}) collective-permute-start(bf16[160,2560]{1,0:T(8,128)(2,1)S(1)} %get-tuple-element.45.own), channel_id=1, source_target_pairs={{0,6},{1,7},{2,0},{3,1},{4,2},{5,3},{6,4},{7,5},{8,14},{9,15},{10,... | collective-permute-start | bytes 2457608 | tf_op jit(solution)/shard_map/first/ppermute | solution.py:35
  27.1 9.7 %collective-permute-done.6.refs_1_ = bf16[160,2560]{1,0:T(8,128)(2,1)} collective-permute-done((bf16[160,2560]{1,0:T(8,128)(2,1)S(1)}, bf16[160,2560]{1,0:T(8,128)(2,1)}, u32[]{:S(2)}, u32[]{:S(2)}) %collective-permute-start.6) | collective-permute-done | bytes 819232 | tf_op jit(solution)/shard_map/first/ppermute | solution.py:30
  36.8 1.7 %collective-permute-done.5.refs_0_ = bf16[160,2560]{1,0:T(8,128)(2,1)} collective-permute-done((bf16[160,2560]{1,0:T(8,128)(2,1)S(1)}, bf16[160,2560]{1,0:T(8,128)(2,1)}, u32[]{:S(2)}, u32[]{:S(2)}) %collective-permute-start.5) | collective-permute-done | bytes 819232 | tf_op jit(solution)/shard_map/first/ppermute | solution.py:40
  38.6 2.8 %collective-permute-done.4.refs_2_.refs_1_ = bf16[160,2560]{1,0:T(8,128)(2,1)S(1)} collective-permute-done((bf16[160,2560]{1,0:T(8,128)(2,1)S(1)}, bf16[160,2560]{1,0:T(8,128)(2,1)S(1)}, u32[]{:S(2)}, u32[]{:S(2)}) %collective-permute-start.4) | collective-permute-done | bytes 819232 | tf_op jit(solution)/shard_map/first/ppermute | solution.py:30
  41.4 0.9 collective-permute-start.10
  42.3 2.7 %collective-permute-start.9 = (bf16[160,2560]{1,0:T(8,128)(2,1)}, bf16[160,2560]{1,0:T(8,128)(2,1)S(1)}, u32[]{:S(2)}, u32[]{:S(2)}) collective-permute-start(bf16[160,2560]{1,0:T(8,128)(2,1)} %get-tuple-element.47.refs_2_), channel_id=1, source_target_pairs={{0,24},{1,25},{2,26},{3,27},{4,28},{5,29},{6,30},{7,31},{8,0},{9,1... | collective-permute-start | bytes 2457608 | tf_op jit(solution)/shard_map/second/ppermute | solution.py:30
  45.0 2.5 %collective-permute-start.7 = (bf16[160,2560]{1,0:T(8,128)(2,1)}, bf16[160,2560]{1,0:T(8,128)(2,1)S(1)}, u32[]{:S(2)}, u32[]{:S(2)}) collective-permute-start(bf16[160,2560]{1,0:T(8,128)(2,1)} %collective-permute-done.2.ax), channel_id=1, source_target_pairs={{0,6},{1,7},{2,0},{3,1},{4,2},{5,3},{6,4},{7,5},{8,14},{9,15},{10,... | collective-permute-start | bytes 2457608 | tf_op jit(solution)/shard_map/second/ppermute | solution.py:35
  47.4 4.8 %pair_first.1 = (f32[640,640]{1,0:T(8,128)S(1)}, bf16[1280,2560]{1,0:T(8,128)(2,1)S(1)}, bf16[640,2560]{1,0:T(8,128)(2,1)S(1)}) custom-call(bf16[160,2560]{1,0:T(8,128)(2,1)S(1)} %get-tuple-element.45.own, bf16[160,2560]{1,0:T(8,128)(2,1)} %collective-permute-done.2.ax, bf16[160,2560]{1,0:T(8,128)(2,1)S(1)} %collective-permute-done.3.am, ...), custom_call_target="tpu_custom_call" | custom-call | flops 1000 | bytes 1000 | tf_op jit(solution)/shard_map/pair_first/pallas_call | solution.py:85
  52.3 7.3 %collective-permute-done.8.refs_0_.refs_1_ = bf16[160,2560]{1,0:T(8,128)(2,1)S(1)} collective-permute-done((bf16[160,2560]{1,0:T(8,128)(2,1)}, bf16[160,2560]{1,0:T(8,128)(2,1)S(1)}, u32[]{:S(2)}, u32[]{:S(2)}) %collective-permute-start.8) | collective-permute-done | bytes 819232 | tf_op jit(solution)/shard_map/second/ppermute | solution.py:30
  60.4 1.8 %collective-permute-start.11 = (bf16[64,2560]{1,0:T(8,128)(2,1)S(1)}, bf16[64,2560]{1,0:T(8,128)(2,1)S(1)}, u32[]{:S(2)}, u32[]{:S(2)}) collective-permute-start(bf16[64,2560]{1,0:T(8,128)(2,1)S(1)} %get-tuple-element.56), channel_id=1, source_target_pairs={{0,1},{1,0},{2,3},{3,2},{4,5},{5,4},{6,7},{7,6},{8,9},{9,8},{10,11... | collective-permute-start | bytes 983048 | tf_op jit(solution)/shard_map/third/ppermute | solution.py:40
  62.1 3.0 %collective-permute-start.13 = (bf16[48,2560]{1,0:T(8,128)(2,1)S(1)}, bf16[48,2560]{1,0:T(8,128)(2,1)S(1)}, u32[]{:S(2)}, u32[]{:S(2)}) collective-permute-start(bf16[48,2560]{1,0:T(8,128)(2,1)S(1)} %get-tuple-element.58), channel_id=1, source_target_pairs={{0,24},{1,25},{2,26},{3,27},{4,28},{5,29},{6,30},{7,31},{8,0},{9,1... | collective-permute-start | bytes 737288 | tf_op jit(solution)/shard_map/third/ppermute | solution.py:30
  65.2 3.6 %pair_early.1 = (f32[640,640]{1,0:T(8,128)S(1)}, bf16[1280,2560]{1,0:T(8,128)(2,1)S(1)}, bf16[640,2560]{1,0:T(8,128)(2,1)S(1)}, f32[640,640]{1,0:T(8,128)S(1)}, bf16[640,640]{1,0:T(8,128)(2,1)S(1)}) custom-call(f32[640,640]{1,0:T(8,128)S(1)} %get-tuple-element.49.first_in.refs_3_, ...), custom_call_target="tpu_custom_call", output_to_operand_aliasing={{0}: (0, {}), {1}: (1, {}), {2}: (2, {})} | custom-call | flops 1000 | bytes 1000 | tf_op jit(solution)/shard_map/pair_early/pallas_call | solution.py:85
  68.8 1.1 collective-permute-done.12.refs_1_
  69.9 1.5 pair_late.1
  71.5 2.3 %collective-permute-done.14.got = bf16[640,640]{1,0:T(8,128)(2,1)S(1)} collective-permute-done((bf16[640,640]{1,0:T(8,128)(2,1)S(1)}, bf16[640,640]{1,0:T(8,128)(2,1)S(1)}, u32[]{:S(2)}, u32[]{:S(2)}) %collective-permute-start.14) | collective-permute-done | bytes 819232 | tf_op jit(solution)/shard_map/core/ppermute | solution.py:44
  74.0 11.8 %collective-permute-start.15 = (bf16[160,640]{1,0:T(8,128)(2,1)S(1)}, bf16[160,640]{1,0:T(8,128)(2,1)S(1)}, u32[]{:S(2)}, u32[]{:S(2)}) collective-permute-start(bf16[160,640]{1,0:T(8,128)(2,1)S(1)} %get-tuple-element.62), channel_id=1, source_target_pairs={{0,128},{32,160},{64,192},{96,224},{128,0},{160,32},{192,64},{224,... | collective-permute-start | bytes 614408 | tf_op jit(solution)/shard_map/shares/ppermute | solution.py:48
  85.8 3.6 %collective-permute-start.17 = (bf16[160,640]{1,0:T(8,128)(2,1)S(1)}, bf16[160,640]{1,0:T(8,128)(2,1)S(1)}, u32[]{:S(2)}, u32[]{:S(2)}) collective-permute-start(bf16[160,640]{1,0:T(8,128)(2,1)S(1)} %get-tuple-element.64), channel_id=1, source_target_pairs={{0,192},{32,224},{64,0},{96,32},{128,64},{160,96},{192,128},{224,1... | collective-permute-start | bytes 614408 | tf_op jit(solution)/shard_map/shares/ppermute | solution.py:48
  89.4 6.2 %collective-permute-done.15.refs_0_ = bf16[160,640]{1,0:T(8,128)(2,1)S(1)} collective-permute-done((bf16[160,640]{1,0:T(8,128)(2,1)S(1)}, bf16[160,640]{1,0:T(8,128)(2,1)S(1)}, u32[]{:S(2)}, u32[]{:S(2)}) %collective-permute-start.15) | collective-permute-done | bytes 204832 | tf_op jit(solution)/shard_map/shares/ppermute | solution.py:48
  95.6 4.5 %collective-permute-done.16.refs_1_ = bf16[160,640]{1,0:T(8,128)(2,1)S(1)} collective-permute-done((bf16[160,640]{1,0:T(8,128)(2,1)S(1)}, bf16[160,640]{1,0:T(8,128)(2,1)S(1)}, u32[]{:S(2)}, u32[]{:S(2)}) %collective-permute-start.16) | collective-permute-done | bytes 204832 | tf_op jit(solution)/shard_map/shares/ppermute | solution.py:48
  100.1 1.2 collective-permute-done.17.refs_2_
  102.2 4.4 %collective-permute-start.27 = (bf16[80,640]{1,0:T(8,128)(2,1)S(1)}, bf16[80,640]{1,0:T(8,128)(2,1)S(1)}, u32[]{:S(2)}, u32[]{:S(2)}) collective-permute-start(bf16[80,640]{1,0:T(8,128)(2,1)S(1)} %get-tuple-element.67.refs_0_), channel_id=1, source_target_pairs={{0,192},{32,224},{64,0},{96,32},{128,64},{160,96},{192,128},{224,1... | collective-permute-start | bytes 307208 | tf_op jit(solution)/shard_map/spread_0/ppermute | solution.py:48
  106.6 4.3 %collective-permute-start.26 = (bf16[80,640]{1,0:T(8,128)(2,1)S(1)}, bf16[80,640]{1,0:T(8,128)(2,1)S(1)}, u32[]{:S(2)}, u32[]{:S(2)}) collective-permute-start(bf16[80,640]{1,0:T(8,128)(2,1)S(1)} %get-tuple-element.67.refs_0_), channel_id=1, source_target_pairs={{0,128},{32,160},{64,192},{96,224},{128,0},{160,32},{192,64},{224,... | collective-permute-start | bytes 307208 | tf_op jit(solution)/shard_map/spread_0/ppermute | solution.py:48
  110.8 1.1 collective-permute-start.28
  112.0 1.8 %collective-permute-start.31 = (bf16[80,640]{1,0:T(8,128)(2,1)S(1)}, bf16[80,640]{1,0:T(8,128)(2,1)S(1)}, u32[]{:S(2)}, u32[]{:S(2)}) collective-permute-start(bf16[80,640]{1,0:T(8,128)(2,1)S(1)} %collective-permute-done.27.refs_3_), channel_id=1, source_target_pairs={{0,32},{32,0},{64,96},{96,64},{128,160},{160,128},{192,224},{224,1... | collective-permute-start | bytes 307208 | tf_op jit(solution)/shard_map/other_0/ppermute | solution.py:44
  113.8 3.4 %collective-permute-done.26.refs_2_ = bf16[80,640]{1,0:T(8,128)(2,1)S(1)} collective-permute-done((bf16[80,640]{1,0:T(8,128)(2,1)S(1)}, bf16[80,640]{1,0:T(8,128)(2,1)S(1)}, u32[]{:S(2)}, u32[]{:S(2)}) %collective-permute-start.26) | collective-permute-done | bytes 102432 | tf_op jit(solution)/shard_map/spread_0/ppermute | solution.py:48
  117.2 2.2 %collective-permute-start.30 = (bf16[80,640]{1,0:T(8,128)(2,1)S(1)}, bf16[80,640]{1,0:T(8,128)(2,1)S(1)}, u32[]{:S(2)}, u32[]{:S(2)}) collective-permute-start(bf16[80,640]{1,0:T(8,128)(2,1)S(1)} %collective-permute-done.26.refs_2_), channel_id=1, source_target_pairs={{0,32},{32,0},{64,96},{96,64},{128,160},{160,128},{192,224},{224,1... | collective-permute-start | bytes 307208 | tf_op jit(solution)/shard_map/other_0/ppermute | solution.py:44
  121.1 2.5 %density_first.1 = (bf16[160,2560]{1,0:T(8,128)(2,1)S(1)}, bf16[160,2560]{1,0:T(8,128)(2,1)S(1)}) custom-call(bf16[80,640]{1,0:T(8,128)(2,1)S(1)} %get-tuple-element.67.refs_0_, bf16[80,640]{1,0:T(8,128)(2,1)S(1)} %collective-permute-done.25.refs_1_, bf16[80,640]{1,0:T(8,128)(2,1)S(1)} %collective-permute-done.26.refs_2_, ...), custom_call_target="tpu_custom_call" | custom-call | flops 1000 | bytes 1000 | tf_op jit(solution)/shard_map/density_first/pallas_call | solution.py:85
  123.7 1.0 collective-permute-start.32
  124.7 1.7 %collective-permute-start.33 = (bf16[160,2560]{1,0:T(8,128)(2,1)S(1)}, bf16[160,2560]{1,0:T(8,128)(2,1)S(1)}, u32[]{:S(2)}, u32[]{:S(2)}) collective-permute-start(bf16[160,2560]{1,0:T(8,128)(2,1)S(1)} %get-tuple-element.69), channel_id=1, source_target_pairs={{0,6},{1,7},{2,0},{3,1},{4,2},{5,3},{6,4},{7,5},{8,14},{9,15},{10,... | collective-permute-start | bytes 2457608 | tf_op jit(solution)/shard_map/out/ppermute | solution.py:35
  126.4 0.9 collective-permute-start.21
  127.4 1.4 collective-permute-start.20
  128.8 3.7 %collective-permute-start.19 = (bf16[80,640]{1,0:T(8,128)(2,1)S(1)}, bf16[80,640]{1,0:T(8,128)(2,1)S(1)}, u32[]{:S(2)}, u32[]{:S(2)}) collective-permute-start(bf16[80,640]{1,0:T(8,128)(2,1)S(1)} %get-tuple-element.65.refs_0_), channel_id=1, source_target_pairs={{0,128},{32,160},{64,192},{96,224},{128,0},{160,32},{192,64},{224,... | collective-permute-start | bytes 307208 | tf_op jit(solution)/shard_map/spread_1/ppermute | solution.py:48
  132.8 0.9 collective-permute-start.24
  133.7 3.3 %collective-permute-done.19.refs_2_ = bf16[80,640]{1,0:T(8,128)(2,1)S(1)} collective-permute-done((bf16[80,640]{1,0:T(8,128)(2,1)S(1)}, bf16[80,640]{1,0:T(8,128)(2,1)S(1)}, u32[]{:S(2)}, u32[]{:S(2)}) %collective-permute-start.19) | collective-permute-done | bytes 102432 | tf_op jit(solution)/shard_map/spread_1/ppermute | solution.py:48
  136.9 4.2 %collective-permute-start.23 = (bf16[80,640]{1,0:T(8,128)(2,1)S(1)}, bf16[80,640]{1,0:T(8,128)(2,1)S(1)}, u32[]{:S(2)}, u32[]{:S(2)}) collective-permute-start(bf16[80,640]{1,0:T(8,128)(2,1)S(1)} %collective-permute-done.19.refs_2_), channel_id=1, source_target_pairs={{0,32},{32,0},{64,96},{96,64},{128,160},{160,128},{192,224},{224,1... | collective-permute-start | bytes 307208 | tf_op jit(solution)/shard_map/other_1/ppermute | solution.py:44
  142.4 2.0 %collective-permute-done.32.refs_9_.got_m = bf16[160,2560]{1,0:T(8,128)(2,1)S(1)} collective-permute-done((bf16[160,2560]{1,0:T(8,128)(2,1)S(1)}, bf16[160,2560]{1,0:T(8,128)(2,1)S(1)}, u32[]{:S(2)}, u32[]{:S(2)}) %collective-permute-start.32) | collective-permute-done | bytes 819232 | tf_op jit(solution)/shard_map/out/ppermute | solution.py:35
  144.5 1.5 density_second.1
  146.7 2.1 %collective-permute-start.35 = (bf16[80,2560]{1,0:T(8,128)(2,1)S(1)}, bf16[80,2560]{1,0:T(8,128)(2,1)S(1)}, u32[]{:S(2)}, u32[]{:S(2)}) collective-permute-start(bf16[80,2560]{1,0:T(8,128)(2,1)S(1)} %get-tuple-element.72), channel_id=1, source_target_pairs={{0,6},{1,7},{2,0},{3,1},{4,2},{5,3},{6,4},{7,5},{8,14},{9,15},{10,... | collective-permute-start | bytes 1228808 | tf_op jit(solution)/shard_map/out/ppermute | solution.py:35
  148.7 1.4 density_own.1.own
  150.2 6.9 %collective-permute-done.34.one = bf16[80,2560]{1,0:T(8,128)(2,1)S(1)} collective-permute-done((bf16[80,2560]{1,0:T(8,128)(2,1)S(1)}, bf16[80,2560]{1,0:T(8,128)(2,1)S(1)}, u32[]{:S(2)}, u32[]{:S(2)}) %collective-permute-start.34) | collective-permute-done | bytes 409632 | tf_op jit(solution)/shard_map/out/ppermute | solution.py:35
  157.1 1.0 add.1
  (45 shorter events, 6.1 us)
Async XLA Ops:
  1.1 16.2 %collective-permute-start = (bf16[320,512]{1,0:T(8,128)(2,1)S(1)}, bf16[320,512]{1,0:T(8,128)(2,1)S(1)}, u32[]{:S(2)}, u32[]{:S(2)}) collective-permute-start(bf16[320,512]{1,0:T(8,128)(2,1)S(1)} %get-tuple-element.39), channel_id=1, source_target_pairs={{0,32},{32,64},{64,96},{96,128},{128,160},{160,192},{192,224},{1,3... | collective-permute-start | bytes 983048 | tf_op jit(solution)/shard_map/ppermute | solution.py:559
  7.4 12.8 %collective-permute-start.1 = (bf16[320,512]{1,0:T(8,128)(2,1)S(1)}, bf16[320,512]{1,0:T(8,128)(2,1)S(1)}, u32[]{:S(2)}, u32[]{:S(2)}) collective-permute-start(bf16[320,512]{1,0:T(8,128)(2,1)S(1)} %get-tuple-element.40), channel_id=1, source_target_pairs={{32,0},{64,32},{96,64},{128,96},{160,128},{192,160},{224,192},{33,... | collective-permute-start | bytes 983048 | tf_op jit(solution)/shard_map/ppermute | solution.py:560
  20.2 6.8 %copy-start.2 = (f32[5120]{0:T(1024)S(1)}, f32[5120]{0:T(1024)}, u32[]{:S(2)}) copy-start(f32[5120]{0:T(1024)} %param.9) | copy-start | bytes 61444
  21.2 15.6 %collective-permute-start.6 = (bf16[160,2560]{1,0:T(8,128)(2,1)S(1)}, bf16[160,2560]{1,0:T(8,128)(2,1)}, u32[]{:S(2)}, u32[]{:S(2)}) collective-permute-start(bf16[160,2560]{1,0:T(8,128)(2,1)S(1)} %get-tuple-element.46.refs_0_), channel_id=1, source_target_pairs={{0,24},{1,25},{2,26},{3,27},{4,28},{5,29},{6,30},{7,31},{8,0},{9,1... | collective-permute-start | bytes 2457608 | tf_op jit(solution)/shard_map/first/ppermute | solution.py:30
  24.5 14.1 %collective-permute-start.5 = (bf16[160,2560]{1,0:T(8,128)(2,1)S(1)}, bf16[160,2560]{1,0:T(8,128)(2,1)}, u32[]{:S(2)}, u32[]{:S(2)}) collective-permute-start(bf16[160,2560]{1,0:T(8,128)(2,1)S(1)} %get-tuple-element.46.refs_0_), channel_id=1, source_target_pairs={{0,1},{1,0},{2,3},{3,2},{4,5},{5,4},{6,7},{7,6},{8,9},{9,8},{10,11... | collective-permute-start | bytes 2457608 | tf_op jit(solution)/shard_map/first/ppermute | solution.py:40
  24.5 16.9 %collective-permute-start.4 = (bf16[160,2560]{1,0:T(8,128)(2,1)S(1)}, bf16[160,2560]{1,0:T(8,128)(2,1)S(1)}, u32[]{:S(2)}, u32[]{:S(2)}) collective-permute-start(bf16[160,2560]{1,0:T(8,128)(2,1)S(1)} %get-tuple-element.46.refs_0_), channel_id=1, source_target_pairs={{0,8},{1,9},{2,10},{3,11},{4,12},{5,13},{6,14},{7,15},{8,16},{9,17... | collective-permute-start | bytes 2457608 | tf_op jit(solution)/shard_map/first/ppermute | solution.py:30
  24.5 20.5 %collective-permute-start.2 = (bf16[160,2560]{1,0:T(8,128)(2,1)S(1)}, bf16[160,2560]{1,0:T(8,128)(2,1)}, u32[]{:S(2)}, u32[]{:S(2)}) collective-permute-start(bf16[160,2560]{1,0:T(8,128)(2,1)S(1)} %get-tuple-element.45.own), channel_id=1, source_target_pairs={{0,6},{1,7},{2,0},{3,1},{4,2},{5,3},{6,4},{7,5},{8,14},{9,15},{10,... | collective-permute-start | bytes 2457608 | tf_op jit(solution)/shard_map/first/ppermute | solution.py:35
  27.0 20.4 %collective-permute-start.3 = (bf16[160,2560]{1,0:T(8,128)(2,1)S(1)}, bf16[160,2560]{1,0:T(8,128)(2,1)S(1)}, u32[]{:S(2)}, u32[]{:S(2)}) collective-permute-start(bf16[160,2560]{1,0:T(8,128)(2,1)S(1)} %get-tuple-element.45.own), channel_id=1, source_target_pairs={{0,2},{1,3},{2,4},{3,5},{4,6},{5,7},{6,0},{7,1},{8,10},{9,11},{10,... | collective-permute-start | bytes 2457608 | tf_op jit(solution)/shard_map/first/ppermute | solution.py:35
  41.4 18.2 %collective-permute-start.8 = (bf16[160,2560]{1,0:T(8,128)(2,1)}, bf16[160,2560]{1,0:T(8,128)(2,1)S(1)}, u32[]{:S(2)}, u32[]{:S(2)}) collective-permute-start(bf16[160,2560]{1,0:T(8,128)(2,1)} %get-tuple-element.48.refs_3_), channel_id=1, source_target_pairs={{0,8},{1,9},{2,10},{3,11},{4,12},{5,13},{6,14},{7,15},{8,16},{9,17... | collective-permute-start | bytes 2457608 | tf_op jit(solution)/shard_map/second/ppermute | solution.py:30
  41.4 18.2 %collective-permute-start.10 = (bf16[160,2560]{1,0:T(8,128)(2,1)}, bf16[160,2560]{1,0:T(8,128)(2,1)S(1)}, u32[]{:S(2)}, u32[]{:S(2)}) collective-permute-start(bf16[160,2560]{1,0:T(8,128)(2,1)} %get-tuple-element.47.refs_2_), channel_id=1, source_target_pairs={{0,1},{1,0},{2,3},{3,2},{4,5},{5,4},{6,7},{7,6},{8,9},{9,8},{10,11... | collective-permute-start | bytes 2457608 | tf_op jit(solution)/shard_map/second/ppermute | solution.py:40
  42.3 17.3 %collective-permute-start.9 = (bf16[160,2560]{1,0:T(8,128)(2,1)}, bf16[160,2560]{1,0:T(8,128)(2,1)S(1)}, u32[]{:S(2)}, u32[]{:S(2)}) collective-permute-start(bf16[160,2560]{1,0:T(8,128)(2,1)} %get-tuple-element.47.refs_2_), channel_id=1, source_target_pairs={{0,24},{1,25},{2,26},{3,27},{4,28},{5,29},{6,30},{7,31},{8,0},{9,1... | collective-permute-start | bytes 2457608 | tf_op jit(solution)/shard_map/second/ppermute | solution.py:30
  45.0 20.2 %collective-permute-start.7 = (bf16[160,2560]{1,0:T(8,128)(2,1)}, bf16[160,2560]{1,0:T(8,128)(2,1)S(1)}, u32[]{:S(2)}, u32[]{:S(2)}) collective-permute-start(bf16[160,2560]{1,0:T(8,128)(2,1)} %collective-permute-done.2.ax), channel_id=1, source_target_pairs={{0,6},{1,7},{2,0},{3,1},{4,2},{5,3},{6,4},{7,5},{8,14},{9,15},{10,... | collective-permute-start | bytes 2457608 | tf_op jit(solution)/shard_map/second/ppermute | solution.py:35
  60.4 9.5 %collective-permute-start.11 = (bf16[64,2560]{1,0:T(8,128)(2,1)S(1)}, bf16[64,2560]{1,0:T(8,128)(2,1)S(1)}, u32[]{:S(2)}, u32[]{:S(2)}) collective-permute-start(bf16[64,2560]{1,0:T(8,128)(2,1)S(1)} %get-tuple-element.56), channel_id=1, source_target_pairs={{0,1},{1,0},{2,3},{3,2},{4,5},{5,4},{6,7},{7,6},{8,9},{9,8},{10,11... | collective-permute-start | bytes 983048 | tf_op jit(solution)/shard_map/third/ppermute | solution.py:40
  62.1 7.7 %collective-permute-start.12 = (bf16[48,2560]{1,0:T(8,128)(2,1)S(1)}, bf16[48,2560]{1,0:T(8,128)(2,1)S(1)}, u32[]{:S(2)}, u32[]{:S(2)}) collective-permute-start(bf16[48,2560]{1,0:T(8,128)(2,1)S(1)} %get-tuple-element.57), channel_id=1, source_target_pairs={{0,8},{1,9},{2,10},{3,11},{4,12},{5,13},{6,14},{7,15},{8,16},{9,17... | collective-permute-start | bytes 737288 | tf_op jit(solution)/shard_map/third/ppermute | solution.py:30
  62.1 7.7 %collective-permute-start.13 = (bf16[48,2560]{1,0:T(8,128)(2,1)S(1)}, bf16[48,2560]{1,0:T(8,128)(2,1)S(1)}, u32[]{:S(2)}, u32[]{:S(2)}) collective-permute-start(bf16[48,2560]{1,0:T(8,128)(2,1)S(1)} %get-tuple-element.58), channel_id=1, source_target_pairs={{0,24},{1,25},{2,26},{3,27},{4,28},{5,29},{6,30},{7,31},{8,0},{9,1... | collective-permute-start | bytes 737288 | tf_op jit(solution)/shard_map/third/ppermute | solution.py:30
  69.8 31.5 %copy-start = (f32[1000]{0:T(1024)S(1)}, f32[1000]{0:T(1024)}, u32[]{:S(2)}) copy-start(f32[1000]{0:T(1024)} %occ.1) | copy-start | bytes 12004
  69.8 31.5 %copy-start.1 = (s32[2]{0:T(128)S(1)}, s32[2]{0:T(128)}, u32[]{:S(2)}) copy-start(s32[2]{0:T(128)} %chosen.1) | copy-start | bytes 28
  71.4 2.4 %collective-permute-start.14 = (bf16[640,640]{1,0:T(8,128)(2,1)S(1)}, bf16[640,640]{1,0:T(8,128)(2,1)S(1)}, u32[]{:S(2)}, u32[]{:S(2)}) collective-permute-start(bf16[640,640]{1,0:T(8,128)(2,1)S(1)} %get-tuple-element.60), channel_id=1, source_target_pairs={{0,32},{32,0},{64,96},{96,64},{128,160},{160,128},{192,224},{224,1... | collective-permute-start | bytes 2457608 | tf_op jit(solution)/shard_map/core/ppermute | solution.py:44
  74.0 21.6 %collective-permute-start.15 = (bf16[160,640]{1,0:T(8,128)(2,1)S(1)}, bf16[160,640]{1,0:T(8,128)(2,1)S(1)}, u32[]{:S(2)}, u32[]{:S(2)}) collective-permute-start(bf16[160,640]{1,0:T(8,128)(2,1)S(1)} %get-tuple-element.62), channel_id=1, source_target_pairs={{0,128},{32,160},{64,192},{96,224},{128,0},{160,32},{192,64},{224,... | collective-permute-start | bytes 614408 | tf_op jit(solution)/shard_map/shares/ppermute | solution.py:48
  85.8 14.3 %collective-permute-start.16 = (bf16[160,640]{1,0:T(8,128)(2,1)S(1)}, bf16[160,640]{1,0:T(8,128)(2,1)S(1)}, u32[]{:S(2)}, u32[]{:S(2)}) collective-permute-start(bf16[160,640]{1,0:T(8,128)(2,1)S(1)} %get-tuple-element.63), channel_id=1, source_target_pairs={{0,64},{32,96},{64,128},{96,160},{128,192},{160,224},{192,0},{224,... | collective-permute-start | bytes 614408 | tf_op jit(solution)/shard_map/shares/ppermute | solution.py:48
  85.8 15.5 %collective-permute-start.17 = (bf16[160,640]{1,0:T(8,128)(2,1)S(1)}, bf16[160,640]{1,0:T(8,128)(2,1)S(1)}, u32[]{:S(2)}, u32[]{:S(2)}) collective-permute-start(bf16[160,640]{1,0:T(8,128)(2,1)S(1)} %get-tuple-element.64), channel_id=1, source_target_pairs={{0,192},{32,224},{64,0},{96,32},{128,64},{160,96},{192,128},{224,1... | collective-permute-start | bytes 614408 | tf_op jit(solution)/shard_map/shares/ppermute | solution.py:48
  102.2 9.8 %collective-permute-start.27 = (bf16[80,640]{1,0:T(8,128)(2,1)S(1)}, bf16[80,640]{1,0:T(8,128)(2,1)S(1)}, u32[]{:S(2)}, u32[]{:S(2)}) collective-permute-start(bf16[80,640]{1,0:T(8,128)(2,1)S(1)} %get-tuple-element.67.refs_0_), channel_id=1, source_target_pairs={{0,192},{32,224},{64,0},{96,32},{128,64},{160,96},{192,128},{224,1... | collective-permute-start | bytes 307208 | tf_op jit(solution)/shard_map/spread_0/ppermute | solution.py:48
  106.6 10.6 %collective-permute-start.26 = (bf16[80,640]{1,0:T(8,128)(2,1)S(1)}, bf16[80,640]{1,0:T(8,128)(2,1)S(1)}, u32[]{:S(2)}, u32[]{:S(2)}) collective-permute-start(bf16[80,640]{1,0:T(8,128)(2,1)S(1)} %get-tuple-element.67.refs_0_), channel_id=1, source_target_pairs={{0,128},{32,160},{64,192},{96,224},{128,0},{160,32},{192,64},{224,... | collective-permute-start | bytes 307208 | tf_op jit(solution)/shard_map/spread_0/ppermute | solution.py:48
  110.8 8.6 %collective-permute-start.25 = (bf16[80,640]{1,0:T(8,128)(2,1)S(1)}, bf16[80,640]{1,0:T(8,128)(2,1)S(1)}, u32[]{:S(2)}, u32[]{:S(2)}) collective-permute-start(bf16[80,640]{1,0:T(8,128)(2,1)S(1)} %get-tuple-element.67.refs_0_), channel_id=1, source_target_pairs={{0,64},{32,96},{64,128},{96,160},{128,192},{160,224},{192,0},{224,... | collective-permute-start | bytes 307208 | tf_op jit(solution)/shard_map/spread_0/ppermute | solution.py:48
  110.8 9.3 %collective-permute-start.28 = (bf16[80,640]{1,0:T(8,128)(2,1)S(1)}, bf16[80,640]{1,0:T(8,128)(2,1)S(1)}, u32[]{:S(2)}, u32[]{:S(2)}) collective-permute-start(bf16[80,640]{1,0:T(8,128)(2,1)S(1)} %get-tuple-element.67.refs_0_), channel_id=1, source_target_pairs={{0,32},{32,0},{64,96},{96,64},{128,160},{160,128},{192,224},{224,1... | collective-permute-start | bytes 307208 | tf_op jit(solution)/shard_map/other_0/ppermute | solution.py:44
  112.0 8.2 %collective-permute-start.31 = (bf16[80,640]{1,0:T(8,128)(2,1)S(1)}, bf16[80,640]{1,0:T(8,128)(2,1)S(1)}, u32[]{:S(2)}, u32[]{:S(2)}) collective-permute-start(bf16[80,640]{1,0:T(8,128)(2,1)S(1)} %collective-permute-done.27.refs_3_), channel_id=1, source_target_pairs={{0,32},{32,0},{64,96},{96,64},{128,160},{160,128},{192,224},{224,1... | collective-permute-start | bytes 307208 | tf_op jit(solution)/shard_map/other_0/ppermute | solution.py:44
  117.2 3.1 %collective-permute-start.30 = (bf16[80,640]{1,0:T(8,128)(2,1)S(1)}, bf16[80,640]{1,0:T(8,128)(2,1)S(1)}, u32[]{:S(2)}, u32[]{:S(2)}) collective-permute-start(bf16[80,640]{1,0:T(8,128)(2,1)S(1)} %collective-permute-done.26.refs_2_), channel_id=1, source_target_pairs={{0,32},{32,0},{64,96},{96,64},{128,160},{160,128},{192,224},{224,1... | collective-permute-start | bytes 307208 | tf_op jit(solution)/shard_map/other_0/ppermute | solution.py:44
  119.4 1.7 %collective-permute-start.29 = (bf16[80,640]{1,0:T(8,128)(2,1)S(1)}, bf16[80,640]{1,0:T(8,128)(2,1)S(1)}, u32[]{:S(2)}, u32[]{:S(2)}) collective-permute-start(bf16[80,640]{1,0:T(8,128)(2,1)S(1)} %collective-permute-done.25.refs_1_), channel_id=1, source_target_pairs={{0,32},{32,0},{64,96},{96,64},{128,160},{160,128},{192,224},{224,1... | collective-permute-start | bytes 307208 | tf_op jit(solution)/shard_map/other_0/ppermute | solution.py:44
  123.7 20.8 %collective-permute-start.32 = (bf16[160,2560]{1,0:T(8,128)(2,1)S(1)}, bf16[160,2560]{1,0:T(8,128)(2,1)S(1)}, u32[]{:S(2)}, u32[]{:S(2)}) collective-permute-start(bf16[160,2560]{1,0:T(8,128)(2,1)S(1)} %get-tuple-element.68), channel_id=1, source_target_pairs={{0,2},{1,3},{2,4},{3,5},{4,6},{5,7},{6,0},{7,1},{8,10},{9,11},{10,... | collective-permute-start | bytes 2457608 | tf_op jit(solution)/shard_map/out/ppermute | solution.py:35
  124.7 19.7 %collective-permute-start.33 = (bf16[160,2560]{1,0:T(8,128)(2,1)S(1)}, bf16[160,2560]{1,0:T(8,128)(2,1)S(1)}, u32[]{:S(2)}, u32[]{:S(2)}) collective-permute-start(bf16[160,2560]{1,0:T(8,128)(2,1)S(1)} %get-tuple-element.69), channel_id=1, source_target_pairs={{0,6},{1,7},{2,0},{3,1},{4,2},{5,3},{6,4},{7,5},{8,14},{9,15},{10,... | collective-permute-start | bytes 2457608 | tf_op jit(solution)/shard_map/out/ppermute | solution.py:35
  126.4 6.1 %collective-permute-start.21 = (bf16[80,640]{1,0:T(8,128)(2,1)S(1)}, bf16[80,640]{1,0:T(8,128)(2,1)S(1)}, u32[]{:S(2)}, u32[]{:S(2)}) collective-permute-start(bf16[80,640]{1,0:T(8,128)(2,1)S(1)} %get-tuple-element.65.refs_0_), channel_id=1, source_target_pairs={{0,32},{32,0},{64,96},{96,64},{128,160},{160,128},{192,224},{224,1... | collective-permute-start | bytes 307208 | tf_op jit(solution)/shard_map/other_1/ppermute | solution.py:44
  127.4 5.4 %collective-permute-start.20 = (bf16[80,640]{1,0:T(8,128)(2,1)S(1)}, bf16[80,640]{1,0:T(8,128)(2,1)S(1)}, u32[]{:S(2)}, u32[]{:S(2)}) collective-permute-start(bf16[80,640]{1,0:T(8,128)(2,1)S(1)} %get-tuple-element.65.refs_0_), channel_id=1, source_target_pairs={{0,192},{32,224},{64,0},{96,32},{128,64},{160,96},{192,128},{224,1... | collective-permute-start | bytes 307208 | tf_op jit(solution)/shard_map/spread_1/ppermute | solution.py:48
  128.8 8.1 %collective-permute-start.19 = (bf16[80,640]{1,0:T(8,128)(2,1)S(1)}, bf16[80,640]{1,0:T(8,128)(2,1)S(1)}, u32[]{:S(2)}, u32[]{:S(2)}) collective-permute-start(bf16[80,640]{1,0:T(8,128)(2,1)S(1)} %get-tuple-element.65.refs_0_), channel_id=1, source_target_pairs={{0,128},{32,160},{64,192},{96,224},{128,0},{160,32},{192,64},{224,... | collective-permute-start | bytes 307208 | tf_op jit(solution)/shard_map/spread_1/ppermute | solution.py:48
  132.5 8.6 %collective-permute-start.18 = (bf16[80,640]{1,0:T(8,128)(2,1)S(1)}, bf16[80,640]{1,0:T(8,128)(2,1)S(1)}, u32[]{:S(2)}, u32[]{:S(2)}) collective-permute-start(bf16[80,640]{1,0:T(8,128)(2,1)S(1)} %get-tuple-element.65.refs_0_), channel_id=1, source_target_pairs={{0,64},{32,96},{64,128},{96,160},{128,192},{160,224},{192,0},{224,... | collective-permute-start | bytes 307208 | tf_op jit(solution)/shard_map/spread_1/ppermute | solution.py:48
  132.8 8.7 %collective-permute-start.24 = (bf16[80,640]{1,0:T(8,128)(2,1)S(1)}, bf16[80,640]{1,0:T(8,128)(2,1)S(1)}, u32[]{:S(2)}, u32[]{:S(2)}) collective-permute-start(bf16[80,640]{1,0:T(8,128)(2,1)S(1)} %collective-permute-done.20.refs_3_), channel_id=1, source_target_pairs={{0,32},{32,0},{64,96},{96,64},{128,160},{160,128},{192,224},{224,1... | collective-permute-start | bytes 307208 | tf_op jit(solution)/shard_map/other_1/ppermute | solution.py:44
  136.9 5.1 %collective-permute-start.23 = (bf16[80,640]{1,0:T(8,128)(2,1)S(1)}, bf16[80,640]{1,0:T(8,128)(2,1)S(1)}, u32[]{:S(2)}, u32[]{:S(2)}) collective-permute-start(bf16[80,640]{1,0:T(8,128)(2,1)S(1)} %collective-permute-done.19.refs_2_), channel_id=1, source_target_pairs={{0,32},{32,0},{64,96},{96,64},{128,160},{160,128},{192,224},{224,1... | collective-permute-start | bytes 307208 | tf_op jit(solution)/shard_map/other_1/ppermute | solution.py:44
  141.1 1.3 collective-permute-start.22
  146.0 11.1 %collective-permute-start.34 = (bf16[80,2560]{1,0:T(8,128)(2,1)S(1)}, bf16[80,2560]{1,0:T(8,128)(2,1)S(1)}, u32[]{:S(2)}, u32[]{:S(2)}) collective-permute-start(bf16[80,2560]{1,0:T(8,128)(2,1)S(1)} %get-tuple-element.71), channel_id=1, source_target_pairs={{0,2},{1,3},{2,4},{3,5},{4,6},{5,7},{6,0},{7,1},{8,10},{9,11},{10,... | collective-permute-start | bytes 1228808 | tf_op jit(solution)/shard_map/out/ppermute | solution.py:35
  146.7 10.4 %collective-permute-start.35 = (bf16[80,2560]{1,0:T(8,128)(2,1)S(1)}, bf16[80,2560]{1,0:T(8,128)(2,1)S(1)}, u32[]{:S(2)}, u32[]{:S(2)}) collective-permute-start(bf16[80,2560]{1,0:T(8,128)(2,1)S(1)} %get-tuple-element.72), channel_id=1, source_target_pairs={{0,6},{1,7},{2,0},{3,1},{4,2},{5,3},{6,4},{7,5},{8,14},{9,15},{10,... | collective-permute-start | bytes 1228808 | tf_op jit(solution)/shard_map/out/ppermute | solution.py:35

commit v5 on v4

--- a/solution.py
+++ b/solution.py
@@ -196,26 +196,15 @@
 
 def cut(parts, after=(), name=None):
     def kernel(*refs):
-        ins, outs, sems = refs[: len(parts)], refs[-1 - len(parts) : -1], refs[-1]
-        copies = [
-            pltpu.make_async_copy(i.at[pl.ds(r, n)], o, sems.at[j])
-            for j, (i, o, (_, r, n)) in enumerate(zip(ins, outs, parts))
-        ]
-        for c in copies:
-            c.start()
-        for c in copies:
-            c.wait()
-
-    return pl.pallas_call(
+        for i, o, (_, r, n) in zip(refs, refs[len(parts) + len(after) :], parts):
+            o[...] = i[r : r + n]
+
+    return call(
         kernel,
-        in_specs=[ANY] * (len(parts) + len(after)),
-        out_specs=[ANY] * len(parts),
-        out_shape=[hbm((n, AUX)) for _, _, n in parts],
-        scratch_shapes=[DMA((len(parts),))],
-        compiler_params=params(),
-        cost_estimate=cost(),
+        [(p[0], VMEM) for p in parts] + [(v, ANY) for v in after],
+        [hbm((n, AUX)) for _, _, n in parts],
         name=name,
-    )(*[p[0] for p in parts], *after)
+    )
 
 
 def arrive(parts, after):
@@ -360,29 +349,31 @@
 
 def pair_late_kernel(keep_in, send_in, acat, bcat_in, *refs):
     b_refs = refs[:3]
-    keep, send, bcat, late, sems = refs[3:]
-    products(
-        lambda part: row_copies(b_moves(b_refs, 7 * ROWS), bcat, sems, part),
-        acat, bcat, [(slice(0, WIDE), slice(7 * ROWS, 8 * ROWS), late)], unroll=True,
+    keep, send, bcat = refs[3:]
+    at = 7 * ROWS
+    for v in b_refs:
+        bcat[at : at + v.shape[0]] = v[...]
+        at += v.shape[0]
+    late = lax.dot_general(
+        acat[...], bcat[7 * ROWS :], (((1,), (1,)), ((), ())), preferred_element_type=f32
     )
     core = position()[1]
     columns = slice(3 * ROWS, WIDE)
 
     @pl.when(core == 0)
     def _():
-        send[:, columns] = late[...].astype(bf16)
+        send[:, columns] = late.astype(bf16)
 
     @pl.when(core == 1)
     def _():
-        keep[:, columns] = late[...]
+        keep[:, columns] = late
 
 
 def pair_late(keep, send, acat, bcat, b_parts):
     return call(
         pair_late_kernel,
-        [(v, VMEM) for v in (keep, send, acat, bcat)] + [(v, ANY) for v in b_parts],
+        [(v, VMEM) for v in (keep, send, acat, bcat, *b_parts)],
         [vmem((WIDE, WIDE), f32), vmem((WIDE, WIDE)), vmem((2 * WIDE, AUX))],
-        [pltpu.VMEM((WIDE, ROWS), f32), DMA((3, 4))],
         name="pair_late",
         aliases={0: 0, 1: 1, 3: 2},
     )

time: 161 us -> 160 us (level)
    pallas_call x12 -> x13, Pallas kernels: 27.6 us -> 27.3 us  [call(): pl.pallas_call(kernel, in_specs=[spec for _, spec in args], out_specs=[VM...]
  transfers between devices with their start and end apart: 36 -> 36, of which waited for: 20 -> 20; matrix products, arithmetic and copies ran while one was open for 0% -> 0% of each run, Pallas kernels for 12% -> 11%
where the time goes in v5:
time: 160 us; the launch traced here: 157 us
  starting transfers between devices  71.9 us (45%)
  waiting for transfers between devices  57.7 us (36%)
  Pallas kernels  27.3 us (17%)
    ppermute x9, starting transfers between devices, send_high(): return lax.ppermute(v, 'grp', [(g, (g + 2 * step) % 8) for g in range(8)])  29.3 us
    pallas_call x13, Pallas kernels, call(): pl.pallas_call(kernel, in_specs=[spec for _, spec in args], out_specs=[VM...  27.3 us
    ppermute x6, waiting for transfers between devices, send_y(): return lax.ppermute(v, 'blk', pairs)  21 us
    ppermute x9, waiting for transfers between devices, send_high(): return lax.ppermute(v, 'grp', [(g, (g + 2 * step) % 8) for g in range(8)])  18.9 us
    ppermute x9, starting transfers between devices, send_core(): return lax.ppermute(v, 'grp', [(g, g ^ 1) for g in range(8)])  12.2 us
    ppermute x7, starting transfers between devices, send_x(): return lax.ppermute(v, 'blk', pairs)  10.5 us
    ppermute x7, waiting for transfers between devices, send_x(): return lax.ppermute(v, 'blk', pairs)  8.94 us
    ppermute x6, starting transfers between devices, send_y(): return lax.ppermute(v, 'blk', pairs)  8.94 us
  transfers between devices with their start and end apart: 36, of which 20 were waited for; matrix products, arithmetic and copies ran while one was open for 0% of the time, Pallas kernels for 11%

profile of v5, /device:TPU:1, one launch (start us, length us, event | category | flops | bytes accessed | tf_op | source)
XLA Modules:
  0.0 157.1 jit_solution(2977761556329759302)
XLA Ops:
  0.0 1.1 ends.1
  1.1 6.3 %collective-permute-start = (bf16[320,512]{1,0:T(8,128)(2,1)S(1)}, bf16[320,512]{1,0:T(8,128)(2,1)S(1)}, u32[]{:S(2)}, u32[]{:S(2)}) collective-permute-start(bf16[320,512]{1,0:T(8,128)(2,1)S(1)} %get-tuple-element.39), channel_id=1, source_target_pairs={{0,32},{32,64},{64,96},{96,128},{128,160},{160,192},{192,224},{1,3... | collective-permute-start | bytes 983048 | tf_op jit(solution)/shard_map/ppermute | solution.py:550
  7.4 1.9 %collective-permute-start.1 = (bf16[320,512]{1,0:T(8,128)(2,1)S(1)}, bf16[320,512]{1,0:T(8,128)(2,1)S(1)}, u32[]{:S(2)}, u32[]{:S(2)}) collective-permute-start(bf16[320,512]{1,0:T(8,128)(2,1)S(1)} %get-tuple-element.40), channel_id=1, source_target_pairs={{32,0},{64,32},{96,64},{128,96},{160,128},{192,160},{224,192},{33,... | collective-permute-start | bytes 983048 | tf_op jit(solution)/shard_map/ppermute | solution.py:551
  9.3 8.0 %fit_inner.1 = (bf16[160,2560]{1,0:T(8,128)(2,1)S(1)}, bf16[160,2560]{1,0:T(8,128)(2,1)S(1)}, bf16[320,2560]{1,0:T(8,128)(2,1)S(1)}, bf16[4,1280,256]{2,1,0:T(8,128)(2,1)S(1)}) custom-call(s32[2,180]{1,0:T(2,128)} %bitcast.4, bf16[320,2560]{1,0:T(8,128)(2,1)} %bitcast.3, bf16[180,128,128]{2,1,0:T(8,128)(2,1)} %tiles_in.1), custom_call_target="tpu_custom_call" | custom-call | flops 1000 | bytes 1000 | tf_op jit(solution)/shard_map/fit_inner/pallas_call | solution.py:85
  17.3 2.9 %collective-permute-done.1.right = bf16[320,512]{1,0:T(8,128)(2,1)S(1)} collective-permute-done((bf16[320,512]{1,0:T(8,128)(2,1)S(1)}, bf16[320,512]{1,0:T(8,128)(2,1)S(1)}, u32[]{:S(2)}, u32[]{:S(2)}) %collective-permute-start.1) | collective-permute-done | bytes 327712 | tf_op jit(solution)/shard_map/ppermute | solution.py:551
  20.2 1.0 fit_edge.1
  21.2 3.2 %collective-permute-start.6 = (bf16[160,2560]{1,0:T(8,128)(2,1)S(1)}, bf16[160,2560]{1,0:T(8,128)(2,1)}, u32[]{:S(2)}, u32[]{:S(2)}) collective-permute-start(bf16[160,2560]{1,0:T(8,128)(2,1)S(1)} %get-tuple-element.46.refs_0_), channel_id=1, source_target_pairs={{0,24},{1,25},{2,26},{3,27},{4,28},{5,29},{6,30},{7,31},{8,0},{9,1... | collective-permute-start | bytes 2457608 | tf_op jit(solution)/shard_map/first/ppermute | solution.py:30
  24.5 2.5 %collective-permute-start.2 = (bf16[160,2560]{1,0:T(8,128)(2,1)S(1)}, bf16[160,2560]{1,0:T(8,128)(2,1)}, u32[]{:S(2)}, u32[]{:S(2)}) collective-permute-start(bf16[160,2560]{1,0:T(8,128)(2,1)S(1)} %get-tuple-element.45.own), channel_id=1, source_target_pairs={{0,6},{1,7},{2,0},{3,1},{4,2},{5,3},{6,4},{7,5},{8,14},{9,15},{10,... | collective-permute-start | bytes 2457608 | tf_op jit(solution)/shard_map/first/ppermute | solution.py:35
  27.1 9.7 %collective-permute-done.6.refs_1_ = bf16[160,2560]{1,0:T(8,128)(2,1)} collective-permute-done((bf16[160,2560]{1,0:T(8,128)(2,1)S(1)}, bf16[160,2560]{1,0:T(8,128)(2,1)}, u32[]{:S(2)}, u32[]{:S(2)}) %collective-permute-start.6) | collective-permute-done | bytes 819232 | tf_op jit(solution)/shard_map/first/ppermute | solution.py:30
  36.8 1.7 %collective-permute-done.5.refs_0_ = bf16[160,2560]{1,0:T(8,128)(2,1)} collective-permute-done((bf16[160,2560]{1,0:T(8,128)(2,1)S(1)}, bf16[160,2560]{1,0:T(8,128)(2,1)}, u32[]{:S(2)}, u32[]{:S(2)}) %collective-permute-start.5) | collective-permute-done | bytes 819232 | tf_op jit(solution)/shard_map/first/ppermute | solution.py:40
  38.6 2.8 %collective-permute-done.4.refs_2_.refs_1_ = bf16[160,2560]{1,0:T(8,128)(2,1)S(1)} collective-permute-done((bf16[160,2560]{1,0:T(8,128)(2,1)S(1)}, bf16[160,2560]{1,0:T(8,128)(2,1)S(1)}, u32[]{:S(2)}, u32[]{:S(2)}) %collective-permute-start.4) | collective-permute-done | bytes 819232 | tf_op jit(solution)/shard_map/first/ppermute | solution.py:30
  41.4 0.9 collective-permute-start.10
  42.3 2.7 %collective-permute-start.9 = (bf16[160,2560]{1,0:T(8,128)(2,1)}, bf16[160,2560]{1,0:T(8,128)(2,1)S(1)}, u32[]{:S(2)}, u32[]{:S(2)}) collective-permute-start(bf16[160,2560]{1,0:T(8,128)(2,1)} %get-tuple-element.47.refs_2_), channel_id=1, source_target_pairs={{0,24},{1,25},{2,26},{3,27},{4,28},{5,29},{6,30},{7,31},{8,0},{9,1... | collective-permute-start | bytes 2457608 | tf_op jit(solution)/shard_map/second/ppermute | solution.py:30
  45.0 2.5 %collective-permute-start.7 = (bf16[160,2560]{1,0:T(8,128)(2,1)}, bf16[160,2560]{1,0:T(8,128)(2,1)S(1)}, u32[]{:S(2)}, u32[]{:S(2)}) collective-permute-start(bf16[160,2560]{1,0:T(8,128)(2,1)} %collective-permute-done.2.ax), channel_id=1, source_target_pairs={{0,6},{1,7},{2,0},{3,1},{4,2},{5,3},{6,4},{7,5},{8,14},{9,15},{10,... | collective-permute-start | bytes 2457608 | tf_op jit(solution)/shard_map/second/ppermute | solution.py:35
  47.4 4.8 %pair_first.1 = (f32[640,640]{1,0:T(8,128)S(1)}, bf16[1280,2560]{1,0:T(8,128)(2,1)S(1)}, bf16[640,2560]{1,0:T(8,128)(2,1)S(1)}) custom-call(bf16[160,2560]{1,0:T(8,128)(2,1)S(1)} %get-tuple-element.45.own, bf16[160,2560]{1,0:T(8,128)(2,1)} %collective-permute-done.2.ax, bf16[160,2560]{1,0:T(8,128)(2,1)S(1)} %collective-permute-done.3.am, ...), custom_call_target="tpu_custom_call" | custom-call | flops 1000 | bytes 1000 | tf_op jit(solution)/shard_map/pair_first/pallas_call | solution.py:85
  52.3 7.3 %collective-permute-done.8.refs_0_.refs_1_ = bf16[160,2560]{1,0:T(8,128)(2,1)S(1)} collective-permute-done((bf16[160,2560]{1,0:T(8,128)(2,1)}, bf16[160,2560]{1,0:T(8,128)(2,1)S(1)}, u32[]{:S(2)}, u32[]{:S(2)}) %collective-permute-start.8) | collective-permute-done | bytes 819232 | tf_op jit(solution)/shard_map/second/ppermute | solution.py:30
  59.7 1.8 %collective-permute-start.11 = (bf16[64,2560]{1,0:T(8,128)(2,1)S(1)}, bf16[64,2560]{1,0:T(8,128)(2,1)S(1)}, u32[]{:S(2)}, u32[]{:S(2)}) collective-permute-start(bf16[64,2560]{1,0:T(8,128)(2,1)S(1)} %get-tuple-element.56), channel_id=1, source_target_pairs={{0,1},{1,0},{2,3},{3,2},{4,5},{5,4},{6,7},{7,6},{8,9},{9,8},{10,11... | collective-permute-start | bytes 983048 | tf_op jit(solution)/shard_map/third/ppermute | solution.py:40
  61.4 3.0 %collective-permute-start.13 = (bf16[48,2560]{1,0:T(8,128)(2,1)S(1)}, bf16[48,2560]{1,0:T(8,128)(2,1)S(1)}, u32[]{:S(2)}, u32[]{:S(2)}) collective-permute-start(bf16[48,2560]{1,0:T(8,128)(2,1)S(1)} %get-tuple-element.58), channel_id=1, source_target_pairs={{0,24},{1,25},{2,26},{3,27},{4,28},{5,29},{6,30},{7,31},{8,0},{9,1... | collective-permute-start | bytes 737288 | tf_op jit(solution)/shard_map/third/ppermute | solution.py:30
  64.5 3.6 %pair_early.1 = (f32[640,640]{1,0:T(8,128)S(1)}, bf16[1280,2560]{1,0:T(8,128)(2,1)S(1)}, bf16[640,2560]{1,0:T(8,128)(2,1)S(1)}, f32[640,640]{1,0:T(8,128)S(1)}, bf16[640,640]{1,0:T(8,128)(2,1)S(1)}) custom-call(f32[640,640]{1,0:T(8,128)S(1)} %get-tuple-element.49.first_in.refs_3_, ...), custom_call_target="tpu_custom_call", output_to_operand_aliasing={{0}: (0, {}), {1}: (1, {}), {2}: (2, {})} | custom-call | flops 1000 | bytes 1000 | tf_op jit(solution)/shard_map/pair_early/pallas_call | solution.py:85
  68.1 1.1 collective-permute-done.12.refs_1_
  69.1 1.3 pair_late.1
  70.5 2.3 %collective-permute-done.14.got = bf16[640,640]{1,0:T(8,128)(2,1)S(1)} collective-permute-done((bf16[640,640]{1,0:T(8,128)(2,1)S(1)}, bf16[640,640]{1,0:T(8,128)(2,1)S(1)}, u32[]{:S(2)}, u32[]{:S(2)}) %collective-permute-start.14) | collective-permute-done | bytes 819232 | tf_op jit(solution)/shard_map/core/ppermute | solution.py:44
  73.0 11.9 %collective-permute-start.15 = (bf16[160,640]{1,0:T(8,128)(2,1)S(1)}, bf16[160,640]{1,0:T(8,128)(2,1)S(1)}, u32[]{:S(2)}, u32[]{:S(2)}) collective-permute-start(bf16[160,640]{1,0:T(8,128)(2,1)S(1)} %get-tuple-element.62), channel_id=1, source_target_pairs={{0,128},{32,160},{64,192},{96,224},{128,0},{160,32},{192,64},{224,... | collective-permute-start | bytes 614408 | tf_op jit(solution)/shard_map/shares/ppermute | solution.py:48
  84.9 3.6 %collective-permute-start.17 = (bf16[160,640]{1,0:T(8,128)(2,1)S(1)}, bf16[160,640]{1,0:T(8,128)(2,1)S(1)}, u32[]{:S(2)}, u32[]{:S(2)}) collective-permute-start(bf16[160,640]{1,0:T(8,128)(2,1)S(1)} %get-tuple-element.64), channel_id=1, source_target_pairs={{0,192},{32,224},{64,0},{96,32},{128,64},{160,96},{192,128},{224,1... | collective-permute-start | bytes 614408 | tf_op jit(solution)/shard_map/shares/ppermute | solution.py:48
  88.4 6.2 %collective-permute-done.15.refs_0_ = bf16[160,640]{1,0:T(8,128)(2,1)S(1)} collective-permute-done((bf16[160,640]{1,0:T(8,128)(2,1)S(1)}, bf16[160,640]{1,0:T(8,128)(2,1)S(1)}, u32[]{:S(2)}, u32[]{:S(2)}) %collective-permute-start.15) | collective-permute-done | bytes 204832 | tf_op jit(solution)/shard_map/shares/ppermute | solution.py:48
  94.6 4.5 %collective-permute-done.16.refs_1_ = bf16[160,640]{1,0:T(8,128)(2,1)S(1)} collective-permute-done((bf16[160,640]{1,0:T(8,128)(2,1)S(1)}, bf16[160,640]{1,0:T(8,128)(2,1)S(1)}, u32[]{:S(2)}, u32[]{:S(2)}) %collective-permute-start.16) | collective-permute-done | bytes 204832 | tf_op jit(solution)/shard_map/shares/ppermute | solution.py:48
  99.2 1.2 collective-permute-done.17.refs_2_
  101.2 4.4 %collective-permute-start.27 = (bf16[80,640]{1,0:T(8,128)(2,1)S(1)}, bf16[80,640]{1,0:T(8,128)(2,1)S(1)}, u32[]{:S(2)}, u32[]{:S(2)}) collective-permute-start(bf16[80,640]{1,0:T(8,128)(2,1)S(1)} %get-tuple-element.67.refs_0_), channel_id=1, source_target_pairs={{0,192},{32,224},{64,0},{96,32},{128,64},{160,96},{192,128},{224,1... | collective-permute-start | bytes 307208 | tf_op jit(solution)/shard_map/spread_0/ppermute | solution.py:48
  105.6 4.2 %collective-permute-start.26 = (bf16[80,640]{1,0:T(8,128)(2,1)S(1)}, bf16[80,640]{1,0:T(8,128)(2,1)S(1)}, u32[]{:S(2)}, u32[]{:S(2)}) collective-permute-start(bf16[80,640]{1,0:T(8,128)(2,1)S(1)} %get-tuple-element.67.refs_0_), channel_id=1, source_target_pairs={{0,128},{32,160},{64,192},{96,224},{128,0},{160,32},{192,64},{224,... | collective-permute-start | bytes 307208 | tf_op jit(solution)/shard_map/spread_0/ppermute | solution.py:48
  109.9 1.1 collective-permute-start.28
  111.0 1.8 %collective-permute-start.31 = (bf16[80,640]{1,0:T(8,128)(2,1)S(1)}, bf16[80,640]{1,0:T(8,128)(2,1)S(1)}, u32[]{:S(2)}, u32[]{:S(2)}) collective-permute-start(bf16[80,640]{1,0:T(8,128)(2,1)S(1)} %collective-permute-done.27.refs_3_), channel_id=1, source_target_pairs={{0,32},{32,0},{64,96},{96,64},{128,160},{160,128},{192,224},{224,1... | collective-permute-start | bytes 307208 | tf_op jit(solution)/shard_map/other_0/ppermute | solution.py:44
  112.8 3.5 %collective-permute-done.26.refs_2_ = bf16[80,640]{1,0:T(8,128)(2,1)S(1)} collective-permute-done((bf16[80,640]{1,0:T(8,128)(2,1)S(1)}, bf16[80,640]{1,0:T(8,128)(2,1)S(1)}, u32[]{:S(2)}, u32[]{:S(2)}) %collective-permute-start.26) | collective-permute-done | bytes 102432 | tf_op jit(solution)/shard_map/spread_0/ppermute | solution.py:48
  116.3 2.1 %collective-permute-start.30 = (bf16[80,640]{1,0:T(8,128)(2,1)S(1)}, bf16[80,640]{1,0:T(8,128)(2,1)S(1)}, u32[]{:S(2)}, u32[]{:S(2)}) collective-permute-start(bf16[80,640]{1,0:T(8,128)(2,1)S(1)} %collective-permute-done.26.refs_2_), channel_id=1, source_target_pairs={{0,32},{32,0},{64,96},{96,64},{128,160},{160,128},{192,224},{224,1... | collective-permute-start | bytes 307208 | tf_op jit(solution)/shard_map/other_0/ppermute | solution.py:44
  120.2 2.5 %density_first.1 = (bf16[160,2560]{1,0:T(8,128)(2,1)S(1)}, bf16[160,2560]{1,0:T(8,128)(2,1)S(1)}) custom-call(bf16[80,640]{1,0:T(8,128)(2,1)S(1)} %get-tuple-element.67.refs_0_, bf16[80,640]{1,0:T(8,128)(2,1)S(1)} %collective-permute-done.25.refs_1_, bf16[80,640]{1,0:T(8,128)(2,1)S(1)} %collective-permute-done.26.refs_2_, ...), custom_call_target="tpu_custom_call" | custom-call | flops 1000 | bytes 1000 | tf_op jit(solution)/shard_map/density_first/pallas_call | solution.py:85
  122.7 1.1 collective-permute-start.32
  123.8 1.7 %collective-permute-start.33 = (bf16[160,2560]{1,0:T(8,128)(2,1)S(1)}, bf16[160,2560]{1,0:T(8,128)(2,1)S(1)}, u32[]{:S(2)}, u32[]{:S(2)}) collective-permute-start(bf16[160,2560]{1,0:T(8,128)(2,1)S(1)} %get-tuple-element.69), channel_id=1, source_target_pairs={{0,6},{1,7},{2,0},{3,1},{4,2},{5,3},{6,4},{7,5},{8,14},{9,15},{10,... | collective-permute-start | bytes 2457608 | tf_op jit(solution)/shard_map/out/ppermute | solution.py:35
  125.5 0.9 collective-permute-start.21
  126.4 1.4 collective-permute-start.20
  127.8 3.7 %collective-permute-start.19 = (bf16[80,640]{1,0:T(8,128)(2,1)S(1)}, bf16[80,640]{1,0:T(8,128)(2,1)S(1)}, u32[]{:S(2)}, u32[]{:S(2)}) collective-permute-start(bf16[80,640]{1,0:T(8,128)(2,1)S(1)} %get-tuple-element.65.refs_0_), channel_id=1, source_target_pairs={{0,128},{32,160},{64,192},{96,224},{128,0},{160,32},{192,64},{224,... | collective-permute-start | bytes 307208 | tf_op jit(solution)/shard_map/spread_1/ppermute | solution.py:48
  131.8 0.9 collective-permute-start.24
  132.7 3.2 %collective-permute-done.19.refs_2_ = bf16[80,640]{1,0:T(8,128)(2,1)S(1)} collective-permute-done((bf16[80,640]{1,0:T(8,128)(2,1)S(1)}, bf16[80,640]{1,0:T(8,128)(2,1)S(1)}, u32[]{:S(2)}, u32[]{:S(2)}) %collective-permute-start.19) | collective-permute-done | bytes 102432 | tf_op jit(solution)/shard_map/spread_1/ppermute | solution.py:48
  135.9 4.2 %collective-permute-start.23 = (bf16[80,640]{1,0:T(8,128)(2,1)S(1)}, bf16[80,640]{1,0:T(8,128)(2,1)S(1)}, u32[]{:S(2)}, u32[]{:S(2)}) collective-permute-start(bf16[80,640]{1,0:T(8,128)(2,1)S(1)} %collective-permute-done.19.refs_2_), channel_id=1, source_target_pairs={{0,32},{32,0},{64,96},{96,64},{128,160},{160,128},{192,224},{224,1... | collective-permute-start | bytes 307208 | tf_op jit(solution)/shard_map/other_1/ppermute | solution.py:44
  141.4 2.0 %collective-permute-done.32.refs_9_.got_m = bf16[160,2560]{1,0:T(8,128)(2,1)S(1)} collective-permute-done((bf16[160,2560]{1,0:T(8,128)(2,1)S(1)}, bf16[160,2560]{1,0:T(8,128)(2,1)S(1)}, u32[]{:S(2)}, u32[]{:S(2)}) %collective-permute-start.32) | collective-permute-done | bytes 819232 | tf_op jit(solution)/shard_map/out/ppermute | solution.py:35
  143.5 1.5 density_second.1
  145.8 2.0 %collective-permute-start.35 = (bf16[80,2560]{1,0:T(8,128)(2,1)S(1)}, bf16[80,2560]{1,0:T(8,128)(2,1)S(1)}, u32[]{:S(2)}, u32[]{:S(2)}) collective-permute-start(bf16[80,2560]{1,0:T(8,128)(2,1)S(1)} %get-tuple-element.72), channel_id=1, source_target_pairs={{0,6},{1,7},{2,0},{3,1},{4,2},{5,3},{6,4},{7,5},{8,14},{9,15},{10,... | collective-permute-start | bytes 1228808 | tf_op jit(solution)/shard_map/out/ppermute | solution.py:35
  147.8 1.4 density_own.1.own
  149.2 6.9 %collective-permute-done.34.one = bf16[80,2560]{1,0:T(8,128)(2,1)S(1)} collective-permute-done((bf16[80,2560]{1,0:T(8,128)(2,1)S(1)}, bf16[80,2560]{1,0:T(8,128)(2,1)S(1)}, u32[]{:S(2)}, u32[]{:S(2)}) %collective-permute-start.34) | collective-permute-done | bytes 409632 | tf_op jit(solution)/shard_map/out/ppermute | solution.py:35
  156.1 1.0 add.1
  (45 shorter events, 5.5 us)
Async XLA Ops:
  1.1 16.2 %collective-permute-start = (bf16[320,512]{1,0:T(8,128)(2,1)S(1)}, bf16[320,512]{1,0:T(8,128)(2,1)S(1)}, u32[]{:S(2)}, u32[]{:S(2)}) collective-permute-start(bf16[320,512]{1,0:T(8,128)(2,1)S(1)} %get-tuple-element.39), channel_id=1, source_target_pairs={{0,32},{32,64},{64,96},{96,128},{128,160},{160,192},{192,224},{1,3... | collective-permute-start | bytes 983048 | tf_op jit(solution)/shard_map/ppermute | solution.py:550
  7.4 12.8 %collective-permute-start.1 = (bf16[320,512]{1,0:T(8,128)(2,1)S(1)}, bf16[320,512]{1,0:T(8,128)(2,1)S(1)}, u32[]{:S(2)}, u32[]{:S(2)}) collective-permute-start(bf16[320,512]{1,0:T(8,128)(2,1)S(1)} %get-tuple-element.40), channel_id=1, source_target_pairs={{32,0},{64,32},{96,64},{128,96},{160,128},{192,160},{224,192},{33,... | collective-permute-start | bytes 983048 | tf_op jit(solution)/shard_map/ppermute | solution.py:551
  20.2 6.8 %copy-start.2 = (f32[5120]{0:T(1024)S(1)}, f32[5120]{0:T(1024)}, u32[]{:S(2)}) copy-start(f32[5120]{0:T(1024)} %param.9) | copy-start | bytes 61444
  21.2 15.6 %collective-permute-start.6 = (bf16[160,2560]{1,0:T(8,128)(2,1)S(1)}, bf16[160,2560]{1,0:T(8,128)(2,1)}, u32[]{:S(2)}, u32[]{:S(2)}) collective-permute-start(bf16[160,2560]{1,0:T(8,128)(2,1)S(1)} %get-tuple-element.46.refs_0_), channel_id=1, source_target_pairs={{0,24},{1,25},{2,26},{3,27},{4,28},{5,29},{6,30},{7,31},{8,0},{9,1... | collective-permute-start | bytes 2457608 | tf_op jit(solution)/shard_map/first/ppermute | solution.py:30
  24.5 14.1 %collective-permute-start.5 = (bf16[160,2560]{1,0:T(8,128)(2,1)S(1)}, bf16[160,2560]{1,0:T(8,128)(2,1)}, u32[]{:S(2)}, u32[]{:S(2)}) collective-permute-start(bf16[160,2560]{1,0:T(8,128)(2,1)S(1)} %get-tuple-element.46.refs_0_), channel_id=1, source_target_pairs={{0,1},{1,0},{2,3},{3,2},{4,5},{5,4},{6,7},{7,6},{8,9},{9,8},{10,11... | collective-permute-start | bytes 2457608 | tf_op jit(solution)/shard_map/first/ppermute | solution.py:40
  24.5 16.9 %collective-permute-start.4 = (bf16[160,2560]{1,0:T(8,128)(2,1)S(1)}, bf16[160,2560]{1,0:T(8,128)(2,1)S(1)}, u32[]{:S(2)}, u32[]{:S(2)}) collective-permute-start(bf16[160,2560]{1,0:T(8,128)(2,1)S(1)} %get-tuple-element.46.refs_0_), channel_id=1, source_target_pairs={{0,8},{1,9},{2,10},{3,11},{4,12},{5,13},{6,14},{7,15},{8,16},{9,17... | collective-permute-start | bytes 2457608 | tf_op jit(solution)/shard_map/first/ppermute | solution.py:30
  24.5 20.5 %collective-permute-start.2 = (bf16[160,2560]{1,0:T(8,128)(2,1)S(1)}, bf16[160,2560]{1,0:T(8,128)(2,1)}, u32[]{:S(2)}, u32[]{:S(2)}) collective-permute-start(bf16[160,2560]{1,0:T(8,128)(2,1)S(1)} %get-tuple-element.45.own), channel_id=1, source_target_pairs={{0,6},{1,7},{2,0},{3,1},{4,2},{5,3},{6,4},{7,5},{8,14},{9,15},{10,... | collective-permute-start | bytes 2457608 | tf_op jit(solution)/shard_map/first/ppermute | solution.py:35
  27.0 20.4 %collective-permute-start.3 = (bf16[160,2560]{1,0:T(8,128)(2,1)S(1)}, bf16[160,2560]{1,0:T(8,128)(2,1)S(1)}, u32[]{:S(2)}, u32[]{:S(2)}) collective-permute-start(bf16[160,2560]{1,0:T(8,128)(2,1)S(1)} %get-tuple-element.45.own), channel_id=1, source_target_pairs={{0,2},{1,3},{2,4},{3,5},{4,6},{5,7},{6,0},{7,1},{8,10},{9,11},{10,... | collective-permute-start | bytes 2457608 | tf_op jit(solution)/shard_map/first/ppermute | solution.py:35
  41.4 18.2 %collective-permute-start.8 = (bf16[160,2560]{1,0:T(8,128)(2,1)}, bf16[160,2560]{1,0:T(8,128)(2,1)S(1)}, u32[]{:S(2)}, u32[]{:S(2)}) collective-permute-start(bf16[160,2560]{1,0:T(8,128)(2,1)} %get-tuple-element.48.refs_3_), channel_id=1, source_target_pairs={{0,8},{1,9},{2,10},{3,11},{4,12},{5,13},{6,14},{7,15},{8,16},{9,17... | collective-permute-start | bytes 2457608 | tf_op jit(solution)/shard_map/second/ppermute | solution.py:30
  41.4 18.2 %collective-permute-start.10 = (bf16[160,2560]{1,0:T(8,128)(2,1)}, bf16[160,2560]{1,0:T(8,128)(2,1)S(1)}, u32[]{:S(2)}, u32[]{:S(2)}) collective-permute-start(bf16[160,2560]{1,0:T(8,128)(2,1)} %get-tuple-element.47.refs_2_), channel_id=1, source_target_pairs={{0,1},{1,0},{2,3},{3,2},{4,5},{5,4},{6,7},{7,6},{8,9},{9,8},{10,11... | collective-permute-start | bytes 2457608 | tf_op jit(solution)/shard_map/second/ppermute | solution.py:40
  42.3 17.3 %collective-permute-start.9 = (bf16[160,2560]{1,0:T(8,128)(2,1)}, bf16[160,2560]{1,0:T(8,128)(2,1)S(1)}, u32[]{:S(2)}, u32[]{:S(2)}) collective-permute-start(bf16[160,2560]{1,0:T(8,128)(2,1)} %get-tuple-element.47.refs_2_), channel_id=1, source_target_pairs={{0,24},{1,25},{2,26},{3,27},{4,28},{5,29},{6,30},{7,31},{8,0},{9,1... | collective-permute-start | bytes 2457608 | tf_op jit(solution)/shard_map/second/ppermute | solution.py:30
  45.0 19.5 %collective-permute-start.7 = (bf16[160,2560]{1,0:T(8,128)(2,1)}, bf16[160,2560]{1,0:T(8,128)(2,1)S(1)}, u32[]{:S(2)}, u32[]{:S(2)}) collective-permute-start(bf16[160,2560]{1,0:T(8,128)(2,1)} %collective-permute-done.2.ax), channel_id=1, source_target_pairs={{0,6},{1,7},{2,0},{3,1},{4,2},{5,3},{6,4},{7,5},{8,14},{9,15},{10,... | collective-permute-start | bytes 2457608 | tf_op jit(solution)/shard_map/second/ppermute | solution.py:35
  59.7 9.5 %collective-permute-start.11 = (bf16[64,2560]{1,0:T(8,128)(2,1)S(1)}, bf16[64,2560]{1,0:T(8,128)(2,1)S(1)}, u32[]{:S(2)}, u32[]{:S(2)}) collective-permute-start(bf16[64,2560]{1,0:T(8,128)(2,1)S(1)} %get-tuple-element.56), channel_id=1, source_target_pairs={{0,1},{1,0},{2,3},{3,2},{4,5},{5,4},{6,7},{7,6},{8,9},{9,8},{10,11... | collective-permute-start | bytes 983048 | tf_op jit(solution)/shard_map/third/ppermute | solution.py:40
  61.4 7.7 %collective-permute-start.12 = (bf16[48,2560]{1,0:T(8,128)(2,1)S(1)}, bf16[48,2560]{1,0:T(8,128)(2,1)S(1)}, u32[]{:S(2)}, u32[]{:S(2)}) collective-permute-start(bf16[48,2560]{1,0:T(8,128)(2,1)S(1)} %get-tuple-element.57), channel_id=1, source_target_pairs={{0,8},{1,9},{2,10},{3,11},{4,12},{5,13},{6,14},{7,15},{8,16},{9,17... | collective-permute-start | bytes 737288 | tf_op jit(solution)/shard_map/third/ppermute | solution.py:30
  61.4 7.7 %collective-permute-start.13 = (bf16[48,2560]{1,0:T(8,128)(2,1)S(1)}, bf16[48,2560]{1,0:T(8,128)(2,1)S(1)}, u32[]{:S(2)}, u32[]{:S(2)}) collective-permute-start(bf16[48,2560]{1,0:T(8,128)(2,1)S(1)} %get-tuple-element.58), channel_id=1, source_target_pairs={{0,24},{1,25},{2,26},{3,27},{4,28},{5,29},{6,30},{7,31},{8,0},{9,1... | collective-permute-start | bytes 737288 | tf_op jit(solution)/shard_map/third/ppermute | solution.py:30
  69.1 31.2 %copy-start = (f32[1000]{0:T(1024)S(1)}, f32[1000]{0:T(1024)}, u32[]{:S(2)}) copy-start(f32[1000]{0:T(1024)} %occ.1) | copy-start | bytes 12004
  69.1 31.2 %copy-start.1 = (s32[2]{0:T(128)S(1)}, s32[2]{0:T(128)}, u32[]{:S(2)}) copy-start(s32[2]{0:T(128)} %chosen.1) | copy-start | bytes 28
  70.4 2.4 %collective-permute-start.14 = (bf16[640,640]{1,0:T(8,128)(2,1)S(1)}, bf16[640,640]{1,0:T(8,128)(2,1)S(1)}, u32[]{:S(2)}, u32[]{:S(2)}) collective-permute-start(bf16[640,640]{1,0:T(8,128)(2,1)S(1)} %get-tuple-element.60), channel_id=1, source_target_pairs={{0,32},{32,0},{64,96},{96,64},{128,160},{160,128},{192,224},{224,1... | collective-permute-start | bytes 2457608 | tf_op jit(solution)/shard_map/core/ppermute | solution.py:44
  73.0 21.6 %collective-permute-start.15 = (bf16[160,640]{1,0:T(8,128)(2,1)S(1)}, bf16[160,640]{1,0:T(8,128)(2,1)S(1)}, u32[]{:S(2)}, u32[]{:S(2)}) collective-permute-start(bf16[160,640]{1,0:T(8,128)(2,1)S(1)} %get-tuple-element.62), channel_id=1, source_target_pairs={{0,128},{32,160},{64,192},{96,224},{128,0},{160,32},{192,64},{224,... | collective-permute-start | bytes 614408 | tf_op jit(solution)/shard_map/shares/ppermute | solution.py:48
  84.9 14.3 %collective-permute-start.16 = (bf16[160,640]{1,0:T(8,128)(2,1)S(1)}, bf16[160,640]{1,0:T(8,128)(2,1)S(1)}, u32[]{:S(2)}, u32[]{:S(2)}) collective-permute-start(bf16[160,640]{1,0:T(8,128)(2,1)S(1)} %get-tuple-element.63), channel_id=1, source_target_pairs={{0,64},{32,96},{64,128},{96,160},{128,192},{160,224},{192,0},{224,... | collective-permute-start | bytes 614408 | tf_op jit(solution)/shard_map/shares/ppermute | solution.py:48
  84.9 15.5 %collective-permute-start.17 = (bf16[160,640]{1,0:T(8,128)(2,1)S(1)}, bf16[160,640]{1,0:T(8,128)(2,1)S(1)}, u32[]{:S(2)}, u32[]{:S(2)}) collective-permute-start(bf16[160,640]{1,0:T(8,128)(2,1)S(1)} %get-tuple-element.64), channel_id=1, source_target_pairs={{0,192},{32,224},{64,0},{96,32},{128,64},{160,96},{192,128},{224,1... | collective-permute-start | bytes 614408 | tf_op jit(solution)/shard_map/shares/ppermute | solution.py:48
  101.2 9.8 %collective-permute-start.27 = (bf16[80,640]{1,0:T(8,128)(2,1)S(1)}, bf16[80,640]{1,0:T(8,128)(2,1)S(1)}, u32[]{:S(2)}, u32[]{:S(2)}) collective-permute-start(bf16[80,640]{1,0:T(8,128)(2,1)S(1)} %get-tuple-element.67.refs_0_), channel_id=1, source_target_pairs={{0,192},{32,224},{64,0},{96,32},{128,64},{160,96},{192,128},{224,1... | collective-permute-start | bytes 307208 | tf_op jit(solution)/shard_map/spread_0/ppermute | solution.py:48
  105.6 10.7 %collective-permute-start.26 = (bf16[80,640]{1,0:T(8,128)(2,1)S(1)}, bf16[80,640]{1,0:T(8,128)(2,1)S(1)}, u32[]{:S(2)}, u32[]{:S(2)}) collective-permute-start(bf16[80,640]{1,0:T(8,128)(2,1)S(1)} %get-tuple-element.67.refs_0_), channel_id=1, source_target_pairs={{0,128},{32,160},{64,192},{96,224},{128,0},{160,32},{192,64},{224,... | collective-permute-start | bytes 307208 | tf_op jit(solution)/shard_map/spread_0/ppermute | solution.py:48
  109.9 8.6 %collective-permute-start.25 = (bf16[80,640]{1,0:T(8,128)(2,1)S(1)}, bf16[80,640]{1,0:T(8,128)(2,1)S(1)}, u32[]{:S(2)}, u32[]{:S(2)}) collective-permute-start(bf16[80,640]{1,0:T(8,128)(2,1)S(1)} %get-tuple-element.67.refs_0_), channel_id=1, source_target_pairs={{0,64},{32,96},{64,128},{96,160},{128,192},{160,224},{192,0},{224,... | collective-permute-start | bytes 307208 | tf_op jit(solution)/shard_map/spread_0/ppermute | solution.py:48
  109.9 9.4 %collective-permute-start.28 = (bf16[80,640]{1,0:T(8,128)(2,1)S(1)}, bf16[80,640]{1,0:T(8,128)(2,1)S(1)}, u32[]{:S(2)}, u32[]{:S(2)}) collective-permute-start(bf16[80,640]{1,0:T(8,128)(2,1)S(1)} %get-tuple-element.67.refs_0_), channel_id=1, source_target_pairs={{0,32},{32,0},{64,96},{96,64},{128,160},{160,128},{192,224},{224,1... | collective-permute-start | bytes 307208 | tf_op jit(solution)/shard_map/other_0/ppermute | solution.py:44
  111.0 8.2 %collective-permute-start.31 = (bf16[80,640]{1,0:T(8,128)(2,1)S(1)}, bf16[80,640]{1,0:T(8,128)(2,1)S(1)}, u32[]{:S(2)}, u32[]{:S(2)}) collective-permute-start(bf16[80,640]{1,0:T(8,128)(2,1)S(1)} %collective-permute-done.27.refs_3_), channel_id=1, source_target_pairs={{0,32},{32,0},{64,96},{96,64},{128,160},{160,128},{192,224},{224,1... | collective-permute-start | bytes 307208 | tf_op jit(solution)/shard_map/other_0/ppermute | solution.py:44
  116.3 3.1 %collective-permute-start.30 = (bf16[80,640]{1,0:T(8,128)(2,1)S(1)}, bf16[80,640]{1,0:T(8,128)(2,1)S(1)}, u32[]{:S(2)}, u32[]{:S(2)}) collective-permute-start(bf16[80,640]{1,0:T(8,128)(2,1)S(1)} %collective-permute-done.26.refs_2_), channel_id=1, source_target_pairs={{0,32},{32,0},{64,96},{96,64},{128,160},{160,128},{192,224},{224,1... | collective-permute-start | bytes 307208 | tf_op jit(solution)/shard_map/other_0/ppermute | solution.py:44
  118.4 1.7 %collective-permute-start.29 = (bf16[80,640]{1,0:T(8,128)(2,1)S(1)}, bf16[80,640]{1,0:T(8,128)(2,1)S(1)}, u32[]{:S(2)}, u32[]{:S(2)}) collective-permute-start(bf16[80,640]{1,0:T(8,128)(2,1)S(1)} %collective-permute-done.25.refs_1_), channel_id=1, source_target_pairs={{0,32},{32,0},{64,96},{96,64},{128,160},{160,128},{192,224},{224,1... | collective-permute-start | bytes 307208 | tf_op jit(solution)/shard_map/other_0/ppermute | solution.py:44
  122.7 20.8 %collective-permute-start.32 = (bf16[160,2560]{1,0:T(8,128)(2,1)S(1)}, bf16[160,2560]{1,0:T(8,128)(2,1)S(1)}, u32[]{:S(2)}, u32[]{:S(2)}) collective-permute-start(bf16[160,2560]{1,0:T(8,128)(2,1)S(1)} %get-tuple-element.68), channel_id=1, source_target_pairs={{0,2},{1,3},{2,4},{3,5},{4,6},{5,7},{6,0},{7,1},{8,10},{9,11},{10,... | collective-permute-start | bytes 2457608 | tf_op jit(solution)/shard_map/out/ppermute | solution.py:35
  123.8 19.7 %collective-permute-start.33 = (bf16[160,2560]{1,0:T(8,128)(2,1)S(1)}, bf16[160,2560]{1,0:T(8,128)(2,1)S(1)}, u32[]{:S(2)}, u32[]{:S(2)}) collective-permute-start(bf16[160,2560]{1,0:T(8,128)(2,1)S(1)} %get-tuple-element.69), channel_id=1, source_target_pairs={{0,6},{1,7},{2,0},{3,1},{4,2},{5,3},{6,4},{7,5},{8,14},{9,15},{10,... | collective-permute-start | bytes 2457608 | tf_op jit(solution)/shard_map/out/ppermute | solution.py:35
  125.5 6.1 %collective-permute-start.21 = (bf16[80,640]{1,0:T(8,128)(2,1)S(1)}, bf16[80,640]{1,0:T(8,128)(2,1)S(1)}, u32[]{:S(2)}, u32[]{:S(2)}) collective-permute-start(bf16[80,640]{1,0:T(8,128)(2,1)S(1)} %get-tuple-element.65.refs_0_), channel_id=1, source_target_pairs={{0,32},{32,0},{64,96},{96,64},{128,160},{160,128},{192,224},{224,1... | collective-permute-start | bytes 307208 | tf_op jit(solution)/shard_map/other_1/ppermute | solution.py:44
  126.4 5.4 %collective-permute-start.20 = (bf16[80,640]{1,0:T(8,128)(2,1)S(1)}, bf16[80,640]{1,0:T(8,128)(2,1)S(1)}, u32[]{:S(2)}, u32[]{:S(2)}) collective-permute-start(bf16[80,640]{1,0:T(8,128)(2,1)S(1)} %get-tuple-element.65.refs_0_), channel_id=1, source_target_pairs={{0,192},{32,224},{64,0},{96,32},{128,64},{160,96},{192,128},{224,1... | collective-permute-start | bytes 307208 | tf_op jit(solution)/shard_map/spread_1/ppermute | solution.py:48
  127.8 8.1 %collective-permute-start.19 = (bf16[80,640]{1,0:T(8,128)(2,1)S(1)}, bf16[80,640]{1,0:T(8,128)(2,1)S(1)}, u32[]{:S(2)}, u32[]{:S(2)}) collective-permute-start(bf16[80,640]{1,0:T(8,128)(2,1)S(1)} %get-tuple-element.65.refs_0_), channel_id=1, source_target_pairs={{0,128},{32,160},{64,192},{96,224},{128,0},{160,32},{192,64},{224,... | collective-permute-start | bytes 307208 | tf_op jit(solution)/shard_map/spread_1/ppermute | solution.py:48
  131.5 8.6 %collective-permute-start.18 = (bf16[80,640]{1,0:T(8,128)(2,1)S(1)}, bf16[80,640]{1,0:T(8,128)(2,1)S(1)}, u32[]{:S(2)}, u32[]{:S(2)}) collective-permute-start(bf16[80,640]{1,0:T(8,128)(2,1)S(1)} %get-tuple-element.65.refs_0_), channel_id=1, source_target_pairs={{0,64},{32,96},{64,128},{96,160},{128,192},{160,224},{192,0},{224,... | collective-permute-start | bytes 307208 | tf_op jit(solution)/shard_map/spread_1/ppermute | solution.py:48
  131.8 8.7 %collective-permute-start.24 = (bf16[80,640]{1,0:T(8,128)(2,1)S(1)}, bf16[80,640]{1,0:T(8,128)(2,1)S(1)}, u32[]{:S(2)}, u32[]{:S(2)}) collective-permute-start(bf16[80,640]{1,0:T(8,128)(2,1)S(1)} %collective-permute-done.20.refs_3_), channel_id=1, source_target_pairs={{0,32},{32,0},{64,96},{96,64},{128,160},{160,128},{192,224},{224,1... | collective-permute-start | bytes 307208 | tf_op jit(solution)/shard_map/other_1/ppermute | solution.py:44
  135.9 5.1 %collective-permute-start.23 = (bf16[80,640]{1,0:T(8,128)(2,1)S(1)}, bf16[80,640]{1,0:T(8,128)(2,1)S(1)}, u32[]{:S(2)}, u32[]{:S(2)}) collective-permute-start(bf16[80,640]{1,0:T(8,128)(2,1)S(1)} %collective-permute-done.19.refs_2_), channel_id=1, source_target_pairs={{0,32},{32,0},{64,96},{96,64},{128,160},{160,128},{192,224},{224,1... | collective-permute-start | bytes 307208 | tf_op jit(solution)/shard_map/other_1/ppermute | solution.py:44
  140.1 1.3 collective-permute-start.22
  145.0 11.1 %collective-permute-start.34 = (bf16[80,2560]{1,0:T(8,128)(2,1)S(1)}, bf16[80,2560]{1,0:T(8,128)(2,1)S(1)}, u32[]{:S(2)}, u32[]{:S(2)}) collective-permute-start(bf16[80,2560]{1,0:T(8,128)(2,1)S(1)} %get-tuple-element.71), channel_id=1, source_target_pairs={{0,2},{1,3},{2,4},{3,5},{4,6},{5,7},{6,0},{7,1},{8,10},{9,11},{10,... | collective-permute-start | bytes 1228808 | tf_op jit(solution)/shard_map/out/ppermute | solution.py:35
  145.8 10.3 %collective-permute-start.35 = (bf16[80,2560]{1,0:T(8,128)(2,1)S(1)}, bf16[80,2560]{1,0:T(8,128)(2,1)S(1)}, u32[]{:S(2)}, u32[]{:S(2)}) collective-permute-start(bf16[80,2560]{1,0:T(8,128)(2,1)S(1)} %get-tuple-element.72), channel_id=1, source_target_pairs={{0,6},{1,7},{2,0},{3,1},{4,2},{5,3},{6,4},{7,5},{8,14},{9,15},{10,... | collective-permute-start | bytes 1228808 | tf_op jit(solution)/shard_map/out/ppermute | solution.py:35

commit v6 on v5

--- a/solution.py
+++ b/solution.py
@@ -564,7 +564,9 @@
         bop = send_z(bp)
         ad = send_x(ax, -1)
     early_sums, bcat, acat = pair_first((a, ax, am), (b, bm, bp, bo))
-    c1, c2, c3 = cut([(b2, 0, 64), (bom, 64, 48), (bop, 112, 48)], (early_sums,), name="cut_b")
+    (c1,) = cut([(b2, 0, 64)], (early_sums,), name="cut_b1")
+    (c2,) = cut([(bom, 64, 48)], (early_sums,), name="cut_b2")
+    (c3,) = cut([(bop, 112, 48)], (early_sums,), name="cut_b3")
     with jax.named_scope("third"):
         c1 = send_z(c1)
         c2 = send_y(c2, 1)

time: 160 us -> 158 us (0.988)
  starting transfers between devices: 71.9 us -> 62.7 us
  waiting for transfers between devices: 57.7 us -> 65.7 us
    ppermute x9, waiting for transfers between devices: 18.9 us -> 22.7 us  [send_high(): return lax.ppermute(v, 'grp', [(g, (g + 2 * step) % 8) for g in range(8)])]
    ppermute x9, starting transfers between devices: 12.2 us -> 8.97 us  [send_core(): return lax.ppermute(v, 'grp', [(g, g ^ 1) for g in range(8)])]
    ppermute x3, starting transfers between devices: 2.67 us -> 0.1 us  [send_z(): return lax.ppermute(v, 'blk', pairs)]
    ppermute x6, starting transfers between devices: 8.94 us -> 6.73 us  [send_y(): return lax.ppermute(v, 'blk', pairs)]
    pallas_call x13 -> x15, Pallas kernels: 27.3 us -> 27.3 us  [call(): pl.pallas_call(kernel, in_specs=[spec for _, spec in args], out_specs=[VM...]
  transfers between devices with their start and end apart: 36 -> 36, of which waited for: 20 -> 23; matrix products, arithmetic and copies ran while one was open for 0% -> 0% of each run, Pallas kernels for 11% -> 11%
where the time goes in v6:
time: 158 us; the launch traced here: 156 us
  waiting for transfers between devices  65.7 us (42%)
  starting transfers between devices  62.7 us (40%)
  Pallas kernels  27.3 us (17%)
    ppermute x9, starting transfers between devices, send_high(): return lax.ppermute(v, 'grp', [(g, (g + 2 * step) % 8) for g in range(8)])  27.7 us
    pallas_call x15, Pallas kernels, call(): pl.pallas_call(kernel, in_specs=[spec for _, spec in args], out_specs=[VM...  27.3 us
    ppermute x9, waiting for transfers between devices, send_high(): return lax.ppermute(v, 'grp', [(g, (g + 2 * step) % 8) for g in range(8)])  22.7 us
    ppermute x6, waiting for transfers between devices, send_y(): return lax.ppermute(v, 'blk', pairs)  22.5 us
    ppermute x7, starting transfers between devices, send_x(): return lax.ppermute(v, 'blk', pairs)  10.9 us
    ppermute x7, waiting for transfers between devices, send_x(): return lax.ppermute(v, 'blk', pairs)  9.77 us
    ppermute x9, starting transfers between devices, send_core(): return lax.ppermute(v, 'grp', [(g, g ^ 1) for g in range(8)])  8.97 us
    ppermute x6, starting transfers between devices, send_y(): return lax.ppermute(v, 'blk', pairs)  6.73 us
  transfers between devices with their start and end apart: 36, of which 23 were waited for; matrix products, arithmetic and copies ran while one was open for 0% of the time, Pallas kernels for 11%

profile of v6, /device:TPU:1, one launch (start us, length us, event | category | flops | bytes accessed | tf_op | source)
XLA Modules:
  0.0 156.0 jit_solution(15765803279969560039)
XLA Ops:
  0.0 1.1 ends.1
  1.1 6.3 %collective-permute-start = (bf16[320,512]{1,0:T(8,128)(2,1)S(1)}, bf16[320,512]{1,0:T(8,128)(2,1)S(1)}, u32[]{:S(2)}, u32[]{:S(2)}) collective-permute-start(bf16[320,512]{1,0:T(8,128)(2,1)S(1)} %get-tuple-element.36), channel_id=1, source_target_pairs={{0,32},{32,64},{64,96},{96,128},{128,160},{160,192},{192,224},{1,3... | collective-permute-start | bytes 983048 | tf_op jit(solution)/shard_map/ppermute | solution.py:550
  7.4 1.9 %collective-permute-start.1 = (bf16[320,512]{1,0:T(8,128)(2,1)S(1)}, bf16[320,512]{1,0:T(8,128)(2,1)S(1)}, u32[]{:S(2)}, u32[]{:S(2)}) collective-permute-start(bf16[320,512]{1,0:T(8,128)(2,1)S(1)} %get-tuple-element.37), channel_id=1, source_target_pairs={{32,0},{64,32},{96,64},{128,96},{160,128},{192,160},{224,192},{33,... | collective-permute-start | bytes 983048 | tf_op jit(solution)/shard_map/ppermute | solution.py:551
  9.3 8.0 %fit_inner.1 = (bf16[160,2560]{1,0:T(8,128)(2,1)S(1)}, bf16[160,2560]{1,0:T(8,128)(2,1)S(1)}, bf16[320,2560]{1,0:T(8,128)(2,1)S(1)}, bf16[4,1280,256]{2,1,0:T(8,128)(2,1)S(1)}) custom-call(s32[2,180]{1,0:T(2,128)} %bitcast.4, bf16[320,2560]{1,0:T(8,128)(2,1)} %bitcast.3, bf16[180,128,128]{2,1,0:T(8,128)(2,1)} %tiles_in.1), custom_call_target="tpu_custom_call" | custom-call | flops 1000 | bytes 1000 | tf_op jit(solution)/shard_map/fit_inner/pallas_call | solution.py:85
  17.3 2.9 %collective-permute-done.1.right = bf16[320,512]{1,0:T(8,128)(2,1)S(1)} collective-permute-done((bf16[320,512]{1,0:T(8,128)(2,1)S(1)}, bf16[320,512]{1,0:T(8,128)(2,1)S(1)}, u32[]{:S(2)}, u32[]{:S(2)}) %collective-permute-start.1) | collective-permute-done | bytes 327712 | tf_op jit(solution)/shard_map/ppermute | solution.py:551
  20.2 1.0 fit_edge.1
  21.2 3.2 %collective-permute-start.6 = (bf16[160,2560]{1,0:T(8,128)(2,1)S(1)}, bf16[160,2560]{1,0:T(8,128)(2,1)}, u32[]{:S(2)}, u32[]{:S(2)}) collective-permute-start(bf16[160,2560]{1,0:T(8,128)(2,1)S(1)} %get-tuple-element.43.refs_0_), channel_id=1, source_target_pairs={{0,24},{1,25},{2,26},{3,27},{4,28},{5,29},{6,30},{7,31},{8,0},{9,1... | collective-permute-start | bytes 2457608 | tf_op jit(solution)/shard_map/first/ppermute | solution.py:30
  24.5 2.5 %collective-permute-start.2 = (bf16[160,2560]{1,0:T(8,128)(2,1)S(1)}, bf16[160,2560]{1,0:T(8,128)(2,1)}, u32[]{:S(2)}, u32[]{:S(2)}) collective-permute-start(bf16[160,2560]{1,0:T(8,128)(2,1)S(1)} %get-tuple-element.42.own), channel_id=1, source_target_pairs={{0,6},{1,7},{2,0},{3,1},{4,2},{5,3},{6,4},{7,5},{8,14},{9,15},{10,... | collective-permute-start | bytes 2457608 | tf_op jit(solution)/shard_map/first/ppermute | solution.py:35
  27.1 9.7 %collective-permute-done.6.refs_1_ = bf16[160,2560]{1,0:T(8,128)(2,1)} collective-permute-done((bf16[160,2560]{1,0:T(8,128)(2,1)S(1)}, bf16[160,2560]{1,0:T(8,128)(2,1)}, u32[]{:S(2)}, u32[]{:S(2)}) %collective-permute-start.6) | collective-permute-done | bytes 819232 | tf_op jit(solution)/shard_map/first/ppermute | solution.py:30
  36.8 1.7 %collective-permute-done.5.refs_0_ = bf16[160,2560]{1,0:T(8,128)(2,1)} collective-permute-done((bf16[160,2560]{1,0:T(8,128)(2,1)S(1)}, bf16[160,2560]{1,0:T(8,128)(2,1)}, u32[]{:S(2)}, u32[]{:S(2)}) %collective-permute-start.5) | collective-permute-done | bytes 819232 | tf_op jit(solution)/shard_map/first/ppermute | solution.py:40
  38.6 2.8 %collective-permute-done.4.refs_2_.refs_1_ = bf16[160,2560]{1,0:T(8,128)(2,1)S(1)} collective-permute-done((bf16[160,2560]{1,0:T(8,128)(2,1)S(1)}, bf16[160,2560]{1,0:T(8,128)(2,1)S(1)}, u32[]{:S(2)}, u32[]{:S(2)}) %collective-permute-start.4) | collective-permute-done | bytes 819232 | tf_op jit(solution)/shard_map/first/ppermute | solution.py:30
  41.4 1.5 collective-permute-start.8
  42.9 2.5 %collective-permute-start.7 = (bf16[160,2560]{1,0:T(8,128)(2,1)}, bf16[160,2560]{1,0:T(8,128)(2,1)S(1)}, u32[]{:S(2)}, u32[]{:S(2)}) collective-permute-start(bf16[160,2560]{1,0:T(8,128)(2,1)} %collective-permute-done.2.ax), channel_id=1, source_target_pairs={{0,6},{1,7},{2,0},{3,1},{4,2},{5,3},{6,4},{7,5},{8,14},{9,15},{10,... | collective-permute-start | bytes 2457608 | tf_op jit(solution)/shard_map/second/ppermute | solution.py:35
  45.3 4.8 %pair_first.1 = (f32[640,640]{1,0:T(8,128)S(1)}, bf16[1280,2560]{1,0:T(8,128)(2,1)S(1)}, bf16[640,2560]{1,0:T(8,128)(2,1)S(1)}) custom-call(bf16[160,2560]{1,0:T(8,128)(2,1)S(1)} %get-tuple-element.42.own, bf16[160,2560]{1,0:T(8,128)(2,1)} %collective-permute-done.2.ax, bf16[160,2560]{1,0:T(8,128)(2,1)S(1)} %collective-permute-done.3.am, ...), custom_call_target="tpu_custom_call" | custom-call | flops 1000 | bytes 1000 | tf_op jit(solution)/shard_map/pair_first/pallas_call | solution.py:85
  50.2 8.2 %collective-permute-done.9.refs_1_.refs_0_ = bf16[160,2560]{1,0:T(8,128)(2,1)S(1)} collective-permute-done((bf16[160,2560]{1,0:T(8,128)(2,1)}, bf16[160,2560]{1,0:T(8,128)(2,1)S(1)}, u32[]{:S(2)}, u32[]{:S(2)}) %collective-permute-start.9) | collective-permute-done | bytes 819232 | tf_op jit(solution)/shard_map/second/ppermute | solution.py:30
  58.5 1.1 collective-permute-done.8.refs_0_
  59.6 1.1 collective-permute-start.12
  60.7 1.5 collective-permute-done.10.refs_2_.refs_0_
  62.3 0.9 collective-permute-start.13
  63.2 3.6 %pair_early.1 = (f32[640,640]{1,0:T(8,128)S(1)}, bf16[1280,2560]{1,0:T(8,128)(2,1)S(1)}, bf16[640,2560]{1,0:T(8,128)(2,1)S(1)}, f32[640,640]{1,0:T(8,128)S(1)}, bf16[640,640]{1,0:T(8,128)(2,1)S(1)}) custom-call(f32[640,640]{1,0:T(8,128)S(1)} %get-tuple-element.46.first_in.refs_1_, ...), custom_call_target="tpu_custom_call", output_to_operand_aliasing={{0}: (0, {}), {1}: (1, {}), {2}: (2, {})} | custom-call | flops 1000 | bytes 1000 | tf_op jit(solution)/shard_map/pair_early/pallas_call | solution.py:85
  67.4 1.2 pair_late.1
  68.8 2.3 %collective-permute-done.14.got = bf16[640,640]{1,0:T(8,128)(2,1)S(1)} collective-permute-done((bf16[640,640]{1,0:T(8,128)(2,1)S(1)}, bf16[640,640]{1,0:T(8,128)(2,1)S(1)}, u32[]{:S(2)}, u32[]{:S(2)}) %collective-permute-start.14) | collective-permute-done | bytes 819232 | tf_op jit(solution)/shard_map/core/ppermute | solution.py:44
  71.3 12.9 %collective-permute-start.15 = (bf16[160,640]{1,0:T(8,128)(2,1)S(1)}, bf16[160,640]{1,0:T(8,128)(2,1)S(1)}, u32[]{:S(2)}, u32[]{:S(2)}) collective-permute-start(bf16[160,640]{1,0:T(8,128)(2,1)S(1)} %get-tuple-element.56), channel_id=1, source_target_pairs={{0,128},{32,160},{64,192},{96,224},{128,0},{160,32},{192,64},{224,... | collective-permute-start | bytes 614408 | tf_op jit(solution)/shard_map/shares/ppermute | solution.py:48
  84.2 3.6 %collective-permute-start.17 = (bf16[160,640]{1,0:T(8,128)(2,1)S(1)}, bf16[160,640]{1,0:T(8,128)(2,1)S(1)}, u32[]{:S(2)}, u32[]{:S(2)}) collective-permute-start(bf16[160,640]{1,0:T(8,128)(2,1)S(1)} %get-tuple-element.58), channel_id=1, source_target_pairs={{0,192},{32,224},{64,0},{96,32},{128,64},{160,96},{192,128},{224,1... | collective-permute-start | bytes 614408 | tf_op jit(solution)/shard_map/shares/ppermute | solution.py:48
  87.8 5.6 %collective-permute-done.15.refs_0_ = bf16[160,640]{1,0:T(8,128)(2,1)S(1)} collective-permute-done((bf16[160,640]{1,0:T(8,128)(2,1)S(1)}, bf16[160,640]{1,0:T(8,128)(2,1)S(1)}, u32[]{:S(2)}, u32[]{:S(2)}) %collective-permute-start.15) | collective-permute-done | bytes 204832 | tf_op jit(solution)/shard_map/shares/ppermute | solution.py:48
  93.4 4.7 %collective-permute-done.16.refs_1_ = bf16[160,640]{1,0:T(8,128)(2,1)S(1)} collective-permute-done((bf16[160,640]{1,0:T(8,128)(2,1)S(1)}, bf16[160,640]{1,0:T(8,128)(2,1)S(1)}, u32[]{:S(2)}, u32[]{:S(2)}) %collective-permute-start.16) | collective-permute-done | bytes 204832 | tf_op jit(solution)/shard_map/shares/ppermute | solution.py:48
  98.1 2.3 %collective-permute-done.17.refs_2_ = bf16[160,640]{1,0:T(8,128)(2,1)S(1)} collective-permute-done((bf16[160,640]{1,0:T(8,128)(2,1)S(1)}, bf16[160,640]{1,0:T(8,128)(2,1)S(1)}, u32[]{:S(2)}, u32[]{:S(2)}) %collective-permute-start.17) | collective-permute-done | bytes 204832 | tf_op jit(solution)/shard_map/shares/ppermute | solution.py:48
  101.3 2.8 %collective-permute-start.27 = (bf16[80,640]{1,0:T(8,128)(2,1)S(1)}, bf16[80,640]{1,0:T(8,128)(2,1)S(1)}, u32[]{:S(2)}, u32[]{:S(2)}) collective-permute-start(bf16[80,640]{1,0:T(8,128)(2,1)S(1)} %get-tuple-element.61.refs_0_), channel_id=1, source_target_pairs={{0,192},{32,224},{64,0},{96,32},{128,64},{160,96},{192,128},{224,1... | collective-permute-start | bytes 307208 | tf_op jit(solution)/shard_map/spread_0/ppermute | solution.py:48
  104.1 3.6 %collective-permute-start.26 = (bf16[80,640]{1,0:T(8,128)(2,1)S(1)}, bf16[80,640]{1,0:T(8,128)(2,1)S(1)}, u32[]{:S(2)}, u32[]{:S(2)}) collective-permute-start(bf16[80,640]{1,0:T(8,128)(2,1)S(1)} %get-tuple-element.61.refs_0_), channel_id=1, source_target_pairs={{0,128},{32,160},{64,192},{96,224},{128,0},{160,32},{192,64},{224,... | collective-permute-start | bytes 307208 | tf_op jit(solution)/shard_map/spread_0/ppermute | solution.py:48
  107.7 1.1 collective-permute-start.28
  108.8 0.9 collective-permute-done.27.refs_3_
  109.7 1.2 collective-permute-start.31
  110.9 3.2 %collective-permute-done.26.refs_2_ = bf16[80,640]{1,0:T(8,128)(2,1)S(1)} collective-permute-done((bf16[80,640]{1,0:T(8,128)(2,1)S(1)}, bf16[80,640]{1,0:T(8,128)(2,1)S(1)}, u32[]{:S(2)}, u32[]{:S(2)}) %collective-permute-start.26) | collective-permute-done | bytes 102432 | tf_op jit(solution)/shard_map/spread_0/ppermute | solution.py:48
  114.1 2.7 %collective-permute-start.30 = (bf16[80,640]{1,0:T(8,128)(2,1)S(1)}, bf16[80,640]{1,0:T(8,128)(2,1)S(1)}, u32[]{:S(2)}, u32[]{:S(2)}) collective-permute-start(bf16[80,640]{1,0:T(8,128)(2,1)S(1)} %collective-permute-done.26.refs_2_), channel_id=1, source_target_pairs={{0,32},{32,0},{64,96},{96,64},{128,160},{160,128},{192,224},{224,1... | collective-permute-start | bytes 307208 | tf_op jit(solution)/shard_map/other_0/ppermute | solution.py:44
  116.8 0.9 collective-permute-done.30.refs_6_
  118.1 2.5 %density_first.1 = (bf16[160,2560]{1,0:T(8,128)(2,1)S(1)}, bf16[160,2560]{1,0:T(8,128)(2,1)S(1)}) custom-call(bf16[80,640]{1,0:T(8,128)(2,1)S(1)} %get-tuple-element.61.refs_0_, bf16[80,640]{1,0:T(8,128)(2,1)S(1)} %collective-permute-done.25.refs_1_, bf16[80,640]{1,0:T(8,128)(2,1)S(1)} %collective-permute-done.26.refs_2_, ...), custom_call_target="tpu_custom_call" | custom-call | flops 1000 | bytes 1000 | tf_op jit(solution)/shard_map/density_first/pallas_call | solution.py:85
  120.7 1.5 collective-permute-start.32
  122.2 1.6 %collective-permute-start.33 = (bf16[160,2560]{1,0:T(8,128)(2,1)S(1)}, bf16[160,2560]{1,0:T(8,128)(2,1)S(1)}, u32[]{:S(2)}, u32[]{:S(2)}) collective-permute-start(bf16[160,2560]{1,0:T(8,128)(2,1)S(1)} %get-tuple-element.63), channel_id=1, source_target_pairs={{0,6},{1,7},{2,0},{3,1},{4,2},{5,3},{6,4},{7,5},{8,14},{9,15},{10,... | collective-permute-start | bytes 2457608 | tf_op jit(solution)/shard_map/out/ppermute | solution.py:35
  124.5 1.5 collective-permute-start.20
  125.9 3.3 %collective-permute-start.19 = (bf16[80,640]{1,0:T(8,128)(2,1)S(1)}, bf16[80,640]{1,0:T(8,128)(2,1)S(1)}, u32[]{:S(2)}, u32[]{:S(2)}) collective-permute-start(bf16[80,640]{1,0:T(8,128)(2,1)S(1)} %get-tuple-element.59.refs_0_), channel_id=1, source_target_pairs={{0,128},{32,160},{64,192},{96,224},{128,0},{160,32},{192,64},{224,... | collective-permute-start | bytes 307208 | tf_op jit(solution)/shard_map/spread_1/ppermute | solution.py:48
  130.7 5.4 %collective-permute-done.19.refs_2_ = bf16[80,640]{1,0:T(8,128)(2,1)S(1)} collective-permute-done((bf16[80,640]{1,0:T(8,128)(2,1)S(1)}, bf16[80,640]{1,0:T(8,128)(2,1)S(1)}, u32[]{:S(2)}, u32[]{:S(2)}) %collective-permute-start.19) | collective-permute-done | bytes 102432 | tf_op jit(solution)/shard_map/spread_1/ppermute | solution.py:48
  136.1 2.1 %collective-permute-start.23 = (bf16[80,640]{1,0:T(8,128)(2,1)S(1)}, bf16[80,640]{1,0:T(8,128)(2,1)S(1)}, u32[]{:S(2)}, u32[]{:S(2)}) collective-permute-start(bf16[80,640]{1,0:T(8,128)(2,1)S(1)} %collective-permute-done.19.refs_2_), channel_id=1, source_target_pairs={{0,32},{32,0},{64,96},{96,64},{128,160},{160,128},{192,224},{224,1... | collective-permute-start | bytes 307208 | tf_op jit(solution)/shard_map/other_1/ppermute | solution.py:44
  139.5 2.5 %collective-permute-done.32.refs_9_.got_m = bf16[160,2560]{1,0:T(8,128)(2,1)S(1)} collective-permute-done((bf16[160,2560]{1,0:T(8,128)(2,1)S(1)}, bf16[160,2560]{1,0:T(8,128)(2,1)S(1)}, u32[]{:S(2)}, u32[]{:S(2)}) %collective-permute-start.32) | collective-permute-done | bytes 819232 | tf_op jit(solution)/shard_map/out/ppermute | solution.py:35
  142.1 1.5 density_second.1
  144.4 2.0 %collective-permute-start.35 = (bf16[80,2560]{1,0:T(8,128)(2,1)S(1)}, bf16[80,2560]{1,0:T(8,128)(2,1)S(1)}, u32[]{:S(2)}, u32[]{:S(2)}) collective-permute-start(bf16[80,2560]{1,0:T(8,128)(2,1)S(1)} %get-tuple-element.66), channel_id=1, source_target_pairs={{0,6},{1,7},{2,0},{3,1},{4,2},{5,3},{6,4},{7,5},{8,14},{9,15},{10,... | collective-permute-start | bytes 1228808 | tf_op jit(solution)/shard_map/out/ppermute | solution.py:35
  146.4 1.4 density_own.1.own
  147.8 7.2 %collective-permute-done.34.one = bf16[80,2560]{1,0:T(8,128)(2,1)S(1)} collective-permute-done((bf16[80,2560]{1,0:T(8,128)(2,1)S(1)}, bf16[80,2560]{1,0:T(8,128)(2,1)S(1)}, u32[]{:S(2)}, u32[]{:S(2)}) %collective-permute-start.34) | collective-permute-done | bytes 409632 | tf_op jit(solution)/shard_map/out/ppermute | solution.py:35
  155.0 1.0 add.1
  (47 shorter events, 6.6 us)
Async XLA Ops:
  1.1 16.2 %collective-permute-start = (bf16[320,512]{1,0:T(8,128)(2,1)S(1)}, bf16[320,512]{1,0:T(8,128)(2,1)S(1)}, u32[]{:S(2)}, u32[]{:S(2)}) collective-permute-start(bf16[320,512]{1,0:T(8,128)(2,1)S(1)} %get-tuple-element.36), channel_id=1, source_target_pairs={{0,32},{32,64},{64,96},{96,128},{128,160},{160,192},{192,224},{1,3... | collective-permute-start | bytes 983048 | tf_op jit(solution)/shard_map/ppermute | solution.py:550
  7.4 12.8 %collective-permute-start.1 = (bf16[320,512]{1,0:T(8,128)(2,1)S(1)}, bf16[320,512]{1,0:T(8,128)(2,1)S(1)}, u32[]{:S(2)}, u32[]{:S(2)}) collective-permute-start(bf16[320,512]{1,0:T(8,128)(2,1)S(1)} %get-tuple-element.37), channel_id=1, source_target_pairs={{32,0},{64,32},{96,64},{128,96},{160,128},{192,160},{224,192},{33,... | collective-permute-start | bytes 983048 | tf_op jit(solution)/shard_map/ppermute | solution.py:551
  20.2 6.8 %copy-start.2 = (f32[5120]{0:T(1024)S(1)}, f32[5120]{0:T(1024)}, u32[]{:S(2)}) copy-start(f32[5120]{0:T(1024)} %param.9) | copy-start | bytes 61444
  21.2 15.6 %collective-permute-start.6 = (bf16[160,2560]{1,0:T(8,128)(2,1)S(1)}, bf16[160,2560]{1,0:T(8,128)(2,1)}, u32[]{:S(2)}, u32[]{:S(2)}) collective-permute-start(bf16[160,2560]{1,0:T(8,128)(2,1)S(1)} %get-tuple-element.43.refs_0_), channel_id=1, source_target_pairs={{0,24},{1,25},{2,26},{3,27},{4,28},{5,29},{6,30},{7,31},{8,0},{9,1... | collective-permute-start | bytes 2457608 | tf_op jit(solution)/shard_map/first/ppermute | solution.py:30
  24.5 14.1 %collective-permute-start.5 = (bf16[160,2560]{1,0:T(8,128)(2,1)S(1)}, bf16[160,2560]{1,0:T(8,128)(2,1)}, u32[]{:S(2)}, u32[]{:S(2)}) collective-permute-start(bf16[160,2560]{1,0:T(8,128)(2,1)S(1)} %get-tuple-element.43.refs_0_), channel_id=1, source_target_pairs={{0,1},{1,0},{2,3},{3,2},{4,5},{5,4},{6,7},{7,6},{8,9},{9,8},{10,11... | collective-permute-start | bytes 2457608 | tf_op jit(solution)/shard_map/first/ppermute | solution.py:40
  24.5 16.9 %collective-permute-start.4 = (bf16[160,2560]{1,0:T(8,128)(2,1)S(1)}, bf16[160,2560]{1,0:T(8,128)(2,1)S(1)}, u32[]{:S(2)}, u32[]{:S(2)}) collective-permute-start(bf16[160,2560]{1,0:T(8,128)(2,1)S(1)} %get-tuple-element.43.refs_0_), channel_id=1, source_target_pairs={{0,8},{1,9},{2,10},{3,11},{4,12},{5,13},{6,14},{7,15},{8,16},{9,17... | collective-permute-start | bytes 2457608 | tf_op jit(solution)/shard_map/first/ppermute | solution.py:30
  24.5 18.4 %collective-permute-start.2 = (bf16[160,2560]{1,0:T(8,128)(2,1)S(1)}, bf16[160,2560]{1,0:T(8,128)(2,1)}, u32[]{:S(2)}, u32[]{:S(2)}) collective-permute-start(bf16[160,2560]{1,0:T(8,128)(2,1)S(1)} %get-tuple-element.42.own), channel_id=1, source_target_pairs={{0,6},{1,7},{2,0},{3,1},{4,2},{5,3},{6,4},{7,5},{8,14},{9,15},{10,... | collective-permute-start | bytes 2457608 | tf_op jit(solution)/shard_map/first/ppermute | solution.py:35
  27.0 18.3 %collective-permute-start.3 = (bf16[160,2560]{1,0:T(8,128)(2,1)S(1)}, bf16[160,2560]{1,0:T(8,128)(2,1)S(1)}, u32[]{:S(2)}, u32[]{:S(2)}) collective-permute-start(bf16[160,2560]{1,0:T(8,128)(2,1)S(1)} %get-tuple-element.42.own), channel_id=1, source_target_pairs={{0,2},{1,3},{2,4},{3,5},{4,6},{5,7},{6,0},{7,1},{8,10},{9,11},{10,... | collective-permute-start | bytes 2457608 | tf_op jit(solution)/shard_map/first/ppermute | solution.py:35
  41.4 17.0 %collective-permute-start.9 = (bf16[160,2560]{1,0:T(8,128)(2,1)}, bf16[160,2560]{1,0:T(8,128)(2,1)S(1)}, u32[]{:S(2)}, u32[]{:S(2)}) collective-permute-start(bf16[160,2560]{1,0:T(8,128)(2,1)} %get-tuple-element.44.refs_2_), channel_id=1, source_target_pairs={{0,24},{1,25},{2,26},{3,27},{4,28},{5,29},{6,30},{7,31},{8,0},{9,1... | collective-permute-start | bytes 2457608 | tf_op jit(solution)/shard_map/second/ppermute | solution.py:30
  41.4 18.2 %collective-permute-start.8 = (bf16[160,2560]{1,0:T(8,128)(2,1)}, bf16[160,2560]{1,0:T(8,128)(2,1)S(1)}, u32[]{:S(2)}, u32[]{:S(2)}) collective-permute-start(bf16[160,2560]{1,0:T(8,128)(2,1)} %get-tuple-element.45.refs_3_), channel_id=1, source_target_pairs={{0,8},{1,9},{2,10},{3,11},{4,12},{5,13},{6,14},{7,15},{8,16},{9,17... | collective-permute-start | bytes 2457608 | tf_op jit(solution)/shard_map/second/ppermute | solution.py:30
  42.9 19.4 %collective-permute-start.10 = (bf16[160,2560]{1,0:T(8,128)(2,1)}, bf16[160,2560]{1,0:T(8,128)(2,1)S(1)}, u32[]{:S(2)}, u32[]{:S(2)}) collective-permute-start(bf16[160,2560]{1,0:T(8,128)(2,1)} %get-tuple-element.44.refs_2_), channel_id=1, source_target_pairs={{0,1},{1,0},{2,3},{3,2},{4,5},{5,4},{6,7},{7,6},{8,9},{9,8},{10,11... | collective-permute-start | bytes 2457608 | tf_op jit(solution)/shard_map/second/ppermute | solution.py:40
  42.9 20.3 %collective-permute-start.7 = (bf16[160,2560]{1,0:T(8,128)(2,1)}, bf16[160,2560]{1,0:T(8,128)(2,1)S(1)}, u32[]{:S(2)}, u32[]{:S(2)}) collective-permute-start(bf16[160,2560]{1,0:T(8,128)(2,1)} %collective-permute-done.2.ax), channel_id=1, source_target_pairs={{0,6},{1,7},{2,0},{3,1},{4,2},{5,3},{6,4},{7,5},{8,14},{9,15},{10,... | collective-permute-start | bytes 2457608 | tf_op jit(solution)/shard_map/second/ppermute | solution.py:35
  58.4 9.0 %collective-permute-start.11 = (bf16[64,2560]{1,0:T(8,128)(2,1)S(1)}, bf16[64,2560]{1,0:T(8,128)(2,1)S(1)}, u32[]{:S(2)}, u32[]{:S(2)}) collective-permute-start(bf16[64,2560]{1,0:T(8,128)(2,1)S(1)} %cut_b1.1), channel_id=1, source_target_pairs={{0,1},{1,0},{2,3},{3,2},{4,5},{5,4},{6,7},{7,6},{8,9},{9,8},{10,11... | collective-permute-start | bytes 983048 | tf_op jit(solution)/shard_map/third/ppermute | solution.py:40
  59.6 7.2 %collective-permute-start.12 = (bf16[48,2560]{1,0:T(8,128)(2,1)S(1)}, bf16[48,2560]{1,0:T(8,128)(2,1)S(1)}, u32[]{:S(2)}, u32[]{:S(2)}) collective-permute-start(bf16[48,2560]{1,0:T(8,128)(2,1)S(1)} %cut_b2.1), channel_id=1, source_target_pairs={{0,8},{1,9},{2,10},{3,11},{4,12},{5,13},{6,14},{7,15},{8,16},{9,17... | collective-permute-start | bytes 737288 | tf_op jit(solution)/shard_map/third/ppermute | solution.py:30
  62.3 5.1 %collective-permute-start.13 = (bf16[48,2560]{1,0:T(8,128)(2,1)S(1)}, bf16[48,2560]{1,0:T(8,128)(2,1)S(1)}, u32[]{:S(2)}, u32[]{:S(2)}) collective-permute-start(bf16[48,2560]{1,0:T(8,128)(2,1)S(1)} %cut_b3.1), channel_id=1, source_target_pairs={{0,24},{1,25},{2,26},{3,27},{4,28},{5,29},{6,30},{7,31},{8,0},{9,1... | collective-permute-start | bytes 737288 | tf_op jit(solution)/shard_map/third/ppermute | solution.py:30
  67.4 33.0 %copy-start = (f32[1000]{0:T(1024)S(1)}, f32[1000]{0:T(1024)}, u32[]{:S(2)}) copy-start(f32[1000]{0:T(1024)} %occ.1) | copy-start | bytes 12004
  67.4 33.0 %copy-start.1 = (s32[2]{0:T(128)S(1)}, s32[2]{0:T(128)}, u32[]{:S(2)}) copy-start(s32[2]{0:T(128)} %chosen.1) | copy-start | bytes 28
  68.7 2.4 %collective-permute-start.14 = (bf16[640,640]{1,0:T(8,128)(2,1)S(1)}, bf16[640,640]{1,0:T(8,128)(2,1)S(1)}, u32[]{:S(2)}, u32[]{:S(2)}) collective-permute-start(bf16[640,640]{1,0:T(8,128)(2,1)S(1)} %get-tuple-element.54), channel_id=1, source_target_pairs={{0,32},{32,0},{64,96},{96,64},{128,160},{160,128},{192,224},{224,1... | collective-permute-start | bytes 2457608 | tf_op jit(solution)/shard_map/core/ppermute | solution.py:44
  71.3 22.1 %collective-permute-start.15 = (bf16[160,640]{1,0:T(8,128)(2,1)S(1)}, bf16[160,640]{1,0:T(8,128)(2,1)S(1)}, u32[]{:S(2)}, u32[]{:S(2)}) collective-permute-start(bf16[160,640]{1,0:T(8,128)(2,1)S(1)} %get-tuple-element.56), channel_id=1, source_target_pairs={{0,128},{32,160},{64,192},{96,224},{128,0},{160,32},{192,64},{224,... | collective-permute-start | bytes 614408 | tf_op jit(solution)/shard_map/shares/ppermute | solution.py:48
  84.2 13.9 %collective-permute-start.16 = (bf16[160,640]{1,0:T(8,128)(2,1)S(1)}, bf16[160,640]{1,0:T(8,128)(2,1)S(1)}, u32[]{:S(2)}, u32[]{:S(2)}) collective-permute-start(bf16[160,640]{1,0:T(8,128)(2,1)S(1)} %get-tuple-element.57), channel_id=1, source_target_pairs={{0,64},{32,96},{64,128},{96,160},{128,192},{160,224},{192,0},{224,... | collective-permute-start | bytes 614408 | tf_op jit(solution)/shard_map/shares/ppermute | solution.py:48
  84.2 16.3 %collective-permute-start.17 = (bf16[160,640]{1,0:T(8,128)(2,1)S(1)}, bf16[160,640]{1,0:T(8,128)(2,1)S(1)}, u32[]{:S(2)}, u32[]{:S(2)}) collective-permute-start(bf16[160,640]{1,0:T(8,128)(2,1)S(1)} %get-tuple-element.58), channel_id=1, source_target_pairs={{0,192},{32,224},{64,0},{96,32},{128,64},{160,96},{192,128},{224,1... | collective-permute-start | bytes 614408 | tf_op jit(solution)/shard_map/shares/ppermute | solution.py:48
  101.3 8.4 %collective-permute-start.27 = (bf16[80,640]{1,0:T(8,128)(2,1)S(1)}, bf16[80,640]{1,0:T(8,128)(2,1)S(1)}, u32[]{:S(2)}, u32[]{:S(2)}) collective-permute-start(bf16[80,640]{1,0:T(8,128)(2,1)S(1)} %get-tuple-element.61.refs_0_), channel_id=1, source_target_pairs={{0,192},{32,224},{64,0},{96,32},{128,64},{160,96},{192,128},{224,1... | collective-permute-start | bytes 307208 | tf_op jit(solution)/shard_map/spread_0/ppermute | solution.py:48
  104.1 10.0 %collective-permute-start.26 = (bf16[80,640]{1,0:T(8,128)(2,1)S(1)}, bf16[80,640]{1,0:T(8,128)(2,1)S(1)}, u32[]{:S(2)}, u32[]{:S(2)}) collective-permute-start(bf16[80,640]{1,0:T(8,128)(2,1)S(1)} %get-tuple-element.61.refs_0_), channel_id=1, source_target_pairs={{0,128},{32,160},{64,192},{96,224},{128,0},{160,32},{192,64},{224,... | collective-permute-start | bytes 307208 | tf_op jit(solution)/shard_map/spread_0/ppermute | solution.py:48
  107.7 9.1 %collective-permute-start.25 = (bf16[80,640]{1,0:T(8,128)(2,1)S(1)}, bf16[80,640]{1,0:T(8,128)(2,1)S(1)}, u32[]{:S(2)}, u32[]{:S(2)}) collective-permute-start(bf16[80,640]{1,0:T(8,128)(2,1)S(1)} %get-tuple-element.61.refs_0_), channel_id=1, source_target_pairs={{0,64},{32,96},{64,128},{96,160},{128,192},{160,224},{192,0},{224,... | collective-permute-start | bytes 307208 | tf_op jit(solution)/shard_map/spread_0/ppermute | solution.py:48
  107.7 9.1 %collective-permute-start.28 = (bf16[80,640]{1,0:T(8,128)(2,1)S(1)}, bf16[80,640]{1,0:T(8,128)(2,1)S(1)}, u32[]{:S(2)}, u32[]{:S(2)}) collective-permute-start(bf16[80,640]{1,0:T(8,128)(2,1)S(1)} %get-tuple-element.61.refs_0_), channel_id=1, source_target_pairs={{0,32},{32,0},{64,96},{96,64},{128,160},{160,128},{192,224},{224,1... | collective-permute-start | bytes 307208 | tf_op jit(solution)/shard_map/other_0/ppermute | solution.py:44
  109.7 7.1 %collective-permute-start.31 = (bf16[80,640]{1,0:T(8,128)(2,1)S(1)}, bf16[80,640]{1,0:T(8,128)(2,1)S(1)}, u32[]{:S(2)}, u32[]{:S(2)}) collective-permute-start(bf16[80,640]{1,0:T(8,128)(2,1)S(1)} %collective-permute-done.27.refs_3_), channel_id=1, source_target_pairs={{0,32},{32,0},{64,96},{96,64},{128,160},{160,128},{192,224},{224,1... | collective-permute-start | bytes 307208 | tf_op jit(solution)/shard_map/other_0/ppermute | solution.py:44
  114.1 3.7 %collective-permute-start.30 = (bf16[80,640]{1,0:T(8,128)(2,1)S(1)}, bf16[80,640]{1,0:T(8,128)(2,1)S(1)}, u32[]{:S(2)}, u32[]{:S(2)}) collective-permute-start(bf16[80,640]{1,0:T(8,128)(2,1)S(1)} %collective-permute-done.26.refs_2_), channel_id=1, source_target_pairs={{0,32},{32,0},{64,96},{96,64},{128,160},{160,128},{192,224},{224,1... | collective-permute-start | bytes 307208 | tf_op jit(solution)/shard_map/other_0/ppermute | solution.py:44
  116.8 1.3 collective-permute-start.29
  120.7 21.4 %collective-permute-start.32 = (bf16[160,2560]{1,0:T(8,128)(2,1)S(1)}, bf16[160,2560]{1,0:T(8,128)(2,1)S(1)}, u32[]{:S(2)}, u32[]{:S(2)}) collective-permute-start(bf16[160,2560]{1,0:T(8,128)(2,1)S(1)} %get-tuple-element.62), channel_id=1, source_target_pairs={{0,2},{1,3},{2,4},{3,5},{4,6},{5,7},{6,0},{7,1},{8,10},{9,11},{10,... | collective-permute-start | bytes 2457608 | tf_op jit(solution)/shard_map/out/ppermute | solution.py:35
  122.2 19.9 %collective-permute-start.33 = (bf16[160,2560]{1,0:T(8,128)(2,1)S(1)}, bf16[160,2560]{1,0:T(8,128)(2,1)S(1)}, u32[]{:S(2)}, u32[]{:S(2)}) collective-permute-start(bf16[160,2560]{1,0:T(8,128)(2,1)S(1)} %get-tuple-element.63), channel_id=1, source_target_pairs={{0,6},{1,7},{2,0},{3,1},{4,2},{5,3},{6,4},{7,5},{8,14},{9,15},{10,... | collective-permute-start | bytes 2457608 | tf_op jit(solution)/shard_map/out/ppermute | solution.py:35
  123.8 5.4 %collective-permute-start.21 = (bf16[80,640]{1,0:T(8,128)(2,1)S(1)}, bf16[80,640]{1,0:T(8,128)(2,1)S(1)}, u32[]{:S(2)}, u32[]{:S(2)}) collective-permute-start(bf16[80,640]{1,0:T(8,128)(2,1)S(1)} %get-tuple-element.59.refs_0_), channel_id=1, source_target_pairs={{0,32},{32,0},{64,96},{96,64},{128,160},{160,128},{192,224},{224,1... | collective-permute-start | bytes 307208 | tf_op jit(solution)/shard_map/other_1/ppermute | solution.py:44
  124.5 5.4 %collective-permute-start.20 = (bf16[80,640]{1,0:T(8,128)(2,1)S(1)}, bf16[80,640]{1,0:T(8,128)(2,1)S(1)}, u32[]{:S(2)}, u32[]{:S(2)}) collective-permute-start(bf16[80,640]{1,0:T(8,128)(2,1)S(1)} %get-tuple-element.59.refs_0_), channel_id=1, source_target_pairs={{0,192},{32,224},{64,0},{96,32},{128,64},{160,96},{192,128},{224,1... | collective-permute-start | bytes 307208 | tf_op jit(solution)/shard_map/spread_1/ppermute | solution.py:48
  125.9 10.2 %collective-permute-start.19 = (bf16[80,640]{1,0:T(8,128)(2,1)S(1)}, bf16[80,640]{1,0:T(8,128)(2,1)S(1)}, u32[]{:S(2)}, u32[]{:S(2)}) collective-permute-start(bf16[80,640]{1,0:T(8,128)(2,1)S(1)} %get-tuple-element.59.refs_0_), channel_id=1, source_target_pairs={{0,128},{32,160},{64,192},{96,224},{128,0},{160,32},{192,64},{224,... | collective-permute-start | bytes 307208 | tf_op jit(solution)/shard_map/spread_1/ppermute | solution.py:48
  129.2 9.0 %collective-permute-start.18 = (bf16[80,640]{1,0:T(8,128)(2,1)S(1)}, bf16[80,640]{1,0:T(8,128)(2,1)S(1)}, u32[]{:S(2)}, u32[]{:S(2)}) collective-permute-start(bf16[80,640]{1,0:T(8,128)(2,1)S(1)} %get-tuple-element.59.refs_0_), channel_id=1, source_target_pairs={{0,64},{32,96},{64,128},{96,160},{128,192},{160,224},{192,0},{224,... | collective-permute-start | bytes 307208 | tf_op jit(solution)/shard_map/spread_1/ppermute | solution.py:48
  129.9 8.6 %collective-permute-start.24 = (bf16[80,640]{1,0:T(8,128)(2,1)S(1)}, bf16[80,640]{1,0:T(8,128)(2,1)S(1)}, u32[]{:S(2)}, u32[]{:S(2)}) collective-permute-start(bf16[80,640]{1,0:T(8,128)(2,1)S(1)} %collective-permute-done.20.refs_3_), channel_id=1, source_target_pairs={{0,32},{32,0},{64,96},{96,64},{128,160},{160,128},{192,224},{224,1... | collective-permute-start | bytes 307208 | tf_op jit(solution)/shard_map/other_1/ppermute | solution.py:44
  136.1 3.0 %collective-permute-start.23 = (bf16[80,640]{1,0:T(8,128)(2,1)S(1)}, bf16[80,640]{1,0:T(8,128)(2,1)S(1)}, u32[]{:S(2)}, u32[]{:S(2)}) collective-permute-start(bf16[80,640]{1,0:T(8,128)(2,1)S(1)} %collective-permute-done.19.refs_2_), channel_id=1, source_target_pairs={{0,32},{32,0},{64,96},{96,64},{128,160},{160,128},{192,224},{224,1... | collective-permute-start | bytes 307208 | tf_op jit(solution)/shard_map/other_1/ppermute | solution.py:44
  138.2 1.3 collective-permute-start.22
  143.6 11.4 %collective-permute-start.34 = (bf16[80,2560]{1,0:T(8,128)(2,1)S(1)}, bf16[80,2560]{1,0:T(8,128)(2,1)S(1)}, u32[]{:S(2)}, u32[]{:S(2)}) collective-permute-start(bf16[80,2560]{1,0:T(8,128)(2,1)S(1)} %get-tuple-element.65), channel_id=1, source_target_pairs={{0,2},{1,3},{2,4},{3,5},{4,6},{5,7},{6,0},{7,1},{8,10},{9,11},{10,... | collective-permute-start | bytes 1228808 | tf_op jit(solution)/shard_map/out/ppermute | solution.py:35
  144.4 10.6 %collective-permute-start.35 = (bf16[80,2560]{1,0:T(8,128)(2,1)S(1)}, bf16[80,2560]{1,0:T(8,128)(2,1)S(1)}, u32[]{:S(2)}, u32[]{:S(2)}) collective-permute-start(bf16[80,2560]{1,0:T(8,128)(2,1)S(1)} %get-tuple-element.66), channel_id=1, source_target_pairs={{0,6},{1,7},{2,0},{3,1},{4,2},{5,3},{6,4},{7,5},{8,14},{9,15},{10,... | collective-permute-start | bytes 1228808 | tf_op jit(solution)/shard_map/out/ppermute | solution.py:35

commit v7 on v6

--- a/solution.py
+++ b/solution.py
@@ -557,7 +557,8 @@
         bo = send_z(b)
         bp = send_y(b, -1)
         bm = send_y(b, 1)
-    bo, bp = arrive((bo, bp), (bm, vir))
+    (bp,) = arrive((bp,), (bm, vir))
+    (bo,) = arrive((bo,), (bp,))
     with jax.named_scope("second"):
         bom = send_y(bo, 1)
         b2 = send_y(bp, -1)

time: 158 us -> 156 us (0.987)
  waiting for transfers between devices: 65.7 us -> 53.9 us
  starting transfers between devices: 62.7 us -> 72.6 us
    ppermute x3, starting transfers between devices: 0.1 us -> 5.44 us  [send_z(): return lax.ppermute(v, 'blk', pairs)]
    ppermute x9, waiting for transfers between devices: 22.7 us -> 17.7 us  [send_high(): return lax.ppermute(v, 'grp', [(g, (g + 2 * step) % 8) for g in range(8)])]
    ppermute x9, starting transfers between devices: 8.97 us -> 13.5 us  [send_core(): return lax.ppermute(v, 'grp', [(g, g ^ 1) for g in range(8)])]
    ppermute x3, waiting for transfers between devices: 3.31 us -> 0.07 us  [send_z(): return lax.ppermute(v, 'blk', pairs)]
    ppermute x6, waiting for transfers between devices: 22.5 us -> 20.3 us  [send_y(): return lax.ppermute(v, 'blk', pairs)]
  transfers between devices with their start and end apart: 36 -> 36, of which waited for: 23 -> 19; matrix products, arithmetic and copies ran while one was open for 0% -> 0% of each run, Pallas kernels for 11% -> 12%
where the time goes in v7:
time: 156 us; the launch traced here: 154 us
  starting transfers between devices  72.6 us (47%)
  waiting for transfers between devices  53.9 us (35%)
  Pallas kernels  27.3 us (18%)
    ppermute x9, starting transfers between devices, send_high(): return lax.ppermute(v, 'grp', [(g, (g + 2 * step) % 8) for g in range(8)])  27.4 us
    pallas_call x15, Pallas kernels, call(): pl.pallas_call(kernel, in_specs=[spec for _, spec in args], out_specs=[VM...  27.3 us
    ppermute x6, waiting for transfers between devices, send_y(): return lax.ppermute(v, 'blk', pairs)  20.3 us
    ppermute x9, waiting for transfers between devices, send_high(): return lax.ppermute(v, 'grp', [(g, (g + 2 * step) % 8) for g in range(8)])  17.7 us
    ppermute x9, starting transfers between devices, send_core(): return lax.ppermute(v, 'grp', [(g, g ^ 1) for g in range(8)])  13.5 us
    ppermute x7, starting transfers between devices, send_x(): return lax.ppermute(v, 'blk', pairs)  10.5 us
    ppermute x7, waiting for transfers between devices, send_x(): return lax.ppermute(v, 'blk', pairs)  8.44 us
    ppermute x6, starting transfers between devices, send_y(): return lax.ppermute(v, 'blk', pairs)  7.52 us
  transfers between devices with their start and end apart: 36, of which 19 were waited for; matrix products, arithmetic and copies ran while one was open for 0% of the time, Pallas kernels for 12%

profile of v7, /device:TPU:1, one launch (start us, length us, event | category | flops | bytes accessed | tf_op | source)
XLA Modules:
  0.0 154.2 jit_solution(10632432109111290222)
XLA Ops:
  0.0 1.1 ends.1
  1.1 6.3 %collective-permute-start = (bf16[320,512]{1,0:T(8,128)(2,1)S(1)}, bf16[320,512]{1,0:T(8,128)(2,1)S(1)}, u32[]{:S(2)}, u32[]{:S(2)}) collective-permute-start(bf16[320,512]{1,0:T(8,128)(2,1)S(1)} %get-tuple-element.34), channel_id=1, source_target_pairs={{0,32},{32,64},{64,96},{96,128},{128,160},{160,192},{192,224},{1,3... | collective-permute-start | bytes 983048 | tf_op jit(solution)/shard_map/ppermute | solution.py:550
  7.4 1.9 %collective-permute-start.1 = (bf16[320,512]{1,0:T(8,128)(2,1)S(1)}, bf16[320,512]{1,0:T(8,128)(2,1)S(1)}, u32[]{:S(2)}, u32[]{:S(2)}) collective-permute-start(bf16[320,512]{1,0:T(8,128)(2,1)S(1)} %get-tuple-element.35), channel_id=1, source_target_pairs={{32,0},{64,32},{96,64},{128,96},{160,128},{192,160},{224,192},{33,... | collective-permute-start | bytes 983048 | tf_op jit(solution)/shard_map/ppermute | solution.py:551
  9.3 8.0 %fit_inner.1 = (bf16[160,2560]{1,0:T(8,128)(2,1)S(1)}, bf16[160,2560]{1,0:T(8,128)(2,1)S(1)}, bf16[320,2560]{1,0:T(8,128)(2,1)S(1)}, bf16[4,1280,256]{2,1,0:T(8,128)(2,1)S(1)}) custom-call(s32[2,180]{1,0:T(2,128)} %bitcast.4, bf16[320,2560]{1,0:T(8,128)(2,1)} %bitcast.3, bf16[180,128,128]{2,1,0:T(8,128)(2,1)} %tiles_in.1), custom_call_target="tpu_custom_call" | custom-call | flops 1000 | bytes 1000 | tf_op jit(solution)/shard_map/fit_inner/pallas_call | solution.py:85
  17.3 2.9 %collective-permute-done.1.right = bf16[320,512]{1,0:T(8,128)(2,1)S(1)} collective-permute-done((bf16[320,512]{1,0:T(8,128)(2,1)S(1)}, bf16[320,512]{1,0:T(8,128)(2,1)S(1)}, u32[]{:S(2)}, u32[]{:S(2)}) %collective-permute-start.1) | collective-permute-done | bytes 327712 | tf_op jit(solution)/shard_map/ppermute | solution.py:551
  20.2 1.0 fit_edge.1
  21.2 3.1 %collective-permute-start.5 = (bf16[160,2560]{1,0:T(8,128)(2,1)S(1)}, bf16[160,2560]{1,0:T(8,128)(2,1)S(1)}, u32[]{:S(2)}, u32[]{:S(2)}) collective-permute-start(bf16[160,2560]{1,0:T(8,128)(2,1)S(1)} %get-tuple-element.41.refs_0_), channel_id=1, source_target_pairs={{0,24},{1,25},{2,26},{3,27},{4,28},{5,29},{6,30},{7,31},{8,0},{9,1... | collective-permute-start | bytes 2457608 | tf_op jit(solution)/shard_map/first/ppermute | solution.py:30
  24.3 2.5 %collective-permute-start.2 = (bf16[160,2560]{1,0:T(8,128)(2,1)S(1)}, bf16[160,2560]{1,0:T(8,128)(2,1)}, u32[]{:S(2)}, u32[]{:S(2)}) collective-permute-start(bf16[160,2560]{1,0:T(8,128)(2,1)S(1)} %get-tuple-element.40.own), channel_id=1, source_target_pairs={{0,6},{1,7},{2,0},{3,1},{4,2},{5,3},{6,4},{7,5},{8,14},{9,15},{10,... | collective-permute-start | bytes 2457608 | tf_op jit(solution)/shard_map/first/ppermute | solution.py:35
  27.0 10.3 %collective-permute-done.5.refs_0_ = bf16[160,2560]{1,0:T(8,128)(2,1)S(1)} collective-permute-done((bf16[160,2560]{1,0:T(8,128)(2,1)S(1)}, bf16[160,2560]{1,0:T(8,128)(2,1)S(1)}, u32[]{:S(2)}, u32[]{:S(2)}) %collective-permute-start.5) | collective-permute-done | bytes 819232 | tf_op jit(solution)/shard_map/first/ppermute | solution.py:30
  37.2 3.4 %collective-permute-done.4.refs_1_ = bf16[160,2560]{1,0:T(8,128)(2,1)} collective-permute-done((bf16[160,2560]{1,0:T(8,128)(2,1)S(1)}, bf16[160,2560]{1,0:T(8,128)(2,1)}, u32[]{:S(2)}, u32[]{:S(2)}) %collective-permute-start.4) | collective-permute-done | bytes 819232 | tf_op jit(solution)/shard_map/first/ppermute | solution.py:30
  40.6 1.4 collective-permute-start.8
  42.7 2.5 %collective-permute-start.7 = (bf16[160,2560]{1,0:T(8,128)(2,1)}, bf16[160,2560]{1,0:T(8,128)(2,1)S(1)}, u32[]{:S(2)}, u32[]{:S(2)}) collective-permute-start(bf16[160,2560]{1,0:T(8,128)(2,1)} %collective-permute-done.2.ax), channel_id=1, source_target_pairs={{0,6},{1,7},{2,0},{3,1},{4,2},{5,3},{6,4},{7,5},{8,14},{9,15},{10,... | collective-permute-start | bytes 2457608 | tf_op jit(solution)/shard_map/second/ppermute | solution.py:35
  45.2 4.8 %pair_first.1 = (f32[640,640]{1,0:T(8,128)S(1)}, bf16[1280,2560]{1,0:T(8,128)(2,1)S(1)}, bf16[640,2560]{1,0:T(8,128)(2,1)S(1)}) custom-call(bf16[160,2560]{1,0:T(8,128)(2,1)S(1)} %get-tuple-element.40.own, bf16[160,2560]{1,0:T(8,128)(2,1)} %collective-permute-done.2.ax, bf16[160,2560]{1,0:T(8,128)(2,1)S(1)} %collective-permute-done.3.am, ...), custom_call_target="tpu_custom_call" | custom-call | flops 1000 | bytes 1000 | tf_op jit(solution)/shard_map/pair_first/pallas_call | solution.py:85
  50.0 4.9 %collective-permute-done.9.refs_1_.refs_0_ = bf16[160,2560]{1,0:T(8,128)(2,1)S(1)} collective-permute-done((bf16[160,2560]{1,0:T(8,128)(2,1)S(1)}, bf16[160,2560]{1,0:T(8,128)(2,1)S(1)}, u32[]{:S(2)}, u32[]{:S(2)}) %collective-permute-start.9) | collective-permute-done | bytes 819232 | tf_op jit(solution)/shard_map/second/ppermute | solution.py:30
  54.9 4.8 %collective-permute-start.11 = (bf16[64,2560]{1,0:T(8,128)(2,1)S(1)}, bf16[64,2560]{1,0:T(8,128)(2,1)S(1)}, u32[]{:S(2)}, u32[]{:S(2)}) collective-permute-start(bf16[64,2560]{1,0:T(8,128)(2,1)S(1)} %cut_b1.1), channel_id=1, source_target_pairs={{0,1},{1,0},{2,3},{3,2},{4,5},{5,4},{6,7},{7,6},{8,9},{9,8},{10,11... | collective-permute-start | bytes 983048 | tf_op jit(solution)/shard_map/third/ppermute | solution.py:40
  60.1 2.7 %collective-permute-start.13 = (bf16[48,2560]{1,0:T(8,128)(2,1)S(1)}, bf16[48,2560]{1,0:T(8,128)(2,1)S(1)}, u32[]{:S(2)}, u32[]{:S(2)}) collective-permute-start(bf16[48,2560]{1,0:T(8,128)(2,1)S(1)} %cut_b3.1), channel_id=1, source_target_pairs={{0,24},{1,25},{2,26},{3,27},{4,28},{5,29},{6,30},{7,31},{8,0},{9,1... | collective-permute-start | bytes 737288 | tf_op jit(solution)/shard_map/third/ppermute | solution.py:30
  62.8 3.6 %pair_early.1 = (f32[640,640]{1,0:T(8,128)S(1)}, bf16[1280,2560]{1,0:T(8,128)(2,1)S(1)}, bf16[640,2560]{1,0:T(8,128)(2,1)S(1)}, f32[640,640]{1,0:T(8,128)S(1)}, bf16[640,640]{1,0:T(8,128)(2,1)S(1)}) custom-call(f32[640,640]{1,0:T(8,128)S(1)} %get-tuple-element.42.first_in.refs_1_, ...), custom_call_target="tpu_custom_call", output_to_operand_aliasing={{0}: (0, {}), {1}: (1, {}), {2}: (2, {})} | custom-call | flops 1000 | bytes 1000 | tf_op jit(solution)/shard_map/pair_early/pallas_call | solution.py:85
  66.4 1.7 %collective-permute-done.12.refs_1_ = bf16[48,2560]{1,0:T(8,128)(2,1)S(1)} collective-permute-done((bf16[48,2560]{1,0:T(8,128)(2,1)S(1)}, bf16[48,2560]{1,0:T(8,128)(2,1)S(1)}, u32[]{:S(2)}, u32[]{:S(2)}) %collective-permute-start.12) | collective-permute-done | bytes 245792 | tf_op jit(solution)/shard_map/third/ppermute | solution.py:30
  68.2 1.2 pair_late.1
  69.5 2.3 %collective-permute-done.14.got = bf16[640,640]{1,0:T(8,128)(2,1)S(1)} collective-permute-done((bf16[640,640]{1,0:T(8,128)(2,1)S(1)}, bf16[640,640]{1,0:T(8,128)(2,1)S(1)}, u32[]{:S(2)}, u32[]{:S(2)}) %collective-permute-start.14) | collective-permute-done | bytes 819232 | tf_op jit(solution)/shard_map/core/ppermute | solution.py:44
  72.0 12.0 %collective-permute-start.15 = (bf16[160,640]{1,0:T(8,128)(2,1)S(1)}, bf16[160,640]{1,0:T(8,128)(2,1)S(1)}, u32[]{:S(2)}, u32[]{:S(2)}) collective-permute-start(bf16[160,640]{1,0:T(8,128)(2,1)S(1)} %get-tuple-element.52), channel_id=1, source_target_pairs={{0,128},{32,160},{64,192},{96,224},{128,0},{160,32},{192,64},{224,... | collective-permute-start | bytes 614408 | tf_op jit(solution)/shard_map/shares/ppermute | solution.py:48
  84.1 3.6 %collective-permute-start.17 = (bf16[160,640]{1,0:T(8,128)(2,1)S(1)}, bf16[160,640]{1,0:T(8,128)(2,1)S(1)}, u32[]{:S(2)}, u32[]{:S(2)}) collective-permute-start(bf16[160,640]{1,0:T(8,128)(2,1)S(1)} %get-tuple-element.54), channel_id=1, source_target_pairs={{0,192},{32,224},{64,0},{96,32},{128,64},{160,96},{192,128},{224,1... | collective-permute-start | bytes 614408 | tf_op jit(solution)/shard_map/shares/ppermute | solution.py:48
  87.7 6.6 %collective-permute-done.15.refs_0_ = bf16[160,640]{1,0:T(8,128)(2,1)S(1)} collective-permute-done((bf16[160,640]{1,0:T(8,128)(2,1)S(1)}, bf16[160,640]{1,0:T(8,128)(2,1)S(1)}, u32[]{:S(2)}, u32[]{:S(2)}) %collective-permute-start.15) | collective-permute-done | bytes 204832 | tf_op jit(solution)/shard_map/shares/ppermute | solution.py:48
  94.3 5.6 %collective-permute-done.16.refs_1_ = bf16[160,640]{1,0:T(8,128)(2,1)S(1)} collective-permute-done((bf16[160,640]{1,0:T(8,128)(2,1)S(1)}, bf16[160,640]{1,0:T(8,128)(2,1)S(1)}, u32[]{:S(2)}, u32[]{:S(2)}) %collective-permute-start.16) | collective-permute-done | bytes 204832 | tf_op jit(solution)/shard_map/shares/ppermute | solution.py:48
  100.5 0.8 amplitude.1
  101.4 1.6 %collective-permute-start.27 = (bf16[80,640]{1,0:T(8,128)(2,1)S(1)}, bf16[80,640]{1,0:T(8,128)(2,1)S(1)}, u32[]{:S(2)}, u32[]{:S(2)}) collective-permute-start(bf16[80,640]{1,0:T(8,128)(2,1)S(1)} %get-tuple-element.57.refs_0_), channel_id=1, source_target_pairs={{0,192},{32,224},{64,0},{96,32},{128,64},{160,96},{192,128},{224,1... | collective-permute-start | bytes 307208 | tf_op jit(solution)/shard_map/spread_0/ppermute | solution.py:48
  102.9 3.7 %collective-permute-start.26 = (bf16[80,640]{1,0:T(8,128)(2,1)S(1)}, bf16[80,640]{1,0:T(8,128)(2,1)S(1)}, u32[]{:S(2)}, u32[]{:S(2)}) collective-permute-start(bf16[80,640]{1,0:T(8,128)(2,1)S(1)} %get-tuple-element.57.refs_0_), channel_id=1, source_target_pairs={{0,128},{32,160},{64,192},{96,224},{128,0},{160,32},{192,64},{224,... | collective-permute-start | bytes 307208 | tf_op jit(solution)/shard_map/spread_0/ppermute | solution.py:48
  107.0 1.3 collective-permute-start.28
  108.3 1.6 %collective-permute-done.27.refs_3_ = bf16[80,640]{1,0:T(8,128)(2,1)S(1)} collective-permute-done((bf16[80,640]{1,0:T(8,128)(2,1)S(1)}, bf16[80,640]{1,0:T(8,128)(2,1)S(1)}, u32[]{:S(2)}, u32[]{:S(2)}) %collective-permute-start.27) | collective-permute-done | bytes 102432 | tf_op jit(solution)/shard_map/spread_0/ppermute | solution.py:48
  110.6 5.2 %collective-permute-start.30 = (bf16[80,640]{1,0:T(8,128)(2,1)S(1)}, bf16[80,640]{1,0:T(8,128)(2,1)S(1)}, u32[]{:S(2)}, u32[]{:S(2)}) collective-permute-start(bf16[80,640]{1,0:T(8,128)(2,1)S(1)} %collective-permute-done.26.refs_2_), channel_id=1, source_target_pairs={{0,32},{32,0},{64,96},{96,64},{128,160},{160,128},{192,224},{224,1... | collective-permute-start | bytes 307208 | tf_op jit(solution)/shard_map/other_0/ppermute | solution.py:44
  117.2 2.5 %density_first.1 = (bf16[160,2560]{1,0:T(8,128)(2,1)S(1)}, bf16[160,2560]{1,0:T(8,128)(2,1)S(1)}) custom-call(bf16[80,640]{1,0:T(8,128)(2,1)S(1)} %get-tuple-element.57.refs_0_, bf16[80,640]{1,0:T(8,128)(2,1)S(1)} %collective-permute-done.25.refs_1_, bf16[80,640]{1,0:T(8,128)(2,1)S(1)} %collective-permute-done.26.refs_2_, ...), custom_call_target="tpu_custom_call" | custom-call | flops 1000 | bytes 1000 | tf_op jit(solution)/shard_map/density_first/pallas_call | solution.py:85
  119.8 1.3 collective-permute-start.32
  121.1 1.5 collective-permute-start.33
  122.5 0.9 collective-permute-start.21
  123.5 2.0 %collective-permute-start.20 = (bf16[80,640]{1,0:T(8,128)(2,1)S(1)}, bf16[80,640]{1,0:T(8,128)(2,1)S(1)}, u32[]{:S(2)}, u32[]{:S(2)}) collective-permute-start(bf16[80,640]{1,0:T(8,128)(2,1)S(1)} %get-tuple-element.55.refs_0_), channel_id=1, source_target_pairs={{0,192},{32,224},{64,0},{96,32},{128,64},{160,96},{192,128},{224,1... | collective-permute-start | bytes 307208 | tf_op jit(solution)/shard_map/spread_1/ppermute | solution.py:48
  125.5 3.1 %collective-permute-start.19 = (bf16[80,640]{1,0:T(8,128)(2,1)S(1)}, bf16[80,640]{1,0:T(8,128)(2,1)S(1)}, u32[]{:S(2)}, u32[]{:S(2)}) collective-permute-start(bf16[80,640]{1,0:T(8,128)(2,1)S(1)} %get-tuple-element.55.refs_0_), channel_id=1, source_target_pairs={{0,128},{32,160},{64,192},{96,224},{128,0},{160,32},{192,64},{224,... | collective-permute-start | bytes 307208 | tf_op jit(solution)/shard_map/spread_1/ppermute | solution.py:48
  128.6 1.0 collective-permute-start.18
  129.6 0.8 collective-permute-start.24
  130.5 3.1 %collective-permute-done.19.refs_2_ = bf16[80,640]{1,0:T(8,128)(2,1)S(1)} collective-permute-done((bf16[80,640]{1,0:T(8,128)(2,1)S(1)}, bf16[80,640]{1,0:T(8,128)(2,1)S(1)}, u32[]{:S(2)}, u32[]{:S(2)}) %collective-permute-start.19) | collective-permute-done | bytes 102432 | tf_op jit(solution)/shard_map/spread_1/ppermute | solution.py:48
  133.6 4.1 %collective-permute-start.23 = (bf16[80,640]{1,0:T(8,128)(2,1)S(1)}, bf16[80,640]{1,0:T(8,128)(2,1)S(1)}, u32[]{:S(2)}, u32[]{:S(2)}) collective-permute-start(bf16[80,640]{1,0:T(8,128)(2,1)S(1)} %collective-permute-done.19.refs_2_), channel_id=1, source_target_pairs={{0,32},{32,0},{64,96},{96,64},{128,160},{160,128},{192,224},{224,1... | collective-permute-start | bytes 307208 | tf_op jit(solution)/shard_map/other_1/ppermute | solution.py:44
  137.7 0.9 collective-permute-done.23.refs_6_
  139.0 1.5 collective-permute-done.32.refs_9_.got_m
  140.6 1.5 density_second.1
  142.1 1.0 collective-permute-start.34
  143.1 1.8 %collective-permute-start.35 = (bf16[80,2560]{1,0:T(8,128)(2,1)S(1)}, bf16[80,2560]{1,0:T(8,128)(2,1)S(1)}, u32[]{:S(2)}, u32[]{:S(2)}) collective-permute-start(bf16[80,2560]{1,0:T(8,128)(2,1)S(1)} %get-tuple-element.62), channel_id=1, source_target_pairs={{0,6},{1,7},{2,0},{3,1},{4,2},{5,3},{6,4},{7,5},{8,14},{9,15},{10,... | collective-permute-start | bytes 1228808 | tf_op jit(solution)/shard_map/out/ppermute | solution.py:35
  144.8 1.4 density_own.1.own
  146.3 6.9 %collective-permute-done.34.one = bf16[80,2560]{1,0:T(8,128)(2,1)S(1)} collective-permute-done((bf16[80,2560]{1,0:T(8,128)(2,1)S(1)}, bf16[80,2560]{1,0:T(8,128)(2,1)S(1)}, u32[]{:S(2)}, u32[]{:S(2)}) %collective-permute-start.34) | collective-permute-done | bytes 409632 | tf_op jit(solution)/shard_map/out/ppermute | solution.py:35
  153.1 1.0 add.1
  (48 shorter events, 4.9 us)
Async XLA Ops:
  1.1 16.2 %collective-permute-start = (bf16[320,512]{1,0:T(8,128)(2,1)S(1)}, bf16[320,512]{1,0:T(8,128)(2,1)S(1)}, u32[]{:S(2)}, u32[]{:S(2)}) collective-permute-start(bf16[320,512]{1,0:T(8,128)(2,1)S(1)} %get-tuple-element.34), channel_id=1, source_target_pairs={{0,32},{32,64},{64,96},{96,128},{128,160},{160,192},{192,224},{1,3... | collective-permute-start | bytes 983048 | tf_op jit(solution)/shard_map/ppermute | solution.py:550
  7.4 12.8 %collective-permute-start.1 = (bf16[320,512]{1,0:T(8,128)(2,1)S(1)}, bf16[320,512]{1,0:T(8,128)(2,1)S(1)}, u32[]{:S(2)}, u32[]{:S(2)}) collective-permute-start(bf16[320,512]{1,0:T(8,128)(2,1)S(1)} %get-tuple-element.35), channel_id=1, source_target_pairs={{32,0},{64,32},{96,64},{128,96},{160,128},{192,160},{224,192},{33,... | collective-permute-start | bytes 983048 | tf_op jit(solution)/shard_map/ppermute | solution.py:551
  20.2 6.6 %copy-start.2 = (f32[5120]{0:T(1024)S(1)}, f32[5120]{0:T(1024)}, u32[]{:S(2)}) copy-start(f32[5120]{0:T(1024)} %param.9) | copy-start | bytes 61444
  21.2 16.0 %collective-permute-start.5 = (bf16[160,2560]{1,0:T(8,128)(2,1)S(1)}, bf16[160,2560]{1,0:T(8,128)(2,1)S(1)}, u32[]{:S(2)}, u32[]{:S(2)}) collective-permute-start(bf16[160,2560]{1,0:T(8,128)(2,1)S(1)} %get-tuple-element.41.refs_0_), channel_id=1, source_target_pairs={{0,24},{1,25},{2,26},{3,27},{4,28},{5,29},{6,30},{7,31},{8,0},{9,1... | collective-permute-start | bytes 2457608 | tf_op jit(solution)/shard_map/first/ppermute | solution.py:30
  24.3 16.3 %collective-permute-start.4 = (bf16[160,2560]{1,0:T(8,128)(2,1)S(1)}, bf16[160,2560]{1,0:T(8,128)(2,1)}, u32[]{:S(2)}, u32[]{:S(2)}) collective-permute-start(bf16[160,2560]{1,0:T(8,128)(2,1)S(1)} %get-tuple-element.41.refs_0_), channel_id=1, source_target_pairs={{0,8},{1,9},{2,10},{3,11},{4,12},{5,13},{6,14},{7,15},{8,16},{9,17... | collective-permute-start | bytes 2457608 | tf_op jit(solution)/shard_map/first/ppermute | solution.py:30
  24.3 16.3 %collective-permute-start.6 = (bf16[160,2560]{1,0:T(8,128)(2,1)S(1)}, bf16[160,2560]{1,0:T(8,128)(2,1)}, u32[]{:S(2)}, u32[]{:S(2)}) collective-permute-start(bf16[160,2560]{1,0:T(8,128)(2,1)S(1)} %get-tuple-element.41.refs_0_), channel_id=1, source_target_pairs={{0,1},{1,0},{2,3},{3,2},{4,5},{5,4},{6,7},{7,6},{8,9},{9,8},{10,11... | collective-permute-start | bytes 2457608 | tf_op jit(solution)/shard_map/first/ppermute | solution.py:40
  24.3 18.4 %collective-permute-start.2 = (bf16[160,2560]{1,0:T(8,128)(2,1)S(1)}, bf16[160,2560]{1,0:T(8,128)(2,1)}, u32[]{:S(2)}, u32[]{:S(2)}) collective-permute-start(bf16[160,2560]{1,0:T(8,128)(2,1)S(1)} %get-tuple-element.40.own), channel_id=1, source_target_pairs={{0,6},{1,7},{2,0},{3,1},{4,2},{5,3},{6,4},{7,5},{8,14},{9,15},{10,... | collective-permute-start | bytes 2457608 | tf_op jit(solution)/shard_map/first/ppermute | solution.py:35
  26.9 18.3 %collective-permute-start.3 = (bf16[160,2560]{1,0:T(8,128)(2,1)S(1)}, bf16[160,2560]{1,0:T(8,128)(2,1)S(1)}, u32[]{:S(2)}, u32[]{:S(2)}) collective-permute-start(bf16[160,2560]{1,0:T(8,128)(2,1)S(1)} %get-tuple-element.40.own), channel_id=1, source_target_pairs={{0,2},{1,3},{2,4},{3,5},{4,6},{5,7},{6,0},{7,1},{8,10},{9,11},{10,... | collective-permute-start | bytes 2457608 | tf_op jit(solution)/shard_map/first/ppermute | solution.py:35
  40.6 14.3 %collective-permute-start.9 = (bf16[160,2560]{1,0:T(8,128)(2,1)S(1)}, bf16[160,2560]{1,0:T(8,128)(2,1)S(1)}, u32[]{:S(2)}, u32[]{:S(2)}) collective-permute-start(bf16[160,2560]{1,0:T(8,128)(2,1)S(1)} %arrive.2.refs_1_.refs_2_), channel_id=1, source_target_pairs={{0,24},{1,25},{2,26},{3,27},{4,28},{5,29},{6,30},{7,31},{8,0},{9,1... | collective-permute-start | bytes 2457608 | tf_op jit(solution)/shard_map/second/ppermute | solution.py:30
  40.6 19.1 %collective-permute-start.8 = (bf16[160,2560]{1,0:T(8,128)(2,1)}, bf16[160,2560]{1,0:T(8,128)(2,1)S(1)}, u32[]{:S(2)}, u32[]{:S(2)}) collective-permute-start(bf16[160,2560]{1,0:T(8,128)(2,1)} %arrive.3.refs_3_), channel_id=1, source_target_pairs={{0,8},{1,9},{2,10},{3,11},{4,12},{5,13},{6,14},{7,15},{8,16},{9,17... | collective-permute-start | bytes 2457608 | tf_op jit(solution)/shard_map/second/ppermute | solution.py:30
  42.1 18.0 %collective-permute-start.10 = (bf16[160,2560]{1,0:T(8,128)(2,1)S(1)}, bf16[160,2560]{1,0:T(8,128)(2,1)S(1)}, u32[]{:S(2)}, u32[]{:S(2)}) collective-permute-start(bf16[160,2560]{1,0:T(8,128)(2,1)S(1)} %arrive.2.refs_1_.refs_2_), channel_id=1, source_target_pairs={{0,1},{1,0},{2,3},{3,2},{4,5},{5,4},{6,7},{7,6},{8,9},{9,8},{10,11... | collective-permute-start | bytes 2457608 | tf_op jit(solution)/shard_map/second/ppermute | solution.py:40
  42.7 20.1 %collective-permute-start.7 = (bf16[160,2560]{1,0:T(8,128)(2,1)}, bf16[160,2560]{1,0:T(8,128)(2,1)S(1)}, u32[]{:S(2)}, u32[]{:S(2)}) collective-permute-start(bf16[160,2560]{1,0:T(8,128)(2,1)} %collective-permute-done.2.ax), channel_id=1, source_target_pairs={{0,6},{1,7},{2,0},{3,1},{4,2},{5,3},{6,4},{7,5},{8,14},{9,15},{10,... | collective-permute-start | bytes 2457608 | tf_op jit(solution)/shard_map/second/ppermute | solution.py:35
  54.9 13.3 %collective-permute-start.11 = (bf16[64,2560]{1,0:T(8,128)(2,1)S(1)}, bf16[64,2560]{1,0:T(8,128)(2,1)S(1)}, u32[]{:S(2)}, u32[]{:S(2)}) collective-permute-start(bf16[64,2560]{1,0:T(8,128)(2,1)S(1)} %cut_b1.1), channel_id=1, source_target_pairs={{0,1},{1,0},{2,3},{3,2},{4,5},{5,4},{6,7},{7,6},{8,9},{9,8},{10,11... | collective-permute-start | bytes 983048 | tf_op jit(solution)/shard_map/third/ppermute | solution.py:40
  59.8 8.4 %collective-permute-start.12 = (bf16[48,2560]{1,0:T(8,128)(2,1)S(1)}, bf16[48,2560]{1,0:T(8,128)(2,1)S(1)}, u32[]{:S(2)}, u32[]{:S(2)}) collective-permute-start(bf16[48,2560]{1,0:T(8,128)(2,1)S(1)} %cut_b2.1), channel_id=1, source_target_pairs={{0,8},{1,9},{2,10},{3,11},{4,12},{5,13},{6,14},{7,15},{8,16},{9,17... | collective-permute-start | bytes 737288 | tf_op jit(solution)/shard_map/third/ppermute | solution.py:30
  60.1 8.0 %collective-permute-start.13 = (bf16[48,2560]{1,0:T(8,128)(2,1)S(1)}, bf16[48,2560]{1,0:T(8,128)(2,1)S(1)}, u32[]{:S(2)}, u32[]{:S(2)}) collective-permute-start(bf16[48,2560]{1,0:T(8,128)(2,1)S(1)} %cut_b3.1), channel_id=1, source_target_pairs={{0,24},{1,25},{2,26},{3,27},{4,28},{5,29},{6,30},{7,31},{8,0},{9,1... | collective-permute-start | bytes 737288 | tf_op jit(solution)/shard_map/third/ppermute | solution.py:30
  68.2 32.4 %copy-start = (f32[1000]{0:T(1024)S(1)}, f32[1000]{0:T(1024)}, u32[]{:S(2)}) copy-start(f32[1000]{0:T(1024)} %occ.1) | copy-start | bytes 12004
  68.2 32.4 %copy-start.1 = (s32[2]{0:T(128)S(1)}, s32[2]{0:T(128)}, u32[]{:S(2)}) copy-start(s32[2]{0:T(128)} %chosen.1) | copy-start | bytes 28
  69.4 2.4 %collective-permute-start.14 = (bf16[640,640]{1,0:T(8,128)(2,1)S(1)}, bf16[640,640]{1,0:T(8,128)(2,1)S(1)}, u32[]{:S(2)}, u32[]{:S(2)}) collective-permute-start(bf16[640,640]{1,0:T(8,128)(2,1)S(1)} %get-tuple-element.50), channel_id=1, source_target_pairs={{0,32},{32,0},{64,96},{96,64},{128,160},{160,128},{192,224},{224,1... | collective-permute-start | bytes 2457608 | tf_op jit(solution)/shard_map/core/ppermute | solution.py:44
  72.0 22.3 %collective-permute-start.15 = (bf16[160,640]{1,0:T(8,128)(2,1)S(1)}, bf16[160,640]{1,0:T(8,128)(2,1)S(1)}, u32[]{:S(2)}, u32[]{:S(2)}) collective-permute-start(bf16[160,640]{1,0:T(8,128)(2,1)S(1)} %get-tuple-element.52), channel_id=1, source_target_pairs={{0,128},{32,160},{64,192},{96,224},{128,0},{160,32},{192,64},{224,... | collective-permute-start | bytes 614408 | tf_op jit(solution)/shard_map/shares/ppermute | solution.py:48
  84.1 15.8 %collective-permute-start.16 = (bf16[160,640]{1,0:T(8,128)(2,1)S(1)}, bf16[160,640]{1,0:T(8,128)(2,1)S(1)}, u32[]{:S(2)}, u32[]{:S(2)}) collective-permute-start(bf16[160,640]{1,0:T(8,128)(2,1)S(1)} %get-tuple-element.53), channel_id=1, source_target_pairs={{0,64},{32,96},{64,128},{96,160},{128,192},{160,224},{192,0},{224,... | collective-permute-start | bytes 614408 | tf_op jit(solution)/shard_map/shares/ppermute | solution.py:48
  84.1 16.4 %collective-permute-start.17 = (bf16[160,640]{1,0:T(8,128)(2,1)S(1)}, bf16[160,640]{1,0:T(8,128)(2,1)S(1)}, u32[]{:S(2)}, u32[]{:S(2)}) collective-permute-start(bf16[160,640]{1,0:T(8,128)(2,1)S(1)} %get-tuple-element.54), channel_id=1, source_target_pairs={{0,192},{32,224},{64,0},{96,32},{128,64},{160,96},{192,128},{224,1... | collective-permute-start | bytes 614408 | tf_op jit(solution)/shard_map/shares/ppermute | solution.py:48
  101.4 8.5 %collective-permute-start.27 = (bf16[80,640]{1,0:T(8,128)(2,1)S(1)}, bf16[80,640]{1,0:T(8,128)(2,1)S(1)}, u32[]{:S(2)}, u32[]{:S(2)}) collective-permute-start(bf16[80,640]{1,0:T(8,128)(2,1)S(1)} %get-tuple-element.57.refs_0_), channel_id=1, source_target_pairs={{0,192},{32,224},{64,0},{96,32},{128,64},{160,96},{192,128},{224,1... | collective-permute-start | bytes 307208 | tf_op jit(solution)/shard_map/spread_0/ppermute | solution.py:48
  102.9 7.6 %collective-permute-start.26 = (bf16[80,640]{1,0:T(8,128)(2,1)S(1)}, bf16[80,640]{1,0:T(8,128)(2,1)S(1)}, u32[]{:S(2)}, u32[]{:S(2)}) collective-permute-start(bf16[80,640]{1,0:T(8,128)(2,1)S(1)} %get-tuple-element.57.refs_0_), channel_id=1, source_target_pairs={{0,128},{32,160},{64,192},{96,224},{128,0},{160,32},{192,64},{224,... | collective-permute-start | bytes 307208 | tf_op jit(solution)/shard_map/spread_0/ppermute | solution.py:48
  106.7 9.0 %collective-permute-start.25 = (bf16[80,640]{1,0:T(8,128)(2,1)S(1)}, bf16[80,640]{1,0:T(8,128)(2,1)S(1)}, u32[]{:S(2)}, u32[]{:S(2)}) collective-permute-start(bf16[80,640]{1,0:T(8,128)(2,1)S(1)} %get-tuple-element.57.refs_0_), channel_id=1, source_target_pairs={{0,64},{32,96},{64,128},{96,160},{128,192},{160,224},{192,0},{224,... | collective-permute-start | bytes 307208 | tf_op jit(solution)/shard_map/spread_0/ppermute | solution.py:48
  107.0 9.3 %collective-permute-start.28 = (bf16[80,640]{1,0:T(8,128)(2,1)S(1)}, bf16[80,640]{1,0:T(8,128)(2,1)S(1)}, u32[]{:S(2)}, u32[]{:S(2)}) collective-permute-start(bf16[80,640]{1,0:T(8,128)(2,1)S(1)} %get-tuple-element.57.refs_0_), channel_id=1, source_target_pairs={{0,32},{32,0},{64,96},{96,64},{128,160},{160,128},{192,224},{224,1... | collective-permute-start | bytes 307208 | tf_op jit(solution)/shard_map/other_0/ppermute | solution.py:44
  109.9 6.4 %collective-permute-start.31 = (bf16[80,640]{1,0:T(8,128)(2,1)S(1)}, bf16[80,640]{1,0:T(8,128)(2,1)S(1)}, u32[]{:S(2)}, u32[]{:S(2)}) collective-permute-start(bf16[80,640]{1,0:T(8,128)(2,1)S(1)} %collective-permute-done.27.refs_3_), channel_id=1, source_target_pairs={{0,32},{32,0},{64,96},{96,64},{128,160},{160,128},{192,224},{224,1... | collective-permute-start | bytes 307208 | tf_op jit(solution)/shard_map/other_0/ppermute | solution.py:44
  110.6 6.1 %collective-permute-start.30 = (bf16[80,640]{1,0:T(8,128)(2,1)S(1)}, bf16[80,640]{1,0:T(8,128)(2,1)S(1)}, u32[]{:S(2)}, u32[]{:S(2)}) collective-permute-start(bf16[80,640]{1,0:T(8,128)(2,1)S(1)} %collective-permute-done.26.refs_2_), channel_id=1, source_target_pairs={{0,32},{32,0},{64,96},{96,64},{128,160},{160,128},{192,224},{224,1... | collective-permute-start | bytes 307208 | tf_op jit(solution)/shard_map/other_0/ppermute | solution.py:44
  115.7 1.5 collective-permute-start.29
  119.8 20.8 %collective-permute-start.32 = (bf16[160,2560]{1,0:T(8,128)(2,1)S(1)}, bf16[160,2560]{1,0:T(8,128)(2,1)S(1)}, u32[]{:S(2)}, u32[]{:S(2)}) collective-permute-start(bf16[160,2560]{1,0:T(8,128)(2,1)S(1)} %get-tuple-element.58), channel_id=1, source_target_pairs={{0,2},{1,3},{2,4},{3,5},{4,6},{5,7},{6,0},{7,1},{8,10},{9,11},{10,... | collective-permute-start | bytes 2457608 | tf_op jit(solution)/shard_map/out/ppermute | solution.py:35
  121.1 19.5 %collective-permute-start.33 = (bf16[160,2560]{1,0:T(8,128)(2,1)S(1)}, bf16[160,2560]{1,0:T(8,128)(2,1)S(1)}, u32[]{:S(2)}, u32[]{:S(2)}) collective-permute-start(bf16[160,2560]{1,0:T(8,128)(2,1)S(1)} %get-tuple-element.59), channel_id=1, source_target_pairs={{0,6},{1,7},{2,0},{3,1},{4,2},{5,3},{6,4},{7,5},{8,14},{9,15},{10,... | collective-permute-start | bytes 2457608 | tf_op jit(solution)/shard_map/out/ppermute | solution.py:35
  122.5 6.0 %collective-permute-start.21 = (bf16[80,640]{1,0:T(8,128)(2,1)S(1)}, bf16[80,640]{1,0:T(8,128)(2,1)S(1)}, u32[]{:S(2)}, u32[]{:S(2)}) collective-permute-start(bf16[80,640]{1,0:T(8,128)(2,1)S(1)} %get-tuple-element.55.refs_0_), channel_id=1, source_target_pairs={{0,32},{32,0},{64,96},{96,64},{128,160},{160,128},{192,224},{224,1... | collective-permute-start | bytes 307208 | tf_op jit(solution)/shard_map/other_1/ppermute | solution.py:44
  123.5 6.2 %collective-permute-start.20 = (bf16[80,640]{1,0:T(8,128)(2,1)S(1)}, bf16[80,640]{1,0:T(8,128)(2,1)S(1)}, u32[]{:S(2)}, u32[]{:S(2)}) collective-permute-start(bf16[80,640]{1,0:T(8,128)(2,1)S(1)} %get-tuple-element.55.refs_0_), channel_id=1, source_target_pairs={{0,192},{32,224},{64,0},{96,32},{128,64},{160,96},{192,128},{224,1... | collective-permute-start | bytes 307208 | tf_op jit(solution)/shard_map/spread_1/ppermute | solution.py:48
  125.5 8.1 %collective-permute-start.19 = (bf16[80,640]{1,0:T(8,128)(2,1)S(1)}, bf16[80,640]{1,0:T(8,128)(2,1)S(1)}, u32[]{:S(2)}, u32[]{:S(2)}) collective-permute-start(bf16[80,640]{1,0:T(8,128)(2,1)S(1)} %get-tuple-element.55.refs_0_), channel_id=1, source_target_pairs={{0,128},{32,160},{64,192},{96,224},{128,0},{160,32},{192,64},{224,... | collective-permute-start | bytes 307208 | tf_op jit(solution)/shard_map/spread_1/ppermute | solution.py:48
  128.6 9.1 %collective-permute-start.18 = (bf16[80,640]{1,0:T(8,128)(2,1)S(1)}, bf16[80,640]{1,0:T(8,128)(2,1)S(1)}, u32[]{:S(2)}, u32[]{:S(2)}) collective-permute-start(bf16[80,640]{1,0:T(8,128)(2,1)S(1)} %get-tuple-element.55.refs_0_), channel_id=1, source_target_pairs={{0,64},{32,96},{64,128},{96,160},{128,192},{160,224},{192,0},{224,... | collective-permute-start | bytes 307208 | tf_op jit(solution)/shard_map/spread_1/ppermute | solution.py:48
  129.6 8.1 %collective-permute-start.24 = (bf16[80,640]{1,0:T(8,128)(2,1)S(1)}, bf16[80,640]{1,0:T(8,128)(2,1)S(1)}, u32[]{:S(2)}, u32[]{:S(2)}) collective-permute-start(bf16[80,640]{1,0:T(8,128)(2,1)S(1)} %collective-permute-done.20.refs_3_), channel_id=1, source_target_pairs={{0,32},{32,0},{64,96},{96,64},{128,160},{160,128},{192,224},{224,1... | collective-permute-start | bytes 307208 | tf_op jit(solution)/shard_map/other_1/ppermute | solution.py:44
  133.6 5.1 %collective-permute-start.23 = (bf16[80,640]{1,0:T(8,128)(2,1)S(1)}, bf16[80,640]{1,0:T(8,128)(2,1)S(1)}, u32[]{:S(2)}, u32[]{:S(2)}) collective-permute-start(bf16[80,640]{1,0:T(8,128)(2,1)S(1)} %collective-permute-done.19.refs_2_), channel_id=1, source_target_pairs={{0,32},{32,0},{64,96},{96,64},{128,160},{160,128},{192,224},{224,1... | collective-permute-start | bytes 307208 | tf_op jit(solution)/shard_map/other_1/ppermute | solution.py:44
  137.7 1.3 collective-permute-start.22
  142.1 11.1 %collective-permute-start.34 = (bf16[80,2560]{1,0:T(8,128)(2,1)S(1)}, bf16[80,2560]{1,0:T(8,128)(2,1)S(1)}, u32[]{:S(2)}, u32[]{:S(2)}) collective-permute-start(bf16[80,2560]{1,0:T(8,128)(2,1)S(1)} %get-tuple-element.61), channel_id=1, source_target_pairs={{0,2},{1,3},{2,4},{3,5},{4,6},{5,7},{6,0},{7,1},{8,10},{9,11},{10,... | collective-permute-start | bytes 1228808 | tf_op jit(solution)/shard_map/out/ppermute | solution.py:35
  143.1 10.1 %collective-permute-start.35 = (bf16[80,2560]{1,0:T(8,128)(2,1)S(1)}, bf16[80,2560]{1,0:T(8,128)(2,1)S(1)}, u32[]{:S(2)}, u32[]{:S(2)}) collective-permute-start(bf16[80,2560]{1,0:T(8,128)(2,1)S(1)} %get-tuple-element.62), channel_id=1, source_target_pairs={{0,6},{1,7},{2,0},{3,1},{4,2},{5,3},{6,4},{7,5},{8,14},{9,15},{10,... | collective-permute-start | bytes 1228808 | tf_op jit(solution)/shard_map/out/ppermute | solution.py:35
